TPU v7x, 32 devices: a whole 2x2x4 slice. The times are simulated.
32 devices in a mesh: pb: 4 (over z), ctx: 8 (over y, x, core).
Axes of the slice: x: 2, y: 2, z: 4, core: 2. Of those that a mesh axis runs over, the one named last changes fastest.
Arguments:
- decoder_in: bfloat16 [4, 128, 768], P('pb'), may hold values from -6 to 6
- encoder_out: bfloat16 [4, 1920, 768], P('pb', 'ctx'), may hold values from -6 to 6
- self_projection: bfloat16 [768, 2304], P(('pb', 'ctx')), may hold values from -0.21875 to 0.21875
- self_output: bfloat16 [768, 768], P(('pb', 'ctx')), may hold values from -1 to 1
- cross_query: bfloat16 [768, 768], P(('pb', 'ctx')), may hold values from -0.21875 to 0.21875
- cross_memory: bfloat16 [768, 1536], P(('pb', 'ctx')), may hold values from -0.21875 to 0.21875
- cross_output: bfloat16 [768, 768], P(('pb', 'ctx')), may hold values from -6 to 6
- expand_weight: bfloat16 [768, 3072], P(('pb', 'ctx')), may hold values from -0.21875 to 0.21875
- contract_weight: bfloat16 [3072, 768], P(('pb', 'ctx')), may hold values from -0.109375 to 0.109375
- norm_gains: bfloat16 [3, 768], P(None, ('pb', 'ctx')), may hold values from 0.5 to 1.5
- bias_table: bfloat16 [32, 12], replicated, may hold values from -5 to 5
- bucket_index: int32 [128], replicated, may hold values from 0 to 31, as said below
- passage_mask: int32 [4, 1920], P('pb', 'ctx'), may hold values from 0 to 1, as said below
- target_length: int32 [4], P('pb'), may hold values from 32 to 128, as said below
- task_group: int32 [4], P('pb'), may hold values from 0 to 2
- cotangent: bfloat16 [4, 128, 768], P('pb'), may hold values from -6 to 6
Outputs:
- block_output: bfloat16 [4, 128, 768], P('pb')
- grad_decoder: bfloat16 [4, 128, 768], P('pb')
- grad_encoder: bfloat16 [4, 1920, 768], P('pb', 'ctx')
- grad_self_projection: float32 [768, 2304], P(('pb', 'ctx'))
- grad_self_output: float32 [768, 768], P(('pb', 'ctx'))
- grad_cross_query: float32 [768, 768], P(('pb', 'ctx'))
- grad_cross_memory: float32 [768, 1536], P(('pb', 'ctx'))
- grad_cross_output: float32 [768, 768], P(('pb', 'ctx'))
- grad_expand: float32 [768, 3072], P(('pb', 'ctx'))
- grad_contract: float32 [3072, 768], P(('pb', 'ctx'))
- grad_norm_gains: float32 [3, 768], P(None, ('pb', 'ctx'))
- grad_bias_table: float32 [32, 12], replicated
Inputs may be any that keep to these rules, and one draw needn't show every extreme that they name: bucket_index is 0 at offset 0, equals the offset below 16, never falls, and is 31 at offset 128 - 1. `passage_mask`: each passage of 384 rows has a leading run of 96 or more real rows and padding after it; the last passage of every query is whole. `target_length`: every query with an even index has length 128.
All inputs are finite; a program needn't handle non-finite values.
Results may differ from a plain program's by a relative error of at most 0.022.
Values may be sent and summed in bfloat16 or wider, within the bound.
No kernel may reach another device: no remote copies, remote signals or barrier semaphores. Data moves between devices by JAX's collectives and lax.ppermute only.
A program may use at most 192 MiB of HBM per device.

v0:
```python
import jax
import jax.numpy as jnp
from jax import lax
from jax.sharding import PartitionSpec as P


def product(left, right):
    return jnp.dot(left, right, preferred_element_type=jnp.float32)


def product_t(left, right):
    return lax.dot_general(
        left, right, (((1,), (1,)), ((), ())), preferred_element_type=jnp.float32
    )


def outer_sum(left, right):
    return lax.dot_general(
        left, right, (((0,), (0,)), ((), ())), preferred_element_type=jnp.float32
    )


def to_low(values):
    return values.astype(jnp.bfloat16)


def normalize(values, scale):
    factor = lax.rsqrt(jnp.mean(values * values, axis=-1, keepdims=True) + 1e-06)
    return (values * factor * scale, values * factor, factor)


def norm_back(grad, unit, factor, scale):
    scaled = grad * scale
    return factor * (scaled - unit * jnp.mean(scaled * unit, axis=-1, keepdims=True))


def gelu_tanh(values):
    return jax.nn.gelu(values, approximate=True)


def fetch(shards):
    return (
        lax.all_gather(shards[0], ("pb", "ctx"), axis=0, tiled=True),
        lax.all_gather(shards[1], ("pb", "ctx"), axis=0, tiled=True),
        lax.all_gather(shards[2], ("pb", "ctx"), axis=0, tiled=True),
        lax.all_gather(shards[3], ("pb", "ctx"), axis=0, tiled=True),
        lax.all_gather(shards[4], ("pb", "ctx"), axis=0, tiled=True),
        lax.all_gather(shards[5], ("pb", "ctx"), axis=0, tiled=True),
        lax.all_gather(shards[6], ("pb", "ctx"), axis=0, tiled=True),
        lax.all_gather(shards[7], ("pb", "ctx"), axis=1, tiled=True),
    )


def run_forward(params, decoder, encoder, allowed, visible, rel_bias):
    projection, self_out, cross_in, memory_in, cross_out, expand, contract, gains = params
    scale_gain = gains.astype(jnp.float32)
    count, length, width = decoder.shape
    heads = rel_bias.shape[0]
    head_dim = width // heads
    inverse = head_dim ** (-0.5)
    residual = decoder.astype(jnp.float32).reshape(count * length, width)
    normed_a, unit_a, factor_a = normalize(residual, scale_gain[0])
    normed_a = to_low(normed_a)
    joined = to_low(product(normed_a, projection)).reshape(count, length, 3, heads, head_dim)
    query_rows, key_rows, value_rows = (joined[:, :, 0], joined[:, :, 1], joined[:, :, 2])
    self_scores = (
        jnp.einsum("nihd,njhd->nhij", query_rows, key_rows, preferred_element_type=jnp.float32)
        * inverse
        + rel_bias[None]
    )
    self_probs = jax.nn.softmax(jnp.where(allowed, self_scores, -1000000000.0), axis=-1)
    self_mixed = jnp.einsum(
        "nhij,njhd->nihd", to_low(self_probs), value_rows, preferred_element_type=jnp.float32
    )
    self_mix = to_low(self_mixed.reshape(count * length, width))
    after_self = residual + product(self_mix, self_out)
    normed_b, unit_b, factor_b = normalize(after_self, scale_gain[1])
    normed_b = to_low(normed_b)
    cross_rows = to_low(product(normed_b, cross_in)).reshape(count, length, heads, head_dim)
    ctx_rows = encoder.shape[1]
    memory = to_low(product(encoder.reshape(count * ctx_rows, width), memory_in)).reshape(
        count, ctx_rows, 2, heads, head_dim
    )
    cross_keys, cross_vals = (memory[:, :, 0], memory[:, :, 1])
    cross_scores = (
        jnp.einsum("nihd,njhd->nhij", cross_rows, cross_keys, preferred_element_type=jnp.float32)
        * inverse
    )
    masked = jnp.where(visible, cross_scores, -1000000000.0)
    highest_score = lax.pmax(jnp.max(masked, axis=-1), "ctx")
    total = lax.psum(
        jnp.sum(jnp.where(visible, jnp.exp(masked - highest_score[..., None]), 0.0), axis=-1), "ctx"
    )
    cross_probs = (
        jnp.where(visible, jnp.exp(masked - highest_score[..., None]), 0.0) / total[..., None]
    )
    partial_mix = jnp.einsum(
        "nhij,njhd->nihd", to_low(cross_probs), cross_vals, preferred_element_type=jnp.float32
    )
    cross_mixed = lax.psum(partial_mix, "ctx")
    cross_mix = to_low(cross_mixed.reshape(count * length, width))
    after_cross = after_self + product(cross_mix, cross_out)
    normed_c, unit_c, factor_c = normalize(after_cross, scale_gain[2])
    normed_c = to_low(normed_c)
    hidden = product(normed_c, expand)
    active = to_low(gelu_tanh(hidden))
    output = after_cross + product(active, contract)
    saved = (
        normed_a,
        unit_a,
        factor_a,
        query_rows,
        key_rows,
        value_rows,
        self_probs,
        self_mix,
        normed_b,
        unit_b,
        factor_b,
        cross_rows,
        cross_keys,
        cross_vals,
        cross_probs,
        cross_mix,
        normed_c,
        unit_c,
        factor_c,
        hidden,
        active,
        scale_gain,
    )
    return (output, saved)


def body(
    decoder_in,
    encoder_out,
    self_projection,
    self_output,
    cross_query,
    cross_memory,
    cross_output,
    expand_weight,
    contract_weight,
    norm_gains,
    bias_table,
    bucket_index,
    passage_mask,
    target_length,
    task_group,
    cotangent,
):
    shards = (
        self_projection,
        self_output,
        cross_query,
        cross_memory,
        cross_output,
        expand_weight,
        contract_weight,
        norm_gains,
    )
    count, length, width = decoder_in.shape
    ctx_rows = encoder_out.shape[1]
    buckets, heads = bias_table.shape
    head_dim = width // heads
    inverse = head_dim ** (-0.5)
    positions = jnp.arange(length)
    offsets = jnp.clip(positions[:, None] - positions[None, :], 0, length - 1)
    pair_bucket = jnp.take(bucket_index, offsets.reshape(-1))
    one_hot = (pair_bucket[:, None] == jnp.arange(buckets)[None, :]).astype(jnp.bfloat16)
    rel_bias = product(one_hot, bias_table).T.reshape(heads, length, length)
    causal = positions[None, :] <= positions[:, None]
    allowed = (causal[None] & (positions[None, None, :] < target_length[:, None, None]))[:, None]
    visible = (passage_mask > 0)[:, None, None, :]
    params = fetch(shards)
    output, saved = run_forward(params, decoder_in, encoder_out, allowed, visible, rel_bias)
    params_back = fetch(shards)
    output_again, saved = run_forward(
        params_back, decoder_in, encoder_out, allowed, visible, rel_bias
    )
    projection, self_out, cross_in, memory_in, cross_out, expand, contract, gains = params_back
    (
        normed_a,
        unit_a,
        factor_a,
        query_rows,
        key_rows,
        value_rows,
        self_probs,
        self_mix,
        normed_b,
        unit_b,
        factor_b,
        cross_rows,
        cross_keys,
        cross_vals,
        cross_probs,
        cross_mix,
        normed_c,
        unit_c,
        factor_c,
        hidden,
        active,
        scale_gain,
    ) = saved
    rows_total = count * length
    share = rows_total // lax.axis_size("ctx")
    start = lax.axis_index("ctx") * share

    def sliced(values):
        return lax.dynamic_slice_in_dim(values, start, share, 0)

    task_scale = jnp.where(task_group == 0, 1.0, jnp.where(task_group == 1, 0.5, 2.0)).astype(
        jnp.float32
    )
    row_live = (positions[None, :] < target_length[:, None]).astype(jnp.float32)
    grad_out = (
        cotangent.astype(jnp.float32) * (task_scale[:, None] * row_live)[:, :, None]
    ).reshape(rows_total, width)
    low_out = to_low(grad_out)
    grad_active = product_t(low_out, contract)
    unused_value, gelu_pull = jax.vjp(gelu_tanh, hidden)
    grad_hidden = to_low(gelu_pull(grad_active)[0])
    grad_normed_c = product_t(grad_hidden, expand)
    gain_c = jnp.sum(sliced(grad_normed_c * unit_c), axis=0)
    grad_after_cross = grad_out + norm_back(grad_normed_c, unit_c, factor_c, scale_gain[2])
    low_cross = to_low(grad_after_cross)
    grad_mix = to_low(product_t(low_cross, cross_out)).reshape(count, length, heads, head_dim)
    grad_probs = jnp.einsum(
        "nihd,njhd->nhij", grad_mix, cross_vals, preferred_element_type=jnp.float32
    )
    row_dot = lax.psum(jnp.sum(grad_probs * cross_probs, axis=-1), "ctx")
    grad_scores = to_low(cross_probs * (grad_probs - row_dot[..., None]))
    partial_query = (
        jnp.einsum("nhij,njhd->nihd", grad_scores, cross_keys, preferred_element_type=jnp.float32)
        * inverse
    )
    grad_query = to_low(lax.psum(partial_query, "ctx")).reshape(rows_total, width)
    grad_key = (
        jnp.einsum("nhij,nihd->njhd", grad_scores, cross_rows, preferred_element_type=jnp.float32)
        * inverse
    )
    grad_value = jnp.einsum(
        "nhij,nihd->njhd", to_low(cross_probs), grad_mix, preferred_element_type=jnp.float32
    )
    grad_memory = to_low(jnp.stack([grad_key, grad_value], axis=2)).reshape(
        count * ctx_rows, 2 * width
    )
    encoder_rows = encoder_out.reshape(count * ctx_rows, width)
    grad_cross_memory = outer_sum(encoder_rows, grad_memory)
    grad_encoder = to_low(product_t(grad_memory, memory_in)).reshape(count, ctx_rows, width)
    grad_normed_b = product_t(grad_query, cross_in)
    gain_b = jnp.sum(sliced(grad_normed_b * unit_b), axis=0)
    grad_after_self = grad_after_cross + norm_back(grad_normed_b, unit_b, factor_b, scale_gain[1])
    low_self = to_low(grad_after_self)
    grad_self_mix = to_low(product_t(low_self, self_out)).reshape(count, length, heads, head_dim)
    grad_probs_self = jnp.einsum(
        "nihd,njhd->nhij", grad_self_mix, value_rows, preferred_element_type=jnp.float32
    )
    self_dot = jnp.sum(grad_probs_self * self_probs, axis=-1, keepdims=True)
    grad_scores_self = to_low(self_probs * (grad_probs_self - self_dot))
    pair_grad = jnp.sum(grad_scores_self.astype(jnp.float32), axis=0).reshape(
        heads, length * length
    )
    pair_count = length * length // lax.axis_size("ctx")
    pair_start = lax.axis_index("ctx") * pair_count
    pair_slice = lax.dynamic_slice_in_dim(pair_grad, pair_start, pair_count, 1)
    hot_slice = lax.dynamic_slice_in_dim(one_hot.astype(jnp.float32), pair_start, pair_count, 0)
    table_term = lax.dot_general(
        hot_slice,
        pair_slice,
        (((0,), (1,)), ((), ())),
        precision=lax.Precision.HIGHEST,
        preferred_element_type=jnp.float32,
    )
    grad_table = lax.psum(table_term, ("pb", "ctx"))
    grad_q = (
        jnp.einsum(
            "nhij,njhd->nihd", grad_scores_self, key_rows, preferred_element_type=jnp.float32
        )
        * inverse
    )
    grad_k = (
        jnp.einsum(
            "nhij,nihd->njhd", grad_scores_self, query_rows, preferred_element_type=jnp.float32
        )
        * inverse
    )
    grad_v = jnp.einsum(
        "nhij,nihd->njhd", to_low(self_probs), grad_self_mix, preferred_element_type=jnp.float32
    )
    grad_joined = to_low(jnp.stack([grad_q, grad_k, grad_v], axis=2)).reshape(rows_total, 3 * width)
    grad_normed_a = product_t(grad_joined, projection)
    gain_a = jnp.sum(sliced(grad_normed_a * unit_a), axis=0)
    grad_decoder = to_low(
        grad_after_self + norm_back(grad_normed_a, unit_a, factor_a, scale_gain[0])
    ).reshape(count, length, width)
    gain_grads = jnp.stack([gain_a, gain_b, gain_c])
    pairs = (
        (normed_a, grad_joined),
        (self_mix, low_self),
        (normed_b, grad_query),
        (cross_mix, low_cross),
        (normed_c, grad_hidden),
        (active, low_out),
    )
    partials = tuple((outer_sum(sliced(left), sliced(right)) for left, right in pairs))
    summed = (
        lax.psum_scatter(partials[0], ("pb", "ctx"), scatter_dimension=0, tiled=True),
        lax.psum_scatter(partials[1], ("pb", "ctx"), scatter_dimension=0, tiled=True),
        lax.psum_scatter(partials[2], ("pb", "ctx"), scatter_dimension=0, tiled=True),
        lax.psum_scatter(grad_cross_memory, ("pb", "ctx"), scatter_dimension=0, tiled=True),
        lax.psum_scatter(partials[3], ("pb", "ctx"), scatter_dimension=0, tiled=True),
        lax.psum_scatter(partials[4], ("pb", "ctx"), scatter_dimension=0, tiled=True),
        lax.psum_scatter(partials[5], ("pb", "ctx"), scatter_dimension=0, tiled=True),
        lax.psum_scatter(gain_grads, ("pb", "ctx"), scatter_dimension=1, tiled=True),
    )
    block_output = to_low(output).reshape(count, length, width)
    return (
        block_output,
        grad_decoder,
        grad_encoder,
        summed[0],
        summed[1],
        summed[2],
        summed[3],
        summed[4],
        summed[5],
        summed[6],
        summed[7],
        grad_table,
    )


def solution(mesh):
    return jax.shard_map(
        body,
        mesh=mesh,
        in_specs=(
            P("pb", None, None),
            P("pb", "ctx", None),
            P(("pb", "ctx"), None),
            P(("pb", "ctx"), None),
            P(("pb", "ctx"), None),
            P(("pb", "ctx"), None),
            P(("pb", "ctx"), None),
            P(("pb", "ctx"), None),
            P(("pb", "ctx"), None),
            P(None, ("pb", "ctx")),
            P(),
            P(),
            P("pb", "ctx"),
            P("pb"),
            P("pb"),
            P("pb", None, None),
        ),
        out_specs=(
            P("pb", None, None),
            P("pb", None, None),
            P("pb", "ctx", None),
            P(("pb", "ctx"), None),
            P(("pb", "ctx"), None),
            P(("pb", "ctx"), None),
            P(("pb", "ctx"), None),
            P(("pb", "ctx"), None),
            P(("pb", "ctx"), None),
            P(("pb", "ctx"), None),
            P(None, ("pb", "ctx")),
            P(),
        ),
        check_vma=False,
    )
```

profile of v0, /device:TPU:0, one launch (start us, length us, event | category | flops | bytes accessed | tf_op | source)
XLA Modules:
  0.0 1325.2 jit_solution(8225887909573453328)
XLA Ops:
  12.0 43.5 %all-gather = bf16[32,24,3]{1,2,0:T(4,128)(2,1)S(1)} all-gather(bf16[1,24,3]{1,2,0:T(4,128)(2,1)} %bitcast.203), channel_id=1, replica_groups=mesh['pb'=4,'ctx'=8] {'pb','ctx'}, dimensions={0}, use_global_device_ids=true | all-gather | bytes 4752 | tf_op jit(solution)/shard_map/all_gather | solution.py:50
  55.9 97.2 %gather_fusion = s32[16384]{0:T(1024)S(1)} fusion(s32[128]{0:T(128)S(1)} %copy-done.1, s32[16384]{0:T(1024)S(1)} %broadcast_clamp_fusion), kind=kCustom, calls=%fused_computation | custom fusion | bytes 196608 | tf_op jit(solution)/shard_map/jit(_take)/gather | solution.py:170
  160.4 2.7 convolution_convert_fusion
  165.2 23.4 %all-gather.11.cloned.1.call-done = bf16[768,768]{1,0:T(8,128)(2,1)} async-done(((bf16[24,768]{1,0:T(8,128)(2,1)}), bf16[768,768]{1,0:T(8,128)(2,1)}) %all-gather.11.cloned.1.call-update) | async-done | bytes 1179664 | tf_op jit(solution)/shard_map/all_gather | solution.py:44
  190.5 53.9 %all-gather.15.cloned.1.call-done = bf16[768,768]{1,0:T(8,128)(2,1)} async-done(((bf16[24,768]{1,0:T(8,128)(2,1)}), bf16[768,768]{1,0:T(8,128)(2,1)}) %all-gather.15.cloned.1.call-update) | async-done | bytes 1179664 | tf_op jit(solution)/shard_map/all_gather | solution.py:45
  247.7 13.4 %pmax.6 = f32[12,128]{1,0:T(8,128)S(1)} all-reduce(f32[12,128]{1,0:T(8,128)S(1)} %get-tuple-element.93), channel_id=1, replica_groups=mesh['pb'=4,'ctx'=8] {'ctx'}, use_global_device_ids=true, to_apply=%region_5.6 | all-reduce | flops 1536 | bytes 12288 | tf_op jit(solution)/shard_map/pmax | solution.py:90
  261.4 12.2 psum.34
  275.8 28.6 %all-reduce.4 = bf16[1,128,12,64]{1,3,2,0:T(8,128)(2,1)S(1)} all-reduce(f32[1,128,12,64]{1,3,2,0:T(8,128)} %convolution_bitcast_fusion.2), channel_id=1, replica_groups=mesh['pb'=4,'ctx'=8] {'ctx'}, use_global_device_ids=true, to_apply=%region_8.9 | all-reduce | flops 98304 | bytes 589824 | tf_op jit(solution)/shard_map/psum | solution.py:100
  307.8 58.0 %all-gather.21.cloned.1.call-done = bf16[3072,768]{1,0:T(8,128)(2,1)} async-done(((bf16[96,768]{1,0:T(8,128)(2,1)}), bf16[3072,768]{1,0:T(8,128)(2,1)}) %all-gather.21.cloned.1.call-update) | async-done | bytes 4718608 | tf_op jit(solution)/shard_map/all_gather | solution.py:49
  365.8 5.1 fusion.73
  370.9 60.2 %all-gather.19.cloned.1.call-done = bf16[768,3072]{1,0:T(8,128)(2,1)} async-done(((bf16[24,3072]{1,0:T(8,128)(2,1)}), bf16[768,3072]{1,0:T(8,128)(2,1)}) %all-gather.19.cloned.1.call-update) | async-done | bytes 4718608 | tf_op jit(solution)/shard_map/all_gather | solution.py:48
  431.1 5.8 fusion.7
  441.0 2.7 multiply_reduce_fusion
  443.7 13.4 %psum.43 = f32[12,128]{1,0:T(8,128)S(1)} all-reduce(f32[12,128]{1,0:T(8,128)S(1)} %get-tuple-element.99), channel_id=1, replica_groups=mesh['pb'=4,'ctx'=8] {'ctx'}, use_global_device_ids=true, to_apply=%region_12.13 | all-reduce | flops 1536 | bytes 12288 | tf_op jit(solution)/shard_map/psum | solution.py:233
  460.3 27.8 %all-reduce.5 = bf16[1,128,12,64]{1,3,2,0:T(8,128)(2,1)} all-reduce(f32[1,128,12,64]{1,3,2,0:T(8,128)} %fusion.15), channel_id=1, replica_groups=mesh['pb'=4,'ctx'=8] {'ctx'}, use_global_device_ids=true, to_apply=%region_13.14 | all-reduce | flops 98304 | bytes 589824 | tf_op jit(solution)/shard_map/psum | solution.py:239
  488.0 2.9 fusion.37
  491.0 2.6 fusion.35
  504.1 2.9 convolution_bitcast_fusion
  507.0 6.1 copy.101
  519.4 4.8 fusion.24
  524.3 6.0 fusion.46
  530.3 6.0 fusion.44
  537.7 3.7 multiply_reduce_fusion.2
  545.4 40.3 %all-reduce.1 = (f32[3,768]{1,0:T(4,128)S(1)}, f32[32,12]{0,1:T(8,128)}) all-reduce(f32[3,768]{1,0:T(4,128)S(1)} %pad_maximum_fusion.1, f32[32,12]{0,1:T(8,128)S(1)} %fusion.32), channel_id=9, replica_groups=mesh['pb'=4,'ctx'=8] {'pb','ctx'}, use_global_device_ids=true, to_apply=%region_27.28.clone | all-reduce | flops 2688 | bytes 21504
  586.4 3.3 fusion.16
  589.7 3.8 fusion.23
  593.6 100.6 %reduce-scatter.17.cloned.1.call-done = f32[24,768]{1,0:T(8,128)} async-done(((f32[768,768]{1,0:T(8,128)}), f32[24,768]{1,0:T(8,128)}) %reduce-scatter.17.cloned.1.call-update) | async-done | bytes 73744 | tf_op jit(solution)/shard_map/reduce_scatter | solution.py:314
  694.1 103.8 %reduce-scatter.13.cloned.1.call-done = f32[24,768]{1,0:T(8,128)} async-done(((f32[768,768]{1,0:T(8,128)}), f32[24,768]{1,0:T(8,128)}) %reduce-scatter.13.cloned.1.call-update) | async-done | bytes 73744 | tf_op jit(solution)/shard_map/reduce_scatter | solution.py:311
  797.9 113.0 %reduce-scatter.23.cloned.1.call-done = f32[24,1536]{1,0:T(8,128)} async-done(((f32[768,1536]{1,0:T(8,128)}), f32[24,1536]{1,0:T(8,128)}) %reduce-scatter.23.cloned.1.call-update) | async-done | bytes 147472
  910.9 124.4 %reduce-scatter.11.cloned.1.call-done = f32[24,2304]{1,0:T(8,128)} async-done(((f32[768,2304]{1,0:T(8,128)}), f32[24,2304]{1,0:T(8,128)}) %reduce-scatter.11.cloned.1.call-update) | async-done | bytes 221200 | tf_op jit(solution)/shard_map/reduce_scatter | solution.py:310
  1035.4 142.2 %reduce-scatter.19.cloned.1.call-done = f32[24,3072]{1,0:T(8,128)} async-done(((f32[768,3072]{1,0:T(8,128)}), f32[24,3072]{1,0:T(8,128)}) %reduce-scatter.19.cloned.1.call-update) | async-done | bytes 294928 | tf_op jit(solution)/shard_map/reduce_scatter | solution.py:315
  1177.6 141.1 %reduce-scatter.21.cloned.1.call-done = f32[96,768]{1,0:T(8,128)} async-done(((f32[3072,768]{1,0:T(8,128)}), f32[96,768]{1,0:T(8,128)}) %reduce-scatter.21.cloned.1.call-update) | async-done | bytes 294928 | tf_op jit(solution)/shard_map/reduce_scatter | solution.py:316
  (178 shorter events, 53.9 us)
Async XLA Ops:
  7.2 149.6 %copy-start = (bf16[1,240,768]{2,1,0:T(8,128)(2,1)S(1)}, bf16[1,240,768]{2,1,0:T(8,128)(2,1)}, u32[]{:S(2)}) copy-start(bf16[1,240,768]{2,1,0:T(8,128)(2,1)} %param.17) | copy-start | bytes 1105924
  7.2 48.7 %copy-start.1 = (s32[128]{0:T(128)S(1)}, s32[128]{0:T(128)}, u32[]{:S(2)}) copy-start(s32[128]{0:T(128)} %param.27) | copy-start | bytes 1540
  7.2 149.5 %all-gather.13.cloned.1.call-start = ((), (), s32[]{:S(2)}) async-start(), calls=%async_computation.9 | async-start | bytes 2433024 | tf_op jit(solution)/shard_map/all_gather | solution.py:46
  7.9 152.4 %all-gather.9.cloned.1.call-start = ((), (), s32[]{:S(2)}) async-start(), calls=%async_computation.7 | async-start | bytes 3649536 | tf_op jit(solution)/shard_map/all_gather | solution.py:43
  8.7 179.9 %all-gather.11.cloned.1.call-start = ((), (), s32[]{:S(2)}) async-start(), calls=%async_computation.8 | async-start | bytes 1216512 | tf_op jit(solution)/shard_map/all_gather | solution.py:44
  9.4 234.9 %all-gather.15.cloned.1.call-start = ((), (), s32[]{:S(2)}) async-start(), calls=%async_computation.10 | async-start | bytes 1216512 | tf_op jit(solution)/shard_map/all_gather | solution.py:45
  10.0 294.4 %all-gather.17.cloned.1.call-start = ((), (), s32[]{:S(2)}) async-start(), calls=%async_computation.11 | async-start | bytes 1216512 | tf_op jit(solution)/shard_map/all_gather | solution.py:47
  10.6 355.2 %all-gather.21.cloned.1.call-start = ((), (), s32[]{:S(2)}) async-start(), calls=%async_computation.13 | async-start | bytes 4866048 | tf_op jit(solution)/shard_map/all_gather | solution.py:49
  11.2 420.0 %all-gather.19.cloned.1.call-start = ((), (), s32[]{:S(2)}) async-start(), calls=%async_computation.12 | async-start | bytes 4866048 | tf_op jit(solution)/shard_map/all_gather | solution.py:48
  11.9 581.7 %reduce-scatter.15.cloned.1.call-start = ((), (), s32[]{:S(2)}) async-start(), calls=%async_computation.16 | async-start | bytes 2433024 | tf_op jit(solution)/shard_map/reduce_scatter | solution.py:312
  55.9 97.3 %copy-start.34 = (bf16[32,12]{0,1:T(8,128)(2,1)S(1)}, bf16[32,12]{0,1:T(8,128)(2,1)}, u32[]{:S(2)}) copy-start(bf16[32,12]{0,1:T(8,128)(2,1)} %param.26) | copy-start | bytes 2308
  156.7 3.7 copy-start.24
  165.2 25.1 %copy-start.29 = (bf16[12,64,128]{2,1,0:T(8,128)(2,1)}, bf16[12,64,128]{2,1,0:T(8,128)(2,1)S(1)}, u32[]{:S(2)}) copy-start(bf16[12,64,128]{2,1,0:T(8,128)(2,1)S(1)} %convolution_convert_fusion.7) | copy-start | bytes 589828
  190.4 53.9 %copy-start.25 = (bf16[128,768]{1,0:T(8,128)(2,1)}, bf16[128,768]{1,0:T(8,128)(2,1)S(1)}, u32[]{:S(2)}) copy-start(bf16[128,768]{1,0:T(8,128)(2,1)S(1)} %get-tuple-element.83) | copy-start | bytes 589828
  246.1 15.2 %copy-start.17 = (bf16[128,768]{0,1:T(8,128)(2,1)}, bf16[128,768]{0,1:T(8,128)(2,1)S(1)}, u32[]{:S(2)}) copy-start(bf16[128,768]{0,1:T(8,128)(2,1)S(1)} %copy.89) | copy-start | bytes 589828
  304.4 61.4 %copy-start.23 = (bf16[128,768]{1,0:T(8,128)(2,1)S(1)}, bf16[128,768]{1,0:T(8,128)(2,1)}, u32[]{:S(2)}) copy-start(bf16[128,768]{1,0:T(8,128)(2,1)} %bitcast_convert_fusion) | copy-start | bytes 589828
  307.8 131.0 %copy-start.6 = (f32[128,768]{1,0:T(8,128)}, f32[128,768]{1,0:T(8,128)S(1)}, u32[]{:S(2)}) copy-start(f32[128,768]{1,0:T(8,128)S(1)} %get-tuple-element.82) | copy-start | bytes 1179652
  431.1 5.8 copy-start.3
  439.7 4.0 copy-start.28
  441.0 2.7 copy-start.33
  457.1 2.0 copy-start.11
  491.0 203.1 %reduce-scatter.17.cloned.1.call-start = ((), (), s32[]{:S(2)}) async-start(), calls=%async_computation.17 | async-start | bytes 2433024 | tf_op jit(solution)/shard_map/reduce_scatter | solution.py:314
  493.7 304.2 %reduce-scatter.13.cloned.1.call-start = ((), (), s32[]{:S(2)}) async-start(), calls=%async_computation.15 | async-start | bytes 2433024 | tf_op jit(solution)/shard_map/reduce_scatter | solution.py:311
  493.8 3.6 copy-start.20
  494.6 4.3 copy-start.30
  500.9 410.0 %reduce-scatter.23.cloned.1.call-start = ((), (), s32[]{:S(2)}) async-start(), calls=%async_computation.20 | async-start | bytes 4866048
  513.2 522.2 %reduce-scatter.11.cloned.1.call-start = ((), (), s32[]{:S(2)}) async-start(), calls=%async_computation.14 | async-start | bytes 7299072 | tf_op jit(solution)/shard_map/reduce_scatter | solution.py:310
  524.2 653.3 %reduce-scatter.19.cloned.1.call-start = ((), (), s32[]{:S(2)}) async-start(), calls=%async_computation.18 | async-start | bytes 9732096 | tf_op jit(solution)/shard_map/reduce_scatter | solution.py:315
  530.3 788.4 %reduce-scatter.21.cloned.1.call-start = ((), (), s32[]{:S(2)}) async-start(), calls=%async_computation.19 | async-start | bytes 9732096 | tf_op jit(solution)/shard_map/reduce_scatter | solution.py:316
  537.7 3.7 copy-start.19
  586.4 3.3 copy-start.8
  586.4 3.3 copy-start.21
  (18 other events, 24.7 us)
Sparse Core Ops, SparseCore 0:
  10.9 59.9 all-gather.12
  73.8 58.9 all-gather.8
  135.7 52.8 all-gather.10
  191.3 52.9 all-gather.14
  247.1 53.2 all-gather.16
  303.1 62.5 all-gather.20
  368.7 62.4 all-gather.18
  491.1 98.2 reduce-scatter.14
  596.1 98.0 reduce-scatter.16
  699.8 98.0 reduce-scatter.12
  804.9 105.9 reduce-scatter.22
  917.0 118.2 reduce-scatter.10
  1042.8 134.6 reduce-scatter.18
  1183.9 134.6 reduce-scatter.20
where the time goes:
time: 1330 us
  waiting for transfers between devices  925 us (70%)
  blocking collectives  179 us (13%)
  local copies, waits for them, and re-layouts  113 us (8%)
  matrix products  79.8 us (6%)
  between operations  16 us (1%)
    reduce_scatter x1, waiting for transfers between devices, body(): lax.psum_scatter(partials[4], ('pb', 'ctx'), scatter_dimension=0, tiled=T...  142 us
    reduce_scatter x1, waiting for transfers between devices, body(): lax.psum_scatter(partials[5], ('pb', 'ctx'), scatter_dimension=0, tiled=T...  141 us
    reduce_scatter x1, waiting for transfers between devices, body(): lax.psum_scatter(partials[0], ('pb', 'ctx'), scatter_dimension=0, tiled=T...  124 us
    unnamed x15, waiting for transfers between devices  117 us
    reduce_scatter x1, waiting for transfers between devices, body(): lax.psum_scatter(partials[1], ('pb', 'ctx'), scatter_dimension=0, tiled=T...  104 us
    reduce_scatter x1, waiting for transfers between devices, body(): lax.psum_scatter(partials[3], ('pb', 'ctx'), scatter_dimension=0, tiled=T...  101 us
    gather x1, local copies, waits for them, and re-layouts, body(): pair_bucket = jnp.take(bucket_index, offsets.reshape(-1))  97.2 us
    all_gather x1, waiting for transfers between devices, fetch(): lax.all_gather(shards[5], ('pb', 'ctx'), axis=0, tiled=True)  60.2 us
  transfers between devices with their start and end apart: 14, of which 10 were waited for; matrix products, arithmetic and copies ran while one was open for 14% of the time, Pallas kernels for 0%

commit v1 on v0

v1 whole, which is shorter than its diff:
```python
import jax
import jax.numpy as jnp
from jax import lax
from jax.experimental import pallas as pl
from jax.experimental.pallas import tpu as pltpu
from jax.sharding import PartitionSpec as P

LOW, FULL = jnp.bfloat16, jnp.float32
MASKED = -1000000000.0
EPS = 1e-06
VMEM_BYTES = 56 * 1024 * 1024
HEAD = 64


def dot(left, right, left_axis=1, right_axis=0):
    return lax.dot_general(
        left,
        right,
        (((left_axis,), (right_axis,)), ((), ())),
        preferred_element_type=FULL,
    )


def dot_t(left, right):
    return dot(left, right, 1, 1)


def outer_sum(left, right):
    return dot(left, right, 0, 0)


def rms_unit(values):
    factor = lax.rsqrt(jnp.mean(values * values, axis=-1, keepdims=True) + EPS)
    return values * factor, factor


def norm_back(grad, unit, factor, gain):
    scaled = grad * gain
    return factor * (scaled - unit * jnp.mean(scaled * unit, axis=-1, keepdims=True))


def call(kernel, outs, args, scalars=0):
    spaces = [pltpu.SMEM] * scalars + [pltpu.VMEM] * (len(args) - scalars)
    return pl.pallas_call(
        kernel,
        out_shape=[jax.ShapeDtypeStruct(shape, dtype) for shape, dtype in outs],
        in_specs=[pl.BlockSpec(memory_space=space) for space in spaces],
        out_specs=[pl.BlockSpec(memory_space=pltpu.VMEM) for _ in outs],
        compiler_params=pltpu.CompilerParams(vmem_limit_bytes=VMEM_BYTES),
    )(*args)


def swap_ctx(values, mask):
    size = lax.axis_size("ctx")
    return lax.ppermute(values, "ctx", [(i, i ^ mask) for i in range(size)])


def chip_bits():
    return [b for b in range(1, 16) if (1 << b) < lax.axis_size("ctx")]


def core_groups():
    size = lax.axis_size("ctx")
    return [list(range(core, size, 2)) for core in range(2)]


def exchange(values, axis, groups=None):
    return lax.all_to_all(values, axis, 0, 0, tiled=True, axis_index_groups=groups)


def from_all(values, axis):
    size = lax.axis_size(axis)
    return exchange(jnp.broadcast_to(values[None], (size,) + values.shape), axis)


def place(core, chip, sources, widths):
    pb, ctx = lax.axis_size("pb"), lax.axis_size("ctx")
    rows = sources[0][0].shape[1]
    counts = len(sources)

    def kernel(core_ref, chip_ref, *refs):
        outs = refs[counts:]
        for ref, (array, first, chip_flip, core_flip) in zip(refs, sources):
            for z in range(array.shape[0]):
                slot = (first + z) * ctx + 2 * (chip_ref[0] ^ chip_flip) + (core_ref[0] ^ core_flip)
                at = 0
                for out, width in zip(outs, widths):
                    out[slot] = ref[z, :, at : at + width]
                    at += width

    return call(
        kernel,
        [((pb * ctx, rows, width), LOW) for width in widths],
        [core[None], chip[None]] + [array for array, _, _, _ in sources],
        scalars=2,
    )


def gather_rows(core, chip, shards):
    pb, ctx = lax.axis_size("pb"), lax.axis_size("ctx")
    rows = shards[0].shape[0]
    if rows % 8 or ctx != 8 or pb % 2:
        return [lax.all_gather(s, ("pb", "ctx"), axis=0, tiled=True) for s in shards]
    joined = jnp.concatenate(shards, axis=1) if len(shards) > 1 else shards[0]
    own = from_all(joined, "pb")
    along_x, along_y = swap_ctx(own, 2), swap_ctx(own, 4)
    low = swap_ctx(along_x[: pb // 2], 4)
    high = swap_ctx(along_y[pb // 2 :], 2)
    sources = []
    for array, first, flip in (
        (own, 0, 0),
        (along_x, 0, 1),
        (along_y, 0, 2),
        (low, 0, 3),
        (high, pb // 2, 3),
    ):
        sources.append((array, first, flip, 0))
        sources.append((swap_ctx(array, 1), first, flip, 1))
    whole = place(core, chip, sources, [s.shape[1] for s in shards])
    return [w.reshape(pb * ctx * rows, w.shape[2]) for w in whole]


def halves(values, core):
    middle = values.shape[-1] // 2
    low, high = values[..., :middle], values[..., middle:]
    return jnp.where(core == 0, low, high), jnp.where(core == 0, high, low)


def join(mine, other, core):
    return jnp.where(
        core == 0,
        jnp.concatenate([mine, other], axis=-1),
        jnp.concatenate([other, mine], axis=-1),
    )


def sum_ctx(values, core):
    mine, other = halves(values, core)
    total = mine + swap_ctx(other.astype(LOW), 1).astype(FULL)
    for bit in chip_bits():
        sent = total.astype(LOW)
        total = sent.astype(FULL) + swap_ctx(sent, 1 << bit).astype(FULL)
    sent = total.astype(LOW)
    return join(sent, swap_ctx(sent, 1), core)


def to_owners(partial):
    return jnp.sum(exchange(partial.astype(LOW), "pb").astype(FULL), axis=0)


def lane_mask(values, side):
    lanes = lax.broadcasted_iota(jnp.int32, values.shape, 1)
    middle = values.shape[1] // 2
    keep = lanes < middle if side == 0 else lanes >= middle
    return jnp.where(keep, values, jnp.zeros_like(values))


def pick(low, high):
    lanes = lax.broadcasted_iota(jnp.int32, low.shape, 1)
    return jnp.where(lanes < low.shape[1] // 2, low, high)


def self_kernel(
    length, x, proj, self_out, cross_in, gains, table, p1, probs, mix, x1, h1, h2, cq
):
    rows, width = x.shape
    heads = probs.shape[0]
    pair = 2 * (width // heads)
    inverse = (width // heads) ** (-0.5)
    xf = x[...].astype(FULL)
    unit, _ = rms_unit(xf)
    h1[...] = (unit * gains[0:1, :]).astype(LOW)
    p1[...] = dot(h1[...], proj[...]).astype(LOW)
    row = lax.broadcasted_iota(jnp.int32, (rows, rows), 0)
    col = lax.broadcasted_iota(jnp.int32, (rows, rows), 1)
    allowed = (col <= row) & (col < length[0])
    for g in range(heads // 2):
        at = g * pair
        q = p1[:, at : at + pair]
        k = p1[:, width + at : width + at + pair]
        v = p1[:, 2 * width + at : 2 * width + at + pair]
        mixed = []
        for side in range(2):
            head = 2 * g + side
            bias = pltpu.roll(
                jnp.broadcast_to(table[head : head + 1, :], (rows, rows)),
                1,
                axis=1,
                stride=1,
                stride_axis=0,
            )
            scores = jnp.where(allowed, dot_t(lane_mask(q, side), k) * inverse + bias, MASKED)
            powers = jnp.exp(scores - jnp.max(scores, axis=-1, keepdims=True))
            prob = powers / jnp.sum(powers, axis=-1, keepdims=True)
            probs[head] = prob
            mixed.append(dot(prob.astype(LOW), v))
        mix[:, at : at + pair] = pick(*mixed).astype(LOW)
    after = xf + dot(mix[...], self_out[...])
    x1[...] = after
    unit, _ = rms_unit(after)
    h2[...] = (unit * gains[1:2, :]).astype(LOW)
    cq[...] = dot(h2[...], cross_in[...]).astype(LOW)


def split_three(values):
    high = values.astype(LOW)
    rest = values - high.astype(FULL)
    middle = rest.astype(LOW)
    return high, middle, (rest - middle.astype(FULL)).astype(LOW)


def pack_stats(tops, totals):
    rows = tops[0].shape[0]
    lanes = lax.broadcasted_iota(jnp.int32, (rows, 128), 1)
    columns = jnp.zeros((rows, 128), FULL)
    for index, column in enumerate(tops + totals):
        columns = jnp.where(lanes // 3 == index, column, columns)
    high, middle, low = (part.astype(FULL) for part in split_three(columns))
    kind = lanes % 3
    return jnp.where(kind == 0, high, jnp.where(kind == 1, middle, low)).astype(LOW)


def read_stats(packed, heads):
    values = packed.astype(FULL)
    columns = [
        values[:, 3 * i : 3 * i + 1] + values[:, 3 * i + 1 : 3 * i + 2] + values[:, 3 * i + 2 : 3 * i + 3]
        for i in range(2 * heads)
    ]
    return columns[:heads], columns[heads:]


def cross_kernel(core, cq, memory, visible, mine, other):
    rows, width = cq.shape
    half = width // 2
    heads = width // HEAD
    inverse = HEAD ** (-0.5)
    seen = visible[...] > 0
    tops, totals, mixes = [], [], []
    for g in range(heads // 2):
        at = g * 2 * HEAD
        q = cq[:, at : at + 2 * HEAD]
        k = memory[:, at : at + 2 * HEAD]
        v = memory[:, width + at : width + at + 2 * HEAD]
        mixed = []
        for side in range(2):
            scores = jnp.where(seen, dot_t(lane_mask(q, side), k) * inverse, MASKED)
            top = jnp.max(scores, axis=-1, keepdims=True)
            powers = jnp.where(seen, jnp.exp(scores - top), 0.0)
            tops.append(top)
            totals.append(jnp.sum(powers, axis=-1, keepdims=True))
            mixed.append(dot(powers.astype(LOW), v))
        mixes.append(pick(*mixed).astype(LOW))
    low = jnp.concatenate(mixes[: heads // 4], axis=1)
    high = jnp.concatenate(mixes[heads // 4 :], axis=1)
    stats = pack_stats(tops, totals)
    first = core[0] == 0
    mine[:, :half] = jnp.where(first, low, high)
    other[:, :half] = jnp.where(first, high, low)
    mine[:, half:] = stats
    other[:, half:] = stats


def spread(columns):
    rows = columns[0].shape[0]
    return jnp.concatenate(
        [
            pick(
                jnp.broadcast_to(columns[g], (rows, 2 * HEAD)),
                jnp.broadcast_to(columns[g + 1], (rows, 2 * HEAD)),
            )
            for g in range(0, len(columns), 2)
        ],
        axis=1,
    )


def merge(core, order, parts, heads, final):
    ways = len(parts)
    rows, columns = parts[0].shape
    half = columns - 128

    def kernel(core_ref, order_ref, *refs):
        packed = [ref[...] for ref in refs[:ways]]
        step = 1
        while step < ways:
            flip = (order_ref[0] & step) != 0
            packed = [jnp.where(flip, packed[i ^ step], packed[i]) for i in range(ways)]
            step *= 2
        stats = [read_stats(p[:, half:], heads) for p in packed]
        first = core_ref[0] == 0
        tops, totals, scales = [], [], []
        for h in range(heads):
            top = stats[0][0][h]
            for other in stats[1:]:
                top = jnp.maximum(top, other[0][h])
            scale = [jnp.exp(s[0][h] - top) for s in stats]
            terms = [s[1][h] * w for s, w in zip(stats, scale)]
            while len(terms) > 1:
                terms = [a + b for a, b in zip(terms[0::2], terms[1::2])]
            if final:
                scale = [w / terms[0] for w in scale]
            tops.append(top)
            totals.append(terms[0])
            scales.append(scale)
        terms = []
        for i in range(ways):
            mine = [
                jnp.where(first, scales[h][i], scales[h + heads // 2][i]) for h in range(heads // 2)
            ]
            terms.append(packed[i][:, :half].astype(FULL) * spread(mine))
        while len(terms) > 1:
            terms = [a + b for a, b in zip(terms[0::2], terms[1::2])]
        refs[ways][:, :half] = terms[0].astype(LOW)
        refs[ways][:, half:] = pack_stats(tops, totals)

    return call(
        kernel, [(parts[0].shape, LOW)], [core[None], order[None]] + list(parts), scalars=2
    )[0]


def gelu_parts(values):
    slope = (2.0 / jnp.pi) ** 0.5
    square = values * values
    bent = jnp.tanh(slope * (values + 0.044715 * values * square))
    active = 0.5 * values * (1.0 + bent)
    inner = slope * (1.0 + 3 * 0.044715 * square)
    return active, 0.5 * (1.0 + bent) + 0.5 * values * (1.0 - bent * bent) * inner


def task_rows(length, task, cot):
    rows = lax.broadcasted_iota(jnp.int32, cot.shape, 0)
    weight = jnp.where(task[0] == 0, 1.0, jnp.where(task[0] == 1, 0.5, 2.0)).astype(FULL)
    return jnp.where(rows < length[0], cot[...].astype(FULL) * weight, 0.0)


def feed_kernel(
    length,
    task,
    mix,
    x1,
    cross_out,
    gains,
    expand,
    contract,
    cot,
    x2,
    h3,
    active,
    low_out,
    grad_hidden,
    grad_h3,
    part_out,
):
    after = x1[...] + dot(mix[...], cross_out[...])
    x2[...] = after
    unit, _ = rms_unit(after)
    h3[...] = (unit * gains[2:3, :]).astype(LOW)
    hidden = dot(h3[...], expand[...])
    value, slope = gelu_parts(hidden)
    active[...] = value.astype(LOW)
    low_out[...] = task_rows(length, task, cot).astype(LOW)
    grad_active = dot_t(low_out[...], contract[...])
    grad_hidden[...] = (grad_active * slope).astype(LOW)
    grad_h3[...] = dot_t(grad_hidden[...], expand[...])
    part_out[...] = dot(active[...], contract[...])


def cross_back_kernel(
    length,
    task,
    grad_h3,
    x2,
    gains,
    cot,
    cross_out,
    cq,
    memory,
    visible,
    stats,
    mix,
    dx2,
    low_cross,
    grad_cq,
    grad_memory,
    gain_grad,
):
    rows, width = x2.shape
    heads = width // HEAD
    pair = 2 * HEAD
    inverse = HEAD ** (-0.5)
    unit, factor = rms_unit(x2[...])
    grad = grad_h3[...].astype(FULL)
    gain_grad[...] = jnp.sum(grad * unit, axis=0, keepdims=True)
    back = task_rows(length, task, cot) + norm_back(grad, unit, factor, gains[2:3, :])
    dx2[...] = back
    low_cross[...] = back.astype(LOW)
    grad_mix = dot_t(low_cross[...], cross_out[...]).astype(LOW)
    seen = visible[...] > 0
    tops, totals = read_stats(stats[...], heads)
    for g in range(heads // 2):
        at = g * pair
        q = cq[:, at : at + pair]
        k = memory[:, at : at + pair]
        v = memory[:, width + at : width + at + pair]
        do = grad_mix[:, at : at + pair]
        weighed = do.astype(FULL) * mix[:, at : at + pair].astype(FULL)
        queries, keys, values = [], [], []
        for side in range(2):
            head = 2 * g + side
            qs, ds = lane_mask(q, side), lane_mask(do, side)
            scores = dot_t(qs, k) * inverse
            scores = jnp.where(seen, scores, MASKED)
            prob = jnp.where(seen, jnp.exp(scores - tops[head]) / totals[head], 0.0)
            rho = jnp.sum(lane_mask(weighed, side), axis=-1, keepdims=True)
            grad_scores = (prob * (dot_t(ds, v) - rho)).astype(LOW)
            queries.append(dot(grad_scores, k))
            keys.append(outer_sum(grad_scores, qs))
            values.append(outer_sum(prob.astype(LOW), ds))
        grad_cq[:, at : at + pair] = pick(*queries) * inverse
        grad_memory[:, at : at + pair] = ((keys[0] + keys[1]) * inverse).astype(LOW)
        grad_memory[:, width + at : width + at + pair] = (values[0] + values[1]).astype(LOW)


def self_back_kernel(
    grad_cq,
    cross_in,
    x1,
    gains,
    dx2,
    self_out,
    p1,
    probs,
    x,
    proj,
    low_self,
    grad_p1,
    grad_x,
    gain_grads,
    diagonal,
):
    rows, width = x.shape
    heads = probs.shape[0]
    pair = 2 * (width // heads)
    inverse = (width // heads) ** (-0.5)
    grad = dot_t(grad_cq[...], cross_in[...])
    unit, factor = rms_unit(x1[...])
    gain_grads[1:2, :] = jnp.sum(grad * unit, axis=0, keepdims=True)
    dx1 = dx2[...] + norm_back(grad, unit, factor, gains[1:2, :])
    low_self[...] = dx1.astype(LOW)
    row = lax.broadcasted_iota(jnp.int32, (rows, rows), 0)
    col = lax.broadcasted_iota(jnp.int32, (rows, rows), 1)
    flip = jnp.where(row + col == rows - 1, 1.0, 0.0).astype(LOW)
    grad_mix = dot_t(low_self[...], self_out[...]).astype(LOW)
    for g in range(heads // 2):
        at = g * pair
        q = p1[:, at : at + pair]
        k = p1[:, width + at : width + at + pair]
        v = p1[:, 2 * width + at : 2 * width + at + pair]
        do = grad_mix[:, at : at + pair]
        queries, keys, values = [], [], []
        for side in range(2):
            head = 2 * g + side
            ds = lane_mask(do, side)
            prob = probs[head]
            grad_probs = dot_t(ds, v)
            rho = jnp.sum(prob * grad_probs, axis=-1, keepdims=True)
            grad_scores = (prob * (grad_probs - rho)).astype(LOW)
            turned = pltpu.roll(dot(flip, grad_scores), 0, axis=1, stride=1, stride_axis=0)
            diagonal[head : head + 1, :] = jnp.sum(turned, axis=0, keepdims=True)
            queries.append(dot(grad_scores, k))
            keys.append(outer_sum(grad_scores, lane_mask(q, side)))
            values.append(outer_sum(prob.astype(LOW), ds))
        grad_p1[:, at : at + pair] = (pick(*queries) * inverse).astype(LOW)
        grad_p1[:, width + at : width + at + pair] = ((keys[0] + keys[1]) * inverse).astype(LOW)
        grad_p1[:, 2 * width + at : 2 * width + at + pair] = (values[0] + values[1]).astype(LOW)
    grad = dot_t(grad_p1[...], proj[...])
    unit, factor = rms_unit(x[...].astype(FULL))
    gain_grads[0:1, :] = jnp.sum(grad * unit, axis=0, keepdims=True)
    grad_x[...] = (dx1 + norm_back(grad, unit, factor, gains[0:1, :])).astype(LOW)


def body(
    decoder_in,
    encoder_out,
    self_projection,
    self_output,
    cross_query,
    cross_memory,
    cross_output,
    expand_weight,
    contract_weight,
    norm_gains,
    bias_table,
    bucket_index,
    passage_mask,
    target_length,
    task_group,
    cotangent,
):
    pb, ctx = lax.axis_size("pb"), lax.axis_size("ctx")
    mine_pb, mine_ctx = lax.axis_index("pb"), lax.axis_index("ctx")
    core = (mine_ctx & 1).astype(jnp.int32)
    chip = (mine_ctx >> 1).astype(jnp.int32)
    rows, width = decoder_in.shape[1:]
    passage = encoder_out.shape[1]
    buckets, heads = bias_table.shape
    share = self_projection.shape[0]
    hidden = expand_weight.shape[1]
    slab = contract_weight.shape[0]
    x = decoder_in[0]
    e = encoder_out[0]
    cot = cotangent[0]

    gain_columns = jnp.pad(norm_gains.T, ((0, 0), (0, 128 - norm_gains.shape[0])))
    proj, gain_rows = gather_rows(core, chip, [self_projection, gain_columns])
    self_out, cross_in, cross_out = gather_rows(
        core, chip, [self_output, cross_query, cross_output]
    )
    (memory_in,) = gather_rows(core, chip, [cross_memory])
    mixed = expand_weight.reshape(share, pb, ctx, slab).transpose(2, 0, 1, 3)
    mixed = exchange(mixed.reshape(ctx, share, pb * slab), "ctx")
    expand = from_all(mixed.reshape(ctx * share, pb * slab), "pb").reshape(width, pb * slab)
    contract = from_all(contract_weight, "pb").reshape(pb * slab, width)
    gains = gain_rows[:, : norm_gains.shape[0]].astype(FULL).T

    backward_bucket = bucket_index[::-1]
    hot = (jnp.arange(buckets)[:, None] == backward_bucket[None, :]).astype(LOW)
    table = outer_sum(bias_table, hot)
    table = jnp.pad(table, ((0, 16 - heads % 16 if heads % 16 else 0), (0, 0)))

    p1, probs, mix1, x1, h1, h2, cq = call(
        self_kernel,
        [
            ((rows, 3 * width), LOW),
            ((heads, rows, rows), FULL),
            ((rows, width), LOW),
            ((rows, width), FULL),
            ((rows, width), LOW),
            ((rows, width), LOW),
            ((rows, width), LOW),
        ],
        [target_length, x, proj, self_out, cross_in, gains, table],
        scalars=1,
    )
    memory = dot(e, memory_in).astype(LOW)
    mine, other = call(
        cross_kernel,
        [((rows, width // 2 + 128), LOW)] * 2,
        [core[None], cq, memory, passage_mask],
        scalars=1,
    )
    part = merge(core, core, [mine, swap_ctx(other, 1)], heads, False)
    parts = [part] + [swap_ctx(part, mask) for mask in range(2, ctx, 2)]
    part = merge(core, chip, parts, heads, True)
    stats = part[:, width // 2 :]
    part = part[:, : width // 2]
    mix2 = join(part, swap_ctx(part, 1), core)

    x2, h3, active, low_out, grad_hidden, grad_h3, part_out = call(
        feed_kernel,
        [
            ((rows, width), FULL),
            ((rows, width), LOW),
            ((rows, pb * slab), LOW),
            ((rows, width), LOW),
            ((rows, pb * slab), LOW),
            ((rows, width), FULL),
            ((rows, width), FULL),
        ],
        [target_length, task_group, mix2, x1, cross_out, gains, expand, contract, cot],
        scalars=2,
    )
    grad_h3 = sum_ctx(grad_h3, core)
    block_output = (x2 + sum_ctx(part_out, core).astype(FULL)).astype(LOW)

    block = jnp.arange(pb) * (ctx * share) + mine_ctx * share
    chosen = (block[:, None] + jnp.arange(share)[None, :]).reshape(-1)
    choose = (jnp.arange(width)[:, None] == chosen[None, :]).astype(LOW)

    def owned(left, right):
        columns = dot(left, choose).astype(LOW)
        return to_owners(outer_sum(columns, right).reshape(pb, share, right.shape[1]))

    grad_contract = to_owners(outer_sum(active, low_out).reshape(pb, slab, width))
    every_hidden = from_all(grad_hidden, "ctx")
    columns = dot(h3, choose).astype(LOW)
    partial = jnp.einsum("nf,cnh->fch", columns, every_hidden, preferred_element_type=FULL)
    summed = to_owners(partial.reshape(pb, share, ctx * pb * slab))
    grad_expand = summed.reshape(share, ctx, pb, slab).transpose(0, 2, 1, 3)
    grad_expand = grad_expand.reshape(share, hidden)

    dx2, low_cross, grad_cq, grad_memory, gain_c = call(
        cross_back_kernel,
        [
            ((rows, width), FULL),
            ((rows, width), LOW),
            ((rows, width), FULL),
            ((passage, 2 * width), LOW),
            ((1, width), FULL),
        ],
        [
            target_length,
            task_group,
            grad_h3,
            x2,
            gains,
            cot,
            cross_out,
            cq,
            memory,
            passage_mask,
            stats,
            mix2,
        ],
        scalars=2,
    )
    grad_cq = sum_ctx(grad_cq, core)
    grad_cross_output = owned(mix2, low_cross)
    grad_encoder = dot_t(grad_memory, memory_in).astype(LOW)[None]
    partial = outer_sum(e, grad_memory).reshape(pb, ctx // 2, 2, share, 2 * width)
    kept = lax.dynamic_index_in_dim(partial, core, 2, False)
    sent = lax.dynamic_index_in_dim(partial, 1 - core, 2, False).astype(LOW)
    partial = (kept + swap_ctx(sent, 1).astype(FULL)).astype(LOW).transpose(1, 0, 2, 3)
    partial = jnp.sum(exchange(partial, "ctx", core_groups()).astype(FULL), axis=0)
    grad_cross_memory = to_owners(partial)

    low_self, grad_p1, grad_x, gain_ab, diagonal = call(
        self_back_kernel,
        [
            ((rows, width), LOW),
            ((rows, 3 * width), LOW),
            ((rows, width), LOW),
            ((2, width), FULL),
            ((heads, rows), FULL),
        ],
        [grad_cq, cross_in, x1, gains, dx2, self_out, p1, probs, x, proj],
    )
    grad_cross_query = owned(h2, grad_cq)
    grad_self_output = owned(mix1, low_self)
    grad_self_projection = owned(h1, grad_p1)
    gain_grads = jnp.concatenate([gain_ab, gain_c]).reshape(-1, pb, ctx, share)
    gain_grads = lax.dynamic_index_in_dim(gain_grads, mine_ctx, 2, False).transpose(1, 0, 2)
    grad_table = lax.dot_general(
        diagonal,
        hot.astype(FULL),
        (((1,), (1,)), ((), ())),
        precision=lax.Precision.HIGHEST,
        preferred_element_type=FULL,
    )
    small = jnp.concatenate(
        [
            jnp.pad(gain_grads, ((0, 0), (0, 0), (0, 128 - share))),
            jnp.broadcast_to(
                jnp.pad(grad_table, ((0, 0), (0, 128 - buckets)))[None], (pb, heads, 128)
            ),
        ],
        axis=1,
    )
    small = jnp.sum(exchange(small, "pb"), axis=0)
    grad_norm_gains = small[: gain_grads.shape[1], :share]
    grad_table = small[gain_grads.shape[1] :, :buckets].T
    return (
        block_output[None],
        grad_x[None],
        grad_encoder,
        grad_self_projection,
        grad_self_output,
        grad_cross_query,
        grad_cross_memory,
        grad_cross_output,
        grad_expand,
        grad_contract,
        grad_norm_gains,
        grad_table,
    )


def solution(mesh):
    both = ("pb", "ctx")
    return jax.shard_map(
        body,
        mesh=mesh,
        in_specs=(
            P("pb", None, None),
            P("pb", "ctx", None),
            P(both, None),
            P(both, None),
            P(both, None),
            P(both, None),
            P(both, None),
            P(both, None),
            P(both, None),
            P(None, both),
            P(),
            P(),
            P("pb", "ctx"),
            P("pb"),
            P("pb"),
            P("pb", None, None),
        ),
        out_specs=(
            P("pb", None, None),
            P("pb", None, None),
            P("pb", "ctx", None),
            P(both, None),
            P(both, None),
            P(both, None),
            P(both, None),
            P(both, None),
            P(both, None),
            P(both, None),
            P(None, both),
            P(),
        ),
        check_vma=False,
    )
```

time: 1330 us -> 351 us (0.26)
  waiting for transfers between devices: 925 us -> 128 us
  blocking collectives: 179 us -> 0 us
  starting transfers between devices: 0.77 us -> 95.3 us
  local copies, waits for them, and re-layouts: 113 us -> 29 us
  matrix products: 79.8 us -> 19 us
  Pallas kernels: 0 us -> 51 us
  between operations: 16 us -> 2.59 us
    reduce_scatter x6 -> x0, waiting for transfers between devices: 612 us -> none  [the longest x1 142 us: body(): lax.psum_scatter(partials[4], ('pb', 'ctx'), scatter_dimension=0, tiled=T...]
    all_gather x7 -> x0, waiting for transfers between devices: 196 us -> none  [the longest x1 60.2 us: fetch(): lax.all_gather(shards[5], ('pb', 'ctx'), axis=0, tiled=True)]
    unnamed x15 -> x0, waiting for transfers between devices: 117 us -> none
    gather x1 -> x0, local copies, waits for them, and re-layouts: 97.2 us -> none  [body(): pair_bucket = jnp.take(bucket_index, offsets.reshape(-1))]
    psum x4 -> x0, blocking collectives: 81.9 us -> none  [the longest x1 28.6 us: run_forward(): cross_mixed = lax.psum(partial_mix, 'ctx')]
    all_to_all x0 -> x16, waiting for transfers between devices: none -> 78.9 us  [exchange(): lax.all_to_all(values, axis, 0, 0, tiled=True, axis_index_groups=groups)]
    all_to_all x0 -> x16, starting transfers between devices: none -> 65 us  [exchange(): lax.all_to_all(values, axis, 0, 0, tiled=True, axis_index_groups=groups)]
    dot_general x35 -> x11, matrix products: 79.8 us -> 19 us  [the longest x9 16.6 us: dot(): lax.dot_general(left, right, (((left_axis,), (right_axis,)), ((), ())), p...]
  transfers between devices with their start and end apart: 14 -> 61, of which waited for: 10 -> 28; matrix products, arithmetic and copies ran while one was open for 14% -> 16% of each run, Pallas kernels for 0% -> 11%
where the time goes in v1:
time: 351 us; the launch traced here: 349 us
  waiting for transfers between devices  128 us (36%)
  starting transfers between devices  95.3 us (27%)
  Pallas kernels  51 us (15%)
  local copies, waits for them, and re-layouts  29 us (8%)
  other arithmetic  24.2 us (7%)
  matrix products  19 us (5%)
    all_to_all x16, waiting for transfers between devices, exchange(): lax.all_to_all(values, axis, 0, 0, tiled=True, axis_index_groups=groups)  78.9 us
    all_to_all x16, starting transfers between devices, exchange(): lax.all_to_all(values, axis, 0, 0, tiled=True, axis_index_groups=groups)  65 us
    pallas_call x10, Pallas kernels, call(): pl.pallas_call(kernel, out_shape=[jax.ShapeDtypeStruct(shape, dtype) for...  51 us
    ppermute x45, waiting for transfers between devices, swap_ctx(): return lax.ppermute(values, 'ctx', [(i, i ^ mask) for i in range(size)])  48.9 us
    ppermute x45, starting transfers between devices, swap_ctx(): return lax.ppermute(values, 'ctx', [(i, i ^ mask) for i in range(size)])  30.3 us
    dot_general x9, matrix products, dot(): lax.dot_general(left, right, (((left_axis,), (right_axis,)), ((), ())), p...  16.6 us
    unnamed x91, local copies, waits for them, and re-layouts  8.52 us
    broadcast_in_dim x6, local copies, waits for them, and re-layouts, from_all(): jnp.broadcast_to(values[None], (size,) + values.shape)  7.04 us
  transfers between devices with their start and end apart: 61, of which 28 were waited for; matrix products, arithmetic and copies ran while one was open for 16% of the time, Pallas kernels for 11%

profile of v1, /device:TPU:0, one launch (start us, length us, event | category | flops | bytes accessed | tf_op | source)
XLA Modules:
  0.0 348.8 jit_solution(13550788404592684913)
XLA Ops:
  2.3 6.3 %all-to-all-start.2 = ((bf16[4,24,1536]{2,1,0:T(8,128)(2,1)}), bf16[4,24,1536]{2,1,0:T(8,128)(2,1)S(1)}, u32[]{:S(2)}, u32[]{:S(2)}) async-start(bf16[4,24,1536]{2,1,0:T(8,128)(2,1)} %broadcast_in_dim.30), calls=%async_computation.2 | async-start | bytes 589824 | tf_op jit(solution)/shard_map/all_to_all | solution.py:68
  9.5 8.8 %all-to-all-done.2.refs_0_ = bf16[4,24,1536]{2,1,0:T(8,128)(2,1)S(1)} async-done(((bf16[4,24,1536]{2,1,0:T(8,128)(2,1)}), bf16[4,24,1536]{2,1,0:T(8,128)(2,1)S(1)}, u32[]{:S(2)}, u32[]{:S(2)}) %all-to-all-start.2) | async-done | bytes 294944 | tf_op jit(solution)/shard_map/all_to_all | solution.py:68
  19.1 3.5 all-to-all-start.1
  22.7 11.0 %all-to-all-done.1.refs_0_ = bf16[4,24,2304]{2,1,0:T(8,128)(2,1)S(1)} async-done(((bf16[4,24,2304]{2,1,0:T(8,128)(2,1)}), bf16[4,24,2304]{2,1,0:T(8,128)(2,1)S(1)}, u32[]{:S(2)}, u32[]{:S(2)}) %all-to-all-start.1) | async-done | bytes 442400 | tf_op jit(solution)/shard_map/all_to_all | solution.py:68
  34.6 3.5 all-to-all-start
  41.1 3.7 %collective-permute-done.19.refs_2_ = bf16[4,24,1536]{2,1,0:T(8,128)(2,1)S(1)} collective-permute-done((bf16[4,24,1536]{2,1,0:T(8,128)(2,1)S(1)}, bf16[4,24,1536]{2,1,0:T(8,128)(2,1)S(1)}, u32[]{:S(2)}, u32[]{:S(2)}) %collective-permute-start.19) | collective-permute-done | bytes 294944 | tf_op jit(solution)/shard_map/ppermute | solution.py:55
  63.6 15.7 %all-to-all-done.3 = bf16[8,24,384]{2,1,0:T(8,128)(2,1)S(1)} async-done(((bf16[8,24,384]{2,1,0:T(8,128)(2,1)}), bf16[8,24,384]{2,1,0:T(8,128)(2,1)S(1)}, u32[]{:S(2)}, u32[]{:S(2)}) %all-to-all-start.3) | async-done | bytes 147488 | tf_op jit(solution)/shard_map/all_to_all | solution.py:68
  81.0 5.0 %all-to-all-start.5 = ((bf16[4,96,768]{2,1,0:T(8,128)(2,1)}), bf16[4,96,768]{2,1,0:T(8,128)(2,1)S(1)}, u32[]{:S(2)}, u32[]{:S(2)}) async-start(bf16[4,96,768]{2,1,0:T(8,128)(2,1)} %broadcast_in_dim.33), calls=%async_computation.5 | async-start | bytes 1179648 | tf_op jit(solution)/shard_map/all_to_all | solution.py:68
  96.7 7.4 %collective-permute-done.16.refs_8_ = bf16[2,24,2304]{2,1,0:T(8,128)(2,1)} collective-permute-done((bf16[2,24,2304]{2,1,0:T(8,128)(2,1)S(1)}, bf16[2,24,2304]{2,1,0:T(8,128)(2,1)}, u32[]{:S(2)}, u32[]{:S(2)}) %collective-permute-start.16) | collective-permute-done | bytes 221216 | tf_op jit(solution)/shard_map/ppermute | solution.py:55
  110.1 5.1 %all-to-all-start.4 = ((bf16[4,192,384]{2,1,0:T(8,128)(2,1)}), bf16[4,192,384]{2,1,0:T(8,128)(2,1)S(1)}, u32[]{:S(2)}, u32[]{:S(2)}) async-start(bf16[4,192,384]{2,1,0:T(8,128)(2,1)} %broadcast_in_dim.32), calls=%async_computation.4 | async-start | bytes 1179648 | tf_op jit(solution)/shard_map/all_to_all | solution.py:68
  119.0 4.0 %shard_map.248 = (bf16[32,24,768]{2,1,0:T(8,128)(2,1)}, bf16[32,24,768]{2,1,0:T(8,128)(2,1)}, bf16[32,24,768]{2,1,0:T(8,128)(2,1)}) custom-call(s32[1]{0:T(128)} %bitcast.core_ref.core.order_ref, s32[1]{0:T(128)} %bitcast.1.chip_ref.order_ref, bf16[4,24,2304]{2,1,0:T(8,128)(2,1)} %copy-done.9, bf16[4,24,2304]{2,1,0:T(8,128)(2,1)} %collective-permute-done.9.refs_1_, ...), custom_call_target="tpu_custom_call" | custom-call | tf_op jit(solution)/shard_map/pallas_call | solution.py:44
  124.6 4.1 %shard_map.247 = (bf16[32,24,2304]{2,1,0:T(8,128)(2,1)}, bf16[32,24,128]{2,1,0:T(8,128)(2,1)}) custom-call(s32[1]{0:T(128)} %bitcast.core_ref.core.order_ref, s32[1]{0:T(128)} %bitcast.1.chip_ref.order_ref, bf16[4,24,2432]{2,1,0:T(8,128)(2,1)} %copy-done.6, bf16[4,24,2432]{2,1,0:T(8,128)(2,1)} %copy-done.23, bf16[4,24,2432]{2,1,0:T(8,128)(2,1)} %copy-done.13, ...), custom_call_target="tpu_custom_call" | custom-call | tf_op jit(solution)/shard_map/pallas_call | solution.py:44
  130.4 8.4 %shard_map.249 = (bf16[128,2304]{1,0:T(8,128)(2,1)}, f32[12,128,128]{2,1,0:T(8,128)}, bf16[128,768]{1,0:T(8,128)(2,1)}, f32[128,768]{1,0:T(8,128)}, bf16[128,768...) custom-call(s32[1]{0:T(128)S(6)} %copy.87.length, bf16[128,768]{1,0:T(8,128)(2,1)} %bitcast.97, ...), custom_call_target="tpu_custom_call" | custom-call | tf_op jit(solution)/shard_map/pallas_call | solution.py:44
  138.8 5.1 %shard_map.251 = (bf16[128,512]{1,0:T(8,128)(2,1)}, bf16[128,512]{1,0:T(8,128)(2,1)}) custom-call(s32[1]{0:T(128)} %bitcast.core_ref.core.order_ref, bf16[128,768]{1,0:T(8,128)(2,1)} %get-tuple-element.47.cq, bf16[240,1536]{1,0:T(8,128)(2,1)} %fusion.memory, s32[1,240]{1,0:T(1,128)} %visible.3), custom_call_target="tpu_custom_call" | custom-call | tf_op jit(solution)/shard_map/pallas_call | solution.py:44
  165.7 3.9 %shard_map.254 = (f32[128,768]{1,0:T(8,128)}, bf16[128,768]{1,0:T(8,128)(2,1)}, bf16[128,384]{1,0:T(8,128)(2,1)}, bf16[128,768]{1,0:T(8,128)(2,1)}, bf16[128,384...) custom-call(s32[1]{0:T(128)S(6)} %copy.87.length, s32[1]{0:T(128)S(6)} %copy.88.task, ...), custom_call_target="tpu_custom_call" | custom-call | tf_op jit(solution)/shard_map/pallas_call | solution.py:44
  179.4 3.5 %collective-permute-done.38 = bf16[128,384]{1,0:T(8,128)(2,1)S(1)} collective-permute-done((bf16[128,384]{1,0:T(8,128)(2,1)S(1)}, bf16[128,384]{1,0:T(8,128)(2,1)S(1)}, u32[]{:S(2)}, u32[]{:S(2)}) %collective-permute-start.38) | collective-permute-done | bytes 98336 | tf_op jit(solution)/shard_map/ppermute | solution.py:55
  185.1 7.1 %shard_map.255 = (f32[128,768]{1,0:T(8,128)}, bf16[128,768]{1,0:T(8,128)(2,1)}, f32[128,768]{1,0:T(8,128)}, bf16[240,1536]{1,0:T(8,128)(2,1)}, f32[1,768]{1,0:T(1,128)}) custom-call(s32[1]{0:T(128)S(6)} %copy.87.length, s32[1]{0:T(128)S(6)} %copy.88.task, bf16[128,768]{1,0:T(8,128)(2,1)} %maximum_select_fusion.2.grad_h3, f32[128,768]{1,0:T(8,128)} %get-tuple-element.52.x2, ...), custom_call_target="tpu_custom_call" | custom-call | tf_op jit(solution)/shard_map/pallas_call | solution.py:44
  204.2 5.1 %all-to-all-start.11 = ((bf16[4,24,768]{2,1,0:T(8,128)(2,1)}), bf16[4,24,768]{2,1,0:T(8,128)(2,1)S(1)}, u32[]{:S(2)}, u32[]{:S(2)}) async-start(bf16[4,24,768]{2,1,0:T(8,128)(2,1)} %bitcast.31), calls=%async_computation.11 | async-start | bytes 294912 | tf_op jit(solution)/shard_map/all_to_all | solution.py:68
  209.4 5.9 %all-to-all-done.11 = bf16[4,24,768]{2,1,0:T(8,128)(2,1)S(1)} async-done(((bf16[4,24,768]{2,1,0:T(8,128)(2,1)}), bf16[4,24,768]{2,1,0:T(8,128)(2,1)S(1)}, u32[]{:S(2)}, u32[]{:S(2)}) %all-to-all-start.11) | async-done | bytes 147488 | tf_op jit(solution)/shard_map/all_to_all | solution.py:68
  216.2 3.5 %all-to-all-start.12 = ((bf16[8,128,384]{2,1,0:T(8,128)(2,1)}), bf16[8,128,384]{2,1,0:T(8,128)(2,1)S(1)}, u32[]{:S(2)}, u32[]{:S(2)}) async-start(bf16[8,128,384]{2,1,0:T(8,128)(2,1)} %broadcast_in_dim.37), calls=%async_computation.12 | async-start | bytes 1572864 | tf_op jit(solution)/shard_map/all_to_all | solution.py:68
  220.5 9.1 %shard_map.256 = (bf16[128,768]{1,0:T(8,128)(2,1)}, bf16[128,2304]{1,0:T(8,128)(2,1)}, bf16[128,768]{1,0:T(8,128)(2,1)}, f32[2,768]{1,0:T(2,128)}, f32[12,128]{1,0:T(8,128)}) custom-call(bf16[128,768]{1,0:T(8,128)(2,1)} %maximum_select_fusion.3.grad_cq, bf16[768,768]{1,0:T(8,128)(2,1)} %bitcast.89, f32[128,768]{1,0:T(8,128)} %get-tuple-element.50.x1, ...), custom_call_target="tpu_custom_call" | custom-call | tf_op jit(solution)/shard_map/pallas_call | solution.py:44
  236.7 4.4 %all-to-all-done.15 = f32[4,15,128]{2,1,0:T(8,128)S(1)} async-done(((f32[4,15,128]{2,1,0:T(8,128)}), f32[4,15,128]{2,1,0:T(8,128)S(1)}, u32[]{:S(2)}, u32[]{:S(2)}) %all-to-all-start.15) | async-done | bytes 30752 | tf_op jit(solution)/shard_map/all_to_all | solution.py:68
  241.2 3.5 all-to-all-start.14
  252.2 7.8 %all-to-all-done.14 = bf16[4,96,768]{2,1,0:T(8,128)(2,1)S(1)} async-done(((bf16[4,96,768]{2,1,0:T(8,128)(2,1)}), bf16[4,96,768]{2,1,0:T(8,128)(2,1)S(1)}, u32[]{:S(2)}, u32[]{:S(2)}) %all-to-all-start.14) | async-done | bytes 589856 | tf_op jit(solution)/shard_map/all_to_all | solution.py:68
  264.5 4.8 %all-to-all-done.7 = bf16[4,24,768]{2,1,0:T(8,128)(2,1)S(1)} async-done(((bf16[4,24,768]{2,1,0:T(8,128)(2,1)}), bf16[4,24,768]{2,1,0:T(8,128)(2,1)S(1)}, u32[]{:S(2)}, u32[]{:S(2)}) %all-to-all-start.7) | async-done | bytes 147488 | tf_op jit(solution)/shard_map/all_to_all | solution.py:68
  279.3 3.5 all-to-all-start.6
  288.8 3.9 %all-to-all-done.6 = bf16[4,24,2304]{2,1,0:T(8,128)(2,1)S(1)} async-done(((bf16[4,24,2304]{2,1,0:T(8,128)(2,1)}), bf16[4,24,2304]{2,1,0:T(8,128)(2,1)S(1)}, u32[]{:S(2)}, u32[]{:S(2)}) %all-to-all-start.6) | async-done | bytes 442400 | tf_op jit(solution)/shard_map/all_to_all | solution.py:68
  293.4 3.9 %all-to-all-start.9 = ((bf16[4,4,24,1536]{3,2,1,0:T(8,128)(2,1)}), bf16[4,4,24,1536]{3,2,1,0:T(8,128)(2,1)S(1)}, u32[]{:S(2)}, u32[]{:S(2)}) async-start(bf16[4,4,24,1536]{3,2,1,0:T(8,128)(2,1)} %fusion.3), calls=%async_computation.9 | async-start | bytes 2359296 | tf_op jit(solution)/shard_map/all_to_all | solution.py:68
  300.3 9.4 %collective-permute-done.34 = bf16[128,384]{1,0:T(8,128)(2,1)S(1)} collective-permute-done((bf16[128,384]{1,0:T(8,128)(2,1)S(1)}, bf16[128,384]{1,0:T(8,128)(2,1)S(1)}, u32[]{:S(2)}, u32[]{:S(2)}) %collective-permute-start.34) | collective-permute-done | bytes 98336 | tf_op jit(solution)/shard_map/ppermute | solution.py:55
  313.2 5.5 %all-to-all-start.13 = ((bf16[4,24,3072]{2,1,0:T(8,128)(2,1)}), bf16[4,24,3072]{2,1,0:T(8,128)(2,1)S(1)}, u32[]{:S(2)}, u32[]{:S(2)}) async-start(bf16[4,24,3072]{2,1,0:T(8,128)(2,1)} %convert_element_type.248), calls=%async_computation.13 | async-start | bytes 1179648 | tf_op jit(solution)/shard_map/all_to_all | solution.py:68
  327.5 7.7 %all-to-all-done.13 = bf16[4,24,3072]{2,1,0:T(8,128)(2,1)S(1)} async-done(((bf16[4,24,3072]{2,1,0:T(8,128)(2,1)}), bf16[4,24,3072]{2,1,0:T(8,128)(2,1)S(1)}, u32[]{:S(2)}, u32[]{:S(2)}) %all-to-all-start.13) | async-done | bytes 589856 | tf_op jit(solution)/shard_map/all_to_all | solution.py:68
  343.0 5.1 %all-to-all-done.10 = bf16[4,24,1536]{2,1,0:T(8,128)(2,1)S(1)} async-done(((bf16[4,24,1536]{2,1,0:T(8,128)(2,1)}), bf16[4,24,1536]{2,1,0:T(8,128)(2,1)S(1)}, u32[]{:S(2)}, u32[]{:S(2)}) %all-to-all-start.10) | async-done | bytes 294944 | tf_op jit(solution)/shard_map/all_to_all | solution.py:68
  (267 shorter events, 157.2 us)
Async XLA Ops:
  2.3 15.9 %all-to-all-start.2 = ((bf16[4,24,1536]{2,1,0:T(8,128)(2,1)}), bf16[4,24,1536]{2,1,0:T(8,128)(2,1)S(1)}, u32[]{:S(2)}, u32[]{:S(2)}) async-start(bf16[4,24,1536]{2,1,0:T(8,128)(2,1)} %broadcast_in_dim.30), calls=%async_computation.2 | async-start | bytes 589824 | tf_op jit(solution)/shard_map/all_to_all | solution.py:68
  19.1 14.6 %all-to-all-start.1 = ((bf16[4,24,2304]{2,1,0:T(8,128)(2,1)}), bf16[4,24,2304]{2,1,0:T(8,128)(2,1)S(1)}, u32[]{:S(2)}, u32[]{:S(2)}) async-start(bf16[4,24,2304]{2,1,0:T(8,128)(2,1)} %broadcast_in_dim.29), calls=%async_computation.1 | async-start | bytes 884736 | tf_op jit(solution)/shard_map/all_to_all | solution.py:68
  34.6 19.5 %all-to-all-start = ((bf16[4,24,2432]{2,1,0:T(8,128)(2,1)}), bf16[4,24,2432]{2,1,0:T(8,128)(2,1)S(1)}, u32[]{:S(2)}, u32[]{:S(2)}) async-start(bf16[4,24,2432]{2,1,0:T(8,128)(2,1)} %broadcast_in_dim.28), calls=%async_computation | async-start | bytes 933888 | tf_op jit(solution)/shard_map/all_to_all | solution.py:68
  41.1 13.0 %collective-permute-start.18 = (bf16[4,24,1536]{2,1,0:T(8,128)(2,1)S(1)}, bf16[4,24,1536]{2,1,0:T(8,128)(2,1)S(1)}, u32[]{:S(2)}, u32[]{:S(2)}) collective-permute-start(bf16[4,24,1536]{2,1,0:T(8,128)(2,1)S(1)} %all-to-all-done.2.refs_0_), channel_id=1, source_target_pairs={{0,1},{1,0},{2,3},{3,2},{4,5},{5,4},{6,7},{7,6},{8,9},{9,8},{10,11... | collective-permute-start | bytes 884744 | tf_op jit(solution)/shard_map/ppermute | solution.py:55
  53.3 32.8 %collective-permute-start.10 = (bf16[4,24,2304]{2,1,0:T(8,128)(2,1)S(1)}, bf16[4,24,2304]{2,1,0:T(8,128)(2,1)}, u32[]{:S(2)}, u32[]{:S(2)}) collective-permute-start(bf16[4,24,2304]{2,1,0:T(8,128)(2,1)S(1)} %all-to-all-done.1.refs_0_), channel_id=1, source_target_pairs={{0,2},{1,3},{2,0},{3,1},{4,6},{5,7},{6,4},{7,5},{8,10},{9,11},{10,... | collective-permute-start | bytes 1327112 | tf_op jit(solution)/shard_map/ppermute | solution.py:55
  54.1 34.5 %collective-permute-start.1 = (bf16[4,24,2432]{2,1,0:T(8,128)(2,1)S(1)}, bf16[4,24,2432]{2,1,0:T(8,128)(2,1)S(1)}, u32[]{:S(2)}, u32[]{:S(2)}) collective-permute-start(bf16[4,24,2432]{2,1,0:T(8,128)(2,1)S(1)} %all-to-all-done.refs_0_), channel_id=1, source_target_pairs={{0,2},{1,3},{2,0},{3,1},{4,6},{5,7},{6,4},{7,5},{8,10},{9,11},{10,... | collective-permute-start | bytes 1400840 | tf_op jit(solution)/shard_map/ppermute | solution.py:55
  55.6 33.2 %collective-permute-start.3 = (bf16[4,24,2432]{2,1,0:T(8,128)(2,1)S(1)}, bf16[4,24,2432]{2,1,0:T(8,128)(2,1)S(1)}, u32[]{:S(2)}, u32[]{:S(2)}) collective-permute-start(bf16[4,24,2432]{2,1,0:T(8,128)(2,1)S(1)} %all-to-all-done.refs_0_), channel_id=1, source_target_pairs={{0,4},{1,5},{2,6},{3,7},{4,0},{5,1},{6,2},{7,3},{8,12},{9,13},{10,... | collective-permute-start | bytes 1400840 | tf_op jit(solution)/shard_map/ppermute | solution.py:55
  57.1 29.9 %collective-permute-start.12 = (bf16[4,24,2304]{2,1,0:T(8,128)(2,1)S(1)}, bf16[4,24,2304]{2,1,0:T(8,128)(2,1)}, u32[]{:S(2)}, u32[]{:S(2)}) collective-permute-start(bf16[4,24,2304]{2,1,0:T(8,128)(2,1)S(1)} %all-to-all-done.1.refs_0_), channel_id=1, source_target_pairs={{0,4},{1,5},{2,6},{3,7},{4,0},{5,1},{6,2},{7,3},{8,12},{9,13},{10,... | collective-permute-start | bytes 1327112 | tf_op jit(solution)/shard_map/ppermute | solution.py:55
  59.8 19.5 %all-to-all-start.3 = ((bf16[8,24,384]{2,1,0:T(8,128)(2,1)}), bf16[8,24,384]{2,1,0:T(8,128)(2,1)S(1)}, u32[]{:S(2)}, u32[]{:S(2)}) async-start(bf16[8,24,384]{2,1,0:T(8,128)(2,1)} %reshape.113), calls=%async_computation.3 | async-start | bytes 294912 | tf_op jit(solution)/shard_map/all_to_all | solution.py:68
  63.2 27.9 %collective-permute-start.9 = (bf16[4,24,2304]{2,1,0:T(8,128)(2,1)S(1)}, bf16[4,24,2304]{2,1,0:T(8,128)(2,1)}, u32[]{:S(2)}, u32[]{:S(2)}) collective-permute-start(bf16[4,24,2304]{2,1,0:T(8,128)(2,1)S(1)} %all-to-all-done.1.refs_0_), channel_id=1, source_target_pairs={{0,1},{1,0},{2,3},{3,2},{4,5},{5,4},{6,7},{7,6},{8,9},{9,8},{10,11... | collective-permute-start | bytes 1327112 | tf_op jit(solution)/shard_map/ppermute | solution.py:55
  81.0 28.1 %all-to-all-start.5 = ((bf16[4,96,768]{2,1,0:T(8,128)(2,1)}), bf16[4,96,768]{2,1,0:T(8,128)(2,1)S(1)}, u32[]{:S(2)}, u32[]{:S(2)}) async-start(bf16[4,96,768]{2,1,0:T(8,128)(2,1)} %broadcast_in_dim.33), calls=%async_computation.5 | async-start | bytes 1179648 | tf_op jit(solution)/shard_map/all_to_all | solution.py:68
  88.6 16.1 %collective-permute-start.11 = (bf16[4,24,2304]{2,1,0:T(8,128)(2,1)}, bf16[4,24,2304]{2,1,0:T(8,128)(2,1)}, u32[]{:S(2)}, u32[]{:S(2)}) collective-permute-start(bf16[4,24,2304]{2,1,0:T(8,128)(2,1)} %collective-permute-done.10.refs_2_), channel_id=1, source_target_pairs={{0,1},{1,0},{2,3},{3,2},{4,5},{5,4},{6,7},{7,6},{8,9},{9,8},{10,11... | collective-permute-start | bytes 1327112 | tf_op jit(solution)/shard_map/ppermute | solution.py:55
  88.8 16.3 %collective-permute-start.13 = (bf16[4,24,2304]{2,1,0:T(8,128)(2,1)}, bf16[4,24,2304]{2,1,0:T(8,128)(2,1)}, u32[]{:S(2)}, u32[]{:S(2)}) collective-permute-start(bf16[4,24,2304]{2,1,0:T(8,128)(2,1)} %collective-permute-done.12.refs_4_), channel_id=1, source_target_pairs={{0,1},{1,0},{2,3},{3,2},{4,5},{5,4},{6,7},{7,6},{8,9},{9,8},{10,11... | collective-permute-start | bytes 1327112 | tf_op jit(solution)/shard_map/ppermute | solution.py:55
  90.5 13.6 %collective-permute-start.5 = (bf16[2,24,2432]{2,1,0:T(8,128)(2,1)}, bf16[2,24,2432]{2,1,0:T(8,128)(2,1)}, u32[]{:S(2)}, u32[]{:S(2)}) collective-permute-start(bf16[2,24,2432]{2,1,0:T(8,128)(2,1)} %slice.68), channel_id=1, source_target_pairs={{0,4},{1,5},{2,6},{3,7},{4,0},{5,1},{6,2},{7,3},{8,12},{9,13},{10,... | collective-permute-start | bytes 700424 | tf_op jit(solution)/shard_map/ppermute | solution.py:55
  91.2 13.4 %collective-permute-start.7 = (bf16[2,24,2432]{2,1,0:T(8,128)(2,1)}, bf16[2,24,2432]{2,1,0:T(8,128)(2,1)S(1)}, u32[]{:S(2)}, u32[]{:S(2)}) collective-permute-start(bf16[2,24,2432]{2,1,0:T(8,128)(2,1)} %slice.69), channel_id=1, source_target_pairs={{0,2},{1,3},{2,0},{3,1},{4,6},{5,7},{6,4},{7,5},{8,10},{9,11},{10,... | collective-permute-start | bytes 700424 | tf_op jit(solution)/shard_map/ppermute | solution.py:55
  104.1 18.9 %collective-permute-start = (bf16[4,24,2432]{2,1,0:T(8,128)(2,1)S(1)}, bf16[4,24,2432]{2,1,0:T(8,128)(2,1)S(1)}, u32[]{:S(2)}, u32[]{:S(2)}) collective-permute-start(bf16[4,24,2432]{2,1,0:T(8,128)(2,1)S(1)} %all-to-all-done.refs_0_), channel_id=1, source_target_pairs={{0,1},{1,0},{2,3},{3,2},{4,5},{5,4},{6,7},{7,6},{8,9},{9,8},{10,11... | collective-permute-start | bytes 1400840 | tf_op jit(solution)/shard_map/ppermute | solution.py:55
  104.1 18.9 %collective-permute-start.2 = (bf16[4,24,2432]{2,1,0:T(8,128)(2,1)S(1)}, bf16[4,24,2432]{2,1,0:T(8,128)(2,1)}, u32[]{:S(2)}, u32[]{:S(2)}) collective-permute-start(bf16[4,24,2432]{2,1,0:T(8,128)(2,1)S(1)} %collective-permute-done.1.refs_2_), channel_id=1, source_target_pairs={{0,1},{1,0},{2,3},{3,2},{4,5},{5,4},{6,7},{7,6},{8,9},{9,8},{10,11... | collective-permute-start | bytes 1400840 | tf_op jit(solution)/shard_map/ppermute | solution.py:55
  104.6 18.4 %collective-permute-start.4 = (bf16[4,24,2432]{2,1,0:T(8,128)(2,1)S(1)}, bf16[4,24,2432]{2,1,0:T(8,128)(2,1)}, u32[]{:S(2)}, u32[]{:S(2)}) collective-permute-start(bf16[4,24,2432]{2,1,0:T(8,128)(2,1)S(1)} %collective-permute-done.3.refs_4_), channel_id=1, source_target_pairs={{0,1},{1,0},{2,3},{3,2},{4,5},{5,4},{6,7},{7,6},{8,9},{9,8},{10,11... | collective-permute-start | bytes 1400840 | tf_op jit(solution)/shard_map/ppermute | solution.py:55
  104.7 10.5 %collective-permute-start.15 = (bf16[2,24,2304]{2,1,0:T(8,128)(2,1)}, bf16[2,24,2304]{2,1,0:T(8,128)(2,1)}, u32[]{:S(2)}, u32[]{:S(2)}) collective-permute-start(bf16[2,24,2304]{2,1,0:T(8,128)(2,1)} %copy-done.29), channel_id=1, source_target_pairs={{0,1},{1,0},{2,3},{3,2},{4,5},{5,4},{6,7},{7,6},{8,9},{9,8},{10,11... | collective-permute-start | bytes 663560 | tf_op jit(solution)/shard_map/ppermute | solution.py:55
  110.1 54.8 %all-to-all-start.4 = ((bf16[4,192,384]{2,1,0:T(8,128)(2,1)}), bf16[4,192,384]{2,1,0:T(8,128)(2,1)S(1)}, u32[]{:S(2)}, u32[]{:S(2)}) async-start(bf16[4,192,384]{2,1,0:T(8,128)(2,1)} %broadcast_in_dim.32), calls=%async_computation.4 | async-start | bytes 1179648 | tf_op jit(solution)/shard_map/all_to_all | solution.py:68
  204.2 11.0 %all-to-all-start.11 = ((bf16[4,24,768]{2,1,0:T(8,128)(2,1)}), bf16[4,24,768]{2,1,0:T(8,128)(2,1)S(1)}, u32[]{:S(2)}, u32[]{:S(2)}) async-start(bf16[4,24,768]{2,1,0:T(8,128)(2,1)} %bitcast.31), calls=%async_computation.11 | async-start | bytes 294912 | tf_op jit(solution)/shard_map/all_to_all | solution.py:68
  209.3 10.4 %collective-permute-start.43 = (bf16[128,384]{1,0:T(8,128)(2,1)S(1)}, bf16[128,384]{1,0:T(8,128)(2,1)S(1)}, u32[]{:S(2)}, u32[]{:S(2)}) collective-permute-start(bf16[128,384]{1,0:T(8,128)(2,1)S(1)} %add_convert_fusion.1), channel_id=1, source_target_pairs={{0,1},{1,0},{2,3},{3,2},{4,5},{5,4},{6,7},{7,6},{8,9},{9,8},{10,11... | collective-permute-start | bytes 294920 | tf_op jit(solution)/shard_map/ppermute | solution.py:55
  216.2 16.1 %all-to-all-start.12 = ((bf16[8,128,384]{2,1,0:T(8,128)(2,1)}), bf16[8,128,384]{2,1,0:T(8,128)(2,1)S(1)}, u32[]{:S(2)}, u32[]{:S(2)}) async-start(bf16[8,128,384]{2,1,0:T(8,128)(2,1)} %broadcast_in_dim.37), calls=%async_computation.12 | async-start | bytes 1572864 | tf_op jit(solution)/shard_map/all_to_all | solution.py:68
  241.2 18.9 %all-to-all-start.14 = ((bf16[4,96,768]{2,1,0:T(8,128)(2,1)}), bf16[4,96,768]{2,1,0:T(8,128)(2,1)S(1)}, u32[]{:S(2)}, u32[]{:S(2)}) async-start(bf16[4,96,768]{2,1,0:T(8,128)(2,1)} %bitcast.34), calls=%async_computation.14 | async-start | bytes 1179648 | tf_op jit(solution)/shard_map/all_to_all | solution.py:68
  248.9 36.7 %collective-permute-start.44 = (bf16[4,4,24,1536]{3,2,0,1:T(8,128)(2,1)}, bf16[4,4,24,1536]{3,2,0,1:T(8,128)(2,1)S(1)}, u32[]{:S(2)}, u32[]{:S(2)}) collective-permute-start(bf16[4,4,24,1536]{3,2,0,1:T(8,128)(2,1)} %fusion.4), channel_id=1, source_target_pairs={{0,1},{1,0},{2,3},{3,2},{4,5},{5,4},{6,7},{7,6},{8,9},{9,8},{10,11... | collective-permute-start | bytes 3538952 | tf_op jit(solution)/shard_map/ppermute | solution.py:55
  249.6 33.2 %collective-permute-start.32 = (bf16[128,384]{1,0:T(8,128)(2,1)}, bf16[128,384]{1,0:T(8,128)(2,1)}, u32[]{:S(2)}, u32[]{:S(2)}) collective-permute-start(bf16[128,384]{1,0:T(8,128)(2,1)} %select_convert_fusion.2), channel_id=1, source_target_pairs={{0,1},{1,0},{2,3},{3,2},{4,5},{5,4},{6,7},{7,6},{8,9},{9,8},{10,11... | collective-permute-start | bytes 294920 | tf_op jit(solution)/shard_map/ppermute | solution.py:55
  279.3 13.3 %all-to-all-start.6 = ((bf16[4,24,2304]{2,1,0:T(8,128)(2,1)}), bf16[4,24,2304]{2,1,0:T(8,128)(2,1)S(1)}, u32[]{:S(2)}, u32[]{:S(2)}) async-start(bf16[4,24,2304]{2,1,0:T(8,128)(2,1)} %bitcast.22), calls=%async_computation.6 | async-start | bytes 884736 | tf_op jit(solution)/shard_map/all_to_all | solution.py:68
  283.9 13.4 %collective-permute-start.33 = (bf16[128,384]{1,0:T(8,128)(2,1)S(1)}, bf16[128,384]{1,0:T(8,128)(2,1)}, u32[]{:S(2)}, u32[]{:S(2)}) collective-permute-start(bf16[128,384]{1,0:T(8,128)(2,1)S(1)} %add_convert_fusion.9), channel_id=1, source_target_pairs={{0,2},{1,3},{2,0},{3,1},{4,6},{5,7},{6,4},{7,5},{8,10},{9,11},{10,... | collective-permute-start | bytes 294920 | tf_op jit(solution)/shard_map/ppermute | solution.py:55
  293.4 19.8 %all-to-all-start.9 = ((bf16[4,4,24,1536]{3,2,1,0:T(8,128)(2,1)}), bf16[4,4,24,1536]{3,2,1,0:T(8,128)(2,1)S(1)}, u32[]{:S(2)}, u32[]{:S(2)}) async-start(bf16[4,4,24,1536]{3,2,1,0:T(8,128)(2,1)} %fusion.3), calls=%async_computation.9 | async-start | bytes 2359296 | tf_op jit(solution)/shard_map/all_to_all | solution.py:68
  298.2 11.5 %collective-permute-start.34 = (bf16[128,384]{1,0:T(8,128)(2,1)S(1)}, bf16[128,384]{1,0:T(8,128)(2,1)S(1)}, u32[]{:S(2)}, u32[]{:S(2)}) collective-permute-start(bf16[128,384]{1,0:T(8,128)(2,1)S(1)} %add_convert_fusion.8), channel_id=1, source_target_pairs={{0,4},{1,5},{2,6},{3,7},{4,0},{5,1},{6,2},{7,3},{8,12},{9,13},{10,... | collective-permute-start | bytes 294920 | tf_op jit(solution)/shard_map/ppermute | solution.py:55
  313.2 22.0 %all-to-all-start.13 = ((bf16[4,24,3072]{2,1,0:T(8,128)(2,1)}), bf16[4,24,3072]{2,1,0:T(8,128)(2,1)S(1)}, u32[]{:S(2)}, u32[]{:S(2)}) async-start(bf16[4,24,3072]{2,1,0:T(8,128)(2,1)} %convert_element_type.248), calls=%async_computation.13 | async-start | bytes 1179648 | tf_op jit(solution)/shard_map/all_to_all | solution.py:68
  335.2 12.9 %all-to-all-start.10 = ((bf16[4,24,1536]{2,1,0:T(8,128)(2,1)}), bf16[4,24,1536]{2,1,0:T(8,128)(2,1)S(1)}, u32[]{:S(2)}, u32[]{:S(2)}) async-start(bf16[4,24,1536]{2,1,0:T(8,128)(2,1)} %reduce_sum.87), calls=%async_computation.10 | async-start | bytes 589824 | tf_op jit(solution)/shard_map/all_to_all | solution.py:68
  (73 other events, 923.0 us)

commit v2 on v0

--- a/solution.py
+++ b/solution.py
@@ -1,23 +1,56 @@
+import functools
+
 import jax
 import jax.numpy as jnp
 from jax import lax
+from jax.experimental import pallas as pl
+from jax.experimental.pallas import tpu as pltpu
 from jax.sharding import PartitionSpec as P
 
-
-def product(left, right):
-    return jnp.dot(left, right, preferred_element_type=jnp.float32)
-
-
-def product_t(left, right):
+LOW, FULL = jnp.bfloat16, jnp.float32
+MASKED = -1000000000.0
+EPS = 1e-06
+HEAD = 64
+VMEM_BYTES = 56 * 1024 * 1024
+
+
+def dot(left, right, left_axis=1, right_axis=0):
     return lax.dot_general(
-        left, right, (((1,), (1,)), ((), ())), preferred_element_type=jnp.float32
-    )
+        left,
+        right,
+        (((left_axis,), (right_axis,)), ((), ())),
+        preferred_element_type=FULL,
+    )
+
+
+def dot_t(left, right):
+    return dot(left, right, 1, 1)
 
 
 def outer_sum(left, right):
-    return lax.dot_general(
-        left, right, (((0,), (0,)), ((), ())), preferred_element_type=jnp.float32
-    )
+    return dot(left, right, 0, 0)
+
+
+def rms_unit(values):
+    factor = lax.rsqrt(jnp.mean(values * values, axis=-1, keepdims=True) + EPS)
+    return values * factor, factor
+
+
+def norm_back(grad, unit, factor, gain):
+    scaled = grad * gain
+    return factor * (scaled - unit * jnp.mean(scaled * unit, axis=-1, keepdims=True))
+
+
+def call(kernel, outs, args, scalars=0, scratch=()):
+    spaces = [pltpu.SMEM] * scalars + [pltpu.VMEM] * (len(args) - scalars)
+    return pl.pallas_call(
+        kernel,
+        out_shape=[jax.ShapeDtypeStruct(shape, dtype) for shape, dtype in outs],
+        in_specs=[pl.BlockSpec(memory_space=space) for space in spaces],
+        out_specs=[pl.BlockSpec(memory_space=pltpu.VMEM) for _ in outs],
+        scratch_shapes=list(scratch),
+        compiler_params=pltpu.CompilerParams(vmem_limit_bytes=VMEM_BYTES),
+    )(*args)
 
 
 def to_low(values):
@@ -27,11 +60,6 @@
 def normalize(values, scale):
     factor = lax.rsqrt(jnp.mean(values * values, axis=-1, keepdims=True) + 1e-06)
     return (values * factor * scale, values * factor, factor)
-
-
-def norm_back(grad, unit, factor, scale):
-    scaled = grad * scale
-    return factor * (scaled - unit * jnp.mean(scaled * unit, axis=-1, keepdims=True))
 
 
 def gelu_tanh(values):
@@ -61,7 +89,7 @@
     residual = decoder.astype(jnp.float32).reshape(count * length, width)
     normed_a, unit_a, factor_a = normalize(residual, scale_gain[0])
     normed_a = to_low(normed_a)
-    joined = to_low(product(normed_a, projection)).reshape(count, length, 3, heads, head_dim)
+    joined = to_low(dot(normed_a, projection)).reshape(count, length, 3, heads, head_dim)
     query_rows, key_rows, value_rows = (joined[:, :, 0], joined[:, :, 1], joined[:, :, 2])
     self_scores = (
         jnp.einsum("nihd,njhd->nhij", query_rows, key_rows, preferred_element_type=jnp.float32)
@@ -73,12 +101,12 @@
         "nhij,njhd->nihd", to_low(self_probs), value_rows, preferred_element_type=jnp.float32
     )
     self_mix = to_low(self_mixed.reshape(count * length, width))
-    after_self = residual + product(self_mix, self_out)
+    after_self = residual + dot(self_mix, self_out)
     normed_b, unit_b, factor_b = normalize(after_self, scale_gain[1])
     normed_b = to_low(normed_b)
-    cross_rows = to_low(product(normed_b, cross_in)).reshape(count, length, heads, head_dim)
+    cross_rows = to_low(dot(normed_b, cross_in)).reshape(count, length, heads, head_dim)
     ctx_rows = encoder.shape[1]
-    memory = to_low(product(encoder.reshape(count * ctx_rows, width), memory_in)).reshape(
+    memory = to_low(dot(encoder.reshape(count * ctx_rows, width), memory_in)).reshape(
         count, ctx_rows, 2, heads, head_dim
     )
     cross_keys, cross_vals = (memory[:, :, 0], memory[:, :, 1])
@@ -99,12 +127,12 @@
     )
     cross_mixed = lax.psum(partial_mix, "ctx")
     cross_mix = to_low(cross_mixed.reshape(count * length, width))
-    after_cross = after_self + product(cross_mix, cross_out)
+    after_cross = after_self + dot(cross_mix, cross_out)
     normed_c, unit_c, factor_c = normalize(after_cross, scale_gain[2])
     normed_c = to_low(normed_c)
-    hidden = product(normed_c, expand)
+    hidden = dot(normed_c, expand)
     active = to_low(gelu_tanh(hidden))
-    output = after_cross + product(active, contract)
+    output = after_cross + dot(active, contract)
     saved = (
         normed_a,
         unit_a,
@@ -132,7 +160,7 @@
     return (output, saved)
 
 
-def body(
+def plain_body(
     decoder_in,
     encoder_out,
     self_projection,
@@ -169,17 +197,13 @@
     offsets = jnp.clip(positions[:, None] - positions[None, :], 0, length - 1)
     pair_bucket = jnp.take(bucket_index, offsets.reshape(-1))
     one_hot = (pair_bucket[:, None] == jnp.arange(buckets)[None, :]).astype(jnp.bfloat16)
-    rel_bias = product(one_hot, bias_table).T.reshape(heads, length, length)
+    rel_bias = dot(one_hot, bias_table).T.reshape(heads, length, length)
     causal = positions[None, :] <= positions[:, None]
     allowed = (causal[None] & (positions[None, None, :] < target_length[:, None, None]))[:, None]
     visible = (passage_mask > 0)[:, None, None, :]
     params = fetch(shards)
     output, saved = run_forward(params, decoder_in, encoder_out, allowed, visible, rel_bias)
-    params_back = fetch(shards)
-    output_again, saved = run_forward(
-        params_back, decoder_in, encoder_out, allowed, visible, rel_bias
-    )
-    projection, self_out, cross_in, memory_in, cross_out, expand, contract, gains = params_back
+    projection, self_out, cross_in, memory_in, cross_out, expand, contract, gains = params
     (
         normed_a,
         unit_a,
@@ -219,14 +243,14 @@
         cotangent.astype(jnp.float32) * (task_scale[:, None] * row_live)[:, :, None]
     ).reshape(rows_total, width)
     low_out = to_low(grad_out)
-    grad_active = product_t(low_out, contract)
+    grad_active = dot_t(low_out, contract)
     unused_value, gelu_pull = jax.vjp(gelu_tanh, hidden)
     grad_hidden = to_low(gelu_pull(grad_active)[0])
-    grad_normed_c = product_t(grad_hidden, expand)
+    grad_normed_c = dot_t(grad_hidden, expand)
     gain_c = jnp.sum(sliced(grad_normed_c * unit_c), axis=0)
     grad_after_cross = grad_out + norm_back(grad_normed_c, unit_c, factor_c, scale_gain[2])
     low_cross = to_low(grad_after_cross)
-    grad_mix = to_low(product_t(low_cross, cross_out)).reshape(count, length, heads, head_dim)
+    grad_mix = to_low(dot_t(low_cross, cross_out)).reshape(count, length, heads, head_dim)
     grad_probs = jnp.einsum(
         "nihd,njhd->nhij", grad_mix, cross_vals, preferred_element_type=jnp.float32
     )
@@ -249,12 +273,12 @@
     )
     encoder_rows = encoder_out.reshape(count * ctx_rows, width)
     grad_cross_memory = outer_sum(encoder_rows, grad_memory)
-    grad_encoder = to_low(product_t(grad_memory, memory_in)).reshape(count, ctx_rows, width)
-    grad_normed_b = product_t(grad_query, cross_in)
+    grad_encoder = to_low(dot_t(grad_memory, memory_in)).reshape(count, ctx_rows, width)
+    grad_normed_b = dot_t(grad_query, cross_in)
     gain_b = jnp.sum(sliced(grad_normed_b * unit_b), axis=0)
     grad_after_self = grad_after_cross + norm_back(grad_normed_b, unit_b, factor_b, scale_gain[1])
     low_self = to_low(grad_after_self)
-    grad_self_mix = to_low(product_t(low_self, self_out)).reshape(count, length, heads, head_dim)
+    grad_self_mix = to_low(dot_t(low_self, self_out)).reshape(count, length, heads, head_dim)
     grad_probs_self = jnp.einsum(
         "nihd,njhd->nhij", grad_self_mix, value_rows, preferred_element_type=jnp.float32
     )
@@ -291,7 +315,7 @@
         "nhij,nihd->njhd", to_low(self_probs), grad_self_mix, preferred_element_type=jnp.float32
     )
     grad_joined = to_low(jnp.stack([grad_q, grad_k, grad_v], axis=2)).reshape(rows_total, 3 * width)
-    grad_normed_a = product_t(grad_joined, projection)
+    grad_normed_a = dot_t(grad_joined, projection)
     gain_a = jnp.sum(sliced(grad_normed_a * unit_a), axis=0)
     grad_decoder = to_low(
         grad_after_self + norm_back(grad_normed_a, unit_a, factor_a, scale_gain[0])
@@ -333,6 +357,835 @@
     )
 
 
+def swap_ctx(values, mask):
+    size = lax.axis_size("ctx")
+    return lax.ppermute(values, "ctx", [(i, i ^ mask) for i in range(size)])
+
+
+def swap_pb(values, mask):
+    size = lax.axis_size("pb")
+    return lax.ppermute(values, "pb", [(i, i ^ mask) for i in range(size)])
+
+
+def exchange(values, axis):
+    return lax.all_to_all(values, axis, 0, 0, tiled=True)
+
+
+def from_all(values, axis):
+    size = lax.axis_size(axis)
+    return exchange(jnp.broadcast_to(values[None], (size,) + values.shape), axis)
+
+
+def all_chips(values):
+    return [values] + [swap_ctx(values, mask) for mask in range(2, lax.axis_size("ctx"), 2)]
+
+
+def tree(terms):
+    while len(terms) > 1:
+        terms = [a + b for a, b in zip(terms[0::2], terms[1::2])]
+    return terms[0]
+
+
+def sum_chips(values):
+    return tree([part.astype(FULL) for part in all_chips(values)]).astype(LOW)
+
+
+def to_owners(parts):
+    return [parts[0]] + [swap_pb(part, r) for r, part in enumerate(parts) if r]
+
+
+def pick(low, high):
+    lanes = lax.broadcasted_iota(jnp.int32, low.shape, 1)
+    return jnp.where(lanes < low.shape[1] // 2, low, high)
+
+
+def lane_mask(values, side):
+    zeros = jnp.zeros_like(values)
+    return pick(values, zeros) if side == 0 else pick(zeros, values)
+
+
+def join(first, mine, other, axis=1):
+    return jnp.where(
+        first,
+        jnp.concatenate([mine, other], axis=axis),
+        jnp.concatenate([other, mine], axis=axis),
+    )
+
+
+def half_of(first, values, axis=1):
+    middle = values.shape[axis] // 2
+    if axis == 0:
+        return jnp.where(first, values[:middle], values[middle:])
+    return jnp.where(first, values[:, :middle], values[:, middle:])
+
+
+CORE, CHIP, PB, CTX = range(4)
+
+
+def place_kernel(sources, widths, rows, ctx, here, *refs):
+    ins, outs = refs[: 2 * len(sources)], refs[2 * len(sources) :]
+    first = here[CORE] == 0
+    for i, (begin, flip) in enumerate(sources):
+        mine, other = ins[2 * i], ins[2 * i + 1]
+        chip = here[CHIP] ^ flip
+        for z in range(mine.shape[0]):
+            both = join(first, mine[z], other[z], 0)
+            slot = pl.multiple_of(((begin + z) * (ctx // 2) + chip) * 2 * rows, 16)
+            at = 0
+            for out, width in zip(outs, widths):
+                out[pl.ds(slot, 2 * rows), :] = both[:, at : at + width]
+                at += width
+
+
+def gather_rows(here, shards):
+    pb, ctx = lax.axis_size("pb"), lax.axis_size("ctx")
+    rows = shards[0].shape[0]
+    widths = [s.shape[1] for s in shards]
+    own = from_all(jnp.concatenate(shards, axis=1), "pb")
+    along_x, along_y = swap_ctx(own, 2), swap_ctx(own, 4)
+    low = swap_ctx(along_x[: pb // 2], 4)
+    high = swap_ctx(along_y[pb // 2 :], 2)
+    arrays = [own, along_x, along_y, low, high]
+    sources = [(0, 0), (0, 1), (0, 2), (0, 3), (pb // 2, 3)]
+    args = []
+    for array in arrays:
+        args += [array, swap_ctx(array, 1)]
+    return call(
+        functools.partial(place_kernel, sources, widths, rows, ctx),
+        [((pb * ctx * rows, width), LOW) for width in widths],
+        [here] + args,
+        scalars=1,
+    ), own
+
+
+def self_kernel(
+    here, length, x, proj, self_out, cross_in, gains, table, p1, probs, mix, x1, h1, h2, cq
+):
+    rows, width = x.shape
+    heads = width // HEAD
+    pair = 2 * HEAD
+    inverse = HEAD ** (-0.5)
+    xf = x[...].astype(FULL)
+    unit, _ = rms_unit(xf)
+    normed = (unit * gains[0:1, :]).astype(LOW)
+    h1[...] = normed
+    joined = dot(normed, proj[...]).astype(LOW)
+    p1[...] = joined
+    row = lax.broadcasted_iota(jnp.int32, (rows, rows), 0)
+    col = lax.broadcasted_iota(jnp.int32, (rows, rows), 1)
+    allowed = (col <= row) & (col < length[0])
+    mixes = []
+    for g in range(heads // 2):
+        at = g * pair
+        q = joined[:, at : at + pair]
+        k = joined[:, width + at : width + at + pair]
+        v = joined[:, 2 * width + at : 2 * width + at + pair]
+        mixed = []
+        for side in range(2):
+            head = 2 * g + side
+            bias = pltpu.roll(
+                jnp.broadcast_to(table[head : head + 1, :], (rows, rows)),
+                1,
+                axis=1,
+                stride=1,
+                stride_axis=0,
+            )
+            scores = jnp.where(allowed, dot_t(lane_mask(q, side), k) * inverse + bias, MASKED)
+            powers = jnp.exp(scores - jnp.max(scores, axis=-1, keepdims=True))
+            prob = powers / jnp.sum(powers, axis=-1, keepdims=True)
+            probs[head] = prob
+            mixed.append(dot(prob.astype(LOW), v))
+        mixes.append(pick(*mixed).astype(LOW))
+    mixes = jnp.concatenate(mixes, axis=1)
+    mix[...] = mixes
+    after = xf + dot(mixes, self_out[...])
+    x1[...] = after
+    unit, _ = rms_unit(after)
+    normed = (unit * gains[1:2, :]).astype(LOW)
+    h2[...] = normed
+    cq[...] = dot(normed, half_of(here[CORE] == 0, cross_in[...])).astype(LOW)
+
+
+def memory_kernel(here, mine, other, memory_in, memory):
+    first = here[CORE] == 0
+    width = mine.shape[1]
+    keys = half_of(first, memory_in[:, :width])
+    values = half_of(first, memory_in[:, width:])
+    weight = jnp.concatenate([keys, values], axis=1)
+    rows = mine.shape[0]
+    memory[:rows] = dot(mine[...], weight).astype(LOW)
+    memory[rows:] = dot(other[...], weight).astype(LOW)
+
+
+def pack_stats(tops, totals):
+    rows = tops[0].shape[0]
+    lanes = lax.broadcasted_iota(jnp.int32, (rows, 128), 1)
+    columns = jnp.zeros((rows, 128), FULL)
+    for index, column in enumerate(tops + totals):
+        columns = jnp.where(lanes // 3 == index, column, columns)
+    high = columns.astype(LOW).astype(FULL)
+    middle = (columns - high).astype(LOW).astype(FULL)
+    kind = lanes % 3
+    return jnp.where(kind == 0, high, jnp.where(kind == 1, middle, columns - high - middle)).astype(
+        LOW
+    )
+
+
+def read_stats(packed, heads):
+    values = packed.astype(FULL)
+    columns = [
+        values[:, i : i + 1] + values[:, i + 1 : i + 2] + values[:, i + 2 : i + 3]
+        for i in range(0, 6 * heads, 3)
+    ]
+    return columns[:heads], columns[heads:]
+
+
+def cross_kernel(cq, memory, visible, packed):
+    half = cq.shape[1]
+    pair = 2 * HEAD
+    inverse = HEAD ** (-0.5)
+    seen = visible[...] > 0
+    tops, totals, mixes = [], [], []
+    for at in range(0, half, pair):
+        q = cq[:, at : at + pair]
+        k = memory[:, at : at + pair]
+        v = memory[:, half + at : half + at + pair]
+        mixed = []
+        for side in range(2):
+            scores = jnp.where(seen, dot_t(lane_mask(q, side), k) * inverse, MASKED)
+            top = jnp.max(scores, axis=-1, keepdims=True)
+            powers = jnp.where(seen, jnp.exp(scores - top), 0.0)
+            tops.append(top)
+            totals.append(jnp.sum(powers, axis=-1, keepdims=True))
+            mixed.append(dot(powers.astype(LOW), v))
+        mixes.append(pick(*mixed).astype(LOW))
+    packed[...] = jnp.concatenate(mixes + [pack_stats(tops, totals)], axis=1)
+
+
+def spread(columns):
+    shape = (columns[0].shape[0], 2 * HEAD)
+    return jnp.concatenate(
+        [
+            pick(jnp.broadcast_to(a, shape), jnp.broadcast_to(b, shape))
+            for a, b in zip(columns[0::2], columns[1::2])
+        ],
+        axis=1,
+    )
+
+
+def merge_kernel(here, *refs):
+    ins, mix, stats = refs[:-2], refs[-2], refs[-1]
+    half = mix.shape[1]
+    heads = half // HEAD
+    packed = [ref[...] for ref in ins]
+    step = 1
+    while step < len(packed):
+        flip = (here[CHIP] & step) != 0
+        packed = [jnp.where(flip, packed[i ^ step], packed[i]) for i in range(len(packed))]
+        step *= 2
+    read = [read_stats(p[:, half:], heads) for p in packed]
+    tops, totals, scales = [], [], []
+    for h in range(heads):
+        top = read[0][0][h]
+        for other in read[1:]:
+            top = jnp.maximum(top, other[0][h])
+        scale = [jnp.exp(r[0][h] - top) for r in read]
+        total = tree([r[1][h] * w for r, w in zip(read, scale)])
+        tops.append(top)
+        totals.append(total)
+        scales.append([w / total for w in scale])
+    terms = [
+        p[:, :half].astype(FULL) * spread([scale[i] for scale in scales])
+        for i, p in enumerate(packed)
+    ]
+    mix[...] = tree(terms).astype(LOW)
+    stats[...] = pack_stats(tops, totals)
+
+
+def gelu_parts(values):
+    slope = (2.0 / jnp.pi) ** 0.5
+    square = values * values
+    bent = jnp.tanh(slope * (values + 0.044715 * values * square))
+    active = 0.5 * values * (1.0 + bent)
+    inner = slope * (1.0 + 3 * 0.044715 * square)
+    return active, 0.5 * (1.0 + bent) + 0.5 * values * (1.0 - bent * bent) * inner
+
+
+def task_rows(length, task, cot):
+    rows = lax.broadcasted_iota(jnp.int32, cot.shape, 0)
+    weight = jnp.where(task[0] == 0, 1.0, jnp.where(task[0] == 1, 0.5, 2.0)).astype(FULL)
+    return jnp.where(rows < length[0], cot[...].astype(FULL) * weight, 0.0)
+
+
+def feed_weights(packed, width):
+    pb = packed.shape[0]
+    side = (packed.shape[2] - width) // 2
+    expand = []
+    for z in range(pb):
+        expand += [packed[z, :, width : width + side], packed[z, :, width + side :]]
+    contract = [packed[z, :, :width] for z in range(pb)]
+    return jnp.concatenate(expand, axis=0), jnp.concatenate(contract, axis=0)
+
+
+def feed_kernel(
+    here,
+    length,
+    task,
+    mix_mine,
+    mix_other,
+    x1,
+    cross_out,
+    gains,
+    feed_mine,
+    feed_other,
+    cot,
+    x2,
+    h3,
+    active,
+    low_out,
+    grad_hidden,
+    partial,
+):
+    first = here[CORE] == 0
+    width = x1.shape[1]
+    after = x1[...] + dot(join(first, mix_mine[...], mix_other[...]), cross_out[...])
+    x2[...] = after
+    unit, _ = rms_unit(after)
+    normed = (unit * gains[2:3, :]).astype(LOW)
+    h3[...] = normed
+    low = task_rows(length, task, cot).astype(LOW)
+    low_out[...] = low
+    mine, other = feed_weights(feed_mine, width), feed_weights(feed_other, width)
+    expand = jnp.concatenate([mine[0], other[0]], axis=1)
+    contract = jnp.concatenate([mine[1], other[1]], axis=0)
+    value, slope = gelu_parts(dot(normed, expand))
+    value = value.astype(LOW)
+    grad = (dot_t(low, contract) * slope).astype(LOW)
+    units = active.shape[1]
+    active[...] = value[:, :units]
+    grad_hidden[...] = grad[:, :units]
+    partial[:, : width // 2] = dot_t(grad, half_of(first, expand, 0)).astype(LOW)
+    partial[:, width // 2 :] = dot(value, half_of(first, contract)).astype(LOW)
+
+
+def feed_grad_kernel(here, active, low_out, h3, grad_hidden, *refs):
+    outs, contract, expand = refs[:-2], refs[-2], refs[-1]
+    contract[...] = outer_sum(active[...], low_out[...])
+    expand[...] = outer_sum(h3[...], grad_hidden[...])
+    slab = contract.shape[0] // len(outs)
+    block = expand.shape[0] // len(outs)
+    for r, out in enumerate(outs):
+        z = here[PB] ^ r
+        out[:slab] = contract[pl.ds(pl.multiple_of(z * slab, 16), slab)].astype(LOW)
+        at = pl.multiple_of(z * block, 16)
+        low = expand[pl.ds(at, block // 2)]
+        high = expand[pl.ds(at + block // 2, block // 2)]
+        out[slab:] = jnp.concatenate([low, high], axis=1).astype(LOW)
+
+
+def cross_back_kernel(
+    here,
+    length,
+    task,
+    sums_mine,
+    sums_other,
+    x2,
+    gains,
+    cot,
+    cross_out,
+    cq,
+    memory,
+    visible,
+    stats,
+    mix,
+    dx2,
+    low_cross,
+    grad_cq,
+    grad_memory,
+    gain_grad,
+    output,
+):
+    first = here[CORE] == 0
+    half = mix.shape[1]
+    heads = half // HEAD
+    pair = 2 * HEAD
+    inverse = HEAD ** (-0.5)
+    after = x2[...]
+    unit, factor = rms_unit(after)
+    sums = [join(first, sums_mine[:, a : a + half], sums_other[:, a : a + half]) for a in (0, half)]
+    grad = sums[0].astype(FULL)
+    output[...] = (after + sums[1].astype(FULL)).astype(LOW)
+    gain_grad[...] = jnp.sum(grad * unit, axis=0, keepdims=True)
+    back = task_rows(length, task, cot) + norm_back(grad, unit, factor, gains[2:3, :])
+    dx2[...] = back
+    low = back.astype(LOW)
+    low_cross[...] = low
+    grad_mix = dot_t(low, half_of(first, cross_out[...], 0)).astype(LOW)
+    seen = visible[...] > 0
+    tops, totals = read_stats(stats[...], heads)
+    for g in range(heads // 2):
+        at = g * pair
+        q = cq[:, at : at + pair]
+        k = memory[:, at : at + pair]
+        v = memory[:, half + at : half + at + pair]
+        do = grad_mix[:, at : at + pair]
+        weighed = do.astype(FULL) * mix[:, at : at + pair].astype(FULL)
+        queries, keys, values = [], [], []
+        for side in range(2):
+            head = 2 * g + side
+            qs, ds = lane_mask(q, side), lane_mask(do, side)
+            scores = jnp.where(seen, dot_t(qs, k) * inverse, MASKED)
+            prob = jnp.where(seen, jnp.exp(scores - tops[head]) * (1.0 / totals[head]), 0.0)
+            rho = jnp.sum(lane_mask(weighed, side), axis=-1, keepdims=True)
+            grad_scores = (prob * (dot_t(ds, v) - rho)).astype(LOW)
+            queries.append(dot(grad_scores, k))
+            keys.append(outer_sum(grad_scores, qs))
+            values.append(outer_sum(prob.astype(LOW), ds))
+        grad_cq[:, at : at + pair] = (pick(*queries) * inverse).astype(LOW)
+        grad_memory[:, at : at + pair] = ((keys[0] + keys[1]) * inverse).astype(LOW)
+        grad_memory[:, half + at : half + at + pair] = (values[0] + values[1]).astype(LOW)
+
+
+def memory_grad_kernel(here, mine, other, grad_memory, *refs):
+    outs, whole = refs[:-1], refs[-1]
+    rows = mine.shape[0]
+    whole[...] = outer_sum(mine[...], grad_memory[:rows]) + outer_sum(other[...], grad_memory[rows:])
+    share = outs[0].shape[1]
+    for r, out in enumerate(outs):
+        chip = here[CHIP] ^ r
+        for z in range(out.shape[0]):
+            at = pl.multiple_of((z * len(outs) + chip) * share, 16)
+            out[z] = whole[pl.ds(at, share)].astype(LOW)
+
+
+def encoder_grad_kernel(here, mine, other, memory_in, grad):
+    first = here[CORE] == 0
+    half = mine.shape[1] // 2
+    keys = join(first, mine[:, :half], other[:, :half])
+    values = join(first, mine[:, half:], other[:, half:])
+    grad[...] = dot_t(jnp.concatenate([keys, values], axis=1), memory_in[...]).astype(LOW)
+
+
+def owned(left, choose):
+    return dot(left, choose).astype(LOW)
+
+
+def cross_grad_kernel(
+    count, here, mix_mine, mix_other, low_cross, h2, cq_mine, cq_other, choose, *refs
+):
+    pieces, outs, first_sum, second_sum = refs[:count], refs[count:-2], refs[-2], refs[-1]
+    first = here[CORE] == 0
+    chosen = choose[...]
+    mix = join(first, mix_mine[...], mix_other[...])
+    first_sum[...] = outer_sum(owned(mix, chosen), low_cross[...])
+    cq = join(first, cq_mine[...], cq_other[...])
+    second_sum[...] = outer_sum(owned(h2[...], chosen), cq)
+    share = first_sum.shape[0] // len(outs)
+    both = pieces[0].shape[1]
+    for r, out in enumerate(outs):
+        z = here[PB] ^ r
+        out[:both] = tree([piece[z].astype(FULL) for piece in pieces]).astype(LOW)
+        at = pl.multiple_of(z * share, 8)
+        out[both:] = jnp.concatenate(
+            [first_sum[pl.ds(at, share)], second_sum[pl.ds(at, share)]], axis=0
+        ).astype(LOW)
+
+
+def self_back_kernel(
+    here,
+    cq_mine,
+    cq_other,
+    cross_in,
+    x1,
+    gains,
+    dx2,
+    self_out,
+    p1,
+    probs,
+    x,
+    proj,
+    gain_grad,
+    low_self,
+    grad_p1,
+    grad_x,
+    small,
+):
+    rows, width = x.shape
+    heads = width // HEAD
+    pair = 2 * HEAD
+    inverse = HEAD ** (-0.5)
+    grad = dot_t(join(here[CORE] == 0, cq_mine[...], cq_other[...]), cross_in[...])
+    unit, factor = rms_unit(x1[...])
+    small[...] = jnp.zeros_like(small)
+    small[1:2, :] = jnp.sum(grad * unit, axis=0, keepdims=True)
+    small[2:3, :] = gain_grad[...]
+    dx1 = dx2[...] + norm_back(grad, unit, factor, gains[1:2, :])
+    low = dx1.astype(LOW)
+    low_self[...] = low
+    row = lax.broadcasted_iota(jnp.int32, (rows, rows), 0)
+    col = lax.broadcasted_iota(jnp.int32, (rows, rows), 1)
+    flip = jnp.where(row + col == rows - 1, 1.0, 0.0).astype(LOW)
+    grad_mix = dot_t(low, self_out[...]).astype(LOW)
+    parts = [[], [], []]
+    for g in range(heads // 2):
+        at = g * pair
+        q = p1[:, at : at + pair]
+        k = p1[:, width + at : width + at + pair]
+        v = p1[:, 2 * width + at : 2 * width + at + pair]
+        do = grad_mix[:, at : at + pair]
+        queries, keys, values = [], [], []
+        for side in range(2):
+            head = 2 * g + side
+            ds = lane_mask(do, side)
+            prob = probs[head]
+            grad_probs = dot_t(ds, v)
+            rho = jnp.sum(prob * grad_probs, axis=-1, keepdims=True)
+            grad_scores = (prob * (grad_probs - rho)).astype(LOW)
+            turned = pltpu.roll(dot(flip, grad_scores), 0, axis=1, stride=1, stride_axis=0)
+            small[3 + head : 4 + head, :rows] = jnp.sum(turned, axis=0, keepdims=True)
+            queries.append(dot(grad_scores, k))
+            keys.append(outer_sum(grad_scores, lane_mask(q, side)))
+            values.append(outer_sum(prob.astype(LOW), ds))
+        parts[0].append((pick(*queries) * inverse).astype(LOW))
+        parts[1].append(((keys[0] + keys[1]) * inverse).astype(LOW))
+        parts[2].append((values[0] + values[1]).astype(LOW))
+    joined = jnp.concatenate(parts[0] + parts[1] + parts[2], axis=1)
+    grad_p1[...] = joined
+    grad = dot_t(joined, proj[...])
+    unit, factor = rms_unit(x[...].astype(FULL))
+    small[0:1, :] = jnp.sum(grad * unit, axis=0, keepdims=True)
+    grad_x[...] = (dx1 + norm_back(grad, unit, factor, gains[0:1, :])).astype(LOW)
+
+
+def self_grad_kernel(here, mix, low_self, h1, grad_p1, small, choose, *refs):
+    outs, sums = refs[:-1], refs[-1]
+    chosen = choose[...]
+    width = mix.shape[1]
+    sums[:, :width] = outer_sum(owned(mix[...], chosen), low_self[...])
+    sums[:, width:] = outer_sum(owned(h1[...], chosen), grad_p1[...])
+    share = sums.shape[0] // len(outs)
+    for r, out in enumerate(outs):
+        at = pl.multiple_of((here[PB] ^ r) * share, 8)
+        mine = sums[pl.ds(at, share)]
+        blocks = [mine[:, a : a + width] for a in range(0, sums.shape[1], width)]
+        out[...] = jnp.concatenate(blocks + [small[...]], axis=0).astype(LOW)
+
+
+def total_of(refs):
+    return tree([ref[...].astype(FULL) for ref in refs])
+
+
+def feed_total_kernel(*refs):
+    parts, contract, expand = refs[:-2], refs[-2], refs[-1]
+    total = total_of(parts)
+    slab = contract.shape[0]
+    contract[...] = total[:slab]
+    rows = total[slab:].astype(LOW).astype(FULL)
+    share, units = expand.shape[1:]
+    for c in range(expand.shape[0]):
+        side, at = divmod(c * share, rows.shape[0])
+        expand[c] = rows[at : at + share, side * units : (side + 1) * units].astype(LOW)
+
+
+def cross_total_kernel(share, here, *refs):
+    parts, mine, other, out_grad, query_grad = refs[:-4], *refs[-4:]
+    total = total_of(parts)
+    first = here[CORE] == 0
+    mine[...] = half_of(first, total[: 2 * share], 0)
+    other[...] = half_of(jnp.logical_not(first), total[: 2 * share], 0)
+    out_grad[...] = total[2 * share : 3 * share]
+    query_grad[...] = total[3 * share :]
+
+
+def self_total_kernel(here, *refs):
+    parts, hot, out_grad, proj_grad, gain_grad, table = refs[:-5], *refs[-5:]
+    total = total_of(parts)
+    share, width = out_grad.shape
+    blocks = [total[a : a + share] for a in range(0, 4 * share, share)]
+    out_grad[...] = blocks[0]
+    proj_grad[...] = jnp.concatenate(blocks[1:], axis=1)
+    small = total[4 * share :]
+    gains = gain_grad.shape[0]
+    rows = hot.shape[1]
+    shape = (width, share)
+    mine = lax.broadcasted_iota(jnp.int32, shape, 1) + (here[PB] * here[4] + here[CTX]) * share
+    chosen = jnp.where(lax.broadcasted_iota(jnp.int32, shape, 0) == mine, 1.0, 0.0)
+    highest = lax.Precision.HIGHEST
+    gain_grad[...] = jnp.dot(small, chosen, precision=highest, preferred_element_type=FULL)[:gains]
+    heads = table.shape[1]
+    whole = lax.dot_general(
+        hot[...].astype(FULL),
+        small[:, :rows],
+        (((1,), (1,)), ((), ())),
+        precision=highest,
+        preferred_element_type=FULL,
+    )
+    table[...] = whole[:, gains : gains + heads]
+
+
+def fast_body(
+    decoder_in,
+    encoder_out,
+    self_projection,
+    self_output,
+    cross_query,
+    cross_memory,
+    cross_output,
+    expand_weight,
+    contract_weight,
+    norm_gains,
+    bias_table,
+    bucket_index,
+    passage_mask,
+    target_length,
+    task_group,
+    cotangent,
+):
+    pb, ctx = lax.axis_size("pb"), lax.axis_size("ctx")
+    mine_pb, mine_ctx = lax.axis_index("pb"), lax.axis_index("ctx")
+    here = jnp.stack([mine_ctx & 1, mine_ctx >> 1, mine_pb, mine_ctx, jnp.int32(ctx)])
+    here = here.astype(jnp.int32)
+    rows, width = decoder_in.shape[1:]
+    half = width // 2
+    passage = encoder_out.shape[1]
+    buckets, heads = bias_table.shape
+    share = self_projection.shape[0]
+    hidden = expand_weight.shape[1]
+    slab = contract_weight.shape[0]
+    units = pb * slab
+    chips = ctx // 2
+    x, e, cot = decoder_in[0], encoder_out[0], cotangent[0]
+
+    late = jnp.concatenate([cross_memory, cross_output], axis=1)
+    late = lax.all_gather(late, ("pb", "ctx"), axis=0, tiled=True)
+    memory_in, cross_out = late[:, : 2 * width], late[:, 2 * width :]
+    gain_columns = jnp.pad(norm_gains.T, ((0, 0), (0, 128 - norm_gains.shape[0])))
+    (proj, self_out, cross_in, gain_rows), arrived = gather_rows(
+        here, [self_projection, self_output, cross_query, gain_columns]
+    )
+    gains = gain_rows[:, : norm_gains.shape[0]].astype(FULL).T
+    e_other = swap_ctx(e, 1)
+    visible = jnp.concatenate([passage_mask, swap_ctx(passage_mask, 1)], axis=1)
+
+    expand_weight, _ = lax.optimization_barrier((expand_weight, arrived))
+    mixed = expand_weight.reshape(share, pb, ctx, slab).transpose(2, 0, 1, 3)
+    mixed = exchange(mixed.reshape(ctx, share, units), "ctx").reshape(2, ctx * share // 2, units)
+    feed = from_all(jnp.concatenate([contract_weight, mixed[0], mixed[1]], axis=1), "pb")
+    feed_other = swap_ctx(feed, 1)
+
+    hot = (jnp.arange(buckets)[:, None] == bucket_index[::-1][None, :]).astype(LOW)
+    table = outer_sum(bias_table, hot)
+
+    p1, probs, mix1, x1, h1, h2, cq = call(
+        self_kernel,
+        [
+            ((rows, 3 * width), LOW),
+            ((heads, rows, rows), FULL),
+            ((rows, width), LOW),
+            ((rows, width), FULL),
+            ((rows, width), LOW),
+            ((rows, width), LOW),
+            ((rows, half), LOW),
+        ],
+        [here, target_length, x, proj, self_out, cross_in, gains, table],
+        scalars=2,
+    )
+    (memory,) = call(
+        memory_kernel, [((2 * passage, width), LOW)], [here, e, e_other, memory_in], scalars=1
+    )
+    (packed,) = call(cross_kernel, [((rows, half + 128), LOW)], [cq, memory, visible])
+    mix2, stats = call(
+        merge_kernel,
+        [((rows, half), LOW), ((rows, 128), LOW)],
+        [here] + all_chips(packed),
+        scalars=1,
+    )
+    mix2_other = swap_ctx(mix2, 1)
+
+    x2, h3, active, low_out, grad_hidden, partial = call(
+        feed_kernel,
+        [
+            ((rows, width), FULL),
+            ((rows, width), LOW),
+            ((rows, units), LOW),
+            ((rows, width), LOW),
+            ((rows, units), LOW),
+            ((rows, width), LOW),
+        ],
+        [
+            here,
+            target_length,
+            task_group,
+            mix2,
+            mix2_other,
+            x1,
+            cross_out,
+            gains,
+            feed,
+            feed_other,
+            cot,
+        ],
+        scalars=3,
+    )
+    sums = sum_chips(partial)
+    sums_other = swap_ctx(sums, 1)
+    feed_grads = call(
+        feed_grad_kernel,
+        [((2 * slab, width), LOW)] * pb,
+        [here, active, low_out, h3, grad_hidden],
+        scalars=1,
+        scratch=[pltpu.VMEM((units, width), FULL), pltpu.VMEM((width, units), FULL)],
+    )
+    grad_contract, expand_rows = call(
+        feed_total_kernel,
+        [((slab, width), FULL), ((ctx, share, units), LOW)],
+        to_owners(feed_grads),
+    )
+    grad_expand = exchange(expand_rows, "ctx").astype(FULL).reshape(ctx, share, pb, slab)
+    grad_expand = grad_expand.transpose(1, 2, 0, 3).reshape(share, hidden)
+
+    dx2, low_cross, grad_cq, grad_memory, gain_grad, block_output = call(
+        cross_back_kernel,
+        [
+            ((rows, width), FULL),
+            ((rows, width), LOW),
+            ((rows, half), LOW),
+            ((2 * passage, width), LOW),
+            ((1, width), FULL),
+            ((rows, width), LOW),
+        ],
+        [
+            here,
+            target_length,
+            task_group,
+            sums,
+            sums_other,
+            x2,
+            gains,
+            cot,
+            cross_out,
+            cq,
+            memory,
+            visible,
+            stats,
+            mix2,
+        ],
+        scalars=3,
+    )
+    grad_cq = sum_chips(grad_cq)
+    cq_other = swap_ctx(grad_cq, 1)
+    pieces = call(
+        memory_grad_kernel,
+        [((pb, 2 * share, width), LOW)] * chips,
+        [here, e, e_other, grad_memory],
+        scalars=1,
+        scratch=[pltpu.VMEM((width, width), FULL)],
+    )
+    pieces = [pieces[0]] + [swap_ctx(pieces[r], 2 * r) for r in range(1, chips)]
+    (grad_encoder,) = call(
+        encoder_grad_kernel,
+        [((passage, width), LOW)],
+        [here, grad_memory[:passage], swap_ctx(grad_memory[passage:], 1), memory_in],
+        scalars=1,
+    )
+
+    low_self, grad_p1, grad_x, small = call(
+        self_back_kernel,
+        [
+            ((rows, width), LOW),
+            ((rows, 3 * width), LOW),
+            ((rows, width), LOW),
+            ((16, width), FULL),
+        ],
+        [
+            here,
+            grad_cq,
+            cq_other,
+            cross_in,
+            x1,
+            gains,
+            dx2,
+            self_out,
+            p1,
+            probs,
+            x,
+            proj,
+            gain_grad,
+        ],
+        scalars=1,
+    )
+
+    block = jnp.arange(pb) * (ctx * share) + mine_ctx * share
+    chosen = (block[:, None] + jnp.arange(share)[None, :]).reshape(-1)
+    choose = (jnp.arange(width)[:, None] == chosen[None, :]).astype(LOW)
+    cross_grads = call(
+        functools.partial(cross_grad_kernel, chips),
+        [((4 * share, width), LOW)] * pb,
+        [here, mix2, mix2_other, low_cross, h2, grad_cq, cq_other, choose] + pieces,
+        scalars=1,
+        scratch=[pltpu.VMEM((pb * share, width), FULL)] * 2,
+    )
+    self_grads = call(
+        self_grad_kernel,
+        [((4 * share + 16, width), LOW)] * pb,
+        [here, mix1, low_self, h1, grad_p1, small, choose],
+        scalars=1,
+        scratch=[pltpu.VMEM((pb * share, 4 * width), FULL)],
+    )
+    mine, other, grad_cross_output, grad_cross_query = call(
+        functools.partial(cross_total_kernel, share),
+        [((share, width), FULL)] * 4,
+        [here] + to_owners(cross_grads),
+        scalars=1,
+    )
+    other = swap_ctx(other, 1)
+    first = (mine_ctx & 1) == 0
+    grad_cross_memory = jnp.concatenate(
+        [join(first, mine[:, :half], other[:, :half]), join(first, mine[:, half:], other[:, half:])],
+        axis=1,
+    )
+    grad_self_output, grad_self_projection, grad_norm_gains, grad_table = call(
+        self_total_kernel,
+        [
+            ((share, width), FULL),
+            ((share, 3 * width), FULL),
+            (norm_gains.shape[:1] + (share,), FULL),
+            (bias_table.shape, FULL),
+        ],
+        [here] + to_owners(self_grads) + [hot],
+        scalars=1,
+    )
+    return (
+        block_output[None],
+        grad_x[None],
+        grad_encoder[None],
+        grad_self_projection,
+        grad_self_output,
+        grad_cross_query,
+        grad_cross_memory,
+        grad_cross_output,
+        grad_expand,
+        grad_contract,
+        grad_norm_gains,
+        grad_table,
+    )
+
+
+def body(*args):
+    decoder_in, encoder_out, self_projection = args[:3]
+    contract_weight = args[8]
+    fits = (
+        lax.axis_size("ctx") == 8
+        and lax.axis_size("pb") == 4
+        and decoder_in.shape[0] == 1
+        and decoder_in.shape[1] == 128
+        and self_projection.shape[0] % 8 == 0
+        and contract_weight.shape[0] * 2 == self_projection.shape[0] * lax.axis_size("ctx")
+        and encoder_out.shape[1] % 16 == 0
+    )
+    return (fast_body if fits else plain_body)(*args)
+
+
 def solution(mesh):
     return jax.shard_map(
         body,

time: 1330 us -> 244 us (0.18)
  waiting for transfers between devices: 925 us -> 53.4 us
  blocking collectives: 179 us -> 38 us
  local copies, waits for them, and re-layouts: 113 us -> 22.3 us
  matrix products: 79.8 us -> 0.72 us
  Pallas kernels: 0 us -> 65.3 us
  starting transfers between devices: 0.77 us -> 40.7 us
    reduce_scatter x6 -> x0, waiting for transfers between devices: 612 us -> none  [the longest x1 142 us: body(): lax.psum_scatter(partials[4], ('pb', 'ctx'), scatter_dimension=0, tiled=T...]
    all_gather x7 -> x1, waiting for transfers between devices: 196 us -> 0.01 us  [fast_body(): late = lax.all_gather(late, ('pb', 'ctx'), axis=0, tiled=True)]
    unnamed x15 -> x1, waiting for transfers between devices: 117 us -> 0.02 us
    gather x1 -> x0, local copies, waits for them, and re-layouts: 97.2 us -> none  [body(): pair_bucket = jnp.take(bucket_index, offsets.reshape(-1))]
    psum x4 -> x0, blocking collectives: 81.9 us -> none  [the longest x1 28.6 us: run_forward(): cross_mixed = lax.psum(partial_mix, 'ctx')]
    dot_general x35 -> x1, matrix products: 79.8 us -> 0.72 us  [dot(): lax.dot_general(left, right, (((left_axis,), (right_axis,)), ((), ())), p...]
    pallas_call x0 -> x16, Pallas kernels: none -> 65.3 us  [call(): pl.pallas_call(kernel, out_shape=[jax.ShapeDtypeStruct(shape, dtype) for...]
    ppermute x0 -> x38, waiting for transfers between devices: none -> 43.9 us  [the longest x29 43.9 us: swap_ctx(): return lax.ppermute(values, 'ctx', [(i, i ^ mask) for i in range(size)])]
  transfers between devices with their start and end apart: 14 -> 41, of which waited for: 10 -> 10; matrix products, arithmetic and copies ran while one was open for 14% -> 8% of each run, Pallas kernels for 0% -> 22%
where the time goes in v2:
time: 244 us; the launch traced here: 243 us
  Pallas kernels  65.3 us (27%)
  waiting for transfers between devices  53.4 us (22%)
  starting transfers between devices  40.7 us (17%)
  blocking collectives  38 us (16%)
  local copies, waits for them, and re-layouts  22.3 us (9%)
  between operations  15.7 us (6%)
  other arithmetic  6.99 us (3%)
    pallas_call x16, Pallas kernels, call(): pl.pallas_call(kernel, out_shape=[jax.ShapeDtypeStruct(shape, dtype) for...  65.3 us
    ppermute x29, waiting for transfers between devices, swap_ctx(): return lax.ppermute(values, 'ctx', [(i, i ^ mask) for i in range(size)])  43.9 us
    all_to_all x2, blocking collectives, exchange(): return lax.all_to_all(values, axis, 0, 0, tiled=True)  38 us
    ppermute x29, starting transfers between devices, swap_ctx(): return lax.ppermute(values, 'ctx', [(i, i ^ mask) for i in range(size)])  18.3 us
    ppermute x9, starting transfers between devices, swap_pb(): return lax.ppermute(values, 'pb', [(i, i ^ mask) for i in range(size)])  15.3 us
    all_to_all x2, waiting for transfers between devices, exchange(): return lax.all_to_all(values, axis, 0, 0, tiled=True)  9.46 us
    unnamed x74, local copies, waits for them, and re-layouts  8.51 us
    all_to_all x2, starting transfers between devices, exchange(): return lax.all_to_all(values, axis, 0, 0, tiled=True)  7.11 us
  transfers between devices with their start and end apart: 41, of which 10 were waited for; matrix products, arithmetic and copies ran while one was open for 8% of the time, Pallas kernels for 22%

profile of v2, /device:TPU:0, one launch (start us, length us, event | category | flops | bytes accessed | tf_op | source)
XLA Modules:
  0.0 243.2 jit_solution(11558821078255203575)
XLA Ops:
  10.6 28.1 %all_to_all.20.refs_0_ = bf16[4,24,3968]{2,1,0:T(8,128)(2,1)S(1)} all-to-all(bf16[4,24,3968]{2,1,0:T(8,128)(2,1)S(1)} %broadcast_in_dim.10), channel_id=1, replica_groups=mesh['pb'=4,'ctx'=8] {'pb'}, dimensions={0} | all-to-all | bytes 1523712 | tf_op jit(solution)/shard_map/all_to_all | solution.py:371
  39.2 9.9 %all_to_all.21 = bf16[8,24,384]{2,1,0:T(8,128)(2,1)S(1)} all-to-all(bf16[8,24,384]{2,1,0:T(8,128)(2,1)S(1)} %reshape.68), channel_id=1, replica_groups=mesh['pb'=4,'ctx'=8] {'ctx'}, dimensions={0} | all-to-all | bytes 294912 | tf_op jit(solution)/shard_map/all_to_all | solution.py:371
  50.2 3.7 %all-to-all-start.2 = ((bf16[4,96,1536]{2,1,0:T(8,128)(2,1)}), bf16[4,96,1536]{2,1,0:T(8,128)(2,1)S(1)}, u32[]{:S(2)}, u32[]{:S(2)}) async-start(bf16[4,96,1536]{2,1,0:T(8,128)(2,1)} %broadcast_in_dim.11), calls=%async_computation.2 | async-start | bytes 2359296 | tf_op jit(solution)/shard_map/all_to_all | solution.py:371
  55.1 23.3 %collective-permute-done.3.refs_4_ = bf16[4,24,3968]{2,1,0:T(8,128)(2,1)S(1)} collective-permute-done((bf16[4,24,3968]{2,1,0:T(8,128)(2,1)S(1)}, bf16[4,24,3968]{2,1,0:T(8,128)(2,1)S(1)}, u32[]{:S(2)}, u32[]{:S(2)}) %collective-permute-start.3) | collective-permute-done | bytes 761888 | tf_op jit(solution)/shard_map/ppermute | solution.py:362
  82.1 9.5 %all-to-all-done.2.feed_mine = bf16[4,96,1536]{2,1,0:T(8,128)(2,1)S(1)} async-done(((bf16[4,96,1536]{2,1,0:T(8,128)(2,1)}), bf16[4,96,1536]{2,1,0:T(8,128)(2,1)S(1)}, u32[]{:S(2)}, u32[]{:S(2)}) %all-to-all-start.2) | async-done | bytes 1179680 | tf_op jit(solution)/shard_map/all_to_all | solution.py:371
  92.2 3.1 %collective-permute-done.8.refs_9_ = bf16[2,24,3968]{2,1,0:T(8,128)(2,1)S(1)} collective-permute-done((bf16[2,24,3968]{2,1,0:T(8,128)(2,1)}, bf16[2,24,3968]{2,1,0:T(8,128)(2,1)S(1)}, u32[]{:S(2)}, u32[]{:S(2)}) %collective-permute-start.8) | collective-permute-done | bytes 380960 | tf_op jit(solution)/shard_map/ppermute | solution.py:362
  98.4 6.4 %shard_map.247 = (bf16[768,2304]{1,0:T(8,128)(2,1)}, bf16[768,768]{1,0:T(8,128)(2,1)}, bf16[768,768]{1,0:T(8,128)(2,1)}, bf16[768,128]{1,0:T(8,128)(2,1)}) custom-call(s32[5]{0:T(128)} %stack.19.here, bf16[4,24,3968]{2,1,0:T(8,128)(2,1)} %copy-done.2, bf16[4,24,3968]{2,1,0:T(8,128)(2,1)} %collective-permute-done.refs_1_, bf16[4,24,3968]{2,1,0:T(8,128)(2,1)} %copy-done.5, ...), custom_call_target="tpu_custom_call" | custom-call | tf_op jit(solution)/shard_map/pallas_call | solution.py:46
  106.4 8.0 %shard_map.248 = (bf16[128,2304]{1,0:T(8,128)(2,1)}, f32[12,128,128]{2,1,0:T(8,128)}, bf16[128,768]{1,0:T(8,128)(2,1)}, f32[128,768]{1,0:T(8,128)}, bf16[128,768...) custom-call(s32[5]{0:T(128)} %stack.19.here, s32[1]{0:T(128)S(6)} %copy.34.length, ...), custom_call_target="tpu_custom_call" | custom-call | tf_op jit(solution)/shard_map/pallas_call | solution.py:46
  114.5 3.3 %slice.57.memory_in = bf16[768,1536]{1,0:T(8,128)(2,1)} slice(bf16[768,2304]{1,0:T(8,128)(2,1)} %all-gather.2.cloned.1.call-done), slice={[0:768], [0:1536]} | slice | bytes 4718592 | tf_op jit(solution)/shard_map/slice | solution.py:961
  118.5 3.6 %shard_map.249.memory = bf16[480,768]{1,0:T(8,128)(2,1)} custom-call(s32[5]{0:T(128)} %stack.19.here, bf16[240,768]{1,0:T(8,128)(2,1)} %bitcast.24, bf16[240,768]{1,0:T(8,128)(2,1)} %copy-done.6, bf16[768,1536]{1,0:T(8,128)(2,1)} %slice.57.memory_in), custom_call_target="tpu_custom_call" | custom-call | tf_op jit(solution)/shard_map/pallas_call | solution.py:46
  122.1 3.7 %shard_map.250.refs_0_ = bf16[128,512]{1,0:T(8,128)(2,1)} custom-call(bf16[128,384]{1,0:T(8,128)(2,1)} %get-tuple-element.72.cq, bf16[480,768]{1,0:T(8,128)(2,1)} %shard_map.249.memory, s32[1,480]{1,0:T(1,128)} %pad_add_fusion.visible), custom_call_target="tpu_custom_call" | custom-call | tf_op jit(solution)/shard_map/pallas_call | solution.py:46
  126.9 2.4 %collective-permute-start.11 = (bf16[128,512]{1,0:T(8,128)(2,1)}, bf16[128,512]{1,0:T(8,128)(2,1)S(1)}, u32[]{:S(2)}, u32[]{:S(2)}) collective-permute-start(bf16[128,512]{1,0:T(8,128)(2,1)} %shard_map.250.refs_0_), channel_id=1, source_target_pairs={{0,2},{1,3},{2,0},{3,1},{4,6},{5,7},{6,4},{7,5},{8,10},{9,11},{10,... | collective-permute-start | bytes 393224 | tf_op jit(solution)/shard_map/ppermute | solution.py:362
  129.3 4.0 %collective-permute-done.13.refs_3_ = bf16[128,512]{1,0:T(8,128)(2,1)S(1)} collective-permute-done((bf16[128,512]{1,0:T(8,128)(2,1)}, bf16[128,512]{1,0:T(8,128)(2,1)S(1)}, u32[]{:S(2)}, u32[]{:S(2)}) %collective-permute-start.13) | collective-permute-done | bytes 131104 | tf_op jit(solution)/shard_map/ppermute | solution.py:362
  136.2 2.8 %shard_map.251 = (bf16[128,384]{1,0:T(8,128)(2,1)}, bf16[128,128]{1,0:T(8,128)(2,1)}) custom-call(s32[5]{0:T(128)} %stack.19.here, bf16[128,512]{1,0:T(8,128)(2,1)} %shard_map.250.refs_0_, bf16[128,512]{1,0:T(8,128)(2,1)} %copy-done.30, bf16[128,512]{1,0:T(8,128)(2,1)} %copy-done.29, bf16[128,512]{1,0:T(8,128)(2,1)} %copy-done.28), custom_call_target="tpu_custom_call" | custom-call | tf_op jit(solution)/shard_map/pallas_call | solution.py:46
  139.7 2.4 slice.58.cross_out
  142.8 4.3 %shard_map.252 = (f32[128,768]{1,0:T(8,128)}, bf16[128,768]{1,0:T(8,128)(2,1)}, bf16[128,384]{1,0:T(8,128)(2,1)}, bf16[128,768]{1,0:T(8,128)(2,1)}, bf16[128,384]{1,0:T(8,128)(2,1)}, /*index=5*/bf16[128,768]{1,0:T(8,128)(2,1)}) custom-call(s32[5]{0:T(128)} %stack.19.here, s32[1]{0:T(128)S(6)} %copy.34.length, s32[1]{0:T(128)S(6)} %copy.35.task, ...), custom_call_target="tpu_custom_call" | custom-call | tf_op jit(solution)/shard_map/pallas_call | solution.py:46
  150.6 5.4 %collective-permute-done.18 = bf16[128,768]{1,0:T(8,128)(2,1)S(1)} collective-permute-done((bf16[128,768]{1,0:T(8,128)(2,1)}, bf16[128,768]{1,0:T(8,128)(2,1)S(1)}, u32[]{:S(2)}, u32[]{:S(2)}) %collective-permute-start.18) | collective-permute-done | bytes 196640 | tf_op jit(solution)/shard_map/ppermute | solution.py:362
  155.9 3.8 %collective-permute-done.17 = bf16[128,768]{1,0:T(8,128)(2,1)S(1)} collective-permute-done((bf16[128,768]{1,0:T(8,128)(2,1)}, bf16[128,768]{1,0:T(8,128)(2,1)S(1)}, u32[]{:S(2)}, u32[]{:S(2)}) %collective-permute-start.17) | collective-permute-done | bytes 196640 | tf_op jit(solution)/shard_map/ppermute | solution.py:362
  162.9 5.4 %shard_map.253 = (f32[128,768]{1,0:T(8,128)}, bf16[128,768]{1,0:T(8,128)(2,1)}, bf16[128,384]{1,0:T(8,128)(2,1)}, bf16[480,768]{1,0:T(8,128)(2,1)}, f32[1,768]{1,0:T(1,128)}, /*index=5*/bf16[128,768]{1,0:T(8,128)(2,1)}) custom-call(s32[5]{0:T(128)} %stack.19.here, s32[1]{0:T(128)S(6)} %copy.34.length, s32[1]{0:T(128)S(6)} %copy.35.task, ...), custom_call_target="tpu_custom_call" | custom-call | tf_op jit(solution)/shard_map/pallas_call | solution.py:46
  172.1 2.7 %shard_map.261 = (bf16[192,768]{1,0:T(8,128)(2,1)}, bf16[192,768]{1,0:T(8,128)(2,1)}, bf16[192,768]{1,0:T(8,128)(2,1)}, bf16[192,768]{1,0:T(8,128)(2,1)}) custom-call(s32[5]{0:T(128)} %stack.19.here, bf16[128,384]{1,0:T(8,128)(2,1)} %get-tuple-element.112.active, bf16[128,768]{1,0:T(8,128)(2,1)} %get-tuple-element.113.low_out, ...), custom_call_target="tpu_custom_call" | custom-call | tf_op jit(solution)/shard_map/pallas_call | solution.py:46
  176.6 3.2 %shard_map.258 = (bf16[4,48,768]{2,1,0:T(8,128)(2,1)}, bf16[4,48,768]{2,1,0:T(8,128)(2,1)}, bf16[4,48,768]{2,1,0:T(8,128)(2,1)}, bf16[4,48,768]{2,1,0:T(8,128)(2,1)}) custom-call(s32[5]{0:T(128)} %stack.19.here, bf16[240,768]{1,0:T(8,128)(2,1)} %bitcast.25, bf16[240,768]{1,0:T(8,128)(2,1)} %copy-done.6, bf16[480,768]{1,0:T(8,128)(2,1)} %get-tuple-element.86.grad_memory), custom_call_target="tpu_custom_call" | custom-call | tf_op jit(solution)/shard_map/pallas_call | solution.py:46
  179.8 2.7 %collective-permute-start.37 = (bf16[192,768]{1,0:T(8,128)(2,1)S(1)}, bf16[192,768]{1,0:T(8,128)(2,1)S(1)}, u32[]{:S(2)}, u32[]{:S(2)}) collective-permute-start(bf16[192,768]{1,0:T(8,128)(2,1)S(1)} %copy-done.34), channel_id=1, source_target_pairs={{0,24},{8,16},{16,8},{24,0},{1,25},{9,17},{17,9},{25,1},{2,26},{10... | collective-permute-start | bytes 884744 | tf_op jit(solution)/shard_map/ppermute | solution.py:367
  185.6 9.1 %shard_map.254 = (bf16[128,768]{1,0:T(8,128)(2,1)}, bf16[128,2304]{1,0:T(8,128)(2,1)}, bf16[128,768]{1,0:T(8,128)(2,1)}, f32[16,768]{1,0:T(8,128)}) custom-call(s32[5]{0:T(128)} %stack.19.here, bf16[128,384]{1,0:T(8,128)(2,1)} %copy-done.7, bf16[128,384]{1,0:T(8,128)(2,1)} %copy-done.9, bf16[768,768]{1,0:T(8,128)(2,1)} %get-tuple-element.70.cross_in, ...), custom_call_target="tpu_custom_call" | custom-call | tf_op jit(solution)/shard_map/pallas_call | solution.py:46
  194.7 3.1 %shard_map.256 = (bf16[112,768]{1,0:T(8,128)(2,1)}, bf16[112,768]{1,0:T(8,128)(2,1)}, bf16[112,768]{1,0:T(8,128)(2,1)}, bf16[112,768]{1,0:T(8,128)(2,1)}) custom-call(s32[5]{0:T(128)} %stack.19.here, bf16[128,768]{1,0:T(8,128)(2,1)} %get-tuple-element.87.mix, bf16[128,768]{1,0:T(8,128)(2,1)} %get-tuple-element.88.low_self, ...), custom_call_target="tpu_custom_call" | custom-call | tf_op jit(solution)/shard_map/pallas_call | solution.py:46
  199.8 3.9 %collective-permute-start.26 = (bf16[112,768]{1,0:T(8,128)(2,1)}, bf16[112,768]{1,0:T(8,128)(2,1)S(1)}, u32[]{:S(2)}, u32[]{:S(2)}) collective-permute-start(bf16[112,768]{1,0:T(8,128)(2,1)} %get-tuple-element.94), channel_id=1, source_target_pairs={{0,16},{8,24},{16,0},{24,8},{1,17},{9,25},{17,1},{25,9},{2,18},{10... | collective-permute-start | bytes 516104 | tf_op jit(solution)/shard_map/ppermute | solution.py:367
  204.5 2.1 shard_map.262
  206.6 3.4 %all-to-all-start.3 = ((bf16[8,24,384]{2,1,0:T(8,128)(2,1)}), bf16[8,24,384]{2,1,0:T(8,128)(2,1)S(1)}, u32[]{:S(2)}, u32[]{:S(2)}) async-start(bf16[8,24,384]{2,1,0:T(8,128)(2,1)} %get-tuple-element.120), calls=%async_computation.3 | async-start | bytes 294912 | tf_op jit(solution)/shard_map/all_to_all | solution.py:371
  210.0 2.5 %collective-permute-start.27 = (bf16[112,768]{1,0:T(8,128)(2,1)}, bf16[112,768]{1,0:T(8,128)(2,1)S(1)}, u32[]{:S(2)}, u32[]{:S(2)}) collective-permute-start(bf16[112,768]{1,0:T(8,128)(2,1)} %get-tuple-element.95), channel_id=1, source_target_pairs={{0,24},{8,16},{16,8},{24,0},{1,25},{9,17},{17,9},{25,1},{2,26},{10... | collective-permute-start | bytes 516104 | tf_op jit(solution)/shard_map/ppermute | solution.py:367
  213.3 3.2 %shard_map.259 = (bf16[96,768]{1,0:T(8,128)(2,1)}, bf16[96,768]{1,0:T(8,128)(2,1)}, bf16[96,768]{1,0:T(8,128)(2,1)}, bf16[96,768]{1,0:T(8,128)(2,1)}) custom-call(s32[5]{0:T(128)} %stack.19.here, bf16[128,384]{1,0:T(8,128)(2,1)} %get-tuple-element.73.mix_mine.mix, bf16[128,384]{1,0:T(8,128)(2,1)} %copy-done.10, ...), custom_call_target="tpu_custom_call" | custom-call | tf_op jit(solution)/shard_map/pallas_call | solution.py:46
  218.4 2.4 collective-permute-start.33
  223.6 2.3 shard_map.257
  228.0 3.5 %shard_map.255 = bf16[240,768]{1,0:T(8,128)(2,1)} custom-call(s32[5]{0:T(128)} %stack.19.here, bf16[240,768]{1,0:T(8,128)(2,1)} %get-tuple-element.137.mine, bf16[240,768]{1,0:T(8,128)(2,1)} %copy-done.12, bf16[768,1536]{1,0:T(8,128)(2,1)} %slice.57.memory_in), custom_call_target="tpu_custom_call" | custom-call | tf_op jit(solution)/shard_map/pallas_call | solution.py:46
  (177 shorter events, 50.2 us)
Async XLA Ops:
  7.2 107.3 %all-gather.2.cloned.1.call-start = ((), (), s32[]{:S(2)}) async-start(), calls=%async_computation.4 | async-start | bytes 3649536 | tf_op jit(solution)/shard_map/all_gather | solution.py:960
  50.2 41.3 %all-to-all-start.2 = ((bf16[4,96,1536]{2,1,0:T(8,128)(2,1)}), bf16[4,96,1536]{2,1,0:T(8,128)(2,1)S(1)}, u32[]{:S(2)}, u32[]{:S(2)}) async-start(bf16[4,96,1536]{2,1,0:T(8,128)(2,1)} %broadcast_in_dim.11), calls=%async_computation.2 | async-start | bytes 2359296 | tf_op jit(solution)/shard_map/all_to_all | solution.py:371
  54.0 24.5 %collective-permute-start.3 = (bf16[4,24,3968]{2,1,0:T(8,128)(2,1)S(1)}, bf16[4,24,3968]{2,1,0:T(8,128)(2,1)S(1)}, u32[]{:S(2)}, u32[]{:S(2)}) collective-permute-start(bf16[4,24,3968]{2,1,0:T(8,128)(2,1)S(1)} %all_to_all.20.refs_0_), channel_id=1, source_target_pairs={{0,4},{1,5},{2,6},{3,7},{4,0},{5,1},{6,2},{7,3},{8,12},{9,13},{10,... | collective-permute-start | bytes 2285576 | tf_op jit(solution)/shard_map/ppermute | solution.py:362
  54.5 24.9 %collective-permute-start.1 = (bf16[4,24,3968]{2,1,0:T(8,128)(2,1)S(1)}, bf16[4,24,3968]{2,1,0:T(8,128)(2,1)S(1)}, u32[]{:S(2)}, u32[]{:S(2)}) collective-permute-start(bf16[4,24,3968]{2,1,0:T(8,128)(2,1)S(1)} %all_to_all.20.refs_0_), channel_id=1, source_target_pairs={{0,2},{1,3},{2,0},{3,1},{4,6},{5,7},{6,4},{7,5},{8,10},{9,11},{10,... | collective-permute-start | bytes 2285576 | tf_op jit(solution)/shard_map/ppermute | solution.py:362
  55.1 27.0 %collective-permute-start = (bf16[4,24,3968]{2,1,0:T(8,128)(2,1)S(1)}, bf16[4,24,3968]{2,1,0:T(8,128)(2,1)}, u32[]{:S(2)}, u32[]{:S(2)}) collective-permute-start(bf16[4,24,3968]{2,1,0:T(8,128)(2,1)S(1)} %all_to_all.20.refs_0_), channel_id=1, source_target_pairs={{0,1},{1,0},{2,3},{3,2},{4,5},{5,4},{6,7},{7,6},{8,9},{9,8},{10,11... | collective-permute-start | bytes 2285576 | tf_op jit(solution)/shard_map/ppermute | solution.py:362
  79.3 12.3 %collective-permute-start.7 = (bf16[2,24,3968]{2,1,0:T(8,128)(2,1)}, bf16[2,24,3968]{2,1,0:T(8,128)(2,1)}, u32[]{:S(2)}, u32[]{:S(2)}) collective-permute-start(bf16[2,24,3968]{2,1,0:T(8,128)(2,1)} %slice.55), channel_id=1, source_target_pairs={{0,2},{1,3},{2,0},{3,1},{4,6},{5,7},{6,4},{7,5},{8,10},{9,11},{10,... | collective-permute-start | bytes 1142792 | tf_op jit(solution)/shard_map/ppermute | solution.py:362
  80.3 11.8 %collective-permute-start.5 = (bf16[2,24,3968]{2,1,0:T(8,128)(2,1)}, bf16[2,24,3968]{2,1,0:T(8,128)(2,1)}, u32[]{:S(2)}, u32[]{:S(2)}) collective-permute-start(bf16[2,24,3968]{2,1,0:T(8,128)(2,1)} %slice.54), channel_id=1, source_target_pairs={{0,4},{1,5},{2,6},{3,7},{4,0},{5,1},{6,2},{7,3},{8,12},{9,13},{10,... | collective-permute-start | bytes 1142792 | tf_op jit(solution)/shard_map/ppermute | solution.py:362
  81.5 16.8 %collective-permute-start.4 = (bf16[4,24,3968]{2,1,0:T(8,128)(2,1)S(1)}, bf16[4,24,3968]{2,1,0:T(8,128)(2,1)}, u32[]{:S(2)}, u32[]{:S(2)}) collective-permute-start(bf16[4,24,3968]{2,1,0:T(8,128)(2,1)S(1)} %collective-permute-done.3.refs_4_), channel_id=1, source_target_pairs={{0,1},{1,0},{2,3},{3,2},{4,5},{5,4},{6,7},{7,6},{8,9},{9,8},{10,11... | collective-permute-start | bytes 2285576 | tf_op jit(solution)/shard_map/ppermute | solution.py:362
  81.8 16.6 %collective-permute-start.2 = (bf16[4,24,3968]{2,1,0:T(8,128)(2,1)S(1)}, bf16[4,24,3968]{2,1,0:T(8,128)(2,1)}, u32[]{:S(2)}, u32[]{:S(2)}) collective-permute-start(bf16[4,24,3968]{2,1,0:T(8,128)(2,1)S(1)} %collective-permute-done.1.refs_2_), channel_id=1, source_target_pairs={{0,1},{1,0},{2,3},{3,2},{4,5},{5,4},{6,7},{7,6},{8,9},{9,8},{10,11... | collective-permute-start | bytes 2285576 | tf_op jit(solution)/shard_map/ppermute | solution.py:362
  91.5 50.6 %collective-permute-start.15 = (bf16[4,96,1536]{2,1,0:T(8,128)(2,1)S(1)}, bf16[4,96,1536]{2,1,0:T(8,128)(2,1)}, u32[]{:S(2)}, u32[]{:S(2)}) collective-permute-start(bf16[4,96,1536]{2,1,0:T(8,128)(2,1)S(1)} %all-to-all-done.2.feed_mine), channel_id=1, source_target_pairs={{0,1},{1,0},{2,3},{3,2},{4,5},{5,4},{6,7},{7,6},{8,9},{9,8},{10,11... | collective-permute-start | bytes 3538952 | tf_op jit(solution)/shard_map/ppermute | solution.py:362
  95.3 22.5 %collective-permute-start.9 = (bf16[240,768]{1,0:T(8,128)(2,1)}, bf16[240,768]{1,0:T(8,128)(2,1)S(1)}, u32[]{:S(2)}, u32[]{:S(2)}) collective-permute-start(bf16[240,768]{1,0:T(8,128)(2,1)} %bitcast.23), channel_id=1, source_target_pairs={{0,1},{1,0},{2,3},{3,2},{4,5},{5,4},{6,7},{7,6},{8,9},{9,8},{10,11... | collective-permute-start | bytes 1105928 | tf_op jit(solution)/shard_map/ppermute | solution.py:362
  126.6 8.3 %collective-permute-start.12 = (bf16[128,512]{1,0:T(8,128)(2,1)}, bf16[128,512]{1,0:T(8,128)(2,1)S(1)}, u32[]{:S(2)}, u32[]{:S(2)}) collective-permute-start(bf16[128,512]{1,0:T(8,128)(2,1)} %shard_map.250.refs_0_), channel_id=1, source_target_pairs={{0,4},{1,5},{2,6},{3,7},{4,0},{5,1},{6,2},{7,3},{8,12},{9,13},{10,... | collective-permute-start | bytes 393224 | tf_op jit(solution)/shard_map/ppermute | solution.py:362
  147.1 8.8 %collective-permute-start.18 = (bf16[128,768]{1,0:T(8,128)(2,1)}, bf16[128,768]{1,0:T(8,128)(2,1)S(1)}, u32[]{:S(2)}, u32[]{:S(2)}) collective-permute-start(bf16[128,768]{1,0:T(8,128)(2,1)} %get-tuple-element.76), channel_id=1, source_target_pairs={{0,6},{1,7},{2,4},{3,5},{4,2},{5,3},{6,0},{7,1},{8,14},{9,15},{10,... | collective-permute-start | bytes 589832 | tf_op jit(solution)/shard_map/ppermute | solution.py:362
  148.3 11.4 %collective-permute-start.17 = (bf16[128,768]{1,0:T(8,128)(2,1)}, bf16[128,768]{1,0:T(8,128)(2,1)S(1)}, u32[]{:S(2)}, u32[]{:S(2)}) collective-permute-start(bf16[128,768]{1,0:T(8,128)(2,1)} %get-tuple-element.76), channel_id=1, source_target_pairs={{0,4},{1,5},{2,6},{3,7},{4,0},{5,1},{6,2},{7,3},{8,12},{9,13},{10,... | collective-permute-start | bytes 589832 | tf_op jit(solution)/shard_map/ppermute | solution.py:362
  148.5 11.2 %collective-permute-start.16 = (bf16[128,768]{1,0:T(8,128)(2,1)}, bf16[128,768]{1,0:T(8,128)(2,1)S(1)}, u32[]{:S(2)}, u32[]{:S(2)}) collective-permute-start(bf16[128,768]{1,0:T(8,128)(2,1)} %get-tuple-element.76), channel_id=1, source_target_pairs={{0,2},{1,3},{2,0},{3,1},{4,6},{5,7},{6,4},{7,5},{8,10},{9,11},{10,... | collective-permute-start | bytes 589832 | tf_op jit(solution)/shard_map/ppermute | solution.py:362
  168.4 11.4 %collective-permute-start.22 = (bf16[128,384]{1,0:T(8,128)(2,1)}, bf16[128,384]{1,0:T(8,128)(2,1)S(1)}, u32[]{:S(2)}, u32[]{:S(2)}) collective-permute-start(bf16[128,384]{1,0:T(8,128)(2,1)} %get-tuple-element.80), channel_id=1, source_target_pairs={{0,6},{1,7},{2,4},{3,5},{4,2},{5,3},{6,0},{7,1},{8,14},{9,15},{10,... | collective-permute-start | bytes 294920 | tf_op jit(solution)/shard_map/ppermute | solution.py:362
  169.6 12.8 %collective-permute-start.21 = (bf16[128,384]{1,0:T(8,128)(2,1)}, bf16[128,384]{1,0:T(8,128)(2,1)S(1)}, u32[]{:S(2)}, u32[]{:S(2)}) collective-permute-start(bf16[128,384]{1,0:T(8,128)(2,1)} %get-tuple-element.80), channel_id=1, source_target_pairs={{0,4},{1,5},{2,6},{3,7},{4,0},{5,1},{6,2},{7,3},{8,12},{9,13},{10,... | collective-permute-start | bytes 294920 | tf_op jit(solution)/shard_map/ppermute | solution.py:362
  170.2 12.5 %collective-permute-start.20 = (bf16[128,384]{1,0:T(8,128)(2,1)}, bf16[128,384]{1,0:T(8,128)(2,1)S(1)}, u32[]{:S(2)}, u32[]{:S(2)}) collective-permute-start(bf16[128,384]{1,0:T(8,128)(2,1)} %get-tuple-element.80), channel_id=1, source_target_pairs={{0,2},{1,3},{2,0},{3,1},{4,6},{5,7},{6,4},{7,5},{8,10},{9,11},{10,... | collective-permute-start | bytes 294920 | tf_op jit(solution)/shard_map/ppermute | solution.py:362
  174.8 23.1 %collective-permute-start.35 = (bf16[192,768]{1,0:T(8,128)(2,1)}, bf16[192,768]{1,0:T(8,128)(2,1)S(1)}, u32[]{:S(2)}, u32[]{:S(2)}) collective-permute-start(bf16[192,768]{1,0:T(8,128)(2,1)} %get-tuple-element.117), channel_id=1, source_target_pairs={{0,8},{8,0},{16,24},{24,16},{1,9},{9,1},{17,25},{25,17},{2,10},{10... | collective-permute-start | bytes 884744 | tf_op jit(solution)/shard_map/ppermute | solution.py:367
  174.8 24.9 %collective-permute-start.36 = (bf16[192,768]{1,0:T(8,128)(2,1)}, bf16[192,768]{1,0:T(8,128)(2,1)S(1)}, u32[]{:S(2)}, u32[]{:S(2)}) collective-permute-start(bf16[192,768]{1,0:T(8,128)(2,1)} %get-tuple-element.118), channel_id=1, source_target_pairs={{0,16},{8,24},{16,0},{24,8},{1,17},{9,25},{17,1},{25,9},{2,18},{10... | collective-permute-start | bytes 884744 | tf_op jit(solution)/shard_map/ppermute | solution.py:367
  179.8 20.0 %collective-permute-start.37 = (bf16[192,768]{1,0:T(8,128)(2,1)S(1)}, bf16[192,768]{1,0:T(8,128)(2,1)S(1)}, u32[]{:S(2)}, u32[]{:S(2)}) collective-permute-start(bf16[192,768]{1,0:T(8,128)(2,1)S(1)} %copy-done.34), channel_id=1, source_target_pairs={{0,24},{8,16},{16,8},{24,0},{1,25},{9,17},{17,9},{25,1},{2,26},{10... | collective-permute-start | bytes 884744 | tf_op jit(solution)/shard_map/ppermute | solution.py:367
  182.5 22.0 %collective-permute-start.28 = (bf16[4,48,768]{2,1,0:T(8,128)(2,1)}, bf16[4,48,768]{2,1,0:T(8,128)(2,1)S(1)}, u32[]{:S(2)}, u32[]{:S(2)}) collective-permute-start(bf16[4,48,768]{2,1,0:T(8,128)(2,1)} %get-tuple-element.101), channel_id=1, source_target_pairs={{0,2},{1,3},{2,0},{3,1},{4,6},{5,7},{6,4},{7,5},{8,10},{9,11},{10,... | collective-permute-start | bytes 884744 | tf_op jit(solution)/shard_map/ppermute | solution.py:362
  184.2 25.8 %collective-permute-start.29 = (bf16[4,48,768]{2,1,0:T(8,128)(2,1)}, bf16[4,48,768]{2,1,0:T(8,128)(2,1)S(1)}, u32[]{:S(2)}, u32[]{:S(2)}) collective-permute-start(bf16[4,48,768]{2,1,0:T(8,128)(2,1)} %get-tuple-element.102), channel_id=1, source_target_pairs={{0,4},{1,5},{2,6},{3,7},{4,0},{5,1},{6,2},{7,3},{8,12},{9,13},{10,... | collective-permute-start | bytes 884744 | tf_op jit(solution)/shard_map/ppermute | solution.py:362
  197.9 14.7 %collective-permute-start.30 = (bf16[4,48,768]{2,1,0:T(8,128)(2,1)S(1)}, bf16[4,48,768]{2,1,0:T(8,128)(2,1)S(1)}, u32[]{:S(2)}, u32[]{:S(2)}) collective-permute-start(bf16[4,48,768]{2,1,0:T(8,128)(2,1)S(1)} %copy-done.33), channel_id=1, source_target_pairs={{0,6},{1,7},{2,4},{3,5},{4,2},{5,3},{6,0},{7,1},{8,14},{9,15},{10,... | collective-permute-start | bytes 884744 | tf_op jit(solution)/shard_map/ppermute | solution.py:362
  199.7 16.7 %collective-permute-start.25 = (bf16[112,768]{1,0:T(8,128)(2,1)}, bf16[112,768]{1,0:T(8,128)(2,1)S(1)}, u32[]{:S(2)}, u32[]{:S(2)}) collective-permute-start(bf16[112,768]{1,0:T(8,128)(2,1)} %get-tuple-element.93), channel_id=1, source_target_pairs={{0,8},{8,0},{16,24},{24,16},{1,9},{9,1},{17,25},{25,17},{2,10},{10... | collective-permute-start | bytes 516104 | tf_op jit(solution)/shard_map/ppermute | solution.py:367
  199.8 18.7 %collective-permute-start.26 = (bf16[112,768]{1,0:T(8,128)(2,1)}, bf16[112,768]{1,0:T(8,128)(2,1)S(1)}, u32[]{:S(2)}, u32[]{:S(2)}) collective-permute-start(bf16[112,768]{1,0:T(8,128)(2,1)} %get-tuple-element.94), channel_id=1, source_target_pairs={{0,16},{8,24},{16,0},{24,8},{1,17},{9,25},{17,1},{25,9},{2,18},{10... | collective-permute-start | bytes 516104 | tf_op jit(solution)/shard_map/ppermute | solution.py:367
  204.5 22.8 %collective-permute-start.24 = (bf16[240,768]{1,0:T(8,128)(2,1)S(1)}, bf16[240,768]{1,0:T(8,128)(2,1)S(1)}, u32[]{:S(2)}, u32[]{:S(2)}) collective-permute-start(bf16[240,768]{1,0:T(8,128)(2,1)S(1)} %get-tuple-element.136), channel_id=1, source_target_pairs={{0,1},{1,0},{2,3},{3,2},{4,5},{5,4},{6,7},{7,6},{8,9},{9,8},{10,11... | collective-permute-start | bytes 1105928 | tf_op jit(solution)/shard_map/ppermute | solution.py:362
  206.6 14.8 %all-to-all-start.3 = ((bf16[8,24,384]{2,1,0:T(8,128)(2,1)}), bf16[8,24,384]{2,1,0:T(8,128)(2,1)S(1)}, u32[]{:S(2)}, u32[]{:S(2)}) async-start(bf16[8,24,384]{2,1,0:T(8,128)(2,1)} %get-tuple-element.120), calls=%async_computation.3 | async-start | bytes 294912 | tf_op jit(solution)/shard_map/all_to_all | solution.py:371
  210.0 12.9 %collective-permute-start.27 = (bf16[112,768]{1,0:T(8,128)(2,1)}, bf16[112,768]{1,0:T(8,128)(2,1)S(1)}, u32[]{:S(2)}, u32[]{:S(2)}) collective-permute-start(bf16[112,768]{1,0:T(8,128)(2,1)} %get-tuple-element.95), channel_id=1, source_target_pairs={{0,24},{8,16},{16,8},{24,0},{1,25},{9,17},{17,9},{25,1},{2,26},{10... | collective-permute-start | bytes 516104 | tf_op jit(solution)/shard_map/ppermute | solution.py:367
  216.4 15.0 %collective-permute-start.31 = (bf16[96,768]{1,0:T(8,128)(2,1)}, bf16[96,768]{1,0:T(8,128)(2,1)S(1)}, u32[]{:S(2)}, u32[]{:S(2)}) collective-permute-start(bf16[96,768]{1,0:T(8,128)(2,1)} %get-tuple-element.105), channel_id=1, source_target_pairs={{0,8},{8,0},{16,24},{24,16},{1,9},{9,1},{17,25},{25,17},{2,10},{10... | collective-permute-start | bytes 442376 | tf_op jit(solution)/shard_map/ppermute | solution.py:367
  216.5 15.0 %collective-permute-start.32 = (bf16[96,768]{1,0:T(8,128)(2,1)}, bf16[96,768]{1,0:T(8,128)(2,1)S(1)}, u32[]{:S(2)}, u32[]{:S(2)}) collective-permute-start(bf16[96,768]{1,0:T(8,128)(2,1)} %get-tuple-element.106), channel_id=1, source_target_pairs={{0,16},{8,24},{16,0},{24,8},{1,17},{9,25},{17,1},{25,9},{2,18},{10... | collective-permute-start | bytes 442376 | tf_op jit(solution)/shard_map/ppermute | solution.py:367
  218.4 13.1 %collective-permute-start.33 = (bf16[96,768]{1,0:T(8,128)(2,1)}, bf16[96,768]{1,0:T(8,128)(2,1)S(1)}, u32[]{:S(2)}, u32[]{:S(2)}) collective-permute-start(bf16[96,768]{1,0:T(8,128)(2,1)} %get-tuple-element.107), channel_id=1, source_target_pairs={{0,24},{8,16},{16,8},{24,0},{1,25},{9,17},{17,9},{25,1},{2,26},{10... | collective-permute-start | bytes 442376 | tf_op jit(solution)/shard_map/ppermute | solution.py:367
  (45 other events, 385.5 us)
Sparse Core Ops, SparseCore 0:
  11.5 76.8 all-gather.1

commit v3 on v2

--- a/solution.py
+++ b/solution.py
@@ -42,15 +42,24 @@
 
 
 def call(kernel, outs, args, scalars=0, scratch=()):
-    spaces = [pltpu.SMEM] * scalars + [pltpu.VMEM] * (len(args) - scalars)
+    arrays, specs, grid = [], [], ()
+    for index, arg in enumerate(args):
+        if isinstance(arg, tuple):
+            arg, shape, place = arg
+            specs.append(pl.BlockSpec(shape, lambda i, place=place: place))
+            grid = (1,)
+        else:
+            specs.append(pl.BlockSpec(memory_space=pltpu.SMEM if index < scalars else pltpu.VMEM))
+        arrays.append(arg)
     return pl.pallas_call(
         kernel,
+        grid=grid,
         out_shape=[jax.ShapeDtypeStruct(shape, dtype) for shape, dtype in outs],
-        in_specs=[pl.BlockSpec(memory_space=space) for space in spaces],
+        in_specs=specs,
         out_specs=[pl.BlockSpec(memory_space=pltpu.VMEM) for _ in outs],
         scratch_shapes=list(scratch),
         compiler_params=pltpu.CompilerParams(vmem_limit_bytes=VMEM_BYTES),
-    )(*args)
+    )(*arrays)
 
 
 def to_low(values):
@@ -371,9 +380,13 @@
     return lax.all_to_all(values, axis, 0, 0, tiled=True)
 
 
-def from_all(values, axis):
-    size = lax.axis_size(axis)
-    return exchange(jnp.broadcast_to(values[None], (size,) + values.shape), axis)
+def all_pb(values):
+    size = lax.axis_size("pb")
+    return [values] + [swap_pb(values, r) for r in range(1, size)]
+
+
+def after(values, earlier):
+    return lax.optimization_barrier((values, earlier))[0]
 
 
 def all_chips(values):
@@ -422,49 +435,58 @@
 CORE, CHIP, PB, CTX = range(4)
 
 
-def place_kernel(sources, widths, rows, ctx, here, *refs):
-    ins, outs = refs[: 2 * len(sources)], refs[2 * len(sources) :]
+def prepare_kernel(proj, self_out, cross_in, gains, out):
+    count = gains.shape[0]
+    row = lax.broadcasted_iota(jnp.int32, (count, 128), 0)
+    lane = lax.broadcasted_iota(jnp.int32, (count, 128), 1)
+    columns = outer_sum(gains[...], jnp.where(row == lane, 1.0, 0.0).astype(LOW)).astype(LOW)
+    at = 0
+    for part in (proj[...], self_out[...], cross_in[...], columns):
+        out[:, at : at + part.shape[1]] = part
+        at += part.shape[1]
+
+
+def place(here, ins, outs, ctx):
     first = here[CORE] == 0
-    for i, (begin, flip) in enumerate(sources):
+    pb, rows = ins[0].shape[:2]
+    for i, (begin, flip) in enumerate([(0, 0), (0, 1), (0, 2), (0, 3), (pb // 2, 3)]):
         mine, other = ins[2 * i], ins[2 * i + 1]
         chip = here[CHIP] ^ flip
         for z in range(mine.shape[0]):
             both = join(first, mine[z], other[z], 0)
-            slot = pl.multiple_of(((begin + z) * (ctx // 2) + chip) * 2 * rows, 16)
+            owner = (begin + z) ^ here[PB]
+            slot = pl.multiple_of((owner * (ctx // 2) + chip) * 2 * rows, 16)
             at = 0
-            for out, width in zip(outs, widths):
+            for out in outs:
+                width = out.shape[1]
                 out[pl.ds(slot, 2 * rows), :] = both[:, at : at + width]
                 at += width
 
 
-def gather_rows(here, shards):
-    pb, ctx = lax.axis_size("pb"), lax.axis_size("ctx")
-    rows = shards[0].shape[0]
-    widths = [s.shape[1] for s in shards]
-    own = from_all(jnp.concatenate(shards, axis=1), "pb")
-    along_x, along_y = swap_ctx(own, 2), swap_ctx(own, 4)
-    low = swap_ctx(along_x[: pb // 2], 4)
-    high = swap_ctx(along_y[pb // 2 :], 2)
-    arrays = [own, along_x, along_y, low, high]
-    sources = [(0, 0), (0, 1), (0, 2), (0, 3), (pb // 2, 3)]
-    args = []
-    for array in arrays:
-        args += [array, swap_ctx(array, 1)]
-    return call(
-        functools.partial(place_kernel, sources, widths, rows, ctx),
-        [((pb * ctx * rows, width), LOW) for width in widths],
-        [here] + args,
-        scalars=1,
-    ), own
-
-
-def self_kernel(
-    here, length, x, proj, self_out, cross_in, gains, table, p1, probs, mix, x1, h1, h2, cq
-):
+def first_hop(own):
+    return swap_ctx(own, 2), swap_ctx(own, 4)
+
+
+def second_hop(own, along):
+    middle = own.shape[0] // 2
+    low = swap_ctx(along[0][:middle], 4)
+    high = swap_ctx(along[1][middle:], 2)
+    blocks = []
+    for array in (own, *along, low, high):
+        blocks += [array, swap_ctx(array, 1)]
+    return blocks
+
+
+def self_kernel(ctx, here, length, x, table, *refs):
+    blocks, refs = refs[:-12], refs[-12:]
+    proj, self_out, cross_in, gains_out, p1, probs, mix, x1, h1, h2, cq, columns = refs
     rows, width = x.shape
     heads = width // HEAD
     pair = 2 * HEAD
     inverse = HEAD ** (-0.5)
+    place(here, blocks, [proj, self_out, cross_in, columns], ctx)
+    gains = columns[...].astype(FULL).T
+    gains_out[...] = gains[: gains_out.shape[0]]
     xf = x[...].astype(FULL)
     unit, _ = rms_unit(xf)
     normed = (unit * gains[0:1, :]).astype(LOW)
@@ -498,15 +520,17 @@
         mixes.append(pick(*mixed).astype(LOW))
     mixes = jnp.concatenate(mixes, axis=1)
     mix[...] = mixes
-    after = xf + dot(mixes, self_out[...])
-    x1[...] = after
-    unit, _ = rms_unit(after)
+    after_self = xf + dot(mixes, self_out[...])
+    x1[...] = after_self
+    unit, _ = rms_unit(after_self)
     normed = (unit * gains[1:2, :]).astype(LOW)
     h2[...] = normed
     cq[...] = dot(normed, half_of(here[CORE] == 0, cross_in[...])).astype(LOW)
 
 
-def memory_kernel(here, mine, other, memory_in, memory):
+def memory_kernel(ctx, here, mine, other, *refs):
+    blocks, (memory_in, memory) = refs[:-2], refs[-2:]
+    place(here, blocks, [memory_in], ctx)
     first = here[CORE] == 0
     width = mine.shape[1]
     keys = half_of(first, memory_in[:, :width])
@@ -617,70 +641,98 @@
     return jnp.where(rows < length[0], cot[...].astype(FULL) * weight, 0.0)
 
 
-def feed_weights(packed, width):
-    pb = packed.shape[0]
-    side = (packed.shape[2] - width) // 2
-    expand = []
-    for z in range(pb):
-        expand += [packed[z, :, width : width + side], packed[z, :, width + side :]]
-    contract = [packed[z, :, :width] for z in range(pb)]
-    return jnp.concatenate(expand, axis=0), jnp.concatenate(contract, axis=0)
+def feed_weights(here, mine, other, expand, contract):
+    first = here[CORE] == 0
+    width = contract.shape[1]
+    slab = mine.shape[1]
+    share = slab // 4
+    for z in range(mine.shape[0]):
+        owner = z
+        contract[pl.ds(pl.multiple_of(2 * owner * slab, 16), 2 * slab), :] = join(
+            first, mine[z, :, :width], other[z, :, :width], 0
+        )
+        for r in range(4):
+            rows = slice(r * share, (r + 1) * share)
+            both = join(first, mine[z, rows, width:], other[z, rows, width:], 0)
+            at = pl.multiple_of((owner * 4 + (here[CHIP] ^ r)) * 2 * share, 16)
+            expand[pl.ds(at, 2 * share), :] = both
 
 
 def feed_kernel(
+    ctx,
     here,
     length,
     task,
     mix_mine,
     mix_other,
     x1,
-    cross_out,
     gains,
     feed_mine,
     feed_other,
     cot,
+    *refs,
+):
+    blocks, outs = refs[:-10], refs[-10:]
+    place(here, blocks, [outs[0]], ctx)
+    feed_step(
+        here, length, task, mix_mine, mix_other, x1, gains, feed_mine, feed_other, cot, *outs
+    )
+
+
+def feed_step(
+    here,
+    length,
+    task,
+    mix_mine,
+    mix_other,
+    x1,
+    gains,
+    feed_mine,
+    feed_other,
+    cot,
+    cross_out,
     x2,
     h3,
     active,
     low_out,
     grad_hidden,
     partial,
+    part_out,
+    expand,
+    contract,
 ):
     first = here[CORE] == 0
-    width = x1.shape[1]
-    after = x1[...] + dot(join(first, mix_mine[...], mix_other[...]), cross_out[...])
-    x2[...] = after
-    unit, _ = rms_unit(after)
+    after_cross = x1[...] + dot(join(first, mix_mine[...], mix_other[...]), cross_out[...])
+    x2[...] = after_cross
+    unit, _ = rms_unit(after_cross)
     normed = (unit * gains[2:3, :]).astype(LOW)
     h3[...] = normed
     low = task_rows(length, task, cot).astype(LOW)
     low_out[...] = low
-    mine, other = feed_weights(feed_mine, width), feed_weights(feed_other, width)
-    expand = jnp.concatenate([mine[0], other[0]], axis=1)
-    contract = jnp.concatenate([mine[1], other[1]], axis=0)
-    value, slope = gelu_parts(dot(normed, expand))
+    feed_weights(here, feed_mine, feed_other, expand, contract)
+    value, slope = gelu_parts(dot(normed, expand[...]))
     value = value.astype(LOW)
-    grad = (dot_t(low, contract) * slope).astype(LOW)
-    units = active.shape[1]
-    active[...] = value[:, :units]
-    grad_hidden[...] = grad[:, :units]
-    partial[:, : width // 2] = dot_t(grad, half_of(first, expand, 0)).astype(LOW)
-    partial[:, width // 2 :] = dot(value, half_of(first, contract)).astype(LOW)
-
-
-def feed_grad_kernel(here, active, low_out, h3, grad_hidden, *refs):
-    outs, contract, expand = refs[:-2], refs[-2], refs[-1]
+    grad = (dot_t(low, contract[...]) * slope).astype(LOW)
+    active[...] = value
+    grad_hidden[...] = grad
+    partial[...] = dot_t(grad, half_of(first, expand[...], 0)).astype(LOW)
+    part_out[...] = dot(value, half_of(first, contract[...])).astype(LOW)
+
+
+def feed_grad_kernel(share, here, active, low_out, h3, grad_hidden, out, contract, expand):
     contract[...] = outer_sum(active[...], low_out[...])
     expand[...] = outer_sum(h3[...], grad_hidden[...])
-    slab = contract.shape[0] // len(outs)
-    block = expand.shape[0] // len(outs)
-    for r, out in enumerate(outs):
-        z = here[PB] ^ r
-        out[:slab] = contract[pl.ds(pl.multiple_of(z * slab, 16), slab)].astype(LOW)
-        at = pl.multiple_of(z * block, 16)
-        low = expand[pl.ds(at, block // 2)]
-        high = expand[pl.ds(at + block // 2, block // 2)]
-        out[slab:] = jnp.concatenate([low, high], axis=1).astype(LOW)
+    pb = out.shape[0]
+    slab = contract.shape[0] // pb // 2
+    block = expand.shape[0] // pb
+    for z in range(pb):
+        at = pl.multiple_of((2 * z + here[CORE]) * slab, 16)
+        out[z, :slab] = contract[pl.ds(at, slab)].astype(LOW)
+        rows = [
+            expand[pl.ds(pl.multiple_of(z * block + at + here[CORE] * share, 8), share)]
+            for at in range(0, block, 2 * share)
+        ]
+        out[z, slab:] = jnp.concatenate(rows, axis=0).astype(LOW)
 
 
 def cross_back_kernel(
@@ -701,20 +753,17 @@
     dx2,
     low_cross,
     grad_cq,
-    grad_memory,
+    grad_mine,
+    grad_other,
     gain_grad,
-    output,
 ):
     first = here[CORE] == 0
     half = mix.shape[1]
     heads = half // HEAD
     pair = 2 * HEAD
     inverse = HEAD ** (-0.5)
-    after = x2[...]
-    unit, factor = rms_unit(after)
-    sums = [join(first, sums_mine[:, a : a + half], sums_other[:, a : a + half]) for a in (0, half)]
-    grad = sums[0].astype(FULL)
-    output[...] = (after + sums[1].astype(FULL)).astype(LOW)
+    unit, factor = rms_unit(x2[...])
+    grad = join(first, sums_mine[...], sums_other[...]).astype(FULL)
     gain_grad[...] = jnp.sum(grad * unit, axis=0, keepdims=True)
     back = task_rows(length, task, cot) + norm_back(grad, unit, factor, gains[2:3, :])
     dx2[...] = back
@@ -742,20 +791,23 @@
             keys.append(outer_sum(grad_scores, qs))
             values.append(outer_sum(prob.astype(LOW), ds))
         grad_cq[:, at : at + pair] = (pick(*queries) * inverse).astype(LOW)
-        grad_memory[:, at : at + pair] = ((keys[0] + keys[1]) * inverse).astype(LOW)
-        grad_memory[:, half + at : half + at + pair] = (values[0] + values[1]).astype(LOW)
-
-
-def memory_grad_kernel(here, mine, other, grad_memory, *refs):
+        keys = ((keys[0] + keys[1]) * inverse).astype(LOW)
+        values = (values[0] + values[1]).astype(LOW)
+        passage = grad_mine.shape[0]
+        for ref, begin in ((grad_mine, 0), (grad_other, passage)):
+            ref[:, at : at + pair] = keys[begin : begin + passage]
+            ref[:, half + at : half + at + pair] = values[begin : begin + passage]
+
+
+def memory_grad_kernel(pb, here, mine, other, grad_mine, grad_other, *refs):
     outs, whole = refs[:-1], refs[-1]
-    rows = mine.shape[0]
-    whole[...] = outer_sum(mine[...], grad_memory[:rows]) + outer_sum(other[...], grad_memory[rows:])
-    share = outs[0].shape[1]
+    whole[...] = outer_sum(mine[...], grad_mine[...]) + outer_sum(other[...], grad_other[...])
+    share = whole.shape[0] // pb // len(outs)
     for r, out in enumerate(outs):
         chip = here[CHIP] ^ r
-        for z in range(out.shape[0]):
+        for z in range(pb):
             at = pl.multiple_of((z * len(outs) + chip) * share, 16)
-            out[z] = whole[pl.ds(at, share)].astype(LOW)
+            out[z * share : (z + 1) * share] = whole[pl.ds(at, share)].astype(LOW)
 
 
 def encoder_grad_kernel(here, mine, other, memory_in, grad):
@@ -768,27 +820,6 @@
 
 def owned(left, choose):
     return dot(left, choose).astype(LOW)
-
-
-def cross_grad_kernel(
-    count, here, mix_mine, mix_other, low_cross, h2, cq_mine, cq_other, choose, *refs
-):
-    pieces, outs, first_sum, second_sum = refs[:count], refs[count:-2], refs[-2], refs[-1]
-    first = here[CORE] == 0
-    chosen = choose[...]
-    mix = join(first, mix_mine[...], mix_other[...])
-    first_sum[...] = outer_sum(owned(mix, chosen), low_cross[...])
-    cq = join(first, cq_mine[...], cq_other[...])
-    second_sum[...] = outer_sum(owned(h2[...], chosen), cq)
-    share = first_sum.shape[0] // len(outs)
-    both = pieces[0].shape[1]
-    for r, out in enumerate(outs):
-        z = here[PB] ^ r
-        out[:both] = tree([piece[z].astype(FULL) for piece in pieces]).astype(LOW)
-        at = pl.multiple_of(z * share, 8)
-        out[both:] = jnp.concatenate(
-            [first_sum[pl.ds(at, share)], second_sum[pl.ds(at, share)]], axis=0
-        ).astype(LOW)
 
 
 def self_back_kernel(
@@ -857,70 +888,104 @@
     grad_x[...] = (dx1 + norm_back(grad, unit, factor, gains[0:1, :])).astype(LOW)
 
 
-def self_grad_kernel(here, mix, low_self, h1, grad_p1, small, choose, *refs):
-    outs, sums = refs[:-1], refs[-1]
-    chosen = choose[...]
-    width = mix.shape[1]
-    sums[:, :width] = outer_sum(owned(mix[...], chosen), low_self[...])
-    sums[:, width:] = outer_sum(owned(h1[...], chosen), grad_p1[...])
-    share = sums.shape[0] // len(outs)
-    for r, out in enumerate(outs):
-        at = pl.multiple_of((here[PB] ^ r) * share, 8)
-        mine = sums[pl.ds(at, share)]
-        blocks = [mine[:, a : a + width] for a in range(0, sums.shape[1], width)]
-        out[...] = jnp.concatenate(blocks + [small[...]], axis=0).astype(LOW)
-
-
-def total_of(refs):
-    return tree([ref[...].astype(FULL) for ref in refs])
-
-
-def feed_total_kernel(*refs):
-    parts, contract, expand = refs[:-2], refs[-2], refs[-1]
-    total = total_of(parts)
+def feed_total_kernel(here, parts, contract, *refs):
+    outs, rows = refs[:-1], refs[-1]
+    total = tree([parts[z].astype(FULL) for z in range(parts.shape[0])])
     slab = contract.shape[0]
     contract[...] = total[:slab]
-    rows = total[slab:].astype(LOW).astype(FULL)
-    share, units = expand.shape[1:]
-    for c in range(expand.shape[0]):
-        side, at = divmod(c * share, rows.shape[0])
-        expand[c] = rows[at : at + share, side * units : (side + 1) * units].astype(LOW)
-
-
-def cross_total_kernel(share, here, *refs):
-    parts, mine, other, out_grad, query_grad = refs[:-4], *refs[-4:]
-    total = total_of(parts)
+    rows[...] = total[slab:]
+    share = outs[0].shape[0]
+    for r, out in enumerate(outs):
+        out[...] = rows[pl.ds(pl.multiple_of((here[CHIP] ^ r) * share, 8), share)].astype(LOW)
+
+
+def expand_total_kernel(pb, here, *refs):
+    parts, out = [ref[...].astype(FULL) for ref in refs[:-1]], refs[-1]
+    step = 1
+    while step < len(parts):
+        flip = (here[CHIP] & step) != 0
+        parts = [jnp.where(flip, parts[i ^ step], parts[i]) for i in range(len(parts))]
+        step *= 2
+    units = parts[0].shape[1] // pb
+    out[...] = jnp.concatenate(
+        [part[:, q * units : (q + 1) * units] for q in range(pb) for part in parts], axis=1
+    )
+
+
+def attention_grad_kernel(
+    count,
+    here,
+    mix_mine,
+    mix_other,
+    low_cross,
+    h2,
+    cq_mine,
+    cq_other,
+    mix1,
+    low_self,
+    h1,
+    grad_p1,
+    small,
+    *refs,
+):
+    pieces, out, choose, sums = refs[:count], *refs[count:]
     first = here[CORE] == 0
-    mine[...] = half_of(first, total[: 2 * share], 0)
-    other[...] = half_of(jnp.logical_not(first), total[: 2 * share], 0)
-    out_grad[...] = total[2 * share : 3 * share]
-    query_grad[...] = total[3 * share :]
-
-
-def self_total_kernel(here, *refs):
-    parts, hot, out_grad, proj_grad, gain_grad, table = refs[:-5], *refs[-5:]
-    total = total_of(parts)
+    pb = out.shape[0]
+    width = mix1.shape[1]
+    share = sums.shape[0] // pb
+    lane = lax.broadcasted_iota(jnp.int32, choose.shape, 1)
+    row = lax.broadcasted_iota(jnp.int32, choose.shape, 0)
+    mine = lane // share * (width // pb) + here[CTX] * share + lane % share
+    choose[...] = jnp.where(row == mine, 1.0, 0.0).astype(LOW)
+
+    def owned(left, right):
+        return outer_sum(dot(left, choose[...]).astype(LOW), right)
+
+    sums[:, : 3 * width] = owned(h1[...], grad_p1[...])
+    sums[:, 3 * width : 4 * width] = owned(mix1[...], low_self[...])
+    cq = join(first, cq_mine[...], cq_other[...])
+    sums[:, 4 * width : 5 * width] = owned(h2[...], cq)
+    mix2 = join(first, mix_mine[...], mix_other[...])
+    sums[:, 5 * width :] = owned(mix2, low_cross[...])
+    total = tree([piece[...].astype(FULL) for piece in pieces])
+    both = 2 * share
+    for z in range(pb):
+        rows = sums[z * share : (z + 1) * share]
+        blocks = [rows[:, a : a + width] for a in range(0, 6 * width, width)]
+        blocks += [total[z * both : (z + 1) * both], small[...]]
+        out[z] = jnp.concatenate(blocks, axis=0).astype(LOW)
+
+
+def attention_total_kernel(
+    here, parts, hot, proj_grad, out_grad, query_grad, cross_grad, mine, other, gain_grad, table
+):
+    total = tree([parts[z].astype(FULL) for z in range(parts.shape[0])])
+    first = here[CORE] == 0
     share, width = out_grad.shape
-    blocks = [total[a : a + share] for a in range(0, 4 * share, share)]
-    out_grad[...] = blocks[0]
-    proj_grad[...] = jnp.concatenate(blocks[1:], axis=1)
-    small = total[4 * share :]
+    blocks = [total[a : a + share] for a in range(0, 8 * share, share)]
+    proj_grad[...] = jnp.concatenate(blocks[:3], axis=1)
+    out_grad[...] = blocks[3]
+    query_grad[...] = blocks[4]
+    cross_grad[...] = blocks[5]
+    mine[...] = jnp.where(first, blocks[6], blocks[7])
+    other[...] = jnp.where(first, blocks[7], blocks[6])
+    small = total[8 * share :]
     gains = gain_grad.shape[0]
     rows = hot.shape[1]
     shape = (width, share)
-    mine = lax.broadcasted_iota(jnp.int32, shape, 1) + (here[PB] * here[4] + here[CTX]) * share
-    chosen = jnp.where(lax.broadcasted_iota(jnp.int32, shape, 0) == mine, 1.0, 0.0)
+    place_of = lax.broadcasted_iota(jnp.int32, shape, 1) + (here[PB] * here[4] + here[CTX]) * share
+    chosen = jnp.where(lax.broadcasted_iota(jnp.int32, shape, 0) == place_of, 1.0, 0.0)
     highest = lax.Precision.HIGHEST
     gain_grad[...] = jnp.dot(small, chosen, precision=highest, preferred_element_type=FULL)[:gains]
-    heads = table.shape[1]
+    heads = table.shape[0]
     whole = lax.dot_general(
+        small[:, :rows],
         hot[...].astype(FULL),
-        small[:, :rows],
         (((1,), (1,)), ((), ())),
         precision=highest,
         preferred_element_type=FULL,
     )
-    table[...] = whole[:, gains : gains + heads]
+    table[...] = whole[gains : gains + heads]
 
 
 def fast_body(
@@ -956,29 +1021,40 @@
     chips = ctx // 2
     x, e, cot = decoder_in[0], encoder_out[0], cotangent[0]
 
-    late = jnp.concatenate([cross_memory, cross_output], axis=1)
-    late = lax.all_gather(late, ("pb", "ctx"), axis=0, tiled=True)
-    memory_in, cross_out = late[:, : 2 * width], late[:, 2 * width :]
-    gain_columns = jnp.pad(norm_gains.T, ((0, 0), (0, 128 - norm_gains.shape[0])))
-    (proj, self_out, cross_in, gain_rows), arrived = gather_rows(
-        here, [self_projection, self_output, cross_query, gain_columns]
-    )
-    gains = gain_rows[:, : norm_gains.shape[0]].astype(FULL).T
+    (columns,) = call(
+        prepare_kernel,
+        [((share, 5 * width + 128), LOW)],
+        [self_projection, self_output, cross_query, norm_gains],
+    )
+    columns = jnp.stack(all_pb(columns))
+    mixed = expand_weight.reshape(share, pb, chips, 2 * slab).transpose(2, 0, 1, 3)
+    mixed = mixed.reshape(chips, share, 2 * units)
+    chip = mine_ctx >> 1
+    mixed = [lax.dynamic_index_in_dim(mixed, chip ^ r, 0, False) for r in range(chips)]
+    mixed = jnp.concatenate([mixed[0]] + [swap_ctx(mixed[r], 2 * r) for r in range(1, chips)])
     e_other = swap_ctx(e, 1)
     visible = jnp.concatenate([passage_mask, swap_ctx(passage_mask, 1)], axis=1)
-
-    expand_weight, _ = lax.optimization_barrier((expand_weight, arrived))
-    mixed = expand_weight.reshape(share, pb, ctx, slab).transpose(2, 0, 1, 3)
-    mixed = exchange(mixed.reshape(ctx, share, units), "ctx").reshape(2, ctx * share // 2, units)
-    feed = from_all(jnp.concatenate([contract_weight, mixed[0], mixed[1]], axis=1), "pb")
-    feed_other = swap_ctx(feed, 1)
+    columns = after(columns, (e_other, visible, mixed))
+    early = first_hop(columns)
+    proj_blocks = second_hop(columns, early)
+    others = jnp.concatenate([cross_memory, cross_output], axis=1)
+    others = jnp.stack(all_pb(after(others, columns)))
+    others_early = first_hop(after(others, early))
+    x = after(x, others_early)
+    feed = jnp.concatenate([contract_weight, mixed], axis=1)
+    feed = jnp.broadcast_to(after(feed, others)[None], (pb,) + feed.shape)
+    feed = exchange(feed, "pb")
 
     hot = (jnp.arange(buckets)[:, None] == bucket_index[::-1][None, :]).astype(LOW)
     table = outer_sum(bias_table, hot)
 
-    p1, probs, mix1, x1, h1, h2, cq = call(
-        self_kernel,
+    proj, self_out, cross_in, gains, p1, probs, mix1, x1, h1, h2, cq = call(
+        functools.partial(self_kernel, ctx),
         [
+            ((width, 3 * width), LOW),
+            ((width, width), LOW),
+            ((width, width), LOW),
+            ((norm_gains.shape[0], width), FULL),
             ((rows, 3 * width), LOW),
             ((heads, rows, rows), FULL),
             ((rows, width), LOW),
@@ -987,11 +1063,22 @@
             ((rows, width), LOW),
             ((rows, half), LOW),
         ],
-        [here, target_length, x, proj, self_out, cross_in, gains, table],
+        [here, target_length, x, table] + proj_blocks,
         scalars=2,
-    )
-    (memory,) = call(
-        memory_kernel, [((2 * passage, width), LOW)], [here, e, e_other, memory_in], scalars=1
+        scratch=[pltpu.VMEM((width, 128), LOW)],
+    )
+    others_blocks = second_hop(others, others_early)
+
+    def part(size, index):
+        return [(b, b.shape[:2] + (size * width,), (0, 0, index)) for b in others_blocks]
+
+    feed = after(feed, cq)
+    feed_other = swap_ctx(feed, 1)
+    memory_in, memory = call(
+        functools.partial(memory_kernel, ctx),
+        [((width, 2 * width), LOW), ((2 * passage, width), LOW)],
+        [here, e, e_other] + part(2, 0),
+        scalars=1,
     )
     (packed,) = call(cross_kernel, [((rows, half + 128), LOW)], [cq, memory, visible])
     mix2, stats = call(
@@ -1002,15 +1089,17 @@
     )
     mix2_other = swap_ctx(mix2, 1)
 
-    x2, h3, active, low_out, grad_hidden, partial = call(
-        feed_kernel,
+    cross_out, x2, h3, active, low_out, grad_hidden, partial, part_out = call(
+        functools.partial(feed_kernel, ctx),
         [
+            ((width, width), LOW),
             ((rows, width), FULL),
             ((rows, width), LOW),
-            ((rows, units), LOW),
+            ((rows, 2 * units), LOW),
             ((rows, width), LOW),
-            ((rows, units), LOW),
-            ((rows, width), LOW),
+            ((rows, 2 * units), LOW),
+            ((rows, half), LOW),
+            ((rows, half), LOW),
         ],
         [
             here,
@@ -1019,40 +1108,35 @@
             mix2,
             mix2_other,
             x1,
-            cross_out,
             gains,
             feed,
             feed_other,
             cot,
-        ],
+        ]
+        + part(1, 2),
         scalars=3,
+        scratch=[pltpu.VMEM((width, 2 * units), LOW), pltpu.VMEM((2 * units, width), LOW)],
     )
     sums = sum_chips(partial)
     sums_other = swap_ctx(sums, 1)
-    feed_grads = call(
-        feed_grad_kernel,
-        [((2 * slab, width), LOW)] * pb,
+    (feed_grads,) = call(
+        functools.partial(feed_grad_kernel, share),
+        [((pb, 2 * slab, width), LOW)],
         [here, active, low_out, h3, grad_hidden],
         scalars=1,
-        scratch=[pltpu.VMEM((units, width), FULL), pltpu.VMEM((width, units), FULL)],
-    )
-    grad_contract, expand_rows = call(
-        feed_total_kernel,
-        [((slab, width), FULL), ((ctx, share, units), LOW)],
-        to_owners(feed_grads),
-    )
-    grad_expand = exchange(expand_rows, "ctx").astype(FULL).reshape(ctx, share, pb, slab)
-    grad_expand = grad_expand.transpose(1, 2, 0, 3).reshape(share, hidden)
-
-    dx2, low_cross, grad_cq, grad_memory, gain_grad, block_output = call(
+        scratch=[pltpu.VMEM((2 * units, width), FULL), pltpu.VMEM((width, 2 * units), FULL)],
+    )
+    feed_grads = exchange(feed_grads, "pb")
+
+    dx2, low_cross, grad_cq, grad_mine, grad_other, gain_grad = call(
         cross_back_kernel,
         [
             ((rows, width), FULL),
             ((rows, width), LOW),
             ((rows, half), LOW),
-            ((2 * passage, width), LOW),
+            ((passage, width), LOW),
+            ((passage, width), LOW),
             ((1, width), FULL),
-            ((rows, width), LOW),
         ],
         [
             here,
@@ -1075,19 +1159,14 @@
     grad_cq = sum_chips(grad_cq)
     cq_other = swap_ctx(grad_cq, 1)
     pieces = call(
-        memory_grad_kernel,
-        [((pb, 2 * share, width), LOW)] * chips,
-        [here, e, e_other, grad_memory],
+        functools.partial(memory_grad_kernel, pb),
+        [((pb * 2 * share, width), LOW)] * chips,
+        [here, e, e_other, grad_mine, grad_other],
         scalars=1,
         scratch=[pltpu.VMEM((width, width), FULL)],
     )
     pieces = [pieces[0]] + [swap_ctx(pieces[r], 2 * r) for r in range(1, chips)]
-    (grad_encoder,) = call(
-        encoder_grad_kernel,
-        [((passage, width), LOW)],
-        [here, grad_memory[:passage], swap_ctx(grad_memory[passage:], 1), memory_in],
-        scalars=1,
-    )
+    memory_other = swap_ctx(grad_other, 1)
 
     low_self, grad_p1, grad_x, small = call(
         self_back_kernel,
@@ -1115,45 +1194,72 @@
         scalars=1,
     )
 
-    block = jnp.arange(pb) * (ctx * share) + mine_ctx * share
-    chosen = (block[:, None] + jnp.arange(share)[None, :]).reshape(-1)
-    choose = (jnp.arange(width)[:, None] == chosen[None, :]).astype(LOW)
-    cross_grads = call(
-        functools.partial(cross_grad_kernel, chips),
-        [((4 * share, width), LOW)] * pb,
-        [here, mix2, mix2_other, low_cross, h2, grad_cq, cq_other, choose] + pieces,
+    (grads,) = call(
+        functools.partial(attention_grad_kernel, chips),
+        [((pb, 8 * share + 16, width), LOW)],
+        [
+            here,
+            mix2,
+            mix2_other,
+            low_cross,
+            h2,
+            grad_cq,
+            cq_other,
+            mix1,
+            low_self,
+            h1,
+            grad_p1,
+            small,
+        ]
+        + pieces,
         scalars=1,
-        scratch=[pltpu.VMEM((pb * share, width), FULL)] * 2,
-    )
-    self_grads = call(
-        self_grad_kernel,
-        [((4 * share + 16, width), LOW)] * pb,
-        [here, mix1, low_self, h1, grad_p1, small, choose],
+        scratch=[pltpu.VMEM((width, pb * share), LOW), pltpu.VMEM((pb * share, 6 * width), FULL)],
+    )
+    output = sum_chips(after(part_out, grads))
+    grads = exchange(grads, "pb")
+    (grad_encoder,) = call(
+        encoder_grad_kernel,
+        [((passage, width), LOW)],
+        [here, after(grad_mine, grad_p1), memory_other, memory_in],
         scalars=1,
-        scratch=[pltpu.VMEM((pb * share, 4 * width), FULL)],
-    )
-    mine, other, grad_cross_output, grad_cross_query = call(
-        functools.partial(cross_total_kernel, share),
-        [((share, width), FULL)] * 4,
-        [here] + to_owners(cross_grads),
+    )
+    grad_contract, *expand_rows = call(
+        feed_total_kernel,
+        [((slab, width), FULL)] + [((share, 2 * units), LOW)] * chips,
+        [here, after(feed_grads, grad_p1)],
         scalars=1,
+        scratch=[pltpu.VMEM((chips * share, 2 * units), FULL)],
+    )
+    expand_rows = [expand_rows[0]] + [swap_ctx(expand_rows[r], 2 * r) for r in range(1, chips)]
+    (grad_expand,) = call(
+        functools.partial(expand_total_kernel, pb),
+        [((share, hidden), FULL)],
+        [here] + expand_rows,
+        scalars=1,
+    )
+    first = (mine_ctx & 1) == 0
+    block_output = (x2 + join(first, output, swap_ctx(output, 1)).astype(FULL)).astype(LOW)
+    (
+        grad_self_projection,
+        grad_self_output,
+        grad_cross_query,
+        grad_cross_output,
+        mine,
+        other,
+        grad_norm_gains,
+        grad_table,
+    ) = call(
+        attention_total_kernel,
+        [((share, 3 * width), FULL)]
+        + [((share, width), FULL)] * 5
+        + [(norm_gains.shape[:1] + (share,), FULL), ((heads, buckets), FULL)],
+        [here, grads, hot],
+        scalars=1,
     )
     other = swap_ctx(other, 1)
-    first = (mine_ctx & 1) == 0
     grad_cross_memory = jnp.concatenate(
         [join(first, mine[:, :half], other[:, :half]), join(first, mine[:, half:], other[:, half:])],
         axis=1,
-    )
-    grad_self_output, grad_self_projection, grad_norm_gains, grad_table = call(
-        self_total_kernel,
-        [
-            ((share, width), FULL),
-            ((share, 3 * width), FULL),
-            (norm_gains.shape[:1] + (share,), FULL),
-            (bias_table.shape, FULL),
-        ],
-        [here] + to_owners(self_grads) + [hot],
-        scalars=1,
     )
     return (
         block_output[None],
@@ -1167,7 +1273,7 @@
         grad_expand,
         grad_contract,
         grad_norm_gains,
-        grad_table,
+        grad_table.T,
     )
 
 

time: 244 us -> 214 us (0.88)
  blocking collectives: 38 us -> 0 us
  starting transfers between devices: 40.7 us -> 61.7 us
  waiting for transfers between devices: 53.4 us -> 67.4 us
  between operations: 15.7 us -> 2.49 us
  local copies, waits for them, and re-layouts: 22.3 us -> 14 us
  other arithmetic: 6.99 us -> 3.06 us
    all_to_all x2 -> x0, blocking collectives: 38 us -> none  [exchange(): return lax.all_to_all(values, axis, 0, 0, tiled=True)]
    ppermute x29 -> x48, starting transfers between devices: 18.3 us -> 39.2 us  [swap_ctx(): return lax.ppermute(values, 'ctx', [(i, i ^ mask) for i in range(size)])]
    ppermute x9 -> x6, waiting for transfers between devices: 0.02 us -> 12.9 us  [swap_pb(): return lax.ppermute(values, 'pb', [(i, i ^ mask) for i in range(size)])]
    slice x6 -> x4, local copies, waits for them, and re-layouts: 8.15 us -> 1.08 us  [the longest x2 1.03 us: second_hop(): high = swap_ctx(along[1][middle:], 2)]
    all_to_all x2 -> x3, starting transfers between devices: 7.11 us -> 12.4 us  [exchange(): return lax.all_to_all(values, axis, 0, 0, tiled=True)]
    ppermute x9 -> x6, starting transfers between devices: 15.3 us -> 10.1 us  [swap_pb(): return lax.ppermute(values, 'pb', [(i, i ^ mask) for i in range(size)])]
    ppermute x29 -> x48, waiting for transfers between devices: 43.9 us -> 48.8 us  [swap_ctx(): return lax.ppermute(values, 'ctx', [(i, i ^ mask) for i in range(size)])]
    all_to_all x2 -> x3, waiting for transfers between devices: 9.46 us -> 5.75 us  [exchange(): return lax.all_to_all(values, axis, 0, 0, tiled=True)]
  transfers between devices with their start and end apart: 41 -> 57, of which waited for: 10 -> 26; matrix products, arithmetic and copies ran while one was open for 8% -> 4% of each run, Pallas kernels for 22% -> 24%
where the time goes in v3:
time: 214 us; the launch traced here: 213 us
  waiting for transfers between devices  67.4 us (31%)
  Pallas kernels  63.6 us (30%)
  starting transfers between devices  61.7 us (29%)
  local copies, waits for them, and re-layouts  14 us (7%)
  other arithmetic  3.06 us (1%)
  between operations  2.49 us (1%)
    pallas_call x15, Pallas kernels, call(): pl.pallas_call(kernel, grid=grid, out_shape=[jax.ShapeDtypeStruct(shape,...  63.6 us
    ppermute x48, waiting for transfers between devices, swap_ctx(): return lax.ppermute(values, 'ctx', [(i, i ^ mask) for i in range(size)])  48.8 us
    ppermute x48, starting transfers between devices, swap_ctx(): return lax.ppermute(values, 'ctx', [(i, i ^ mask) for i in range(size)])  39.2 us
    ppermute x6, waiting for transfers between devices, swap_pb(): return lax.ppermute(values, 'pb', [(i, i ^ mask) for i in range(size)])  12.9 us
    all_to_all x3, starting transfers between devices, exchange(): return lax.all_to_all(values, axis, 0, 0, tiled=True)  12.4 us
    ppermute x6, starting transfers between devices, swap_pb(): return lax.ppermute(values, 'pb', [(i, i ^ mask) for i in range(size)])  10.1 us
    unnamed x88, local copies, waits for them, and re-layouts  8.74 us
    all_to_all x3, waiting for transfers between devices, exchange(): return lax.all_to_all(values, axis, 0, 0, tiled=True)  5.75 us
  transfers between devices with their start and end apart: 57, of which 26 were waited for; matrix products, arithmetic and copies ran while one was open for 4% of the time, Pallas kernels for 24%

profile of v3, /device:TPU:0, one launch (start us, length us, event | category | flops | bytes accessed | tf_op | source)
XLA Modules:
  0.0 213.0 jit_solution(10785037349150957077)
XLA Ops:
  2.5 3.0 %collective-permute-start = (bf16[24,3968]{1,0:T(8,128)(2,1)}, bf16[24,3968]{1,0:T(8,128)(2,1)S(1)}, u32[]{:S(2)}, u32[]{:S(2)}) collective-permute-start(bf16[24,3968]{1,0:T(8,128)(2,1)} %shard_map.247), channel_id=1, source_target_pairs={{0,8},{8,0},{16,24},{24,16},{1,9},{9,1},{17,25},{25,17},{2,10},{10... | collective-permute-start | bytes 571400 | tf_op jit(solution)/shard_map/ppermute | solution.py:376
  5.5 2.6 %collective-permute-start.1 = (bf16[24,3968]{1,0:T(8,128)(2,1)}, bf16[24,3968]{1,0:T(8,128)(2,1)S(1)}, u32[]{:S(2)}, u32[]{:S(2)}) collective-permute-start(bf16[24,3968]{1,0:T(8,128)(2,1)} %shard_map.247), channel_id=1, source_target_pairs={{0,16},{8,24},{16,0},{24,8},{1,17},{9,25},{17,1},{25,9},{2,18},{10... | collective-permute-start | bytes 571400 | tf_op jit(solution)/shard_map/ppermute | solution.py:376
  15.5 7.0 %collective-permute-done.1 = bf16[24,3968]{1,0:T(8,128)(2,1)S(1)} collective-permute-done((bf16[24,3968]{1,0:T(8,128)(2,1)}, bf16[24,3968]{1,0:T(8,128)(2,1)S(1)}, u32[]{:S(2)}, u32[]{:S(2)}) %collective-permute-start.1) | collective-permute-done | bytes 190496 | tf_op jit(solution)/shard_map/ppermute | solution.py:376
  22.5 2.4 %collective-permute-start.7 = (bf16[24,768]{1,0:T(8,128)(2,1)S(1)}, bf16[24,768]{1,0:T(8,128)(2,1)S(1)}, u32[]{:S(2)}, u32[]{:S(2)}) collective-permute-start(bf16[24,768]{1,0:T(8,128)(2,1)S(1)} %get-tuple-element.131), channel_id=1, source_target_pairs={{0,6},{1,7},{2,4},{3,5},{4,2},{5,3},{6,0},{7,1},{8,14},{9,15},{10,... | collective-permute-start | bytes 110600 | tf_op jit(solution)/shard_map/ppermute | solution.py:371
  26.0 2.2 %collective-permute-start.9 = (bf16[24,2304]{1,0:T(8,128)(2,1)S(1)}, bf16[24,2304]{1,0:T(8,128)(2,1)S(1)}, u32[]{:S(2)}, u32[]{:S(2)}) collective-permute-start(bf16[24,2304]{1,0:T(8,128)(2,1)S(1)} %pad_maximum_fusion.3), channel_id=1, source_target_pairs={{0,16},{8,24},{16,0},{24,8},{1,17},{9,25},{17,1},{25,9},{2,18},{10... | collective-permute-start | bytes 331784 | tf_op jit(solution)/shard_map/ppermute | solution.py:376
  31.6 4.6 %collective-permute-done.9 = bf16[24,2304]{1,0:T(8,128)(2,1)S(1)} collective-permute-done((bf16[24,2304]{1,0:T(8,128)(2,1)S(1)}, bf16[24,2304]{1,0:T(8,128)(2,1)S(1)}, u32[]{:S(2)}, u32[]{:S(2)}) %collective-permute-start.9) | collective-permute-done | bytes 110624 | tf_op jit(solution)/shard_map/ppermute | solution.py:376
  37.4 4.0 %all-to-all-start = ((bf16[4,96,1536]{2,1,0:T(8,128)(2,1)}), bf16[4,96,1536]{2,1,0:T(8,128)(2,1)S(1)}, u32[]{:S(2)}, u32[]{:S(2)}) async-start(bf16[4,96,1536]{2,1,0:T(8,128)(2,1)} %broadcast_in_dim.8), calls=%async_computation | async-start | bytes 2359296 | tf_op jit(solution)/shard_map/all_to_all | solution.py:380
  41.4 4.2 %collective-permute-done.11.refs_2_ = bf16[4,24,3968]{2,1,0:T(8,128)(2,1)S(1)} collective-permute-done((bf16[4,24,3968]{2,1,0:T(8,128)(2,1)S(1)}, bf16[4,24,3968]{2,1,0:T(8,128)(2,1)S(1)}, u32[]{:S(2)}, u32[]{:S(2)}) %collective-permute-start.11) | collective-permute-done | bytes 761888 | tf_op jit(solution)/shard_map/ppermute | solution.py:371
  52.8 4.8 %collective-permute-done.18.refs_6_ = bf16[2,24,3968]{2,1,0:T(8,128)(2,1)} collective-permute-done((bf16[2,24,3968]{2,1,0:T(8,128)(2,1)S(1)}, bf16[2,24,3968]{2,1,0:T(8,128)(2,1)}, u32[]{:S(2)}, u32[]{:S(2)}) %collective-permute-start.18) | collective-permute-done | bytes 380960 | tf_op jit(solution)/shard_map/ppermute | solution.py:371
  57.6 3.2 %collective-permute-done.20.refs_8_ = bf16[2,24,3968]{2,1,0:T(8,128)(2,1)} collective-permute-done((bf16[2,24,3968]{2,1,0:T(8,128)(2,1)S(1)}, bf16[2,24,3968]{2,1,0:T(8,128)(2,1)}, u32[]{:S(2)}, u32[]{:S(2)}) %collective-permute-start.20) | collective-permute-done | bytes 380960 | tf_op jit(solution)/shard_map/ppermute | solution.py:371
  60.8 4.6 %collective-permute-done.13.refs_2_ = bf16[4,24,2304]{2,1,0:T(8,128)(2,1)S(1)} collective-permute-done((bf16[4,24,2304]{2,1,0:T(8,128)(2,1)S(1)}, bf16[4,24,2304]{2,1,0:T(8,128)(2,1)S(1)}, u32[]{:S(2)}, u32[]{:S(2)}) %collective-permute-start.13) | collective-permute-done | bytes 442400 | tf_op jit(solution)/shard_map/ppermute | solution.py:371
  68.1 11.3 %shard_map.248 = (bf16[768,2304]{1,0:T(8,128)(2,1)}, bf16[768,768]{1,0:T(8,128)(2,1)}, bf16[768,768]{1,0:T(8,128)(2,1)}, f32[3,768]{1,0:T(4,128)}, bf16[128,2304...) custom-call(s32[5]{0:T(128)} %stack.49.here, ...), custom_call_target="tpu_custom_call" | custom-call | tf_op jit(solution)/shard_map/pallas_call | solution.py:54
  84.6 3.0 %collective-permute-done.25.refs_6_ = bf16[2,24,2304]{2,1,0:T(8,128)(2,1)S(1)} collective-permute-done((bf16[2,24,2304]{2,1,0:T(8,128)(2,1)S(1)}, bf16[2,24,2304]{2,1,0:T(8,128)(2,1)S(1)}, u32[]{:S(2)}, u32[]{:S(2)}) %collective-permute-start.25) | collective-permute-done | bytes 221216 | tf_op jit(solution)/shard_map/ppermute | solution.py:371
  87.6 2.9 %collective-permute-done.27.refs_8_ = bf16[2,24,2304]{2,1,0:T(8,128)(2,1)S(1)} collective-permute-done((bf16[2,24,2304]{2,1,0:T(8,128)(2,1)S(1)}, bf16[2,24,2304]{2,1,0:T(8,128)(2,1)S(1)}, u32[]{:S(2)}, u32[]{:S(2)}) %collective-permute-start.27) | collective-permute-done | bytes 221216 | tf_op jit(solution)/shard_map/ppermute | solution.py:371
  92.7 4.0 %shard_map.249 = (bf16[768,1536]{1,0:T(8,128)(2,1)}, bf16[480,768]{1,0:T(8,128)(2,1)}) custom-call(s32[5]{0:T(128)} %stack.49.here, bf16[240,768]{1,0:T(8,128)(2,1)} %bitcast.33, bf16[240,768]{1,0:T(8,128)(2,1)} %copy-done.13, bf16[4,24,2304]{2,1,0:T(8,128)(2,1)} %copy-done.4, bf16[4,24,2304]{2,1,0:T(8,128)(2,1)} %copy-done.8, ...), custom_call_target="tpu_custom_call" | custom-call | tf_op jit(solution)/shard_map/pallas_call | solution.py:54
  96.7 3.7 %shard_map.250.refs_0_ = bf16[128,512]{1,0:T(8,128)(2,1)} custom-call(bf16[128,384]{1,0:T(8,128)(2,1)} %get-tuple-element.75.cq, bf16[480,768]{1,0:T(8,128)(2,1)} %get-tuple-element.76.memory, s32[1,480]{1,0:T(1,128)} %pad_add_fusion.visible), custom_call_target="tpu_custom_call" | custom-call | tf_op jit(solution)/shard_map/pallas_call | solution.py:54
  103.9 2.5 %collective-permute-done.29.refs_1_ = bf16[128,512]{1,0:T(8,128)(2,1)S(1)} collective-permute-done((bf16[128,512]{1,0:T(8,128)(2,1)}, bf16[128,512]{1,0:T(8,128)(2,1)S(1)}, u32[]{:S(2)}, u32[]{:S(2)}) %collective-permute-start.29) | collective-permute-done | bytes 131104 | tf_op jit(solution)/shard_map/ppermute | solution.py:371
  106.4 3.9 %collective-permute-done.30.refs_2_ = bf16[128,512]{1,0:T(8,128)(2,1)S(1)} collective-permute-done((bf16[128,512]{1,0:T(8,128)(2,1)}, bf16[128,512]{1,0:T(8,128)(2,1)S(1)}, u32[]{:S(2)}, u32[]{:S(2)}) %collective-permute-start.30) | collective-permute-done | bytes 131104 | tf_op jit(solution)/shard_map/ppermute | solution.py:371
  111.6 2.8 %shard_map.251 = (bf16[128,384]{1,0:T(8,128)(2,1)}, bf16[128,128]{1,0:T(8,128)(2,1)}) custom-call(s32[5]{0:T(128)} %stack.49.here, bf16[128,512]{1,0:T(8,128)(2,1)} %shard_map.250.refs_0_, bf16[128,512]{1,0:T(8,128)(2,1)} %copy-done.30, bf16[128,512]{1,0:T(8,128)(2,1)} %copy-done.31, bf16[128,512]{1,0:T(8,128)(2,1)} %copy-done.32), custom_call_target="tpu_custom_call" | custom-call | tf_op jit(solution)/shard_map/pallas_call | solution.py:54
  117.1 4.8 %shard_map.252 = (bf16[768,768]{1,0:T(8,128)(2,1)}, f32[128,768]{1,0:T(8,128)}, bf16[128,768]{1,0:T(8,128)(2,1)}, bf16[128,768]{1,0:T(8,128)(2,1)}, bf16[128,768...) custom-call(s32[5]{0:T(128)} %stack.49.here, ...), custom_call_target="tpu_custom_call" | custom-call | tf_op jit(solution)/shard_map/pallas_call | solution.py:54
  121.8 3.1 %shard_map.259 = bf16[4,192,768]{2,1,0:T(8,128)(2,1)} custom-call(s32[5]{0:T(128)} %stack.49.here, bf16[128,768]{1,0:T(8,128)(2,1)} %get-tuple-element.118.active, bf16[128,768]{1,0:T(8,128)(2,1)} %get-tuple-element.119.low_out, bf16[128,768]{1,0:T(8,128)(2,1)} %get-tuple-element.120.h3, bf16[128,768]{1,0:T(8,128)(2,1)} %get-tuple-element.121.grad_hidden), custom_call_target="tpu_custom_call" | custom-call | tf_op jit(solution)/shard_map/pallas_call | solution.py:54
  124.9 3.9 %all-to-all-start.2 = ((bf16[4,192,768]{2,1,0:T(8,128)(2,1)}), bf16[4,192,768]{2,1,0:T(8,128)(2,1)S(1)}, u32[]{:S(2)}, u32[]{:S(2)}) async-start(bf16[4,192,768]{2,1,0:T(8,128)(2,1)} %shard_map.259), calls=%async_computation.2 | async-start | bytes 2359296 | tf_op jit(solution)/shard_map/all_to_all | solution.py:380
  130.0 2.4 %collective-permute-start.36 = (bf16[128,384]{1,0:T(8,128)(2,1)S(1)}, bf16[128,384]{1,0:T(8,128)(2,1)S(1)}, u32[]{:S(2)}, u32[]{:S(2)}) collective-permute-start(bf16[128,384]{1,0:T(8,128)(2,1)S(1)} %copy-done.35), channel_id=1, source_target_pairs={{0,6},{1,7},{2,4},{3,5},{4,2},{5,3},{6,0},{7,1},{8,14},{9,15},{10,... | collective-permute-start | bytes 294920 | tf_op jit(solution)/shard_map/ppermute | solution.py:371
  138.1 5.2 %shard_map.253 = (f32[128,768]{1,0:T(8,128)}, bf16[128,768]{1,0:T(8,128)(2,1)}, bf16[128,384]{1,0:T(8,128)(2,1)}, bf16[240,768]{1,0:T(8,128)(2,1)}, bf16[240,768]{1,0:T(8,128)(2,1)}, /*index=5*/f32[1,768]{1,0:T(1,128)}) custom-call(s32[5]{0:T(128)} %stack.49.here, s32[1]{0:T(128)S(6)} %copy.29.length, s32[1]{0:T(128)S(6)} %copy.30.task, ...), custom_call_target="tpu_custom_call" | custom-call | tf_op jit(solution)/shard_map/pallas_call | solution.py:54
  146.9 3.2 %shard_map.255 = (bf16[192,768]{1,0:T(8,128)(2,1)}, bf16[192,768]{1,0:T(8,128)(2,1)}, bf16[192,768]{1,0:T(8,128)(2,1)}, bf16[192,768]{1,0:T(8,128)(2,1)}) custom-call(s32[5]{0:T(128)} %stack.49.here, bf16[240,768]{1,0:T(8,128)(2,1)} %bitcast.34, bf16[240,768]{1,0:T(8,128)(2,1)} %copy-done.13, bf16[240,768]{1,0:T(8,128)(2,1)} %get-tuple-element.110.grad_mine.mine, ...), custom_call_target="tpu_custom_call" | custom-call | tf_op jit(solution)/shard_map/pallas_call | solution.py:54
  155.6 9.1 %shard_map.254 = (bf16[128,768]{1,0:T(8,128)(2,1)}, bf16[128,2304]{1,0:T(8,128)(2,1)}, bf16[128,768]{1,0:T(8,128)(2,1)}, f32[16,768]{1,0:T(8,128)}) custom-call(s32[5]{0:T(128)} %stack.49.here, bf16[128,384]{1,0:T(8,128)(2,1)} %copy-done.15, bf16[128,384]{1,0:T(8,128)(2,1)} %copy-done.21, bf16[768,768]{1,0:T(8,128)(2,1)} %get-tuple-element.91.cross_in, ...), custom_call_target="tpu_custom_call" | custom-call | tf_op jit(solution)/shard_map/pallas_call | solution.py:54
  166.9 4.7 %shard_map.256 = bf16[4,208,768]{2,1,0:T(8,128)(2,1)} custom-call(s32[5]{0:T(128)} %stack.49.here, bf16[128,384]{1,0:T(8,128)(2,1)} %get-tuple-element.77.mix_mine.mix, bf16[128,384]{1,0:T(8,128)(2,1)} %copy-done.23, bf16[128,768]{1,0:T(8,128)(2,1)} %get-tuple-element.87.low_cross, bf16[128,768]{1,0:T(8,128)(2,1)} %get-tuple-element.88.h2, ...), custom_call_target="tpu_custom_call" | custom-call | tf_op jit(solution)/shard_map/pallas_call | solution.py:54
  172.7 4.6 %all-to-all-start.1 = ((bf16[4,208,768]{2,1,0:T(8,128)(2,1)}), bf16[4,208,768]{2,1,0:T(8,128)(2,1)S(1)}, u32[]{:S(2)}, u32[]{:S(2)}) async-start(bf16[4,208,768]{2,1,0:T(8,128)(2,1)} %shard_map.256), calls=%async_computation.1 | async-start | bytes 2555904 | tf_op jit(solution)/shard_map/all_to_all | solution.py:380
  186.3 3.5 %shard_map.257 = bf16[240,768]{1,0:T(8,128)(2,1)} custom-call(s32[5]{0:T(128)} %stack.49.here, bf16[240,768]{1,0:T(8,128)(2,1)} %get-tuple-element.110.grad_mine.mine, bf16[240,768]{1,0:T(8,128)(2,1)} %copy-done.25, bf16[768,1536]{1,0:T(8,128)(2,1)} %get-tuple-element.111.memory_in), custom_call_target="tpu_custom_call" | custom-call | tf_op jit(solution)/shard_map/pallas_call | solution.py:54
  189.8 2.3 %shard_map.260 = (f32[96,768]{1,0:T(8,128)}, bf16[24,768]{1,0:T(8,128)(2,1)}, bf16[24,768]{1,0:T(8,128)(2,1)}, bf16[24,768]{1,0:T(8,128)(2,1)}, bf16[24,768]{1,0:T(8,128)(2,1)}) custom-call(s32[5]{0:T(128)} %stack.49.here, bf16[4,192,768]{2,1,0:T(8,128)(2,1)} %copy-done.3), custom_call_target="tpu_custom_call" | custom-call | tf_op jit(solution)/shard_map/pallas_call | solution.py:54
  201.4 5.7 %all-to-all-done.1.parts = bf16[4,208,768]{2,1,0:T(8,128)(2,1)S(1)} async-done(((bf16[4,208,768]{2,1,0:T(8,128)(2,1)}), bf16[4,208,768]{2,1,0:T(8,128)(2,1)S(1)}, u32[]{:S(2)}, u32[]{:S(2)}) %all-to-all-start.1) | async-done | bytes 1277984 | tf_op jit(solution)/shard_map/all_to_all | solution.py:380
  208.3 2.5 %shard_map.258 = (f32[24,2304]{1,0:T(8,128)}, f32[24,768]{1,0:T(8,128)}, f32[24,768]{1,0:T(8,128)}, f32[24,768]{1,0:T(8,128)}, f32[24,768]{1,0:T(8,128)}, /*inde...) custom-call(s32[5]{0:T(128)} %stack.49.here, bf16[4,208,768]{2,1,0:T(8,128)(2,1)} %copy-done.1, ...), custom_call_target="tpu_custom_call" | custom-call | tf_op jit(solution)/shard_map/pallas_call | solution.py:54
  (211 shorter events, 78.8 us)
Async XLA Ops:
  2.5 11.3 %collective-permute-start = (bf16[24,3968]{1,0:T(8,128)(2,1)}, bf16[24,3968]{1,0:T(8,128)(2,1)S(1)}, u32[]{:S(2)}, u32[]{:S(2)}) collective-permute-start(bf16[24,3968]{1,0:T(8,128)(2,1)} %shard_map.247), channel_id=1, source_target_pairs={{0,8},{8,0},{16,24},{24,16},{1,9},{9,1},{17,25},{25,17},{2,10},{10... | collective-permute-start | bytes 571400 | tf_op jit(solution)/shard_map/ppermute | solution.py:376
  5.5 17.0 %collective-permute-start.1 = (bf16[24,3968]{1,0:T(8,128)(2,1)}, bf16[24,3968]{1,0:T(8,128)(2,1)S(1)}, u32[]{:S(2)}, u32[]{:S(2)}) collective-permute-start(bf16[24,3968]{1,0:T(8,128)(2,1)} %shard_map.247), channel_id=1, source_target_pairs={{0,16},{8,24},{16,0},{24,8},{1,17},{9,25},{17,1},{25,9},{2,18},{10... | collective-permute-start | bytes 571400 | tf_op jit(solution)/shard_map/ppermute | solution.py:376
  8.1 16.8 %collective-permute-start.2 = (bf16[24,3968]{1,0:T(8,128)(2,1)}, bf16[24,3968]{1,0:T(8,128)(2,1)S(1)}, u32[]{:S(2)}, u32[]{:S(2)}) collective-permute-start(bf16[24,3968]{1,0:T(8,128)(2,1)} %shard_map.247), channel_id=1, source_target_pairs={{0,24},{8,16},{16,8},{24,0},{1,25},{9,17},{17,9},{25,1},{2,26},{10... | collective-permute-start | bytes 571400 | tf_op jit(solution)/shard_map/ppermute | solution.py:376
  8.1 17.0 %collective-permute-start.3 = (bf16[240,768]{1,0:T(8,128)(2,1)}, bf16[240,768]{1,0:T(8,128)(2,1)S(1)}, u32[]{:S(2)}, u32[]{:S(2)}) collective-permute-start(bf16[240,768]{1,0:T(8,128)(2,1)} %bitcast.32), channel_id=1, source_target_pairs={{0,1},{1,0},{2,3},{3,2},{4,5},{5,4},{6,7},{7,6},{8,9},{9,8},{10,11... | collective-permute-start | bytes 1105928 | tf_op jit(solution)/shard_map/ppermute | solution.py:371
  10.2 18.0 %collective-permute-start.5 = (bf16[24,768]{1,0:T(8,128)(2,1)S(1)}, bf16[24,768]{1,0:T(8,128)(2,1)S(1)}, u32[]{:S(2)}, u32[]{:S(2)}) collective-permute-start(bf16[24,768]{1,0:T(8,128)(2,1)S(1)} %get-tuple-element.133), channel_id=1, source_target_pairs={{0,2},{1,3},{2,0},{3,1},{4,6},{5,7},{6,4},{7,5},{8,10},{9,11},{10,... | collective-permute-start | bytes 110600 | tf_op jit(solution)/shard_map/ppermute | solution.py:371
  13.8 15.7 %collective-permute-start.6 = (bf16[24,768]{1,0:T(8,128)(2,1)S(1)}, bf16[24,768]{1,0:T(8,128)(2,1)S(1)}, u32[]{:S(2)}, u32[]{:S(2)}) collective-permute-start(bf16[24,768]{1,0:T(8,128)(2,1)S(1)} %get-tuple-element.132), channel_id=1, source_target_pairs={{0,4},{1,5},{2,6},{3,7},{4,0},{5,1},{6,2},{7,3},{8,12},{9,13},{10,... | collective-permute-start | bytes 110600 | tf_op jit(solution)/shard_map/ppermute | solution.py:371
  26.0 10.2 %collective-permute-start.9 = (bf16[24,2304]{1,0:T(8,128)(2,1)S(1)}, bf16[24,2304]{1,0:T(8,128)(2,1)S(1)}, u32[]{:S(2)}, u32[]{:S(2)}) collective-permute-start(bf16[24,2304]{1,0:T(8,128)(2,1)S(1)} %pad_maximum_fusion.3), channel_id=1, source_target_pairs={{0,16},{8,24},{16,0},{24,8},{1,17},{9,25},{17,1},{25,9},{2,18},{10... | collective-permute-start | bytes 331784 | tf_op jit(solution)/shard_map/ppermute | solution.py:376
  28.2 8.0 %collective-permute-start.10 = (bf16[24,2304]{1,0:T(8,128)(2,1)S(1)}, bf16[24,2304]{1,0:T(8,128)(2,1)S(1)}, u32[]{:S(2)}, u32[]{:S(2)}) collective-permute-start(bf16[24,2304]{1,0:T(8,128)(2,1)S(1)} %pad_maximum_fusion.3), channel_id=1, source_target_pairs={{0,24},{8,16},{16,8},{24,0},{1,25},{9,17},{17,9},{25,1},{2,26},{10... | collective-permute-start | bytes 331784 | tf_op jit(solution)/shard_map/ppermute | solution.py:376
  29.6 16.0 %collective-permute-start.11 = (bf16[4,24,3968]{2,1,0:T(8,128)(2,1)S(1)}, bf16[4,24,3968]{2,1,0:T(8,128)(2,1)S(1)}, u32[]{:S(2)}, u32[]{:S(2)}) collective-permute-start(bf16[4,24,3968]{2,1,0:T(8,128)(2,1)S(1)} %pad_maximum_fusion.refs_0_), channel_id=1, source_target_pairs={{0,2},{1,3},{2,0},{3,1},{4,6},{5,7},{6,4},{7,5},{8,10},{9,11},{10,... | collective-permute-start | bytes 2285576 | tf_op jit(solution)/shard_map/ppermute | solution.py:371
  30.2 18.2 %collective-permute-start.12 = (bf16[4,24,3968]{2,1,0:T(8,128)(2,1)S(1)}, bf16[4,24,3968]{2,1,0:T(8,128)(2,1)}, u32[]{:S(2)}, u32[]{:S(2)}) collective-permute-start(bf16[4,24,3968]{2,1,0:T(8,128)(2,1)S(1)} %pad_maximum_fusion.refs_0_), channel_id=1, source_target_pairs={{0,4},{1,5},{2,6},{3,7},{4,0},{5,1},{6,2},{7,3},{8,12},{9,13},{10,... | collective-permute-start | bytes 2285576 | tf_op jit(solution)/shard_map/ppermute | solution.py:371
  37.4 42.0 %all-to-all-start = ((bf16[4,96,1536]{2,1,0:T(8,128)(2,1)}), bf16[4,96,1536]{2,1,0:T(8,128)(2,1)S(1)}, u32[]{:S(2)}, u32[]{:S(2)}) async-start(bf16[4,96,1536]{2,1,0:T(8,128)(2,1)} %broadcast_in_dim.8), calls=%async_computation | async-start | bytes 2359296 | tf_op jit(solution)/shard_map/all_to_all | solution.py:380
  45.6 12.0 %collective-permute-start.18 = (bf16[2,24,3968]{2,1,0:T(8,128)(2,1)S(1)}, bf16[2,24,3968]{2,1,0:T(8,128)(2,1)}, u32[]{:S(2)}, u32[]{:S(2)}) collective-permute-start(bf16[2,24,3968]{2,1,0:T(8,128)(2,1)S(1)} %slice.32), channel_id=1, source_target_pairs={{0,4},{1,5},{2,6},{3,7},{4,0},{5,1},{6,2},{7,3},{8,12},{9,13},{10,... | collective-permute-start | bytes 1142792 | tf_op jit(solution)/shard_map/ppermute | solution.py:371
  49.4 11.4 %collective-permute-start.20 = (bf16[2,24,3968]{2,1,0:T(8,128)(2,1)S(1)}, bf16[2,24,3968]{2,1,0:T(8,128)(2,1)}, u32[]{:S(2)}, u32[]{:S(2)}) collective-permute-start(bf16[2,24,3968]{2,1,0:T(8,128)(2,1)S(1)} %slice.33), channel_id=1, source_target_pairs={{0,2},{1,3},{2,0},{3,1},{4,6},{5,7},{6,4},{7,5},{8,10},{9,11},{10,... | collective-permute-start | bytes 1142792 | tf_op jit(solution)/shard_map/ppermute | solution.py:371
  49.8 15.7 %collective-permute-start.13 = (bf16[4,24,2304]{2,1,0:T(8,128)(2,1)S(1)}, bf16[4,24,2304]{2,1,0:T(8,128)(2,1)S(1)}, u32[]{:S(2)}, u32[]{:S(2)}) collective-permute-start(bf16[4,24,2304]{2,1,0:T(8,128)(2,1)S(1)} %pad_maximum_fusion.1.refs_0_), channel_id=1, source_target_pairs={{0,2},{1,3},{2,0},{3,1},{4,6},{5,7},{6,4},{7,5},{8,10},{9,11},{10,... | collective-permute-start | bytes 1327112 | tf_op jit(solution)/shard_map/ppermute | solution.py:371
  51.5 13.9 %collective-permute-start.14 = (bf16[4,24,2304]{2,1,0:T(8,128)(2,1)S(1)}, bf16[4,24,2304]{2,1,0:T(8,128)(2,1)S(1)}, u32[]{:S(2)}, u32[]{:S(2)}) collective-permute-start(bf16[4,24,2304]{2,1,0:T(8,128)(2,1)S(1)} %pad_maximum_fusion.1.refs_0_), channel_id=1, source_target_pairs={{0,4},{1,5},{2,6},{3,7},{4,0},{5,1},{6,2},{7,3},{8,12},{9,13},{10,... | collective-permute-start | bytes 1327112 | tf_op jit(solution)/shard_map/ppermute | solution.py:371
  52.8 15.3 %collective-permute-start.15 = (bf16[4,24,3968]{2,1,0:T(8,128)(2,1)S(1)}, bf16[4,24,3968]{2,1,0:T(8,128)(2,1)}, u32[]{:S(2)}, u32[]{:S(2)}) collective-permute-start(bf16[4,24,3968]{2,1,0:T(8,128)(2,1)S(1)} %pad_maximum_fusion.refs_0_), channel_id=1, source_target_pairs={{0,1},{1,0},{2,3},{3,2},{4,5},{5,4},{6,7},{7,6},{8,9},{9,8},{10,11... | collective-permute-start | bytes 2285576 | tf_op jit(solution)/shard_map/ppermute | solution.py:371
  57.6 10.5 %collective-permute-start.16 = (bf16[4,24,3968]{2,1,0:T(8,128)(2,1)}, bf16[4,24,3968]{2,1,0:T(8,128)(2,1)}, u32[]{:S(2)}, u32[]{:S(2)}) collective-permute-start(bf16[4,24,3968]{2,1,0:T(8,128)(2,1)} %copy-done.11), channel_id=1, source_target_pairs={{0,1},{1,0},{2,3},{3,2},{4,5},{5,4},{6,7},{7,6},{8,9},{9,8},{10,11... | collective-permute-start | bytes 2285576 | tf_op jit(solution)/shard_map/ppermute | solution.py:371
  79.5 36.5 %collective-permute-start.33 = (bf16[4,96,1536]{2,1,0:T(8,128)(2,1)S(1)}, bf16[4,96,1536]{2,1,0:T(8,128)(2,1)S(1)}, u32[]{:S(2)}, u32[]{:S(2)}) collective-permute-start(bf16[4,96,1536]{2,1,0:T(8,128)(2,1)S(1)} %all-to-all-done.feed_mine), channel_id=1, source_target_pairs={{0,1},{1,0},{2,3},{3,2},{4,5},{5,4},{6,7},{7,6},{8,9},{9,8},{10,11... | collective-permute-start | bytes 3538952 | tf_op jit(solution)/shard_map/ppermute | solution.py:371
  80.1 7.5 %collective-permute-start.25 = (bf16[2,24,2304]{2,1,0:T(8,128)(2,1)S(1)}, bf16[2,24,2304]{2,1,0:T(8,128)(2,1)S(1)}, u32[]{:S(2)}, u32[]{:S(2)}) collective-permute-start(bf16[2,24,2304]{2,1,0:T(8,128)(2,1)S(1)} %slice.34), channel_id=1, source_target_pairs={{0,4},{1,5},{2,6},{3,7},{4,0},{5,1},{6,2},{7,3},{8,12},{9,13},{10,... | collective-permute-start | bytes 663560 | tf_op jit(solution)/shard_map/ppermute | solution.py:371
  81.4 9.1 %collective-permute-start.23 = (bf16[4,24,2304]{2,1,0:T(8,128)(2,1)S(1)}, bf16[4,24,2304]{2,1,0:T(8,128)(2,1)S(1)}, u32[]{:S(2)}, u32[]{:S(2)}) collective-permute-start(bf16[4,24,2304]{2,1,0:T(8,128)(2,1)S(1)} %collective-permute-done.13.refs_2_), channel_id=1, source_target_pairs={{0,1},{1,0},{2,3},{3,2},{4,5},{5,4},{6,7},{7,6},{8,9},{9,8},{10,11... | collective-permute-start | bytes 1327112 | tf_op jit(solution)/shard_map/ppermute | solution.py:371
  81.5 9.0 %collective-permute-start.24 = (bf16[4,24,2304]{2,1,0:T(8,128)(2,1)S(1)}, bf16[4,24,2304]{2,1,0:T(8,128)(2,1)S(1)}, u32[]{:S(2)}, u32[]{:S(2)}) collective-permute-start(bf16[4,24,2304]{2,1,0:T(8,128)(2,1)S(1)} %collective-permute-done.14.refs_4_), channel_id=1, source_target_pairs={{0,1},{1,0},{2,3},{3,2},{4,5},{5,4},{6,7},{7,6},{8,9},{9,8},{10,11... | collective-permute-start | bytes 1327112 | tf_op jit(solution)/shard_map/ppermute | solution.py:371
  102.0 8.3 %collective-permute-start.30 = (bf16[128,512]{1,0:T(8,128)(2,1)}, bf16[128,512]{1,0:T(8,128)(2,1)S(1)}, u32[]{:S(2)}, u32[]{:S(2)}) collective-permute-start(bf16[128,512]{1,0:T(8,128)(2,1)} %shard_map.250.refs_0_), channel_id=1, source_target_pairs={{0,4},{1,5},{2,6},{3,7},{4,0},{5,1},{6,2},{7,3},{8,12},{9,13},{10,... | collective-permute-start | bytes 393224 | tf_op jit(solution)/shard_map/ppermute | solution.py:371
  102.5 7.8 %collective-permute-start.31 = (bf16[128,512]{1,0:T(8,128)(2,1)}, bf16[128,512]{1,0:T(8,128)(2,1)S(1)}, u32[]{:S(2)}, u32[]{:S(2)}) collective-permute-start(bf16[128,512]{1,0:T(8,128)(2,1)} %shard_map.250.refs_0_), channel_id=1, source_target_pairs={{0,6},{1,7},{2,4},{3,5},{4,2},{5,3},{6,0},{7,1},{8,14},{9,15},{10,... | collective-permute-start | bytes 393224 | tf_op jit(solution)/shard_map/ppermute | solution.py:371
  124.9 46.7 %all-to-all-start.2 = ((bf16[4,192,768]{2,1,0:T(8,128)(2,1)}), bf16[4,192,768]{2,1,0:T(8,128)(2,1)S(1)}, u32[]{:S(2)}, u32[]{:S(2)}) async-start(bf16[4,192,768]{2,1,0:T(8,128)(2,1)} %shard_map.259), calls=%async_computation.2 | async-start | bytes 2359296 | tf_op jit(solution)/shard_map/all_to_all | solution.py:380
  143.3 9.2 %collective-permute-start.38 = (bf16[128,384]{1,0:T(8,128)(2,1)}, bf16[128,384]{1,0:T(8,128)(2,1)S(1)}, u32[]{:S(2)}, u32[]{:S(2)}) collective-permute-start(bf16[128,384]{1,0:T(8,128)(2,1)} %get-tuple-element.89), channel_id=1, source_target_pairs={{0,2},{1,3},{2,0},{3,1},{4,6},{5,7},{6,4},{7,5},{8,10},{9,11},{10,... | collective-permute-start | bytes 294920 | tf_op jit(solution)/shard_map/ppermute | solution.py:371
  145.0 8.6 %collective-permute-start.39 = (bf16[128,384]{1,0:T(8,128)(2,1)}, bf16[128,384]{1,0:T(8,128)(2,1)S(1)}, u32[]{:S(2)}, u32[]{:S(2)}) collective-permute-start(bf16[128,384]{1,0:T(8,128)(2,1)} %get-tuple-element.89), channel_id=1, source_target_pairs={{0,4},{1,5},{2,6},{3,7},{4,0},{5,1},{6,2},{7,3},{8,12},{9,13},{10,... | collective-permute-start | bytes 294920 | tf_op jit(solution)/shard_map/ppermute | solution.py:371
  145.8 7.7 %collective-permute-start.40 = (bf16[128,384]{1,0:T(8,128)(2,1)}, bf16[128,384]{1,0:T(8,128)(2,1)S(1)}, u32[]{:S(2)}, u32[]{:S(2)}) collective-permute-start(bf16[128,384]{1,0:T(8,128)(2,1)} %get-tuple-element.89), channel_id=1, source_target_pairs={{0,6},{1,7},{2,4},{3,5},{4,2},{5,3},{6,0},{7,1},{8,14},{9,15},{10,... | collective-permute-start | bytes 294920 | tf_op jit(solution)/shard_map/ppermute | solution.py:371
  150.0 14.7 %collective-permute-start.42 = (bf16[192,768]{1,0:T(8,128)(2,1)}, bf16[192,768]{1,0:T(8,128)(2,1)S(1)}, u32[]{:S(2)}, u32[]{:S(2)}) collective-permute-start(bf16[192,768]{1,0:T(8,128)(2,1)} %get-tuple-element.105), channel_id=1, source_target_pairs={{0,2},{1,3},{2,0},{3,1},{4,6},{5,7},{6,4},{7,5},{8,10},{9,11},{10,... | collective-permute-start | bytes 884744 | tf_op jit(solution)/shard_map/ppermute | solution.py:371
  151.6 14.5 %collective-permute-start.43 = (bf16[192,768]{1,0:T(8,128)(2,1)}, bf16[192,768]{1,0:T(8,128)(2,1)S(1)}, u32[]{:S(2)}, u32[]{:S(2)}) collective-permute-start(bf16[192,768]{1,0:T(8,128)(2,1)} %get-tuple-element.106), channel_id=1, source_target_pairs={{0,4},{1,5},{2,6},{3,7},{4,0},{5,1},{6,2},{7,3},{8,12},{9,13},{10,... | collective-permute-start | bytes 884744 | tf_op jit(solution)/shard_map/ppermute | solution.py:371
  152.5 13.7 %collective-permute-start.44 = (bf16[192,768]{1,0:T(8,128)(2,1)}, bf16[192,768]{1,0:T(8,128)(2,1)S(1)}, u32[]{:S(2)}, u32[]{:S(2)}) collective-permute-start(bf16[192,768]{1,0:T(8,128)(2,1)} %get-tuple-element.107), channel_id=1, source_target_pairs={{0,6},{1,7},{2,4},{3,5},{4,2},{5,3},{6,0},{7,1},{8,14},{9,15},{10,... | collective-permute-start | bytes 884744 | tf_op jit(solution)/shard_map/ppermute | solution.py:371
  172.7 34.5 %all-to-all-start.1 = ((bf16[4,208,768]{2,1,0:T(8,128)(2,1)}), bf16[4,208,768]{2,1,0:T(8,128)(2,1)S(1)}, u32[]{:S(2)}, u32[]{:S(2)}) async-start(bf16[4,208,768]{2,1,0:T(8,128)(2,1)} %shard_map.256), calls=%async_computation.1 | async-start | bytes 2555904 | tf_op jit(solution)/shard_map/all_to_all | solution.py:380
  184.9 10.7 %collective-permute-start.48 = (bf16[128,384]{1,0:T(8,128)(2,1)S(1)}, bf16[128,384]{1,0:T(8,128)(2,1)S(1)}, u32[]{:S(2)}, u32[]{:S(2)}) collective-permute-start(bf16[128,384]{1,0:T(8,128)(2,1)S(1)} %add_convert_fusion.1), channel_id=1, source_target_pairs={{0,1},{1,0},{2,3},{3,2},{4,5},{5,4},{6,7},{7,6},{8,9},{9,8},{10,11... | collective-permute-start | bytes 294920 | tf_op jit(solution)/shard_map/ppermute | solution.py:371
  (69 other events, 487.1 us)

commit v4 on v3

--- a/solution.py
+++ b/solution.py
@@ -1,4 +1,5 @@
 import functools
+import math
 
 import jax
 import jax.numpy as jnp
@@ -11,7 +12,7 @@
 MASKED = -1000000000.0
 EPS = 1e-06
 HEAD = 64
-VMEM_BYTES = 56 * 1024 * 1024
+SPARE_BYTES = 6 * 1024 * 1024
 
 
 def dot(left, right, left_axis=1, right_axis=0):
@@ -41,8 +42,11 @@
     return factor * (scaled - unit * jnp.mean(scaled * unit, axis=-1, keepdims=True))
 
 
-def call(kernel, outs, args, scalars=0, scratch=()):
+def call(kernel, outs, args, scalars=0, scratch=(), spare=SPARE_BYTES):
     arrays, specs, grid = [], [], ()
+    held = [(arg[1], arg[0].dtype) if isinstance(arg, tuple) else (arg.shape, arg.dtype) for arg in args]
+    held += list(outs) + [(one.shape, one.dtype) for one in scratch]
+    size = sum(math.prod(shape) * jnp.dtype(dtype).itemsize for shape, dtype in held)
     for index, arg in enumerate(args):
         if isinstance(arg, tuple):
             arg, shape, place = arg
@@ -58,7 +62,7 @@
         in_specs=specs,
         out_specs=[pl.BlockSpec(memory_space=pltpu.VMEM) for _ in outs],
         scratch_shapes=list(scratch),
-        compiler_params=pltpu.CompilerParams(vmem_limit_bytes=VMEM_BYTES),
+        compiler_params=pltpu.CompilerParams(vmem_limit_bytes=size + spare),
     )(*arrays)
 
 
@@ -417,6 +421,15 @@
     return pick(values, zeros) if side == 0 else pick(zeros, values)
 
 
+def both_heads(values):
+    return jnp.concatenate([lane_mask(values, 0), lane_mask(values, 1)], axis=0)
+
+
+def pick_rows(values):
+    middle = values.shape[0] // 2
+    return pick(values[:middle], values[middle:])
+
+
 def join(first, mine, other, axis=1):
     return jnp.where(
         first,
@@ -446,16 +459,28 @@
         at += part.shape[1]
 
 
+def block_places(pb):
+    middle = pb // 2
+    return [
+        [(0, 0), (0, 1), (0, 2)],
+        [(r, 0) for r in range(1, pb)],
+        [(r, 1) for r in range(1, pb)],
+        [(r, 2) for r in range(1, pb)],
+        [(r, 3) for r in range(middle)],
+        [(r, 3) for r in range(middle, pb)],
+    ]
+
+
 def place(here, ins, outs, ctx):
     first = here[CORE] == 0
-    pb, rows = ins[0].shape[:2]
-    for i, (begin, flip) in enumerate([(0, 0), (0, 1), (0, 2), (0, 3), (pb // 2, 3)]):
+    pb = ins[2].shape[0] + 1
+    rows = ins[0].shape[1]
+    for i, places in enumerate(block_places(pb)):
         mine, other = ins[2 * i], ins[2 * i + 1]
-        chip = here[CHIP] ^ flip
-        for z in range(mine.shape[0]):
-            both = join(first, mine[z], other[z], 0)
-            owner = (begin + z) ^ here[PB]
-            slot = pl.multiple_of((owner * (ctx // 2) + chip) * 2 * rows, 16)
+        for k, (z, flip) in enumerate(places):
+            both = join(first, mine[k], other[k], 0)
+            owner = (z ^ here[PB]) * (ctx // 2) + (here[CHIP] ^ flip)
+            slot = pl.multiple_of(owner * 2 * rows, 16)
             at = 0
             for out in outs:
                 width = out.shape[1]
@@ -463,18 +488,19 @@
                 at += width
 
 
-def first_hop(own):
+def first_hops(own):
     return swap_ctx(own, 2), swap_ctx(own, 4)
 
 
-def second_hop(own, along):
-    middle = own.shape[0] // 2
-    low = swap_ctx(along[0][:middle], 4)
-    high = swap_ctx(along[1][middle:], 2)
+def gather_rows(own, along, far, far_along):
+    middle = (far.shape[0] + 1) // 2
+    low = jnp.concatenate([along[0][None], far_along[0][: middle - 1]])
+    low = swap_ctx(low, 4)
+    high = swap_ctx(far_along[1][middle - 1 :], 2)
     blocks = []
-    for array in (own, *along, low, high):
+    for array in (jnp.stack([own, *along]), far, *far_along, low, high):
         blocks += [array, swap_ctx(array, 1)]
-    return blocks
+    return blocks, (low, high)
 
 
 def self_kernel(ctx, here, length, x, table, *refs):
@@ -483,7 +509,7 @@
     rows, width = x.shape
     heads = width // HEAD
     pair = 2 * HEAD
-    inverse = HEAD ** (-0.5)
+    inverse = jnp.asarray(HEAD ** (-0.5), LOW)
     place(here, blocks, [proj, self_out, cross_in, columns], ctx)
     gains = columns[...].astype(FULL).T
     gains_out[...] = gains[: gains_out.shape[0]]
@@ -496,28 +522,29 @@
     row = lax.broadcasted_iota(jnp.int32, (rows, rows), 0)
     col = lax.broadcasted_iota(jnp.int32, (rows, rows), 1)
     allowed = (col <= row) & (col < length[0])
+    barred = jnp.where(allowed, 0.0, MASKED)
     mixes = []
     for g in range(heads // 2):
         at = g * pair
-        q = joined[:, at : at + pair]
+        q = both_heads(joined[:, at : at + pair] * inverse)
         k = joined[:, width + at : width + at + pair]
         v = joined[:, 2 * width + at : 2 * width + at + pair]
-        mixed = []
-        for side in range(2):
-            head = 2 * g + side
-            bias = pltpu.roll(
+        bias = [
+            pltpu.roll(
                 jnp.broadcast_to(table[head : head + 1, :], (rows, rows)),
                 1,
                 axis=1,
                 stride=1,
                 stride_axis=0,
             )
-            scores = jnp.where(allowed, dot_t(lane_mask(q, side), k) * inverse + bias, MASKED)
-            powers = jnp.exp(scores - jnp.max(scores, axis=-1, keepdims=True))
-            prob = powers / jnp.sum(powers, axis=-1, keepdims=True)
-            probs[head] = prob
-            mixed.append(dot(prob.astype(LOW), v))
-        mixes.append(pick(*mixed).astype(LOW))
+            + barred
+            for head in (2 * g, 2 * g + 1)
+        ]
+        scores = dot_t(q, k) + jnp.concatenate(bias, axis=0)
+        powers = jnp.exp(scores - jnp.max(scores, axis=-1, keepdims=True))
+        prob = powers * (1.0 / jnp.sum(powers, axis=-1, keepdims=True))
+        probs[g] = prob
+        mixes.append(pick_rows(dot(prob.astype(LOW), v)).astype(LOW))
     mixes = jnp.concatenate(mixes, axis=1)
     mix[...] = mixes
     after_self = xf + dot(mixes, self_out[...])
@@ -555,34 +582,28 @@
     )
 
 
-def read_stats(packed, heads):
+def read_stats(packed):
     values = packed.astype(FULL)
-    columns = [
-        values[:, i : i + 1] + values[:, i + 1 : i + 2] + values[:, i + 2 : i + 3]
-        for i in range(0, 6 * heads, 3)
-    ]
-    return columns[:heads], columns[heads:]
+    return values + pltpu.roll(values, 127, axis=1) + pltpu.roll(values, 126, axis=1)
 
 
 def cross_kernel(cq, memory, visible, packed):
-    half = cq.shape[1]
+    rows, half = cq.shape
     pair = 2 * HEAD
-    inverse = HEAD ** (-0.5)
-    seen = visible[...] > 0
+    inverse = jnp.asarray(HEAD ** (-0.5), LOW)
+    barred = jnp.where(visible[...] > 0, 0.0, MASKED)
     tops, totals, mixes = [], [], []
     for at in range(0, half, pair):
-        q = cq[:, at : at + pair]
+        q = both_heads(cq[:, at : at + pair] * inverse)
         k = memory[:, at : at + pair]
         v = memory[:, half + at : half + at + pair]
-        mixed = []
-        for side in range(2):
-            scores = jnp.where(seen, dot_t(lane_mask(q, side), k) * inverse, MASKED)
-            top = jnp.max(scores, axis=-1, keepdims=True)
-            powers = jnp.where(seen, jnp.exp(scores - top), 0.0)
-            tops.append(top)
-            totals.append(jnp.sum(powers, axis=-1, keepdims=True))
-            mixed.append(dot(powers.astype(LOW), v))
-        mixes.append(pick(*mixed).astype(LOW))
+        scores = dot_t(q, k) + barred
+        top = jnp.max(scores, axis=-1, keepdims=True)
+        powers = jnp.exp(scores - top)
+        total = jnp.sum(powers, axis=-1, keepdims=True)
+        tops += [top[:rows], top[rows:]]
+        totals += [total[:rows], total[rows:]]
+        mixes.append(pick_rows(dot(powers.astype(LOW), v)).astype(LOW))
     packed[...] = jnp.concatenate(mixes + [pack_stats(tops, totals)], axis=1)
 
 
@@ -607,23 +628,22 @@
         flip = (here[CHIP] & step) != 0
         packed = [jnp.where(flip, packed[i ^ step], packed[i]) for i in range(len(packed))]
         step *= 2
-    read = [read_stats(p[:, half:], heads) for p in packed]
-    tops, totals, scales = [], [], []
-    for h in range(heads):
-        top = read[0][0][h]
-        for other in read[1:]:
-            top = jnp.maximum(top, other[0][h])
-        scale = [jnp.exp(r[0][h] - top) for r in read]
-        total = tree([r[1][h] * w for r, w in zip(read, scale)])
-        tops.append(top)
-        totals.append(total)
-        scales.append([w / total for w in scale])
+    read = [read_stats(p[:, half:]) for p in packed]
+    top = read[0]
+    for other in read[1:]:
+        top = jnp.maximum(top, other)
+    lanes = lax.broadcasted_iota(jnp.int32, top.shape, 1)
+    is_top = lanes < 3 * heads
+    scales = [jnp.exp(jnp.where(is_top, r - top, 0.0)) for r in read]
+    total = tree([r * pltpu.roll(w, 3 * heads, axis=1) for r, w in zip(read, scales)])
+    share = 1.0 / pltpu.roll(total, 128 - 3 * heads, axis=1)
+    weights = [w * share for w in scales]
     terms = [
-        p[:, :half].astype(FULL) * spread([scale[i] for scale in scales])
-        for i, p in enumerate(packed)
+        p[:, :half].astype(FULL) * spread([w[:, 3 * h : 3 * h + 1] for h in range(heads)])
+        for p, w in zip(packed, weights)
     ]
     mix[...] = tree(terms).astype(LOW)
-    stats[...] = pack_stats(tops, totals)
+    stats[...] = jnp.where(is_top, top, total)
 
 
 def gelu_parts(values):
@@ -761,7 +781,7 @@
     half = mix.shape[1]
     heads = half // HEAD
     pair = 2 * HEAD
-    inverse = HEAD ** (-0.5)
+    inverse = jnp.asarray(HEAD ** (-0.5), LOW)
     unit, factor = rms_unit(x2[...])
     grad = join(first, sums_mine[...], sums_other[...]).astype(FULL)
     gain_grad[...] = jnp.sum(grad * unit, axis=0, keepdims=True)
@@ -770,30 +790,28 @@
     low = back.astype(LOW)
     low_cross[...] = low
     grad_mix = dot_t(low, half_of(first, cross_out[...], 0)).astype(LOW)
-    seen = visible[...] > 0
-    tops, totals = read_stats(stats[...], heads)
+    barred = jnp.where(visible[...] > 0, 0.0, MASKED)
+    shares = 1.0 / stats[...]
+    passage = grad_mine.shape[0]
     for g in range(heads // 2):
         at = g * pair
-        q = cq[:, at : at + pair]
+        q = both_heads(cq[:, at : at + pair] * inverse)
+        do = both_heads(grad_mix[:, at : at + pair])
         k = memory[:, at : at + pair]
         v = memory[:, half + at : half + at + pair]
-        do = grad_mix[:, at : at + pair]
-        weighed = do.astype(FULL) * mix[:, at : at + pair].astype(FULL)
-        queries, keys, values = [], [], []
-        for side in range(2):
-            head = 2 * g + side
-            qs, ds = lane_mask(q, side), lane_mask(do, side)
-            scores = jnp.where(seen, dot_t(qs, k) * inverse, MASKED)
-            prob = jnp.where(seen, jnp.exp(scores - tops[head]) * (1.0 / totals[head]), 0.0)
-            rho = jnp.sum(lane_mask(weighed, side), axis=-1, keepdims=True)
-            grad_scores = (prob * (dot_t(ds, v) - rho)).astype(LOW)
-            queries.append(dot(grad_scores, k))
-            keys.append(outer_sum(grad_scores, qs))
-            values.append(outer_sum(prob.astype(LOW), ds))
-        grad_cq[:, at : at + pair] = (pick(*queries) * inverse).astype(LOW)
-        keys = ((keys[0] + keys[1]) * inverse).astype(LOW)
-        values = (values[0] + values[1]).astype(LOW)
-        passage = grad_mine.shape[0]
+        mixed = mix[:, at : at + pair].astype(FULL)
+        top, scale = [
+            jnp.concatenate([a[:, c : c + 1], a[:, c + 3 : c + 4]], axis=0)
+            for a, c in ((stats, 6 * g), (shares, 3 * heads + 6 * g))
+        ]
+        rho = jnp.sum(
+            do.astype(FULL) * jnp.concatenate([mixed, mixed], axis=0), axis=-1, keepdims=True
+        )
+        prob = jnp.exp(dot_t(q, k) + barred - top) * scale
+        grad_scores = (prob * (dot_t(do, v) - rho)).astype(LOW)
+        grad_cq[:, at : at + pair] = (pick_rows(dot(grad_scores, k)) * HEAD ** (-0.5)).astype(LOW)
+        keys = outer_sum(grad_scores, q).astype(LOW)
+        values = outer_sum(prob.astype(LOW), do).astype(LOW)
         for ref, begin in ((grad_mine, 0), (grad_other, passage)):
             ref[:, at : at + pair] = keys[begin : begin + passage]
             ref[:, half + at : half + at + pair] = values[begin : begin + passage]
@@ -844,7 +862,7 @@
     rows, width = x.shape
     heads = width // HEAD
     pair = 2 * HEAD
-    inverse = HEAD ** (-0.5)
+    inverse = jnp.asarray(HEAD ** (-0.5), LOW)
     grad = dot_t(join(here[CORE] == 0, cq_mine[...], cq_other[...]), cross_in[...])
     unit, factor = rms_unit(x1[...])
     small[...] = jnp.zeros_like(small)
@@ -860,26 +878,23 @@
     parts = [[], [], []]
     for g in range(heads // 2):
         at = g * pair
-        q = p1[:, at : at + pair]
+        q = both_heads(p1[:, at : at + pair] * inverse)
         k = p1[:, width + at : width + at + pair]
         v = p1[:, 2 * width + at : 2 * width + at + pair]
-        do = grad_mix[:, at : at + pair]
-        queries, keys, values = [], [], []
+        do = both_heads(grad_mix[:, at : at + pair])
+        prob = probs[g]
+        grad_probs = dot_t(do, v)
+        rho = jnp.sum(prob * grad_probs, axis=-1, keepdims=True)
+        grad_scores = (prob * (grad_probs - rho)).astype(LOW)
+        turned = dot(flip, jnp.concatenate([grad_scores[:rows], grad_scores[rows:]], axis=1))
         for side in range(2):
-            head = 2 * g + side
-            ds = lane_mask(do, side)
-            prob = probs[head]
-            grad_probs = dot_t(ds, v)
-            rho = jnp.sum(prob * grad_probs, axis=-1, keepdims=True)
-            grad_scores = (prob * (grad_probs - rho)).astype(LOW)
-            turned = pltpu.roll(dot(flip, grad_scores), 0, axis=1, stride=1, stride_axis=0)
-            small[3 + head : 4 + head, :rows] = jnp.sum(turned, axis=0, keepdims=True)
-            queries.append(dot(grad_scores, k))
-            keys.append(outer_sum(grad_scores, lane_mask(q, side)))
-            values.append(outer_sum(prob.astype(LOW), ds))
-        parts[0].append((pick(*queries) * inverse).astype(LOW))
-        parts[1].append(((keys[0] + keys[1]) * inverse).astype(LOW))
-        parts[2].append((values[0] + values[1]).astype(LOW))
+            part = turned[:, side * rows : (side + 1) * rows]
+            part = pltpu.roll(part, 0, axis=1, stride=1, stride_axis=0)
+            head = 3 + 2 * g + side
+            small[head : head + 1, :rows] = jnp.sum(part, axis=0, keepdims=True)
+        parts[0].append((pick_rows(dot(grad_scores, k)) * HEAD ** (-0.5)).astype(LOW))
+        parts[1].append(outer_sum(grad_scores, q).astype(LOW))
+        parts[2].append(outer_sum(prob.astype(LOW), do).astype(LOW))
     joined = jnp.concatenate(parts[0] + parts[1] + parts[2], axis=1)
     grad_p1[...] = joined
     grad = dot_t(joined, proj[...])
@@ -1026,7 +1041,8 @@
         [((share, 5 * width + 128), LOW)],
         [self_projection, self_output, cross_query, norm_gains],
     )
-    columns = jnp.stack(all_pb(columns))
+    along = first_hops(columns)
+    far = jnp.stack(all_pb(columns)[1:])
     mixed = expand_weight.reshape(share, pb, chips, 2 * slab).transpose(2, 0, 1, 3)
     mixed = mixed.reshape(chips, share, 2 * units)
     chip = mine_ctx >> 1
@@ -1034,15 +1050,16 @@
     mixed = jnp.concatenate([mixed[0]] + [swap_ctx(mixed[r], 2 * r) for r in range(1, chips)])
     e_other = swap_ctx(e, 1)
     visible = jnp.concatenate([passage_mask, swap_ctx(passage_mask, 1)], axis=1)
-    columns = after(columns, (e_other, visible, mixed))
-    early = first_hop(columns)
-    proj_blocks = second_hop(columns, early)
     others = jnp.concatenate([cross_memory, cross_output], axis=1)
-    others = jnp.stack(all_pb(after(others, columns)))
-    others_early = first_hop(after(others, early))
-    x = after(x, others_early)
+    others_along = first_hops(after(others, along))
+    far_along = first_hops(after(far, (e_other, visible, mixed, others_along)))
+    proj_blocks, _ = gather_rows(columns, along, far, far_along)
+    others_far = jnp.stack(all_pb(after(others, far))[1:])
+    others_far_along = first_hops(after(others_far, far_along))
+    others_blocks, last = gather_rows(others, others_along, others_far, others_far_along)
+    x = after(x, others_far_along)
     feed = jnp.concatenate([contract_weight, mixed], axis=1)
-    feed = jnp.broadcast_to(after(feed, others)[None], (pb,) + feed.shape)
+    feed = jnp.broadcast_to(after(feed, others_far)[None], (pb,) + feed.shape)
     feed = exchange(feed, "pb")
 
     hot = (jnp.arange(buckets)[:, None] == bucket_index[::-1][None, :]).astype(LOW)
@@ -1056,7 +1073,7 @@
             ((width, width), LOW),
             ((norm_gains.shape[0], width), FULL),
             ((rows, 3 * width), LOW),
-            ((heads, rows, rows), FULL),
+            ((heads // 2, 2 * rows, rows), FULL),
             ((rows, width), LOW),
             ((rows, width), FULL),
             ((rows, width), LOW),
@@ -1066,9 +1083,8 @@
         [here, target_length, x, table] + proj_blocks,
         scalars=2,
         scratch=[pltpu.VMEM((width, 128), LOW)],
-    )
-    others_blocks = second_hop(others, others_early)
-
+        spare=5 * SPARE_BYTES,
+    )
     def part(size, index):
         return [(b, b.shape[:2] + (size * width,), (0, 0, index)) for b in others_blocks]
 
@@ -1083,7 +1099,7 @@
     (packed,) = call(cross_kernel, [((rows, half + 128), LOW)], [cq, memory, visible])
     mix2, stats = call(
         merge_kernel,
-        [((rows, half), LOW), ((rows, 128), LOW)],
+        [((rows, half), LOW), ((rows, 128), FULL)],
         [here] + all_chips(packed),
         scalars=1,
     )

time: 214 us -> 201 us (0.939)
  Pallas kernels: 63.6 us -> 38.5 us
  local copies, waits for them, and re-layouts: 14 us -> 28.1 us
  waiting for transfers between devices: 67.4 us -> 61.2 us
  starting transfers between devices: 61.7 us -> 64.2 us
    pallas_call x15, Pallas kernels: 63.6 us -> 38.5 us  [call(): pl.pallas_call(kernel, grid=grid, out_shape=[jax.ShapeDtypeStruct(shape,...]
    unnamed x88 -> x133, local copies, waits for them, and re-layouts: 8.74 us -> 23.3 us
    ppermute x6, waiting for transfers between devices: 12.9 us -> 0.88 us  [swap_pb(): return lax.ppermute(values, 'pb', [(i, i ^ mask) for i in range(size)])]
    ppermute x48 -> x54, waiting for transfers between devices: 48.8 us -> 52.2 us  [swap_ctx(): return lax.ppermute(values, 'ctx', [(i, i ^ mask) for i in range(size)])]
    all_to_all x3, waiting for transfers between devices: 5.75 us -> 8.16 us  [exchange(): return lax.all_to_all(values, axis, 0, 0, tiled=True)]
    ppermute x48 -> x54, starting transfers between devices: 39.2 us -> 40.7 us  [swap_ctx(): return lax.ppermute(values, 'ctx', [(i, i ^ mask) for i in range(size)])]
  transfers between devices with their start and end apart: 57 -> 63, of which waited for: 26 -> 31; matrix products, arithmetic and copies ran while one was open for 4% -> 5% of each run, Pallas kernels for 24% -> 16%
where the time goes in v4:
time: 201 us; the launch traced here: 200 us
  starting transfers between devices  64.2 us (32%)
  waiting for transfers between devices  61.2 us (30%)
  Pallas kernels  38.5 us (19%)
  local copies, waits for them, and re-layouts  28.1 us (14%)
  other arithmetic  4.88 us (2%)
  between operations  2.62 us (1%)
    ppermute x54, waiting for transfers between devices, swap_ctx(): return lax.ppermute(values, 'ctx', [(i, i ^ mask) for i in range(size)])  52.2 us
    ppermute x54, starting transfers between devices, swap_ctx(): return lax.ppermute(values, 'ctx', [(i, i ^ mask) for i in range(size)])  40.7 us
    pallas_call x15, Pallas kernels, call(): pl.pallas_call(kernel, grid=grid, out_shape=[jax.ShapeDtypeStruct(shape,...  38.5 us
    unnamed x133, local copies, waits for them, and re-layouts  23.3 us
    all_to_all x3, starting transfers between devices, exchange(): return lax.all_to_all(values, axis, 0, 0, tiled=True)  13.5 us
    ppermute x6, starting transfers between devices, swap_pb(): return lax.ppermute(values, 'pb', [(i, i ^ mask) for i in range(size)])  10.1 us
    all_to_all x3, waiting for transfers between devices, exchange(): return lax.all_to_all(values, axis, 0, 0, tiled=True)  8.16 us
  transfers between devices with their start and end apart: 63, of which 31 were waited for; matrix products, arithmetic and copies ran while one was open for 5% of the time, Pallas kernels for 16%

profile of v4, /device:TPU:0, one launch (start us, length us, event | category | flops | bytes accessed | tf_op | source)
XLA Modules:
  0.0 199.6 jit_solution(13726427219017568835)
XLA Ops:
  4.0 3.0 %collective-permute-start = (bf16[24,3968]{1,0:T(8,128)(2,1)S(1)}, bf16[24,3968]{1,0:T(8,128)(2,1)S(1)}, u32[]{:S(2)}, u32[]{:S(2)}) collective-permute-start(bf16[24,3968]{1,0:T(8,128)(2,1)S(1)} %shard_map.247), channel_id=1, source_target_pairs={{0,8},{8,0},{16,24},{24,16},{1,9},{9,1},{17,25},{25,17},{2,10},{10... | collective-permute-start | bytes 571400 | tf_op jit(solution)/shard_map/ppermute | solution.py:380
  7.0 2.6 %collective-permute-start.1 = (bf16[24,3968]{1,0:T(8,128)(2,1)S(1)}, bf16[24,3968]{1,0:T(8,128)(2,1)S(1)}, u32[]{:S(2)}, u32[]{:S(2)}) collective-permute-start(bf16[24,3968]{1,0:T(8,128)(2,1)S(1)} %shard_map.247), channel_id=1, source_target_pairs={{0,16},{8,24},{16,0},{24,8},{1,17},{9,25},{17,1},{25,9},{2,18},{10... | collective-permute-start | bytes 571400 | tf_op jit(solution)/shard_map/ppermute | solution.py:380
  9.6 1.7 collective-permute-start.11
  15.7 5.3 %collective-permute-done.12 = bf16[24,3968]{1,0:T(8,128)(2,1)S(1)} collective-permute-done((bf16[24,3968]{1,0:T(8,128)(2,1)S(1)}, bf16[24,3968]{1,0:T(8,128)(2,1)S(1)}, u32[]{:S(2)}, u32[]{:S(2)}) %collective-permute-start.12) | collective-permute-done | bytes 190496 | tf_op jit(solution)/shard_map/ppermute | solution.py:375
  26.9 2.6 %collective-permute-start.5 = (bf16[24,2304]{1,0:T(8,128)(2,1)S(1)}, bf16[24,2304]{1,0:T(8,128)(2,1)S(1)}, u32[]{:S(2)}, u32[]{:S(2)}) collective-permute-start(bf16[24,2304]{1,0:T(8,128)(2,1)S(1)} %constant_dynamic-update-slice_fusion), channel_id=1, source_target_pairs={{0,24},{8,16},{16,8},{24,0},{1,25},{9,17},{17,9},{25,1},{2,26},{10... | collective-permute-start | bytes 331784 | tf_op jit(solution)/shard_map/ppermute | solution.py:380
  31.9 4.2 %collective-permute-done.14 = bf16[24,2304]{1,0:T(8,128)(2,1)S(1)} collective-permute-done((bf16[24,2304]{1,0:T(8,128)(2,1)S(1)}, bf16[24,2304]{1,0:T(8,128)(2,1)S(1)}, u32[]{:S(2)}, u32[]{:S(2)}) %collective-permute-start.14) | collective-permute-done | bytes 110624 | tf_op jit(solution)/shard_map/ppermute | solution.py:375
  39.9 3.7 %all-to-all-start = ((bf16[4,96,1536]{2,1,0:T(8,128)(2,1)}), bf16[4,96,1536]{2,1,0:T(8,128)(2,1)S(1)}, u32[]{:S(2)}, u32[]{:S(2)}) async-start(bf16[4,96,1536]{2,1,0:T(8,128)(2,1)} %broadcast_in_dim.8), calls=%async_computation | async-start | bytes 2359296 | tf_op jit(solution)/shard_map/all_to_all | solution.py:384
  43.8 4.2 %collective-permute-done.15.refs_4_ = bf16[3,24,3968]{2,1,0:T(8,128)(2,1)} collective-permute-done((bf16[3,24,3968]{2,1,0:T(8,128)(2,1)S(1)}, bf16[3,24,3968]{2,1,0:T(8,128)(2,1)}, u32[]{:S(2)}, u32[]{:S(2)}) %collective-permute-start.15) | collective-permute-done | bytes 571424 | tf_op jit(solution)/shard_map/ppermute | solution.py:375
  48.0 2.3 %collective-permute-done.16.refs_6_ = bf16[3,24,3968]{2,1,0:T(8,128)(2,1)} collective-permute-done((bf16[3,24,3968]{2,1,0:T(8,128)(2,1)S(1)}, bf16[3,24,3968]{2,1,0:T(8,128)(2,1)}, u32[]{:S(2)}, u32[]{:S(2)}) %collective-permute-start.16) | collective-permute-done | bytes 571424 | tf_op jit(solution)/shard_map/ppermute | solution.py:375
  52.5 2.1 %collective-permute-start.23 = (bf16[2,24,3968]{2,1,0:T(8,128)(2,1)S(1)}, bf16[2,24,3968]{2,1,0:T(8,128)(2,1)}, u32[]{:S(2)}, u32[]{:S(2)}) collective-permute-start(bf16[2,24,3968]{2,1,0:T(8,128)(2,1)S(1)} %pad_maximum_fusion.2), channel_id=1, source_target_pairs={{0,4},{1,5},{2,6},{3,7},{4,0},{5,1},{6,2},{7,3},{8,12},{9,13},{10,... | collective-permute-start | bytes 1142792 | tf_op jit(solution)/shard_map/ppermute | solution.py:375
  55.6 1.8 collective-permute-start.25
  60.4 4.0 %collective-permute-done.23.refs_8_ = bf16[2,24,3968]{2,1,0:T(8,128)(2,1)} collective-permute-done((bf16[2,24,3968]{2,1,0:T(8,128)(2,1)S(1)}, bf16[2,24,3968]{2,1,0:T(8,128)(2,1)}, u32[]{:S(2)}, u32[]{:S(2)}) %collective-permute-start.23) | collective-permute-done | bytes 380960 | tf_op jit(solution)/shard_map/ppermute | solution.py:375
  68.0 7.7 %shard_map.248 = (bf16[768,2304]{1,0:T(8,128)(2,1)}, bf16[768,768]{1,0:T(8,128)(2,1)S(1)}, bf16[768,768]{1,0:T(8,128)(2,1)}, f32[3,768]{1,0:T(4,128)S(1)}, bf16[...) custom-call(s32[5]{0:T(128)S(1)} %stack.67.here, ...), custom_call_target="tpu_custom_call" | custom-call | tf_op jit(solution)/shard_map/pallas_call | solution.py:58
  86.4 5.7 %collective-permute-done.31.refs_8_ = bf16[2,24,2304]{2,1,0:T(8,128)(2,1)S(1)} collective-permute-done((bf16[2,24,2304]{2,1,0:T(8,128)(2,1)S(1)}, bf16[2,24,2304]{2,1,0:T(8,128)(2,1)S(1)}, u32[]{:S(2)}, u32[]{:S(2)}) %collective-permute-start.31) | collective-permute-done | bytes 221216 | tf_op jit(solution)/shard_map/ppermute | solution.py:375
  93.9 2.3 %shard_map.249 = (bf16[768,1536]{1,0:T(8,128)(2,1)S(1)}, bf16[480,768]{1,0:T(8,128)(2,1)S(1)}) custom-call(s32[5]{0:T(128)S(1)} %stack.67.here, bf16[240,768]{1,0:T(8,128)(2,1)S(1)} %bitcast.37, bf16[240,768]{1,0:T(8,128)(2,1)S(1)} %copy-done.14, bf16[3,24,2304]{2,1,0:T(8,128)(2,1)S(1)} %pad_maximum_fusion.4.refs_0_, ...), custom_call_target="tpu_custom_call" | custom-call | tf_op jit(solution)/shard_map/pallas_call | solution.py:58
  102.3 2.8 %collective-permute-done.35.refs_1_ = bf16[128,512]{1,0:T(8,128)(2,1)S(1)} collective-permute-done((bf16[128,512]{1,0:T(8,128)(2,1)S(1)}, bf16[128,512]{1,0:T(8,128)(2,1)S(1)}, u32[]{:S(2)}, u32[]{:S(2)}) %collective-permute-start.35) | collective-permute-done | bytes 131104 | tf_op jit(solution)/shard_map/ppermute | solution.py:375
  105.1 3.0 %collective-permute-done.37.refs_3_ = bf16[128,512]{1,0:T(8,128)(2,1)S(1)} collective-permute-done((bf16[128,512]{1,0:T(8,128)(2,1)S(1)}, bf16[128,512]{1,0:T(8,128)(2,1)S(1)}, u32[]{:S(2)}, u32[]{:S(2)}) %collective-permute-start.37) | collective-permute-done | bytes 131104 | tf_op jit(solution)/shard_map/ppermute | solution.py:375
  110.9 2.9 %shard_map.252 = (bf16[768,768]{1,0:T(8,128)(2,1)S(1)}, f32[128,768]{1,0:T(8,128)S(1)}, bf16[128,768]{1,0:T(8,128)(2,1)S(1)}, bf16[128,768]{1,0:T(8,128)(2,1)S(1...) custom-call(s32[5]{0:T(128)S(1)} %stack.67.here, ...), custom_call_target="tpu_custom_call" | custom-call | tf_op jit(solution)/shard_map/pallas_call | solution.py:58
  116.9 2.4 %shard_map.259 = bf16[4,192,768]{2,1,0:T(8,128)(2,1)} custom-call(s32[5]{0:T(128)S(1)} %stack.67.here, bf16[128,768]{1,0:T(8,128)(2,1)S(1)} %get-tuple-element.120.active, bf16[128,768]{1,0:T(8,128)(2,1)S(1)} %get-tuple-element.121.low_out, bf16[128,768]{1,0:T(8,128)(2,1)S(1)} %get-tuple-element.122.h3, bf16[128,768]{1,0:T(8,128)(2,1)S(1)} %get-tuple-element.123.grad_hidden), custom_call_target="tpu_custom_call" | custom-call | tf_op jit(solution)/shard_map/pallas_call | solution.py:58
  119.4 4.6 %all-to-all-start.2 = ((bf16[4,192,768]{2,1,0:T(8,128)(2,1)}), bf16[4,192,768]{2,1,0:T(8,128)(2,1)S(1)}, u32[]{:S(2)}, u32[]{:S(2)}) async-start(bf16[4,192,768]{2,1,0:T(8,128)(2,1)} %shard_map.259), calls=%async_computation.2 | async-start | bytes 2359296 | tf_op jit(solution)/shard_map/all_to_all | solution.py:384
  125.8 1.8 collective-permute-start.42
  127.5 1.9 collective-permute-done.40
  134.1 2.7 %shard_map.253 = (f32[128,768]{1,0:T(8,128)S(1)}, bf16[128,768]{1,0:T(8,128)(2,1)S(1)}, bf16[128,384]{1,0:T(8,128)(2,1)S(1)}, bf16[240,768]{1,0:T(8,128)(2,1)S(1...) custom-call(s32[5]{0:T(128)S(1)} %stack.67.here, s32[1]{0:T(128)S(6)} %copy.30.length, s32[1]{0:T(128)S(6)} %copy.31.task, ...), custom_call_target="tpu_custom_call" | custom-call | tf_op jit(solution)/shard_map/pallas_call | solution.py:58
  150.5 5.9 %shard_map.254 = (bf16[128,768]{1,0:T(8,128)(2,1)S(1)}, bf16[128,2304]{1,0:T(8,128)(2,1)S(1)}, bf16[128,768]{1,0:T(8,128)(2,1)}, f32[16,768]{1,0:T(8,128)S(1)}) custom-call(s32[5]{0:T(128)S(1)} %stack.67.here, bf16[128,384]{1,0:T(8,128)(2,1)S(1)} %add_convert_fusion.2.cq_mine, bf16[128,384]{1,0:T(8,128)(2,1)S(1)} %collective-permute-done.47.cq_other, ...), custom_call_target="tpu_custom_call" | custom-call | tf_op jit(solution)/shard_map/pallas_call | solution.py:58
  157.6 3.3 %shard_map.256 = bf16[4,208,768]{2,1,0:T(8,128)(2,1)} custom-call(s32[5]{0:T(128)S(1)} %stack.67.here, bf16[128,384]{1,0:T(8,128)(2,1)S(1)} %copy-done.24, bf16[128,384]{1,0:T(8,128)(2,1)S(1)} %copy-done.39, bf16[128,768]{1,0:T(8,128)(2,1)S(1)} %get-tuple-element.89.low_cross, bf16[128,768]{1,0:T(8,128)(2,1)S(1)} %copy-done.47, ...), custom_call_target="tpu_custom_call" | custom-call | tf_op jit(solution)/shard_map/pallas_call | solution.py:58
  160.9 5.2 %all-to-all-start.1 = ((bf16[4,208,768]{2,1,0:T(8,128)(2,1)}), bf16[4,208,768]{2,1,0:T(8,128)(2,1)S(1)}, u32[]{:S(2)}, u32[]{:S(2)}) async-start(bf16[4,208,768]{2,1,0:T(8,128)(2,1)} %shard_map.256), calls=%async_computation.1 | async-start | bytes 2555904 | tf_op jit(solution)/shard_map/all_to_all | solution.py:384
  167.9 1.7 collective-permute-start.53
  169.6 2.0 %collective-permute-done.51 = bf16[128,384]{1,0:T(8,128)(2,1)S(1)} collective-permute-done((bf16[128,384]{1,0:T(8,128)(2,1)S(1)}, bf16[128,384]{1,0:T(8,128)(2,1)S(1)}, u32[]{:S(2)}, u32[]{:S(2)}) %collective-permute-start.51) | collective-permute-done | bytes 98336 | tf_op jit(solution)/shard_map/ppermute | solution.py:375
  175.3 2.5 %shard_map.257 = bf16[240,768]{1,0:T(8,128)(2,1)} custom-call(s32[5]{0:T(128)S(1)} %stack.67.here, bf16[240,768]{1,0:T(8,128)(2,1)S(1)} %copy-done.17, bf16[240,768]{1,0:T(8,128)(2,1)} %collective-permute-done.55.other, bf16[768,1536]{1,0:T(8,128)(2,1)S(1)} %copy-done.3), custom_call_target="tpu_custom_call" | custom-call | tf_op jit(solution)/shard_map/pallas_call | solution.py:58
  184.5 1.9 collective-permute-done.59.refs_3_
  187.8 8.2 %all-to-all-done.1.parts = bf16[4,208,768]{2,1,0:T(8,128)(2,1)S(1)} async-done(((bf16[4,208,768]{2,1,0:T(8,128)(2,1)}), bf16[4,208,768]{2,1,0:T(8,128)(2,1)S(1)}, u32[]{:S(2)}, u32[]{:S(2)}) %all-to-all-start.1) | async-done | bytes 1277984 | tf_op jit(solution)/shard_map/all_to_all | solution.py:384
  196.0 1.7 shard_map.258
  (272 shorter events, 89.4 us)
Async XLA Ops:
  4.0 18.5 %collective-permute-start = (bf16[24,3968]{1,0:T(8,128)(2,1)S(1)}, bf16[24,3968]{1,0:T(8,128)(2,1)S(1)}, u32[]{:S(2)}, u32[]{:S(2)}) collective-permute-start(bf16[24,3968]{1,0:T(8,128)(2,1)S(1)} %shard_map.247), channel_id=1, source_target_pairs={{0,8},{8,0},{16,24},{24,16},{1,9},{9,1},{17,25},{25,17},{2,10},{10... | collective-permute-start | bytes 571400 | tf_op jit(solution)/shard_map/ppermute | solution.py:380
  7.0 16.9 %collective-permute-start.1 = (bf16[24,3968]{1,0:T(8,128)(2,1)S(1)}, bf16[24,3968]{1,0:T(8,128)(2,1)S(1)}, u32[]{:S(2)}, u32[]{:S(2)}) collective-permute-start(bf16[24,3968]{1,0:T(8,128)(2,1)S(1)} %shard_map.247), channel_id=1, source_target_pairs={{0,16},{8,24},{16,0},{24,8},{1,17},{9,25},{17,1},{25,9},{2,18},{10... | collective-permute-start | bytes 571400 | tf_op jit(solution)/shard_map/ppermute | solution.py:380
  9.6 15.7 %collective-permute-start.2 = (bf16[24,3968]{1,0:T(8,128)(2,1)S(1)}, bf16[24,3968]{1,0:T(8,128)(2,1)S(1)}, u32[]{:S(2)}, u32[]{:S(2)}) collective-permute-start(bf16[24,3968]{1,0:T(8,128)(2,1)S(1)} %shard_map.247), channel_id=1, source_target_pairs={{0,24},{8,16},{16,8},{24,0},{1,25},{9,17},{17,9},{25,1},{2,26},{10... | collective-permute-start | bytes 571400 | tf_op jit(solution)/shard_map/ppermute | solution.py:380
  13.7 7.2 %collective-permute-start.12 = (bf16[24,3968]{1,0:T(8,128)(2,1)S(1)}, bf16[24,3968]{1,0:T(8,128)(2,1)S(1)}, u32[]{:S(2)}, u32[]{:S(2)}) collective-permute-start(bf16[24,3968]{1,0:T(8,128)(2,1)S(1)} %shard_map.247), channel_id=1, source_target_pairs={{0,4},{1,5},{2,6},{3,7},{4,0},{5,1},{6,2},{7,3},{8,12},{9,13},{10,... | collective-permute-start | bytes 571400 | tf_op jit(solution)/shard_map/ppermute | solution.py:375
  15.6 20.5 %collective-permute-start.6 = (bf16[240,768]{1,0:T(8,128)(2,1)S(1)}, bf16[240,768]{1,0:T(8,128)(2,1)S(1)}, u32[]{:S(2)}, u32[]{:S(2)}) collective-permute-start(bf16[240,768]{1,0:T(8,128)(2,1)S(1)} %bitcast.36), channel_id=1, source_target_pairs={{0,1},{1,0},{2,3},{3,2},{4,5},{5,4},{6,7},{7,6},{8,9},{9,8},{10,11... | collective-permute-start | bytes 1105928 | tf_op jit(solution)/shard_map/ppermute | solution.py:375
  22.5 7.0 %collective-permute-start.8 = (bf16[24,768]{1,0:T(8,128)(2,1)S(1)}, bf16[24,768]{1,0:T(8,128)(2,1)S(1)}, u32[]{:S(2)}, u32[]{:S(2)}) collective-permute-start(bf16[24,768]{1,0:T(8,128)(2,1)S(1)} %get-tuple-element.135), channel_id=1, source_target_pairs={{0,2},{1,3},{2,0},{3,1},{4,6},{5,7},{6,4},{7,5},{8,10},{9,11},{10,... | collective-permute-start | bytes 110600 | tf_op jit(solution)/shard_map/ppermute | solution.py:375
  26.9 10.9 %collective-permute-start.5 = (bf16[24,2304]{1,0:T(8,128)(2,1)S(1)}, bf16[24,2304]{1,0:T(8,128)(2,1)S(1)}, u32[]{:S(2)}, u32[]{:S(2)}) collective-permute-start(bf16[24,2304]{1,0:T(8,128)(2,1)S(1)} %constant_dynamic-update-slice_fusion), channel_id=1, source_target_pairs={{0,24},{8,16},{16,8},{24,0},{1,25},{9,17},{17,9},{25,1},{2,26},{10... | collective-permute-start | bytes 331784 | tf_op jit(solution)/shard_map/ppermute | solution.py:380
  29.5 8.4 %collective-permute-start.3 = (bf16[24,2304]{1,0:T(8,128)(2,1)S(1)}, bf16[24,2304]{1,0:T(8,128)(2,1)S(1)}, u32[]{:S(2)}, u32[]{:S(2)}) collective-permute-start(bf16[24,2304]{1,0:T(8,128)(2,1)S(1)} %constant_dynamic-update-slice_fusion), channel_id=1, source_target_pairs={{0,8},{8,0},{16,24},{24,16},{1,9},{9,1},{17,25},{25,17},{2,10},{10... | collective-permute-start | bytes 331784 | tf_op jit(solution)/shard_map/ppermute | solution.py:380
  30.2 8.5 %collective-permute-start.4 = (bf16[24,2304]{1,0:T(8,128)(2,1)S(1)}, bf16[24,2304]{1,0:T(8,128)(2,1)S(1)}, u32[]{:S(2)}, u32[]{:S(2)}) collective-permute-start(bf16[24,2304]{1,0:T(8,128)(2,1)S(1)} %constant_dynamic-update-slice_fusion), channel_id=1, source_target_pairs={{0,16},{8,24},{16,0},{24,8},{1,17},{9,25},{17,1},{25,9},{2,18},{10... | collective-permute-start | bytes 331784 | tf_op jit(solution)/shard_map/ppermute | solution.py:380
  36.1 11.9 %collective-permute-start.15 = (bf16[3,24,3968]{2,1,0:T(8,128)(2,1)S(1)}, bf16[3,24,3968]{2,1,0:T(8,128)(2,1)}, u32[]{:S(2)}, u32[]{:S(2)}) collective-permute-start(bf16[3,24,3968]{2,1,0:T(8,128)(2,1)S(1)} %pad_maximum_fusion.refs_2_), channel_id=1, source_target_pairs={{0,2},{1,3},{2,0},{3,1},{4,6},{5,7},{6,4},{7,5},{8,10},{9,11},{10,... | collective-permute-start | bytes 1714184 | tf_op jit(solution)/shard_map/ppermute | solution.py:375
  37.6 12.7 %collective-permute-start.16 = (bf16[3,24,3968]{2,1,0:T(8,128)(2,1)S(1)}, bf16[3,24,3968]{2,1,0:T(8,128)(2,1)}, u32[]{:S(2)}, u32[]{:S(2)}) collective-permute-start(bf16[3,24,3968]{2,1,0:T(8,128)(2,1)S(1)} %pad_maximum_fusion.refs_2_), channel_id=1, source_target_pairs={{0,4},{1,5},{2,6},{3,7},{4,0},{5,1},{6,2},{7,3},{8,12},{9,13},{10,... | collective-permute-start | bytes 1714184 | tf_op jit(solution)/shard_map/ppermute | solution.py:375
  39.9 42.1 %all-to-all-start = ((bf16[4,96,1536]{2,1,0:T(8,128)(2,1)}), bf16[4,96,1536]{2,1,0:T(8,128)(2,1)S(1)}, u32[]{:S(2)}, u32[]{:S(2)}) async-start(bf16[4,96,1536]{2,1,0:T(8,128)(2,1)} %broadcast_in_dim.8), calls=%async_computation | async-start | bytes 2359296 | tf_op jit(solution)/shard_map/all_to_all | solution.py:384
  43.7 13.7 %collective-permute-start.19 = (bf16[3,24,3968]{2,1,0:T(8,128)(2,1)S(1)}, bf16[3,24,3968]{2,1,0:T(8,128)(2,1)S(1)}, u32[]{:S(2)}, u32[]{:S(2)}) collective-permute-start(bf16[3,24,3968]{2,1,0:T(8,128)(2,1)S(1)} %pad_maximum_fusion.1.refs_0_), channel_id=1, source_target_pairs={{0,1},{1,0},{2,3},{3,2},{4,5},{5,4},{6,7},{7,6},{8,9},{9,8},{10,11... | collective-permute-start | bytes 1714184 | tf_op jit(solution)/shard_map/ppermute | solution.py:375
  50.3 9.6 %collective-permute-start.17 = (bf16[3,24,2304]{2,1,0:T(8,128)(2,1)S(1)}, bf16[3,24,2304]{2,1,0:T(8,128)(2,1)S(1)}, u32[]{:S(2)}, u32[]{:S(2)}) collective-permute-start(bf16[3,24,2304]{2,1,0:T(8,128)(2,1)S(1)} %pad_maximum_fusion.3.refs_2_), channel_id=1, source_target_pairs={{0,2},{1,3},{2,0},{3,1},{4,6},{5,7},{6,4},{7,5},{8,10},{9,11},{10,... | collective-permute-start | bytes 995336 | tf_op jit(solution)/shard_map/ppermute | solution.py:375
  50.6 9.6 %collective-permute-start.18 = (bf16[3,24,2304]{2,1,0:T(8,128)(2,1)S(1)}, bf16[3,24,2304]{2,1,0:T(8,128)(2,1)S(1)}, u32[]{:S(2)}, u32[]{:S(2)}) collective-permute-start(bf16[3,24,2304]{2,1,0:T(8,128)(2,1)S(1)} %pad_maximum_fusion.3.refs_2_), channel_id=1, source_target_pairs={{0,4},{1,5},{2,6},{3,7},{4,0},{5,1},{6,2},{7,3},{8,12},{9,13},{10,... | collective-permute-start | bytes 995336 | tf_op jit(solution)/shard_map/ppermute | solution.py:375
  52.5 11.9 %collective-permute-start.23 = (bf16[2,24,3968]{2,1,0:T(8,128)(2,1)S(1)}, bf16[2,24,3968]{2,1,0:T(8,128)(2,1)}, u32[]{:S(2)}, u32[]{:S(2)}) collective-permute-start(bf16[2,24,3968]{2,1,0:T(8,128)(2,1)S(1)} %pad_maximum_fusion.2), channel_id=1, source_target_pairs={{0,4},{1,5},{2,6},{3,7},{4,0},{5,1},{6,2},{7,3},{8,12},{9,13},{10,... | collective-permute-start | bytes 1142792 | tf_op jit(solution)/shard_map/ppermute | solution.py:375
  55.6 8.8 %collective-permute-start.25 = (bf16[2,24,3968]{2,1,0:T(8,128)(2,1)S(1)}, bf16[2,24,3968]{2,1,0:T(8,128)(2,1)}, u32[]{:S(2)}, u32[]{:S(2)}) collective-permute-start(bf16[2,24,3968]{2,1,0:T(8,128)(2,1)S(1)} %slice.33), channel_id=1, source_target_pairs={{0,2},{1,3},{2,0},{3,1},{4,6},{5,7},{6,4},{7,5},{8,10},{9,11},{10,... | collective-permute-start | bytes 1142792 | tf_op jit(solution)/shard_map/ppermute | solution.py:375
  58.3 7.6 %collective-permute-start.20 = (bf16[3,24,3968]{2,1,0:T(8,128)(2,1)S(1)}, bf16[3,24,3968]{2,1,0:T(8,128)(2,1)}, u32[]{:S(2)}, u32[]{:S(2)}) collective-permute-start(bf16[3,24,3968]{2,1,0:T(8,128)(2,1)S(1)} %pad_maximum_fusion.refs_2_), channel_id=1, source_target_pairs={{0,1},{1,0},{2,3},{3,2},{4,5},{5,4},{6,7},{7,6},{8,9},{9,8},{10,11... | collective-permute-start | bytes 1714184 | tf_op jit(solution)/shard_map/ppermute | solution.py:375
  65.9 20.1 %collective-permute-start.28 = (bf16[3,24,2304]{2,1,0:T(8,128)(2,1)S(1)}, bf16[3,24,2304]{2,1,0:T(8,128)(2,1)}, u32[]{:S(2)}, u32[]{:S(2)}) collective-permute-start(bf16[3,24,2304]{2,1,0:T(8,128)(2,1)S(1)} %pad_maximum_fusion.3.refs_2_), channel_id=1, source_target_pairs={{0,1},{1,0},{2,3},{3,2},{4,5},{5,4},{6,7},{7,6},{8,9},{9,8},{10,11... | collective-permute-start | bytes 995336 | tf_op jit(solution)/shard_map/ppermute | solution.py:375
  82.0 28.9 %collective-permute-start.39 = (bf16[4,96,1536]{2,1,0:T(8,128)(2,1)S(1)}, bf16[4,96,1536]{2,1,0:T(8,128)(2,1)S(1)}, u32[]{:S(2)}, u32[]{:S(2)}) collective-permute-start(bf16[4,96,1536]{2,1,0:T(8,128)(2,1)S(1)} %all-to-all-done.feed_mine), channel_id=1, source_target_pairs={{0,1},{1,0},{2,3},{3,2},{4,5},{5,4},{6,7},{7,6},{8,9},{9,8},{10,11... | collective-permute-start | bytes 3538952 | tf_op jit(solution)/shard_map/ppermute | solution.py:375
  84.5 7.6 %collective-permute-start.31 = (bf16[2,24,2304]{2,1,0:T(8,128)(2,1)S(1)}, bf16[2,24,2304]{2,1,0:T(8,128)(2,1)S(1)}, u32[]{:S(2)}, u32[]{:S(2)}) collective-permute-start(bf16[2,24,2304]{2,1,0:T(8,128)(2,1)S(1)} %pad_maximum_fusion.5), channel_id=1, source_target_pairs={{0,4},{1,5},{2,6},{3,7},{4,0},{5,1},{6,2},{7,3},{8,12},{9,13},{10,... | collective-permute-start | bytes 663560 | tf_op jit(solution)/shard_map/ppermute | solution.py:375
  84.9 7.3 %collective-permute-start.33 = (bf16[2,24,2304]{2,1,0:T(8,128)(2,1)S(1)}, bf16[2,24,2304]{2,1,0:T(8,128)(2,1)S(1)}, u32[]{:S(2)}, u32[]{:S(2)}) collective-permute-start(bf16[2,24,2304]{2,1,0:T(8,128)(2,1)S(1)} %slice.35), channel_id=1, source_target_pairs={{0,2},{1,3},{2,0},{3,1},{4,6},{5,7},{6,4},{7,5},{8,10},{9,11},{10,... | collective-permute-start | bytes 663560 | tf_op jit(solution)/shard_map/ppermute | solution.py:375
  85.9 6.7 %collective-permute-start.29 = (bf16[3,24,2304]{2,1,0:T(8,128)(2,1)S(1)}, bf16[3,24,2304]{2,1,0:T(8,128)(2,1)S(1)}, u32[]{:S(2)}, u32[]{:S(2)}) collective-permute-start(bf16[3,24,2304]{2,1,0:T(8,128)(2,1)S(1)} %collective-permute-done.17.refs_4_), channel_id=1, source_target_pairs={{0,1},{1,0},{2,3},{3,2},{4,5},{5,4},{6,7},{7,6},{8,9},{9,8},{10,11... | collective-permute-start | bytes 995336 | tf_op jit(solution)/shard_map/ppermute | solution.py:375
  100.8 7.2 %collective-permute-start.37 = (bf16[128,512]{1,0:T(8,128)(2,1)S(1)}, bf16[128,512]{1,0:T(8,128)(2,1)S(1)}, u32[]{:S(2)}, u32[]{:S(2)}) collective-permute-start(bf16[128,512]{1,0:T(8,128)(2,1)S(1)} %shard_map.250.refs_0_), channel_id=1, source_target_pairs={{0,6},{1,7},{2,4},{3,5},{4,2},{5,3},{6,0},{7,1},{8,14},{9,15},{10,... | collective-permute-start | bytes 393224 | tf_op jit(solution)/shard_map/ppermute | solution.py:375
  119.4 41.5 %all-to-all-start.2 = ((bf16[4,192,768]{2,1,0:T(8,128)(2,1)}), bf16[4,192,768]{2,1,0:T(8,128)(2,1)S(1)}, u32[]{:S(2)}, u32[]{:S(2)}) async-start(bf16[4,192,768]{2,1,0:T(8,128)(2,1)} %shard_map.259), calls=%async_computation.2 | async-start | bytes 2359296 | tf_op jit(solution)/shard_map/all_to_all | solution.py:384
  136.8 7.4 %collective-permute-start.44 = (bf16[128,384]{1,0:T(8,128)(2,1)S(1)}, bf16[128,384]{1,0:T(8,128)(2,1)S(1)}, u32[]{:S(2)}, u32[]{:S(2)}) collective-permute-start(bf16[128,384]{1,0:T(8,128)(2,1)S(1)} %get-tuple-element.91), channel_id=1, source_target_pairs={{0,2},{1,3},{2,0},{3,1},{4,6},{5,7},{6,4},{7,5},{8,10},{9,11},{10,... | collective-permute-start | bytes 294920 | tf_op jit(solution)/shard_map/ppermute | solution.py:375
  138.2 7.2 %collective-permute-start.45 = (bf16[128,384]{1,0:T(8,128)(2,1)S(1)}, bf16[128,384]{1,0:T(8,128)(2,1)S(1)}, u32[]{:S(2)}, u32[]{:S(2)}) collective-permute-start(bf16[128,384]{1,0:T(8,128)(2,1)S(1)} %get-tuple-element.91), channel_id=1, source_target_pairs={{0,4},{1,5},{2,6},{3,7},{4,0},{5,1},{6,2},{7,3},{8,12},{9,13},{10,... | collective-permute-start | bytes 294920 | tf_op jit(solution)/shard_map/ppermute | solution.py:375
  141.9 14.5 %collective-permute-start.48 = (bf16[192,768]{1,0:T(8,128)(2,1)S(1)}, bf16[192,768]{1,0:T(8,128)(2,1)S(1)}, u32[]{:S(2)}, u32[]{:S(2)}) collective-permute-start(bf16[192,768]{1,0:T(8,128)(2,1)S(1)} %get-tuple-element.107), channel_id=1, source_target_pairs={{0,2},{1,3},{2,0},{3,1},{4,6},{5,7},{6,4},{7,5},{8,10},{9,11},{10,... | collective-permute-start | bytes 884744 | tf_op jit(solution)/shard_map/ppermute | solution.py:375
  143.3 14.3 %collective-permute-start.49 = (bf16[192,768]{1,0:T(8,128)(2,1)S(1)}, bf16[192,768]{1,0:T(8,128)(2,1)S(1)}, u32[]{:S(2)}, u32[]{:S(2)}) collective-permute-start(bf16[192,768]{1,0:T(8,128)(2,1)S(1)} %get-tuple-element.108), channel_id=1, source_target_pairs={{0,4},{1,5},{2,6},{3,7},{4,0},{5,1},{6,2},{7,3},{8,12},{9,13},{10,... | collective-permute-start | bytes 884744 | tf_op jit(solution)/shard_map/ppermute | solution.py:375
  144.2 13.4 %collective-permute-start.50 = (bf16[192,768]{1,0:T(8,128)(2,1)S(1)}, bf16[192,768]{1,0:T(8,128)(2,1)S(1)}, u32[]{:S(2)}, u32[]{:S(2)}) collective-permute-start(bf16[192,768]{1,0:T(8,128)(2,1)S(1)} %get-tuple-element.109), channel_id=1, source_target_pairs={{0,6},{1,7},{2,4},{3,5},{4,2},{5,3},{6,0},{7,1},{8,14},{9,15},{10,... | collective-permute-start | bytes 884744 | tf_op jit(solution)/shard_map/ppermute | solution.py:375
  160.9 35.0 %all-to-all-start.1 = ((bf16[4,208,768]{2,1,0:T(8,128)(2,1)}), bf16[4,208,768]{2,1,0:T(8,128)(2,1)S(1)}, u32[]{:S(2)}, u32[]{:S(2)}) async-start(bf16[4,208,768]{2,1,0:T(8,128)(2,1)} %shard_map.256), calls=%async_computation.1 | async-start | bytes 2555904 | tf_op jit(solution)/shard_map/all_to_all | solution.py:384
  173.5 9.3 %collective-permute-start.54 = (bf16[128,384]{1,0:T(8,128)(2,1)S(1)}, bf16[128,384]{1,0:T(8,128)(2,1)S(1)}, u32[]{:S(2)}, u32[]{:S(2)}) collective-permute-start(bf16[128,384]{1,0:T(8,128)(2,1)S(1)} %add_convert_fusion.1), channel_id=1, source_target_pairs={{0,1},{1,0},{2,3},{3,2},{4,5},{5,4},{6,7},{7,6},{8,9},{9,8},{10,11... | collective-permute-start | bytes 294920 | tf_op jit(solution)/shard_map/ppermute | solution.py:375
  (97 other events, 706.2 us)

commit v5 on v4

--- a/solution.py
+++ b/solution.py
@@ -12,6 +12,7 @@
 MASKED = -1000000000.0
 EPS = 1e-06
 HEAD = 64
+ALL_BYTES = 58 * 1024 * 1024
 SPARE_BYTES = 6 * 1024 * 1024
 
 
@@ -42,27 +43,107 @@
     return factor * (scaled - unit * jnp.mean(scaled * unit, axis=-1, keepdims=True))
 
 
-def call(kernel, outs, args, scalars=0, scratch=(), spare=SPARE_BYTES):
-    arrays, specs, grid = [], [], ()
-    held = [(arg[1], arg[0].dtype) if isinstance(arg, tuple) else (arg.shape, arg.dtype) for arg in args]
-    held += list(outs) + [(one.shape, one.dtype) for one in scratch]
-    size = sum(math.prod(shape) * jnp.dtype(dtype).itemsize for shape, dtype in held)
+class Far:
+    def __init__(self, array):
+        self.array, self.shape, self.dtype = array, array.shape, array.dtype
+
+
+class Arriving:
+    def __init__(self, source, held, sem):
+        self.held, self.shape, self.dtype = held, held.shape, held.dtype
+        self.copy = pltpu.make_async_copy(source, held, sem)
+        self.copy.start()
+
+    def wait(self):
+        if self.copy is not None:
+            self.copy.wait()
+            self.copy = None
+
+    def __getitem__(self, index):
+        self.wait()
+        return self.held[index]
+
+
+class Leaving:
+    def __init__(self, held, target, sem):
+        self.held, self.shape, self.dtype = held, held.shape, held.dtype
+        self.copy = pltpu.make_async_copy(held, target, sem)
+        self.left = False
+
+    def leave(self):
+        if not self.left:
+            self.copy.start()
+            self.left = True
+
+    def __getitem__(self, index):
+        return self.held[index]
+
+    def __setitem__(self, index, values):
+        self.held[index] = values
+
+
+def place_of_device():
+    mine_pb, mine_ctx = lax.axis_index("pb"), lax.axis_index("ctx")
+    return mine_ctx & 1, mine_ctx >> 1, mine_pb, mine_ctx, lax.axis_size("ctx")
+
+
+def call(kernel, outs, args, scalars=0, scratch=(), limit=None):
+    placed = args[0] is None
+    if placed:
+        args, scalars = args[1:], scalars - 1
+    arrays, specs, grid, held = [], [], (), []
+    far_ins = [index for index, arg in enumerate(args) if isinstance(arg, Far)]
+    far_outs = [index for index, out in enumerate(outs) if len(out) == 3]
     for index, arg in enumerate(args):
         if isinstance(arg, tuple):
             arg, shape, place = arg
             specs.append(pl.BlockSpec(shape, lambda i, place=place: place))
             grid = (1,)
+            held.append((shape, arg.dtype))
+        elif isinstance(arg, Far):
+            specs.append(pl.BlockSpec(memory_space=pltpu.HBM))
+            held.append((arg.shape, arg.dtype))
+            arg = arg.array
         else:
             specs.append(pl.BlockSpec(memory_space=pltpu.SMEM if index < scalars else pltpu.VMEM))
+            held.append((arg.shape, arg.dtype))
         arrays.append(arg)
+    held += [out[:2] for out in outs] + [(one.shape, one.dtype) for one in scratch]
+    size = sum(math.prod(shape) * jnp.dtype(dtype).itemsize for shape, dtype in held)
+    buffers = [pltpu.VMEM(args[i].shape, args[i].dtype) for i in far_ins]
+    buffers += [pltpu.VMEM(*outs[i][:2]) for i in far_outs]
+    if buffers:
+        buffers.append(pltpu.SemaphoreType.DMA((len(buffers),)))
+
+    def run(*refs):
+        ins, results = list(refs[: len(args)]), list(refs[len(args) : len(args) + len(outs)])
+        rest = refs[len(args) + len(outs) :]
+        own, extra = rest[: len(scratch)], rest[len(scratch) :]
+        moved = []
+        for k, i in enumerate(far_ins):
+            ins[i] = Arriving(ins[i], extra[k], extra[-1].at[k])
+            moved.append(ins[i])
+        for k, i in enumerate(far_outs, len(far_ins)):
+            results[i] = Leaving(extra[k], results[i], extra[-1].at[k])
+            moved.append(results[i])
+        kernel(*([place_of_device()] if placed else []), *ins, *results, *own)
+        for one in moved:
+            if isinstance(one, Leaving):
+                one.leave()
+                one.copy.wait()
+            else:
+                one.wait()
+
     return pl.pallas_call(
-        kernel,
+        run,
         grid=grid,
-        out_shape=[jax.ShapeDtypeStruct(shape, dtype) for shape, dtype in outs],
+        out_shape=[jax.ShapeDtypeStruct(out[0], out[1]) for out in outs],
         in_specs=specs,
-        out_specs=[pl.BlockSpec(memory_space=pltpu.VMEM) for _ in outs],
-        scratch_shapes=list(scratch),
-        compiler_params=pltpu.CompilerParams(vmem_limit_bytes=size + spare),
+        out_specs=[
+            pl.BlockSpec(memory_space=pltpu.HBM if len(out) == 3 else pltpu.VMEM) for out in outs
+        ],
+        scratch_shapes=list(scratch) + buffers,
+        compiler_params=pltpu.CompilerParams(vmem_limit_bytes=limit or size + SPARE_BYTES),
     )(*arrays)
 
 
@@ -403,8 +484,8 @@
     return terms[0]
 
 
-def sum_chips(values):
-    return tree([part.astype(FULL) for part in all_chips(values)]).astype(LOW)
+def add_chips(parts):
+    return tree([part.astype(FULL) for part in parts]).astype(LOW)
 
 
 def to_owners(parts):
@@ -511,6 +592,8 @@
     pair = 2 * HEAD
     inverse = jnp.asarray(HEAD ** (-0.5), LOW)
     place(here, blocks, [proj, self_out, cross_in, columns], ctx)
+    for one in (proj, self_out, cross_in):
+        one.leave()
     gains = columns[...].astype(FULL).T
     gains_out[...] = gains[: gains_out.shape[0]]
     xf = x[...].astype(FULL)
@@ -519,6 +602,7 @@
     h1[...] = normed
     joined = dot(normed, proj[...]).astype(LOW)
     p1[...] = joined
+    p1.leave()
     row = lax.broadcasted_iota(jnp.int32, (rows, rows), 0)
     col = lax.broadcasted_iota(jnp.int32, (rows, rows), 1)
     allowed = (col <= row) & (col < length[0])
@@ -545,6 +629,7 @@
         prob = powers * (1.0 / jnp.sum(powers, axis=-1, keepdims=True))
         probs[g] = prob
         mixes.append(pick_rows(dot(prob.astype(LOW), v)).astype(LOW))
+    probs.leave()
     mixes = jnp.concatenate(mixes, axis=1)
     mix[...] = mixes
     after_self = xf + dot(mixes, self_out[...])
@@ -558,6 +643,7 @@
 def memory_kernel(ctx, here, mine, other, *refs):
     blocks, (memory_in, memory) = refs[:-2], refs[-2:]
     place(here, blocks, [memory_in], ctx)
+    memory_in.leave()
     first = here[CORE] == 0
     width = mine.shape[1]
     keys = half_of(first, memory_in[:, :width])
@@ -694,6 +780,7 @@
 ):
     blocks, outs = refs[:-10], refs[-10:]
     place(here, blocks, [outs[0]], ctx)
+    outs[0].leave()
     feed_step(
         here, length, task, mix_mine, mix_other, x1, gains, feed_mine, feed_other, cot, *outs
     )
@@ -724,6 +811,7 @@
     first = here[CORE] == 0
     after_cross = x1[...] + dot(join(first, mix_mine[...], mix_other[...]), cross_out[...])
     x2[...] = after_cross
+    x2.leave()
     unit, _ = rms_unit(after_cross)
     normed = (unit * gains[2:3, :]).astype(LOW)
     h3[...] = normed
@@ -1023,8 +1111,7 @@
 ):
     pb, ctx = lax.axis_size("pb"), lax.axis_size("ctx")
     mine_pb, mine_ctx = lax.axis_index("pb"), lax.axis_index("ctx")
-    here = jnp.stack([mine_ctx & 1, mine_ctx >> 1, mine_pb, mine_ctx, jnp.int32(ctx)])
-    here = here.astype(jnp.int32)
+    here = None
     rows, width = decoder_in.shape[1:]
     half = width // 2
     passage = encoder_out.shape[1]
@@ -1068,12 +1155,12 @@
     proj, self_out, cross_in, gains, p1, probs, mix1, x1, h1, h2, cq = call(
         functools.partial(self_kernel, ctx),
         [
-            ((width, 3 * width), LOW),
-            ((width, width), LOW),
-            ((width, width), LOW),
+            ((width, 3 * width), LOW, True),
+            ((width, width), LOW, True),
+            ((width, width), LOW, True),
             ((norm_gains.shape[0], width), FULL),
-            ((rows, 3 * width), LOW),
-            ((heads // 2, 2 * rows, rows), FULL),
+            ((rows, 3 * width), LOW, True),
+            ((heads // 2, 2 * rows, rows), FULL, True),
             ((rows, width), LOW),
             ((rows, width), FULL),
             ((rows, width), LOW),
@@ -1083,7 +1170,7 @@
         [here, target_length, x, table] + proj_blocks,
         scalars=2,
         scratch=[pltpu.VMEM((width, 128), LOW)],
-        spare=5 * SPARE_BYTES,
+        limit=ALL_BYTES,
     )
     def part(size, index):
         return [(b, b.shape[:2] + (size * width,), (0, 0, index)) for b in others_blocks]
@@ -1092,7 +1179,7 @@
     feed_other = swap_ctx(feed, 1)
     memory_in, memory = call(
         functools.partial(memory_kernel, ctx),
-        [((width, 2 * width), LOW), ((2 * passage, width), LOW)],
+        [((width, 2 * width), LOW, True), ((2 * passage, width), LOW)],
         [here, e, e_other] + part(2, 0),
         scalars=1,
     )
@@ -1108,8 +1195,8 @@
     cross_out, x2, h3, active, low_out, grad_hidden, partial, part_out = call(
         functools.partial(feed_kernel, ctx),
         [
-            ((width, width), LOW),
-            ((rows, width), FULL),
+            ((width, width), LOW, True),
+            ((rows, width), FULL, True),
             ((rows, width), LOW),
             ((rows, 2 * units), LOW),
             ((rows, width), LOW),
@@ -1133,12 +1220,13 @@
         scalars=3,
         scratch=[pltpu.VMEM((width, 2 * units), LOW), pltpu.VMEM((2 * units, width), LOW)],
     )
-    sums = sum_chips(partial)
+    partials = all_chips(partial)
+    sums = add_chips(partials)
     sums_other = swap_ctx(sums, 1)
     (feed_grads,) = call(
         functools.partial(feed_grad_kernel, share),
         [((pb, 2 * slab, width), LOW)],
-        [here, active, low_out, h3, grad_hidden],
+        [here, after(active, partials), low_out, h3, grad_hidden],
         scalars=1,
         scratch=[pltpu.VMEM((2 * units, width), FULL), pltpu.VMEM((width, 2 * units), FULL)],
     )
@@ -1160,10 +1248,10 @@
             task_group,
             sums,
             sums_other,
-            x2,
+            Far(x2),
             gains,
             cot,
-            cross_out,
+            Far(cross_out),
             cq,
             memory,
             visible,
@@ -1172,7 +1260,7 @@
         ],
         scalars=3,
     )
-    grad_cq = sum_chips(grad_cq)
+    grad_cq = add_chips(all_chips(grad_cq))
     cq_other = swap_ctx(grad_cq, 1)
     pieces = call(
         functools.partial(memory_grad_kernel, pb),
@@ -1196,15 +1284,15 @@
             here,
             grad_cq,
             cq_other,
-            cross_in,
+            Far(cross_in),
             x1,
             gains,
             dx2,
-            self_out,
-            p1,
-            probs,
+            Far(self_out),
+            Far(p1),
+            Far(probs),
             x,
-            proj,
+            Far(proj),
             gain_grad,
         ],
         scalars=1,
@@ -1231,12 +1319,12 @@
         scalars=1,
         scratch=[pltpu.VMEM((width, pb * share), LOW), pltpu.VMEM((pb * share, 6 * width), FULL)],
     )
-    output = sum_chips(after(part_out, grads))
+    output = add_chips(all_chips(after(part_out, grads)))
     grads = exchange(grads, "pb")
     (grad_encoder,) = call(
         encoder_grad_kernel,
         [((passage, width), LOW)],
-        [here, after(grad_mine, grad_p1), memory_other, memory_in],
+        [here, after(grad_mine, grad_p1), memory_other, Far(memory_in)],
         scalars=1,
     )
     grad_contract, *expand_rows = call(

time: 201 us -> 191 us (0.950)
  local copies, waits for them, and re-layouts: 28.1 us -> 20 us
  other arithmetic: 4.88 us -> 1.98 us
    unnamed x133 -> x127, local copies, waits for them, and re-layouts: 23.3 us -> 15.4 us
  transfers between devices with their start and end apart: 63 -> 63, of which waited for: 31 -> 28; matrix products, arithmetic and copies ran while one was open for 5% -> 4% of each run, Pallas kernels for 16% -> 16%
where the time goes in v5:
time: 191 us; the launch traced here: 190 us
  starting transfers between devices  65.7 us (34%)
  waiting for transfers between devices  62 us (32%)
  Pallas kernels  36.6 us (19%)
  local copies, waits for them, and re-layouts  20 us (10%)
  between operations  2.75 us (1%)
  other arithmetic  1.98 us (1%)
    ppermute x54, waiting for transfers between devices, swap_ctx(): return lax.ppermute(values, 'ctx', [(i, i ^ mask) for i in range(size)])  52.3 us
    ppermute x54, starting transfers between devices, swap_ctx(): return lax.ppermute(values, 'ctx', [(i, i ^ mask) for i in range(size)])  42.1 us
    pallas_call x15, Pallas kernels, call(): pl.pallas_call(run, grid=grid, out_shape=[jax.ShapeDtypeStruct(out[0], ou...  36.6 us
    unnamed x127, local copies, waits for them, and re-layouts  15.4 us
    all_to_all x3, starting transfers between devices, exchange(): return lax.all_to_all(values, axis, 0, 0, tiled=True)  13.4 us
    ppermute x6, starting transfers between devices, swap_pb(): return lax.ppermute(values, 'pb', [(i, i ^ mask) for i in range(size)])  10.2 us
    all_to_all x3, waiting for transfers between devices, exchange(): return lax.all_to_all(values, axis, 0, 0, tiled=True)  9.65 us
  transfers between devices with their start and end apart: 63, of which 28 were waited for; matrix products, arithmetic and copies ran while one was open for 4% of the time, Pallas kernels for 16%

profile of v5, /device:TPU:0, one launch (start us, length us, event | category | flops | bytes accessed | tf_op | source)
XLA Modules:
  0.0 189.8 jit_solution(5050366914074153312)
XLA Ops:
  4.0 3.0 %collective-permute-start = (bf16[24,3968]{1,0:T(8,128)(2,1)S(1)}, bf16[24,3968]{1,0:T(8,128)(2,1)S(1)}, u32[]{:S(2)}, u32[]{:S(2)}) collective-permute-start(bf16[24,3968]{1,0:T(8,128)(2,1)S(1)} %shard_map.247), channel_id=1, source_target_pairs={{0,8},{8,0},{16,24},{24,16},{1,9},{9,1},{17,25},{25,17},{2,10},{10... | collective-permute-start | bytes 571400 | tf_op jit(solution)/shard_map/ppermute | solution.py:461
  7.0 2.6 %collective-permute-start.1 = (bf16[24,3968]{1,0:T(8,128)(2,1)S(1)}, bf16[24,3968]{1,0:T(8,128)(2,1)S(1)}, u32[]{:S(2)}, u32[]{:S(2)}) collective-permute-start(bf16[24,3968]{1,0:T(8,128)(2,1)S(1)} %shard_map.247), channel_id=1, source_target_pairs={{0,16},{8,24},{16,0},{24,8},{1,17},{9,25},{17,1},{25,9},{2,18},{10... | collective-permute-start | bytes 571400 | tf_op jit(solution)/shard_map/ppermute | solution.py:461
  9.6 1.7 collective-permute-start.11
  13.7 1.6 collective-permute-start.12
  15.7 5.3 %collective-permute-done.12 = bf16[24,3968]{1,0:T(8,128)(2,1)S(1)} collective-permute-done((bf16[24,3968]{1,0:T(8,128)(2,1)S(1)}, bf16[24,3968]{1,0:T(8,128)(2,1)S(1)}, u32[]{:S(2)}, u32[]{:S(2)}) %collective-permute-start.12) | collective-permute-done | bytes 190496 | tf_op jit(solution)/shard_map/ppermute | solution.py:456
  26.9 1.8 collective-permute-start.3
  32.8 3.5 %collective-permute-done.14 = bf16[24,2304]{1,0:T(8,128)(2,1)S(1)} collective-permute-done((bf16[24,2304]{1,0:T(8,128)(2,1)S(1)}, bf16[24,2304]{1,0:T(8,128)(2,1)S(1)}, u32[]{:S(2)}, u32[]{:S(2)}) %collective-permute-start.14) | collective-permute-done | bytes 110624 | tf_op jit(solution)/shard_map/ppermute | solution.py:456
  40.0 4.4 %all-to-all-start = ((bf16[4,96,1536]{2,1,0:T(8,128)(2,1)}), bf16[4,96,1536]{2,1,0:T(8,128)(2,1)S(1)}, u32[]{:S(2)}, u32[]{:S(2)}) async-start(bf16[4,96,1536]{2,1,0:T(8,128)(2,1)} %broadcast_in_dim.8), calls=%async_computation | async-start | bytes 2359296 | tf_op jit(solution)/shard_map/all_to_all | solution.py:465
  44.6 5.6 %collective-permute-done.15.refs_7_ = bf16[3,24,3968]{2,1,0:T(8,128)(2,1)} collective-permute-done((bf16[3,24,3968]{2,1,0:T(8,128)(2,1)S(1)}, bf16[3,24,3968]{2,1,0:T(8,128)(2,1)}, u32[]{:S(2)}, u32[]{:S(2)}) %collective-permute-start.15) | collective-permute-done | bytes 571424 | tf_op jit(solution)/shard_map/ppermute | solution.py:456
  50.2 1.7 collective-permute-start.17
  56.4 4.2 %collective-permute-done.17.refs_6_.refs_13_ = bf16[3,24,2304]{2,1,0:T(8,128)(2,1)S(1)} collective-permute-done((bf16[3,24,2304]{2,1,0:T(8,128)(2,1)S(1)}, bf16[3,24,2304]{2,1,0:T(8,128)(2,1)S(1)}, u32[]{:S(2)}, u32[]{:S(2)}) %collective-permute-start.17) | collective-permute-done | bytes 331808 | tf_op jit(solution)/shard_map/ppermute | solution.py:456
  61.2 3.6 %collective-permute-done.23.refs_11_ = bf16[2,24,3968]{2,1,0:T(8,128)(2,1)} collective-permute-done((bf16[2,24,3968]{2,1,0:T(8,128)(2,1)S(1)}, bf16[2,24,3968]{2,1,0:T(8,128)(2,1)}, u32[]{:S(2)}, u32[]{:S(2)}) %collective-permute-start.23) | collective-permute-done | bytes 380960 | tf_op jit(solution)/shard_map/ppermute | solution.py:456
  67.4 9.2 %shard_map.248 = (bf16[768,2304]{1,0:T(8,128)(2,1)}, bf16[768,768]{1,0:T(8,128)(2,1)}, bf16[768,768]{1,0:T(8,128)(2,1)}, f32[3,768]{1,0:T(4,128)}, bf16[128,2304...) custom-call(s32[1]{0:T(128)S(6)} %copy.30.refs_0_, ...), custom_call_target="tpu_custom_call" | custom-call | tf_op jit(solution)/shard_map/pallas_call | solution.py:137
  78.1 1.6 collective-permute-start.33
  80.1 4.7 %collective-permute-done.31.refs_10_.refs_17_ = bf16[2,24,2304]{2,1,0:T(8,128)(2,1)S(1)} collective-permute-done((bf16[2,24,2304]{2,1,0:T(8,128)(2,1)S(1)}, bf16[2,24,2304]{2,1,0:T(8,128)(2,1)S(1)}, u32[]{:S(2)}, u32[]{:S(2)}) %collective-permute-start.31) | collective-permute-done | bytes 221216 | tf_op jit(solution)/shard_map/ppermute | solution.py:456
  90.7 1.6 collective-permute-start.35
  94.3 2.4 %collective-permute-done.35.refs_1_ = bf16[128,512]{1,0:T(8,128)(2,1)S(1)} collective-permute-done((bf16[128,512]{1,0:T(8,128)(2,1)S(1)}, bf16[128,512]{1,0:T(8,128)(2,1)S(1)}, u32[]{:S(2)}, u32[]{:S(2)}) %collective-permute-start.35) | collective-permute-done | bytes 131104 | tf_op jit(solution)/shard_map/ppermute | solution.py:456
  96.6 3.7 %collective-permute-done.36.refs_2_ = bf16[128,512]{1,0:T(8,128)(2,1)S(1)} collective-permute-done((bf16[128,512]{1,0:T(8,128)(2,1)S(1)}, bf16[128,512]{1,0:T(8,128)(2,1)S(1)}, u32[]{:S(2)}, u32[]{:S(2)}) %collective-permute-start.36) | collective-permute-done | bytes 131104 | tf_op jit(solution)/shard_map/ppermute | solution.py:456
  102.6 2.5 %shard_map.252 = (bf16[768,768]{1,0:T(8,128)(2,1)S(1)}, f32[128,768]{1,0:T(8,128)S(1)}, bf16[128,768]{1,0:T(8,128)(2,1)S(1)}, bf16[128,768]{1,0:T(8,128)(2,1)S(1...) custom-call(s32[1]{0:T(128)S(6)} %copy.30.refs_0_, ...), custom_call_target="tpu_custom_call" | custom-call | tf_op jit(solution)/shard_map/pallas_call | solution.py:137
  109.6 1.5 collective-permute-start.42
  112.5 2.0 %collective-permute-done.41 = bf16[128,384]{1,0:T(8,128)(2,1)S(1)} collective-permute-done((bf16[128,384]{1,0:T(8,128)(2,1)S(1)}, bf16[128,384]{1,0:T(8,128)(2,1)S(1)}, u32[]{:S(2)}, u32[]{:S(2)}) %collective-permute-start.41) | collective-permute-done | bytes 98336 | tf_op jit(solution)/shard_map/ppermute | solution.py:456
  115.5 2.2 %shard_map.259 = bf16[4,192,768]{2,1,0:T(8,128)(2,1)} custom-call(bf16[128,768]{1,0:T(8,128)(2,1)S(1)} %get-tuple-element.122.refs_0_, bf16[128,768]{1,0:T(8,128)(2,1)S(1)} %get-tuple-element.123.refs_1_, bf16[128,768]{1,0:T(8,128)(2,1)S(1)} %get-tuple-element.124.refs_2_, bf16[128,768]{1,0:T(8,128)(2,1)S(1)} %get-tuple-element.125.refs_3_), custom_call_target="tpu_custom_call" | custom-call | tf_op jit(solution)/shard_map/pallas_call | solution.py:137
  117.7 3.9 %all-to-all-start.2 = ((bf16[4,192,768]{2,1,0:T(8,128)(2,1)}), bf16[4,192,768]{2,1,0:T(8,128)(2,1)S(1)}, u32[]{:S(2)}, u32[]{:S(2)}) async-start(bf16[4,192,768]{2,1,0:T(8,128)(2,1)} %shard_map.259), calls=%async_computation.2 | async-start | bytes 2359296 | tf_op jit(solution)/shard_map/all_to_all | solution.py:465
  124.4 2.7 %shard_map.253 = (f32[128,768]{1,0:T(8,128)S(1)}, bf16[128,768]{1,0:T(8,128)(2,1)S(1)}, bf16[128,384]{1,0:T(8,128)(2,1)S(1)}, bf16[240,768]{1,0:T(8,128)(2,1)S(1...) custom-call(s32[1]{0:T(128)S(6)} %copy.30.refs_0_, s32[1]{0:T(128)S(6)} %copy.31.refs_1_, ...), custom_call_target="tpu_custom_call" | custom-call | tf_op jit(solution)/shard_map/pallas_call | solution.py:137
  140.9 7.0 %shard_map.254 = (bf16[128,768]{1,0:T(8,128)(2,1)S(1)}, bf16[128,2304]{1,0:T(8,128)(2,1)S(1)}, bf16[128,768]{1,0:T(8,128)(2,1)}, f32[16,768]{1,0:T(8,128)S(1)}) custom-call(bf16[128,384]{1,0:T(8,128)(2,1)S(1)} %add_convert_fusion.2.refs_0_.refs_4_, bf16[128,384]{1,0:T(8,128)(2,1)S(1)} %collective-permute-done.47.refs_1_.refs_5_, ...), custom_call_target="tpu_custom_call" | custom-call | tf_op jit(solution)/shard_map/pallas_call | solution.py:137
  148.0 2.8 %shard_map.256 = bf16[4,208,768]{2,1,0:T(8,128)(2,1)} custom-call(bf16[128,384]{1,0:T(8,128)(2,1)S(1)} %copy-done.22, bf16[128,384]{1,0:T(8,128)(2,1)S(1)} %copy-done.31, bf16[128,768]{1,0:T(8,128)(2,1)S(1)} %get-tuple-element.90.refs_2_, bf16[128,768]{1,0:T(8,128)(2,1)S(1)} %copy-done.36, bf16[128,384]{1,0:T(8,128)(2,1)S(1)} %add_convert_fusion.2.refs_0_.refs_4_, ...), custom_call_target="tpu_custom_call" | custom-call | tf_op jit(solution)/shard_map/pallas_call | solution.py:137
  150.8 5.0 %all-to-all-start.1 = ((bf16[4,208,768]{2,1,0:T(8,128)(2,1)}), bf16[4,208,768]{2,1,0:T(8,128)(2,1)S(1)}, u32[]{:S(2)}, u32[]{:S(2)}) async-start(bf16[4,208,768]{2,1,0:T(8,128)(2,1)} %shard_map.256), calls=%async_computation.1 | async-start | bytes 2555904 | tf_op jit(solution)/shard_map/all_to_all | solution.py:465
  160.6 3.1 %collective-permute-done.52 = bf16[128,384]{1,0:T(8,128)(2,1)S(1)} collective-permute-done((bf16[128,384]{1,0:T(8,128)(2,1)S(1)}, bf16[128,384]{1,0:T(8,128)(2,1)S(1)}, u32[]{:S(2)}, u32[]{:S(2)}) %collective-permute-start.52) | collective-permute-done | bytes 98336 | tf_op jit(solution)/shard_map/ppermute | solution.py:456
  163.8 1.7 copy-done.3
  165.5 2.8 %shard_map.257 = bf16[240,768]{1,0:T(8,128)(2,1)} custom-call(bf16[240,768]{1,0:T(8,128)(2,1)S(1)} %copy-done.16, bf16[240,768]{1,0:T(8,128)(2,1)} %collective-permute-done.55.refs_1_, bf16[768,1536]{1,0:T(8,128)(2,1)S(1)} %copy-done.3), custom_call_target="tpu_custom_call" | custom-call | tf_op jit(solution)/shard_map/pallas_call | solution.py:137
  174.2 2.1 %collective-permute-done.59.refs_3_ = bf16[24,768]{1,0:T(8,128)(2,1)S(1)} collective-permute-done((bf16[24,768]{1,0:T(8,128)(2,1)S(1)}, bf16[24,768]{1,0:T(8,128)(2,1)S(1)}, u32[]{:S(2)}, u32[]{:S(2)}) %collective-permute-start.59) | collective-permute-done | bytes 36896 | tf_op jit(solution)/shard_map/ppermute | solution.py:456
  177.1 9.6 %all-to-all-done.1.refs_0_ = bf16[4,208,768]{2,1,0:T(8,128)(2,1)S(1)} async-done(((bf16[4,208,768]{2,1,0:T(8,128)(2,1)}), bf16[4,208,768]{2,1,0:T(8,128)(2,1)S(1)}, u32[]{:S(2)}, u32[]{:S(2)}) %all-to-all-start.1) | async-done | bytes 1277984 | tf_op jit(solution)/shard_map/all_to_all | solution.py:465
  (265 shorter events, 76.0 us)
Async XLA Ops:
  4.0 18.5 %collective-permute-start = (bf16[24,3968]{1,0:T(8,128)(2,1)S(1)}, bf16[24,3968]{1,0:T(8,128)(2,1)S(1)}, u32[]{:S(2)}, u32[]{:S(2)}) collective-permute-start(bf16[24,3968]{1,0:T(8,128)(2,1)S(1)} %shard_map.247), channel_id=1, source_target_pairs={{0,8},{8,0},{16,24},{24,16},{1,9},{9,1},{17,25},{25,17},{2,10},{10... | collective-permute-start | bytes 571400 | tf_op jit(solution)/shard_map/ppermute | solution.py:461
  7.0 16.9 %collective-permute-start.1 = (bf16[24,3968]{1,0:T(8,128)(2,1)S(1)}, bf16[24,3968]{1,0:T(8,128)(2,1)S(1)}, u32[]{:S(2)}, u32[]{:S(2)}) collective-permute-start(bf16[24,3968]{1,0:T(8,128)(2,1)S(1)} %shard_map.247), channel_id=1, source_target_pairs={{0,16},{8,24},{16,0},{24,8},{1,17},{9,25},{17,1},{25,9},{2,18},{10... | collective-permute-start | bytes 571400 | tf_op jit(solution)/shard_map/ppermute | solution.py:461
  9.6 15.7 %collective-permute-start.2 = (bf16[24,3968]{1,0:T(8,128)(2,1)S(1)}, bf16[24,3968]{1,0:T(8,128)(2,1)S(1)}, u32[]{:S(2)}, u32[]{:S(2)}) collective-permute-start(bf16[24,3968]{1,0:T(8,128)(2,1)S(1)} %shard_map.247), channel_id=1, source_target_pairs={{0,24},{8,16},{16,8},{24,0},{1,25},{9,17},{17,9},{25,1},{2,26},{10... | collective-permute-start | bytes 571400 | tf_op jit(solution)/shard_map/ppermute | solution.py:461
  13.7 7.2 %collective-permute-start.12 = (bf16[24,3968]{1,0:T(8,128)(2,1)S(1)}, bf16[24,3968]{1,0:T(8,128)(2,1)S(1)}, u32[]{:S(2)}, u32[]{:S(2)}) collective-permute-start(bf16[24,3968]{1,0:T(8,128)(2,1)S(1)} %shard_map.247), channel_id=1, source_target_pairs={{0,4},{1,5},{2,6},{3,7},{4,0},{5,1},{6,2},{7,3},{8,12},{9,13},{10,... | collective-permute-start | bytes 571400 | tf_op jit(solution)/shard_map/ppermute | solution.py:456
  15.6 20.7 %collective-permute-start.6 = (bf16[240,768]{1,0:T(8,128)(2,1)S(1)}, bf16[240,768]{1,0:T(8,128)(2,1)S(1)}, u32[]{:S(2)}, u32[]{:S(2)}) collective-permute-start(bf16[240,768]{1,0:T(8,128)(2,1)S(1)} %bitcast.32), channel_id=1, source_target_pairs={{0,1},{1,0},{2,3},{3,2},{4,5},{5,4},{6,7},{7,6},{8,9},{9,8},{10,11... | collective-permute-start | bytes 1105928 | tf_op jit(solution)/shard_map/ppermute | solution.py:456
  26.9 11.9 %collective-permute-start.3 = (bf16[24,2304]{1,0:T(8,128)(2,1)S(1)}, bf16[24,2304]{1,0:T(8,128)(2,1)S(1)}, u32[]{:S(2)}, u32[]{:S(2)}) collective-permute-start(bf16[24,2304]{1,0:T(8,128)(2,1)S(1)} %constant_dynamic-update-slice_fusion), channel_id=1, source_target_pairs={{0,8},{8,0},{16,24},{24,16},{1,9},{9,1},{17,25},{25,17},{2,10},{10... | collective-permute-start | bytes 331784 | tf_op jit(solution)/shard_map/ppermute | solution.py:461
  28.7 10.1 %collective-permute-start.4 = (bf16[24,2304]{1,0:T(8,128)(2,1)S(1)}, bf16[24,2304]{1,0:T(8,128)(2,1)S(1)}, u32[]{:S(2)}, u32[]{:S(2)}) collective-permute-start(bf16[24,2304]{1,0:T(8,128)(2,1)S(1)} %constant_dynamic-update-slice_fusion), channel_id=1, source_target_pairs={{0,16},{8,24},{16,0},{24,8},{1,17},{9,25},{17,1},{25,9},{2,18},{10... | collective-permute-start | bytes 331784 | tf_op jit(solution)/shard_map/ppermute | solution.py:461
  30.0 8.8 %collective-permute-start.5 = (bf16[24,2304]{1,0:T(8,128)(2,1)S(1)}, bf16[24,2304]{1,0:T(8,128)(2,1)S(1)}, u32[]{:S(2)}, u32[]{:S(2)}) collective-permute-start(bf16[24,2304]{1,0:T(8,128)(2,1)S(1)} %constant_dynamic-update-slice_fusion), channel_id=1, source_target_pairs={{0,24},{8,16},{16,8},{24,0},{1,25},{9,17},{17,9},{25,1},{2,26},{10... | collective-permute-start | bytes 331784 | tf_op jit(solution)/shard_map/ppermute | solution.py:461
  37.1 13.1 %collective-permute-start.15 = (bf16[3,24,3968]{2,1,0:T(8,128)(2,1)S(1)}, bf16[3,24,3968]{2,1,0:T(8,128)(2,1)}, u32[]{:S(2)}, u32[]{:S(2)}) collective-permute-start(bf16[3,24,3968]{2,1,0:T(8,128)(2,1)S(1)} %pad_maximum_fusion.refs_5_), channel_id=1, source_target_pairs={{0,2},{1,3},{2,0},{3,1},{4,6},{5,7},{6,4},{7,5},{8,10},{9,11},{10,... | collective-permute-start | bytes 1714184 | tf_op jit(solution)/shard_map/ppermute | solution.py:456
  37.6 12.6 %collective-permute-start.16 = (bf16[3,24,3968]{2,1,0:T(8,128)(2,1)S(1)}, bf16[3,24,3968]{2,1,0:T(8,128)(2,1)}, u32[]{:S(2)}, u32[]{:S(2)}) collective-permute-start(bf16[3,24,3968]{2,1,0:T(8,128)(2,1)S(1)} %pad_maximum_fusion.refs_5_), channel_id=1, source_target_pairs={{0,4},{1,5},{2,6},{3,7},{4,0},{5,1},{6,2},{7,3},{8,12},{9,13},{10,... | collective-permute-start | bytes 1714184 | tf_op jit(solution)/shard_map/ppermute | solution.py:456
  40.0 36.6 %all-to-all-start = ((bf16[4,96,1536]{2,1,0:T(8,128)(2,1)}), bf16[4,96,1536]{2,1,0:T(8,128)(2,1)S(1)}, u32[]{:S(2)}, u32[]{:S(2)}) async-start(bf16[4,96,1536]{2,1,0:T(8,128)(2,1)} %broadcast_in_dim.8), calls=%async_computation | async-start | bytes 2359296 | tf_op jit(solution)/shard_map/all_to_all | solution.py:465
  44.5 11.9 %collective-permute-start.19 = (bf16[3,24,3968]{2,1,0:T(8,128)(2,1)S(1)}, bf16[3,24,3968]{2,1,0:T(8,128)(2,1)S(1)}, u32[]{:S(2)}, u32[]{:S(2)}) collective-permute-start(bf16[3,24,3968]{2,1,0:T(8,128)(2,1)S(1)} %pad_maximum_fusion.1.refs_3_), channel_id=1, source_target_pairs={{0,1},{1,0},{2,3},{3,2},{4,5},{5,4},{6,7},{7,6},{8,9},{9,8},{10,11... | collective-permute-start | bytes 1714184 | tf_op jit(solution)/shard_map/ppermute | solution.py:456
  50.2 10.5 %collective-permute-start.17 = (bf16[3,24,2304]{2,1,0:T(8,128)(2,1)S(1)}, bf16[3,24,2304]{2,1,0:T(8,128)(2,1)S(1)}, u32[]{:S(2)}, u32[]{:S(2)}) collective-permute-start(bf16[3,24,2304]{2,1,0:T(8,128)(2,1)S(1)} %pad_maximum_fusion.3.refs_4_.refs_11_), channel_id=1, source_target_pairs={{0,2},{1,3},{2,0},{3,1},{4,6},{5,7},{6,4},{7,5},{8,10},{9,11},{10,... | collective-permute-start | bytes 995336 | tf_op jit(solution)/shard_map/ppermute | solution.py:456
  51.9 8.8 %collective-permute-start.18 = (bf16[3,24,2304]{2,1,0:T(8,128)(2,1)S(1)}, bf16[3,24,2304]{2,1,0:T(8,128)(2,1)S(1)}, u32[]{:S(2)}, u32[]{:S(2)}) collective-permute-start(bf16[3,24,2304]{2,1,0:T(8,128)(2,1)S(1)} %pad_maximum_fusion.3.refs_4_.refs_11_), channel_id=1, source_target_pairs={{0,4},{1,5},{2,6},{3,7},{4,0},{5,1},{6,2},{7,3},{8,12},{9,13},{10,... | collective-permute-start | bytes 995336 | tf_op jit(solution)/shard_map/ppermute | solution.py:456
  53.7 11.1 %collective-permute-start.23 = (bf16[2,24,3968]{2,1,0:T(8,128)(2,1)S(1)}, bf16[2,24,3968]{2,1,0:T(8,128)(2,1)}, u32[]{:S(2)}, u32[]{:S(2)}) collective-permute-start(bf16[2,24,3968]{2,1,0:T(8,128)(2,1)S(1)} %pad_maximum_fusion.2), channel_id=1, source_target_pairs={{0,4},{1,5},{2,6},{3,7},{4,0},{5,1},{6,2},{7,3},{8,12},{9,13},{10,... | collective-permute-start | bytes 1142792 | tf_op jit(solution)/shard_map/ppermute | solution.py:456
  56.0 8.9 %collective-permute-start.25 = (bf16[2,24,3968]{2,1,0:T(8,128)(2,1)S(1)}, bf16[2,24,3968]{2,1,0:T(8,128)(2,1)}, u32[]{:S(2)}, u32[]{:S(2)}) collective-permute-start(bf16[2,24,3968]{2,1,0:T(8,128)(2,1)S(1)} %slice.33), channel_id=1, source_target_pairs={{0,2},{1,3},{2,0},{3,1},{4,6},{5,7},{6,4},{7,5},{8,10},{9,11},{10,... | collective-permute-start | bytes 1142792 | tf_op jit(solution)/shard_map/ppermute | solution.py:456
  56.4 10.4 %collective-permute-start.20 = (bf16[3,24,3968]{2,1,0:T(8,128)(2,1)S(1)}, bf16[3,24,3968]{2,1,0:T(8,128)(2,1)}, u32[]{:S(2)}, u32[]{:S(2)}) collective-permute-start(bf16[3,24,3968]{2,1,0:T(8,128)(2,1)S(1)} %pad_maximum_fusion.refs_5_), channel_id=1, source_target_pairs={{0,1},{1,0},{2,3},{3,2},{4,5},{5,4},{6,7},{7,6},{8,9},{9,8},{10,11... | collective-permute-start | bytes 1714184 | tf_op jit(solution)/shard_map/ppermute | solution.py:456
  66.8 12.8 %collective-permute-start.28 = (bf16[3,24,2304]{2,1,0:T(8,128)(2,1)S(1)}, bf16[3,24,2304]{2,1,0:T(8,128)(2,1)S(1)}, u32[]{:S(2)}, u32[]{:S(2)}) collective-permute-start(bf16[3,24,2304]{2,1,0:T(8,128)(2,1)S(1)} %pad_maximum_fusion.3.refs_4_.refs_11_), channel_id=1, source_target_pairs={{0,1},{1,0},{2,3},{3,2},{4,5},{5,4},{6,7},{7,6},{8,9},{9,8},{10,11... | collective-permute-start | bytes 995336 | tf_op jit(solution)/shard_map/ppermute | solution.py:456
  76.6 26.0 %collective-permute-start.39 = (bf16[4,96,1536]{2,1,0:T(8,128)(2,1)S(1)}, bf16[4,96,1536]{2,1,0:T(8,128)(2,1)S(1)}, u32[]{:S(2)}, u32[]{:S(2)}) collective-permute-start(bf16[4,96,1536]{2,1,0:T(8,128)(2,1)S(1)} %all-to-all-done.refs_6_), channel_id=1, source_target_pairs={{0,1},{1,0},{2,3},{3,2},{4,5},{5,4},{6,7},{7,6},{8,9},{9,8},{10,11... | collective-permute-start | bytes 3538952 | tf_op jit(solution)/shard_map/ppermute | solution.py:456
  77.3 7.5 %collective-permute-start.31 = (bf16[2,24,2304]{2,1,0:T(8,128)(2,1)S(1)}, bf16[2,24,2304]{2,1,0:T(8,128)(2,1)S(1)}, u32[]{:S(2)}, u32[]{:S(2)}) collective-permute-start(bf16[2,24,2304]{2,1,0:T(8,128)(2,1)S(1)} %pad_maximum_fusion.5), channel_id=1, source_target_pairs={{0,4},{1,5},{2,6},{3,7},{4,0},{5,1},{6,2},{7,3},{8,12},{9,13},{10,... | collective-permute-start | bytes 663560 | tf_op jit(solution)/shard_map/ppermute | solution.py:456
  78.1 7.3 %collective-permute-start.33 = (bf16[2,24,2304]{2,1,0:T(8,128)(2,1)S(1)}, bf16[2,24,2304]{2,1,0:T(8,128)(2,1)S(1)}, u32[]{:S(2)}, u32[]{:S(2)}) collective-permute-start(bf16[2,24,2304]{2,1,0:T(8,128)(2,1)S(1)} %slice.35), channel_id=1, source_target_pairs={{0,2},{1,3},{2,0},{3,1},{4,6},{5,7},{6,4},{7,5},{8,10},{9,11},{10,... | collective-permute-start | bytes 663560 | tf_op jit(solution)/shard_map/ppermute | solution.py:456
  92.3 8.1 %collective-permute-start.36 = (bf16[128,512]{1,0:T(8,128)(2,1)S(1)}, bf16[128,512]{1,0:T(8,128)(2,1)S(1)}, u32[]{:S(2)}, u32[]{:S(2)}) collective-permute-start(bf16[128,512]{1,0:T(8,128)(2,1)S(1)} %shard_map.250.refs_0_), channel_id=1, source_target_pairs={{0,4},{1,5},{2,6},{3,7},{4,0},{5,1},{6,2},{7,3},{8,12},{9,13},{10,... | collective-permute-start | bytes 393224 | tf_op jit(solution)/shard_map/ppermute | solution.py:456
  93.7 6.7 %collective-permute-start.37 = (bf16[128,512]{1,0:T(8,128)(2,1)S(1)}, bf16[128,512]{1,0:T(8,128)(2,1)S(1)}, u32[]{:S(2)}, u32[]{:S(2)}) collective-permute-start(bf16[128,512]{1,0:T(8,128)(2,1)S(1)} %shard_map.250.refs_0_), channel_id=1, source_target_pairs={{0,6},{1,7},{2,4},{3,5},{4,2},{5,3},{6,0},{7,1},{8,14},{9,15},{10,... | collective-permute-start | bytes 393224 | tf_op jit(solution)/shard_map/ppermute | solution.py:456
  117.7 33.1 %all-to-all-start.2 = ((bf16[4,192,768]{2,1,0:T(8,128)(2,1)}), bf16[4,192,768]{2,1,0:T(8,128)(2,1)S(1)}, u32[]{:S(2)}, u32[]{:S(2)}) async-start(bf16[4,192,768]{2,1,0:T(8,128)(2,1)} %shard_map.259), calls=%async_computation.2 | async-start | bytes 2359296 | tf_op jit(solution)/shard_map/all_to_all | solution.py:465
  127.2 6.9 %collective-permute-start.44 = (bf16[128,384]{1,0:T(8,128)(2,1)S(1)}, bf16[128,384]{1,0:T(8,128)(2,1)S(1)}, u32[]{:S(2)}, u32[]{:S(2)}) collective-permute-start(bf16[128,384]{1,0:T(8,128)(2,1)S(1)} %get-tuple-element.92), channel_id=1, source_target_pairs={{0,2},{1,3},{2,0},{3,1},{4,6},{5,7},{6,4},{7,5},{8,10},{9,11},{10,... | collective-permute-start | bytes 294920 | tf_op jit(solution)/shard_map/ppermute | solution.py:456
  128.4 6.9 %collective-permute-start.45 = (bf16[128,384]{1,0:T(8,128)(2,1)S(1)}, bf16[128,384]{1,0:T(8,128)(2,1)S(1)}, u32[]{:S(2)}, u32[]{:S(2)}) collective-permute-start(bf16[128,384]{1,0:T(8,128)(2,1)S(1)} %get-tuple-element.92), channel_id=1, source_target_pairs={{0,4},{1,5},{2,6},{3,7},{4,0},{5,1},{6,2},{7,3},{8,12},{9,13},{10,... | collective-permute-start | bytes 294920 | tf_op jit(solution)/shard_map/ppermute | solution.py:456
  131.7 16.2 %collective-permute-start.48 = (bf16[192,768]{1,0:T(8,128)(2,1)S(1)}, bf16[192,768]{1,0:T(8,128)(2,1)S(1)}, u32[]{:S(2)}, u32[]{:S(2)}) collective-permute-start(bf16[192,768]{1,0:T(8,128)(2,1)S(1)} %get-tuple-element.108), channel_id=1, source_target_pairs={{0,2},{1,3},{2,0},{3,1},{4,6},{5,7},{6,4},{7,5},{8,10},{9,11},{10,... | collective-permute-start | bytes 884744 | tf_op jit(solution)/shard_map/ppermute | solution.py:456
  133.0 15.0 %collective-permute-start.49 = (bf16[192,768]{1,0:T(8,128)(2,1)S(1)}, bf16[192,768]{1,0:T(8,128)(2,1)S(1)}, u32[]{:S(2)}, u32[]{:S(2)}) collective-permute-start(bf16[192,768]{1,0:T(8,128)(2,1)S(1)} %get-tuple-element.109), channel_id=1, source_target_pairs={{0,4},{1,5},{2,6},{3,7},{4,0},{5,1},{6,2},{7,3},{8,12},{9,13},{10,... | collective-permute-start | bytes 884744 | tf_op jit(solution)/shard_map/ppermute | solution.py:456
  134.1 13.9 %collective-permute-start.50 = (bf16[192,768]{1,0:T(8,128)(2,1)S(1)}, bf16[192,768]{1,0:T(8,128)(2,1)S(1)}, u32[]{:S(2)}, u32[]{:S(2)}) collective-permute-start(bf16[192,768]{1,0:T(8,128)(2,1)S(1)} %get-tuple-element.110), channel_id=1, source_target_pairs={{0,6},{1,7},{2,4},{3,5},{4,2},{5,3},{6,0},{7,1},{8,14},{9,15},{10,... | collective-permute-start | bytes 884744 | tf_op jit(solution)/shard_map/ppermute | solution.py:456
  150.8 35.9 %all-to-all-start.1 = ((bf16[4,208,768]{2,1,0:T(8,128)(2,1)}), bf16[4,208,768]{2,1,0:T(8,128)(2,1)S(1)}, u32[]{:S(2)}, u32[]{:S(2)}) async-start(bf16[4,208,768]{2,1,0:T(8,128)(2,1)} %shard_map.256), calls=%async_computation.1 | async-start | bytes 2555904 | tf_op jit(solution)/shard_map/all_to_all | solution.py:465
  157.0 6.6 %collective-permute-start.52 = (bf16[128,384]{1,0:T(8,128)(2,1)S(1)}, bf16[128,384]{1,0:T(8,128)(2,1)S(1)}, u32[]{:S(2)}, u32[]{:S(2)}) collective-permute-start(bf16[128,384]{1,0:T(8,128)(2,1)S(1)} %copy-done.40), channel_id=1, source_target_pairs={{0,4},{1,5},{2,6},{3,7},{4,0},{5,1},{6,2},{7,3},{8,12},{9,13},{10,... | collective-permute-start | bytes 294920 | tf_op jit(solution)/shard_map/ppermute | solution.py:456
  163.7 9.0 %collective-permute-start.54 = (bf16[128,384]{1,0:T(8,128)(2,1)S(1)}, bf16[128,384]{1,0:T(8,128)(2,1)S(1)}, u32[]{:S(2)}, u32[]{:S(2)}) collective-permute-start(bf16[128,384]{1,0:T(8,128)(2,1)S(1)} %add_convert_fusion.1), channel_id=1, source_target_pairs={{0,1},{1,0},{2,3},{3,2},{4,5},{5,4},{6,7},{7,6},{8,9},{9,8},{10,11... | collective-permute-start | bytes 294920 | tf_op jit(solution)/shard_map/ppermute | solution.py:456
  (94 other events, 689.8 us)

commit v6 on v5

--- a/solution.py
+++ b/solution.py
@@ -43,27 +43,6 @@
     return factor * (scaled - unit * jnp.mean(scaled * unit, axis=-1, keepdims=True))
 
 
-class Far:
-    def __init__(self, array):
-        self.array, self.shape, self.dtype = array, array.shape, array.dtype
-
-
-class Arriving:
-    def __init__(self, source, held, sem):
-        self.held, self.shape, self.dtype = held, held.shape, held.dtype
-        self.copy = pltpu.make_async_copy(source, held, sem)
-        self.copy.start()
-
-    def wait(self):
-        if self.copy is not None:
-            self.copy.wait()
-            self.copy = None
-
-    def __getitem__(self, index):
-        self.wait()
-        return self.held[index]
-
-
 class Leaving:
     def __init__(self, held, target, sem):
         self.held, self.shape, self.dtype = held, held.shape, held.dtype
@@ -92,7 +71,6 @@
     if placed:
         args, scalars = args[1:], scalars - 1
     arrays, specs, grid, held = [], [], (), []
-    far_ins = [index for index, arg in enumerate(args) if isinstance(arg, Far)]
     far_outs = [index for index, out in enumerate(outs) if len(out) == 3]
     for index, arg in enumerate(args):
         if isinstance(arg, tuple):
@@ -100,18 +78,13 @@
             specs.append(pl.BlockSpec(shape, lambda i, place=place: place))
             grid = (1,)
             held.append((shape, arg.dtype))
-        elif isinstance(arg, Far):
-            specs.append(pl.BlockSpec(memory_space=pltpu.HBM))
-            held.append((arg.shape, arg.dtype))
-            arg = arg.array
         else:
             specs.append(pl.BlockSpec(memory_space=pltpu.SMEM if index < scalars else pltpu.VMEM))
             held.append((arg.shape, arg.dtype))
         arrays.append(arg)
     held += [out[:2] for out in outs] + [(one.shape, one.dtype) for one in scratch]
     size = sum(math.prod(shape) * jnp.dtype(dtype).itemsize for shape, dtype in held)
-    buffers = [pltpu.VMEM(args[i].shape, args[i].dtype) for i in far_ins]
-    buffers += [pltpu.VMEM(*outs[i][:2]) for i in far_outs]
+    buffers = [pltpu.VMEM(*outs[i][:2]) for i in far_outs]
     if buffers:
         buffers.append(pltpu.SemaphoreType.DMA((len(buffers),)))
 
@@ -120,24 +93,20 @@
         rest = refs[len(args) + len(outs) :]
         own, extra = rest[: len(scratch)], rest[len(scratch) :]
         moved = []
-        for k, i in enumerate(far_ins):
-            ins[i] = Arriving(ins[i], extra[k], extra[-1].at[k])
-            moved.append(ins[i])
-        for k, i in enumerate(far_outs, len(far_ins)):
+        for k, i in enumerate(far_outs):
             results[i] = Leaving(extra[k], results[i], extra[-1].at[k])
             moved.append(results[i])
         kernel(*([place_of_device()] if placed else []), *ins, *results, *own)
         for one in moved:
-            if isinstance(one, Leaving):
-                one.leave()
-                one.copy.wait()
-            else:
-                one.wait()
+            one.leave()
+            one.copy.wait()
 
     return pl.pallas_call(
         run,
         grid=grid,
-        out_shape=[jax.ShapeDtypeStruct(out[0], out[1]) for out in outs],
+        out_shape=[
+            pltpu.HBM(*out[:2]) if len(out) == 3 else jax.ShapeDtypeStruct(*out) for out in outs
+        ],
         in_specs=specs,
         out_specs=[
             pl.BlockSpec(memory_space=pltpu.HBM if len(out) == 3 else pltpu.VMEM) for out in outs
@@ -824,6 +793,7 @@
     active[...] = value
     grad_hidden[...] = grad
     partial[...] = dot_t(grad, half_of(first, expand[...], 0)).astype(LOW)
+    partial.leave()
     part_out[...] = dot(value, half_of(first, contract[...])).astype(LOW)
 
 
@@ -1201,7 +1171,7 @@
             ((rows, 2 * units), LOW),
             ((rows, width), LOW),
             ((rows, 2 * units), LOW),
-            ((rows, half), LOW),
+            ((rows, half), LOW, True),
             ((rows, half), LOW),
         ],
         [
@@ -1248,10 +1218,10 @@
             task_group,
             sums,
             sums_other,
-            Far(x2),
+            x2,
             gains,
             cot,
-            Far(cross_out),
+            cross_out,
             cq,
             memory,
             visible,
@@ -1284,15 +1254,15 @@
             here,
             grad_cq,
             cq_other,
-            Far(cross_in),
+            (cross_in, (width, width), (0, 0)),
             x1,
             gains,
             dx2,
-            Far(self_out),
-            Far(p1),
-            Far(probs),
+            (self_out, (width, width), (0, 0)),
+            (p1, (rows, 3 * width), (0, 0)),
+            probs,
             x,
-            Far(proj),
+            (proj, (width, 3 * width), (0, 0)),
             gain_grad,
         ],
         scalars=1,
@@ -1324,7 +1294,7 @@
     (grad_encoder,) = call(
         encoder_grad_kernel,
         [((passage, width), LOW)],
-        [here, after(grad_mine, grad_p1), memory_other, Far(memory_in)],
+        [here, after(grad_mine, grad_p1), memory_other, memory_in],
         scalars=1,
     )
     grad_contract, *expand_rows = call(

time: 191 us -> 187 us (0.979)
  local copies, waits for them, and re-layouts: 20 us -> 17.5 us
  Pallas kernels: 36.6 us -> 34.5 us
    unnamed x127 -> x119, local copies, waits for them, and re-layouts: 15.4 us -> 12.9 us
    pallas_call x15, Pallas kernels: 36.6 us -> 34.5 us  [call(): pl.pallas_call(run, grid=grid, out_shape=[pltpu.HBM(*out[:2]) if len(out)...]
  transfers between devices with their start and end apart: 63 -> 63, of which waited for: 28 -> 30; matrix products, arithmetic and copies ran while one was open for 4% -> 4% of each run, Pallas kernels for 16% -> 15%
where the time goes in v6:
time: 187 us; the launch traced here: 186 us
  starting transfers between devices  65.8 us (35%)
  waiting for transfers between devices  62.6 us (33%)
  Pallas kernels  34.5 us (18%)
  local copies, waits for them, and re-layouts  17.5 us (9%)
  between operations  2.69 us (1%)
  other arithmetic  1.98 us (1%)
    ppermute x54, waiting for transfers between devices, swap_ctx(): return lax.ppermute(values, 'ctx', [(i, i ^ mask) for i in range(size)])  53.7 us
    ppermute x54, starting transfers between devices, swap_ctx(): return lax.ppermute(values, 'ctx', [(i, i ^ mask) for i in range(size)])  42 us
    pallas_call x15, Pallas kernels, call(): pl.pallas_call(run, grid=grid, out_shape=[pltpu.HBM(*out[:2]) if len(out)...  34.5 us
    all_to_all x3, starting transfers between devices, exchange(): return lax.all_to_all(values, axis, 0, 0, tiled=True)  13.5 us
    unnamed x119, local copies, waits for them, and re-layouts  12.9 us
    ppermute x6, starting transfers between devices, swap_pb(): return lax.ppermute(values, 'pb', [(i, i ^ mask) for i in range(size)])  10.2 us
    all_to_all x3, waiting for transfers between devices, exchange(): return lax.all_to_all(values, axis, 0, 0, tiled=True)  8.89 us
  transfers between devices with their start and end apart: 63, of which 30 were waited for; matrix products, arithmetic and copies ran while one was open for 4% of the time, Pallas kernels for 15%

profile of v6, /device:TPU:0, one launch (start us, length us, event | category | flops | bytes accessed | tf_op | source)
XLA Modules:
  0.0 185.9 jit_solution(2962352277671619288)
XLA Ops:
  4.0 3.0 %collective-permute-start = (bf16[24,3968]{1,0:T(8,128)(2,1)S(1)}, bf16[24,3968]{1,0:T(8,128)(2,1)S(1)}, u32[]{:S(2)}, u32[]{:S(2)}) collective-permute-start(bf16[24,3968]{1,0:T(8,128)(2,1)S(1)} %shard_map.247), channel_id=1, source_target_pairs={{0,8},{8,0},{16,24},{24,16},{1,9},{9,1},{17,25},{25,17},{2,10},{10... | collective-permute-start | bytes 571400 | tf_op jit(solution)/shard_map/ppermute | solution.py:430
  7.0 2.6 %collective-permute-start.1 = (bf16[24,3968]{1,0:T(8,128)(2,1)S(1)}, bf16[24,3968]{1,0:T(8,128)(2,1)S(1)}, u32[]{:S(2)}, u32[]{:S(2)}) collective-permute-start(bf16[24,3968]{1,0:T(8,128)(2,1)S(1)} %shard_map.247), channel_id=1, source_target_pairs={{0,16},{8,24},{16,0},{24,8},{1,17},{9,25},{17,1},{25,9},{2,18},{10... | collective-permute-start | bytes 571400 | tf_op jit(solution)/shard_map/ppermute | solution.py:430
  9.6 1.7 collective-permute-start.11
  13.7 1.6 collective-permute-start.12
  15.7 5.3 %collective-permute-done.12 = bf16[24,3968]{1,0:T(8,128)(2,1)S(1)} collective-permute-done((bf16[24,3968]{1,0:T(8,128)(2,1)S(1)}, bf16[24,3968]{1,0:T(8,128)(2,1)S(1)}, u32[]{:S(2)}, u32[]{:S(2)}) %collective-permute-start.12) | collective-permute-done | bytes 190496 | tf_op jit(solution)/shard_map/ppermute | solution.py:425
  26.9 1.8 collective-permute-start.3
  32.8 3.5 %collective-permute-done.14 = bf16[24,2304]{1,0:T(8,128)(2,1)S(1)} collective-permute-done((bf16[24,2304]{1,0:T(8,128)(2,1)S(1)}, bf16[24,2304]{1,0:T(8,128)(2,1)S(1)}, u32[]{:S(2)}, u32[]{:S(2)}) %collective-permute-start.14) | collective-permute-done | bytes 110624 | tf_op jit(solution)/shard_map/ppermute | solution.py:425
  40.0 4.4 %all-to-all-start = ((bf16[4,96,1536]{2,1,0:T(8,128)(2,1)}), bf16[4,96,1536]{2,1,0:T(8,128)(2,1)S(1)}, u32[]{:S(2)}, u32[]{:S(2)}) async-start(bf16[4,96,1536]{2,1,0:T(8,128)(2,1)} %broadcast_in_dim.8), calls=%async_computation | async-start | bytes 2359296 | tf_op jit(solution)/shard_map/all_to_all | solution.py:434
  44.6 5.6 %collective-permute-done.15.refs_7_ = bf16[3,24,3968]{2,1,0:T(8,128)(2,1)} collective-permute-done((bf16[3,24,3968]{2,1,0:T(8,128)(2,1)S(1)}, bf16[3,24,3968]{2,1,0:T(8,128)(2,1)}, u32[]{:S(2)}, u32[]{:S(2)}) %collective-permute-start.15) | collective-permute-done | bytes 571424 | tf_op jit(solution)/shard_map/ppermute | solution.py:425
  50.2 1.7 collective-permute-start.17
  56.4 4.2 %collective-permute-done.17.refs_6_.refs_13_ = bf16[3,24,2304]{2,1,0:T(8,128)(2,1)S(1)} collective-permute-done((bf16[3,24,2304]{2,1,0:T(8,128)(2,1)S(1)}, bf16[3,24,2304]{2,1,0:T(8,128)(2,1)S(1)}, u32[]{:S(2)}, u32[]{:S(2)}) %collective-permute-start.17) | collective-permute-done | bytes 331808 | tf_op jit(solution)/shard_map/ppermute | solution.py:425
  61.2 3.6 %collective-permute-done.23.refs_11_ = bf16[2,24,3968]{2,1,0:T(8,128)(2,1)} collective-permute-done((bf16[2,24,3968]{2,1,0:T(8,128)(2,1)S(1)}, bf16[2,24,3968]{2,1,0:T(8,128)(2,1)}, u32[]{:S(2)}, u32[]{:S(2)}) %collective-permute-start.23) | collective-permute-done | bytes 380960 | tf_op jit(solution)/shard_map/ppermute | solution.py:425
  67.4 9.2 %shard_map.248 = (bf16[768,2304]{1,0:T(8,128)(2,1)}, bf16[768,768]{1,0:T(8,128)(2,1)}, bf16[768,768]{1,0:T(8,128)(2,1)}, f32[3,768]{1,0:T(4,128)}, bf16[128,2304...) custom-call(s32[1]{0:T(128)S(6)} %copy.30.refs_0_, ...), custom_call_target="tpu_custom_call" | custom-call | tf_op jit(solution)/shard_map/pallas_call | solution.py:104
  80.1 4.7 %collective-permute-done.31.refs_10_.refs_17_ = bf16[2,24,2304]{2,1,0:T(8,128)(2,1)S(1)} collective-permute-done((bf16[2,24,2304]{2,1,0:T(8,128)(2,1)S(1)}, bf16[2,24,2304]{2,1,0:T(8,128)(2,1)S(1)}, u32[]{:S(2)}, u32[]{:S(2)}) %collective-permute-start.31) | collective-permute-done | bytes 221216 | tf_op jit(solution)/shard_map/ppermute | solution.py:425
  86.8 1.9 %shard_map.249 = (bf16[768,1536]{1,0:T(8,128)(2,1)}, bf16[480,768]{1,0:T(8,128)(2,1)S(1)}) custom-call(bf16[240,768]{1,0:T(8,128)(2,1)S(1)} %bitcast.33, bf16[240,768]{1,0:T(8,128)(2,1)S(1)} %copy-done.11, bf16[3,24,2304]{2,1,0:T(8,128)(2,1)S(1)} %pad_maximum_fusion.4.refs_2_.refs_9_, bf16[3,24,2304]{2,1,0:T(8,128)(2,1)S(1)} %collective-permute-done.27.refs_3_.refs_10_, ...), custom_call_target="tpu_custom_call" | custom-call | tf_op jit(solution)/shard_map/pallas_call | solution.py:104
  93.4 2.4 %collective-permute-done.35.refs_1_ = bf16[128,512]{1,0:T(8,128)(2,1)S(1)} collective-permute-done((bf16[128,512]{1,0:T(8,128)(2,1)S(1)}, bf16[128,512]{1,0:T(8,128)(2,1)S(1)}, u32[]{:S(2)}, u32[]{:S(2)}) %collective-permute-start.35) | collective-permute-done | bytes 131104 | tf_op jit(solution)/shard_map/ppermute | solution.py:425
  95.8 3.7 %collective-permute-done.36.refs_2_ = bf16[128,512]{1,0:T(8,128)(2,1)S(1)} collective-permute-done((bf16[128,512]{1,0:T(8,128)(2,1)S(1)}, bf16[128,512]{1,0:T(8,128)(2,1)S(1)}, u32[]{:S(2)}, u32[]{:S(2)}) %collective-permute-start.36) | collective-permute-done | bytes 131104 | tf_op jit(solution)/shard_map/ppermute | solution.py:425
  102.3 2.5 %shard_map.252 = (bf16[768,768]{1,0:T(8,128)(2,1)}, f32[128,768]{1,0:T(8,128)}, bf16[128,768]{1,0:T(8,128)(2,1)S(1)}, bf16[128,768]{1,0:T(8,128)(2,1)S(1)}, bf16...) custom-call(s32[1]{0:T(128)S(6)} %copy.30.refs_0_, ...), custom_call_target="tpu_custom_call" | custom-call | tf_op jit(solution)/shard_map/pallas_call | solution.py:104
  109.0 1.6 collective-permute-done.40
  110.6 1.9 %collective-permute-done.41 = bf16[128,384]{1,0:T(8,128)(2,1)S(1)} collective-permute-done((bf16[128,384]{1,0:T(8,128)(2,1)}, bf16[128,384]{1,0:T(8,128)(2,1)S(1)}, u32[]{:S(2)}, u32[]{:S(2)}) %collective-permute-start.41) | collective-permute-done | bytes 98336 | tf_op jit(solution)/shard_map/ppermute | solution.py:425
  113.5 2.1 %shard_map.259 = bf16[4,192,768]{2,1,0:T(8,128)(2,1)} custom-call(bf16[128,768]{1,0:T(8,128)(2,1)S(1)} %get-tuple-element.122.refs_0_, bf16[128,768]{1,0:T(8,128)(2,1)S(1)} %get-tuple-element.123.refs_1_, bf16[128,768]{1,0:T(8,128)(2,1)S(1)} %get-tuple-element.124.refs_2_, bf16[128,768]{1,0:T(8,128)(2,1)S(1)} %get-tuple-element.125.refs_3_), custom_call_target="tpu_custom_call" | custom-call | tf_op jit(solution)/shard_map/pallas_call | solution.py:104
  115.7 4.0 %all-to-all-start.2 = ((bf16[4,192,768]{2,1,0:T(8,128)(2,1)}), bf16[4,192,768]{2,1,0:T(8,128)(2,1)S(1)}, u32[]{:S(2)}, u32[]{:S(2)}) async-start(bf16[4,192,768]{2,1,0:T(8,128)(2,1)} %shard_map.259), calls=%async_computation.2 | async-start | bytes 2359296 | tf_op jit(solution)/shard_map/all_to_all | solution.py:434
  122.4 2.2 %shard_map.253 = (f32[128,768]{1,0:T(8,128)S(1)}, bf16[128,768]{1,0:T(8,128)(2,1)S(1)}, bf16[128,384]{1,0:T(8,128)(2,1)S(1)}, bf16[240,768]{1,0:T(8,128)(2,1)S(1...) custom-call(s32[1]{0:T(128)S(6)} %copy.30.refs_0_, s32[1]{0:T(128)S(6)} %copy.31.refs_1_, ...), custom_call_target="tpu_custom_call" | custom-call | tf_op jit(solution)/shard_map/pallas_call | solution.py:104
  138.4 5.4 %shard_map.254 = (bf16[128,768]{1,0:T(8,128)(2,1)S(1)}, bf16[128,2304]{1,0:T(8,128)(2,1)S(1)}, bf16[128,768]{1,0:T(8,128)(2,1)}, f32[16,768]{1,0:T(8,128)S(1)}) custom-call(bf16[128,384]{1,0:T(8,128)(2,1)S(1)} %add_convert_fusion.2.refs_0_.refs_4_, bf16[128,384]{1,0:T(8,128)(2,1)S(1)} %collective-permute-done.47.refs_1_.refs_5_, ...), custom_call_target="tpu_custom_call" | custom-call | tf_op jit(solution)/shard_map/pallas_call | solution.py:104
  145.3 2.7 %shard_map.256 = bf16[4,208,768]{2,1,0:T(8,128)(2,1)} custom-call(bf16[128,384]{1,0:T(8,128)(2,1)S(1)} %copy-done.19, bf16[128,384]{1,0:T(8,128)(2,1)S(1)} %copy-done.28, bf16[128,768]{1,0:T(8,128)(2,1)S(1)} %get-tuple-element.90.refs_2_, bf16[128,768]{1,0:T(8,128)(2,1)S(1)} %copy-done.33, bf16[128,384]{1,0:T(8,128)(2,1)S(1)} %add_convert_fusion.2.refs_0_.refs_4_, ...), custom_call_target="tpu_custom_call" | custom-call | tf_op jit(solution)/shard_map/pallas_call | solution.py:104
  148.1 5.2 %all-to-all-start.1 = ((bf16[4,208,768]{2,1,0:T(8,128)(2,1)}), bf16[4,208,768]{2,1,0:T(8,128)(2,1)S(1)}, u32[]{:S(2)}, u32[]{:S(2)}) async-start(bf16[4,208,768]{2,1,0:T(8,128)(2,1)} %shard_map.256), calls=%async_computation.1 | async-start | bytes 2555904 | tf_op jit(solution)/shard_map/all_to_all | solution.py:434
  156.7 1.8 collective-permute-done.51
  158.9 1.9 %collective-permute-done.53 = bf16[128,384]{1,0:T(8,128)(2,1)S(1)} collective-permute-done((bf16[128,384]{1,0:T(8,128)(2,1)S(1)}, bf16[128,384]{1,0:T(8,128)(2,1)S(1)}, u32[]{:S(2)}, u32[]{:S(2)}) %collective-permute-start.53) | collective-permute-done | bytes 98336 | tf_op jit(solution)/shard_map/ppermute | solution.py:425
  161.0 1.7 copy-done.2
  162.6 2.5 %shard_map.257 = bf16[240,768]{1,0:T(8,128)(2,1)} custom-call(bf16[240,768]{1,0:T(8,128)(2,1)S(1)} %copy-done.14, bf16[240,768]{1,0:T(8,128)(2,1)} %collective-permute-done.55.refs_1_, bf16[768,1536]{1,0:T(8,128)(2,1)S(1)} %copy-done.2), custom_call_target="tpu_custom_call" | custom-call | tf_op jit(solution)/shard_map/pallas_call | solution.py:104
  171.1 1.9 %collective-permute-done.59.refs_3_ = bf16[24,768]{1,0:T(8,128)(2,1)S(1)} collective-permute-done((bf16[24,768]{1,0:T(8,128)(2,1)S(1)}, bf16[24,768]{1,0:T(8,128)(2,1)S(1)}, u32[]{:S(2)}, u32[]{:S(2)}) %collective-permute-start.59) | collective-permute-done | bytes 36896 | tf_op jit(solution)/shard_map/ppermute | solution.py:425
  173.9 8.9 %all-to-all-done.1.refs_0_ = bf16[4,208,768]{2,1,0:T(8,128)(2,1)S(1)} async-done(((bf16[4,208,768]{2,1,0:T(8,128)(2,1)}), bf16[4,208,768]{2,1,0:T(8,128)(2,1)S(1)}, u32[]{:S(2)}, u32[]{:S(2)}) %all-to-all-start.1) | async-done | bytes 1277984 | tf_op jit(solution)/shard_map/all_to_all | solution.py:434
  (257 shorter events, 76.0 us)
Async XLA Ops:
  4.0 18.5 %collective-permute-start = (bf16[24,3968]{1,0:T(8,128)(2,1)S(1)}, bf16[24,3968]{1,0:T(8,128)(2,1)S(1)}, u32[]{:S(2)}, u32[]{:S(2)}) collective-permute-start(bf16[24,3968]{1,0:T(8,128)(2,1)S(1)} %shard_map.247), channel_id=1, source_target_pairs={{0,8},{8,0},{16,24},{24,16},{1,9},{9,1},{17,25},{25,17},{2,10},{10... | collective-permute-start | bytes 571400 | tf_op jit(solution)/shard_map/ppermute | solution.py:430
  7.0 16.9 %collective-permute-start.1 = (bf16[24,3968]{1,0:T(8,128)(2,1)S(1)}, bf16[24,3968]{1,0:T(8,128)(2,1)S(1)}, u32[]{:S(2)}, u32[]{:S(2)}) collective-permute-start(bf16[24,3968]{1,0:T(8,128)(2,1)S(1)} %shard_map.247), channel_id=1, source_target_pairs={{0,16},{8,24},{16,0},{24,8},{1,17},{9,25},{17,1},{25,9},{2,18},{10... | collective-permute-start | bytes 571400 | tf_op jit(solution)/shard_map/ppermute | solution.py:430
  9.6 15.7 %collective-permute-start.2 = (bf16[24,3968]{1,0:T(8,128)(2,1)S(1)}, bf16[24,3968]{1,0:T(8,128)(2,1)S(1)}, u32[]{:S(2)}, u32[]{:S(2)}) collective-permute-start(bf16[24,3968]{1,0:T(8,128)(2,1)S(1)} %shard_map.247), channel_id=1, source_target_pairs={{0,24},{8,16},{16,8},{24,0},{1,25},{9,17},{17,9},{25,1},{2,26},{10... | collective-permute-start | bytes 571400 | tf_op jit(solution)/shard_map/ppermute | solution.py:430
  13.7 7.2 %collective-permute-start.12 = (bf16[24,3968]{1,0:T(8,128)(2,1)S(1)}, bf16[24,3968]{1,0:T(8,128)(2,1)S(1)}, u32[]{:S(2)}, u32[]{:S(2)}) collective-permute-start(bf16[24,3968]{1,0:T(8,128)(2,1)S(1)} %shard_map.247), channel_id=1, source_target_pairs={{0,4},{1,5},{2,6},{3,7},{4,0},{5,1},{6,2},{7,3},{8,12},{9,13},{10,... | collective-permute-start | bytes 571400 | tf_op jit(solution)/shard_map/ppermute | solution.py:425
  15.6 20.7 %collective-permute-start.6 = (bf16[240,768]{1,0:T(8,128)(2,1)S(1)}, bf16[240,768]{1,0:T(8,128)(2,1)S(1)}, u32[]{:S(2)}, u32[]{:S(2)}) collective-permute-start(bf16[240,768]{1,0:T(8,128)(2,1)S(1)} %bitcast.32), channel_id=1, source_target_pairs={{0,1},{1,0},{2,3},{3,2},{4,5},{5,4},{6,7},{7,6},{8,9},{9,8},{10,11... | collective-permute-start | bytes 1105928 | tf_op jit(solution)/shard_map/ppermute | solution.py:425
  26.9 11.9 %collective-permute-start.3 = (bf16[24,2304]{1,0:T(8,128)(2,1)S(1)}, bf16[24,2304]{1,0:T(8,128)(2,1)S(1)}, u32[]{:S(2)}, u32[]{:S(2)}) collective-permute-start(bf16[24,2304]{1,0:T(8,128)(2,1)S(1)} %constant_dynamic-update-slice_fusion), channel_id=1, source_target_pairs={{0,8},{8,0},{16,24},{24,16},{1,9},{9,1},{17,25},{25,17},{2,10},{10... | collective-permute-start | bytes 331784 | tf_op jit(solution)/shard_map/ppermute | solution.py:430
  28.7 10.1 %collective-permute-start.4 = (bf16[24,2304]{1,0:T(8,128)(2,1)S(1)}, bf16[24,2304]{1,0:T(8,128)(2,1)S(1)}, u32[]{:S(2)}, u32[]{:S(2)}) collective-permute-start(bf16[24,2304]{1,0:T(8,128)(2,1)S(1)} %constant_dynamic-update-slice_fusion), channel_id=1, source_target_pairs={{0,16},{8,24},{16,0},{24,8},{1,17},{9,25},{17,1},{25,9},{2,18},{10... | collective-permute-start | bytes 331784 | tf_op jit(solution)/shard_map/ppermute | solution.py:430
  30.0 8.8 %collective-permute-start.5 = (bf16[24,2304]{1,0:T(8,128)(2,1)S(1)}, bf16[24,2304]{1,0:T(8,128)(2,1)S(1)}, u32[]{:S(2)}, u32[]{:S(2)}) collective-permute-start(bf16[24,2304]{1,0:T(8,128)(2,1)S(1)} %constant_dynamic-update-slice_fusion), channel_id=1, source_target_pairs={{0,24},{8,16},{16,8},{24,0},{1,25},{9,17},{17,9},{25,1},{2,26},{10... | collective-permute-start | bytes 331784 | tf_op jit(solution)/shard_map/ppermute | solution.py:430
  37.1 13.1 %collective-permute-start.15 = (bf16[3,24,3968]{2,1,0:T(8,128)(2,1)S(1)}, bf16[3,24,3968]{2,1,0:T(8,128)(2,1)}, u32[]{:S(2)}, u32[]{:S(2)}) collective-permute-start(bf16[3,24,3968]{2,1,0:T(8,128)(2,1)S(1)} %pad_maximum_fusion.refs_5_), channel_id=1, source_target_pairs={{0,2},{1,3},{2,0},{3,1},{4,6},{5,7},{6,4},{7,5},{8,10},{9,11},{10,... | collective-permute-start | bytes 1714184 | tf_op jit(solution)/shard_map/ppermute | solution.py:425
  37.6 12.6 %collective-permute-start.16 = (bf16[3,24,3968]{2,1,0:T(8,128)(2,1)S(1)}, bf16[3,24,3968]{2,1,0:T(8,128)(2,1)}, u32[]{:S(2)}, u32[]{:S(2)}) collective-permute-start(bf16[3,24,3968]{2,1,0:T(8,128)(2,1)S(1)} %pad_maximum_fusion.refs_5_), channel_id=1, source_target_pairs={{0,4},{1,5},{2,6},{3,7},{4,0},{5,1},{6,2},{7,3},{8,12},{9,13},{10,... | collective-permute-start | bytes 1714184 | tf_op jit(solution)/shard_map/ppermute | solution.py:425
  40.0 36.6 %all-to-all-start = ((bf16[4,96,1536]{2,1,0:T(8,128)(2,1)}), bf16[4,96,1536]{2,1,0:T(8,128)(2,1)S(1)}, u32[]{:S(2)}, u32[]{:S(2)}) async-start(bf16[4,96,1536]{2,1,0:T(8,128)(2,1)} %broadcast_in_dim.8), calls=%async_computation | async-start | bytes 2359296 | tf_op jit(solution)/shard_map/all_to_all | solution.py:434
  44.5 11.8 %collective-permute-start.19 = (bf16[3,24,3968]{2,1,0:T(8,128)(2,1)S(1)}, bf16[3,24,3968]{2,1,0:T(8,128)(2,1)S(1)}, u32[]{:S(2)}, u32[]{:S(2)}) collective-permute-start(bf16[3,24,3968]{2,1,0:T(8,128)(2,1)S(1)} %pad_maximum_fusion.1.refs_3_), channel_id=1, source_target_pairs={{0,1},{1,0},{2,3},{3,2},{4,5},{5,4},{6,7},{7,6},{8,9},{9,8},{10,11... | collective-permute-start | bytes 1714184 | tf_op jit(solution)/shard_map/ppermute | solution.py:425
  50.2 10.5 %collective-permute-start.17 = (bf16[3,24,2304]{2,1,0:T(8,128)(2,1)S(1)}, bf16[3,24,2304]{2,1,0:T(8,128)(2,1)S(1)}, u32[]{:S(2)}, u32[]{:S(2)}) collective-permute-start(bf16[3,24,2304]{2,1,0:T(8,128)(2,1)S(1)} %pad_maximum_fusion.3.refs_4_.refs_11_), channel_id=1, source_target_pairs={{0,2},{1,3},{2,0},{3,1},{4,6},{5,7},{6,4},{7,5},{8,10},{9,11},{10,... | collective-permute-start | bytes 995336 | tf_op jit(solution)/shard_map/ppermute | solution.py:425
  51.9 8.8 %collective-permute-start.18 = (bf16[3,24,2304]{2,1,0:T(8,128)(2,1)S(1)}, bf16[3,24,2304]{2,1,0:T(8,128)(2,1)S(1)}, u32[]{:S(2)}, u32[]{:S(2)}) collective-permute-start(bf16[3,24,2304]{2,1,0:T(8,128)(2,1)S(1)} %pad_maximum_fusion.3.refs_4_.refs_11_), channel_id=1, source_target_pairs={{0,4},{1,5},{2,6},{3,7},{4,0},{5,1},{6,2},{7,3},{8,12},{9,13},{10,... | collective-permute-start | bytes 995336 | tf_op jit(solution)/shard_map/ppermute | solution.py:425
  53.7 11.1 %collective-permute-start.23 = (bf16[2,24,3968]{2,1,0:T(8,128)(2,1)S(1)}, bf16[2,24,3968]{2,1,0:T(8,128)(2,1)}, u32[]{:S(2)}, u32[]{:S(2)}) collective-permute-start(bf16[2,24,3968]{2,1,0:T(8,128)(2,1)S(1)} %pad_maximum_fusion.2), channel_id=1, source_target_pairs={{0,4},{1,5},{2,6},{3,7},{4,0},{5,1},{6,2},{7,3},{8,12},{9,13},{10,... | collective-permute-start | bytes 1142792 | tf_op jit(solution)/shard_map/ppermute | solution.py:425
  56.0 8.9 %collective-permute-start.25 = (bf16[2,24,3968]{2,1,0:T(8,128)(2,1)S(1)}, bf16[2,24,3968]{2,1,0:T(8,128)(2,1)}, u32[]{:S(2)}, u32[]{:S(2)}) collective-permute-start(bf16[2,24,3968]{2,1,0:T(8,128)(2,1)S(1)} %slice.33), channel_id=1, source_target_pairs={{0,2},{1,3},{2,0},{3,1},{4,6},{5,7},{6,4},{7,5},{8,10},{9,11},{10,... | collective-permute-start | bytes 1142792 | tf_op jit(solution)/shard_map/ppermute | solution.py:425
  56.4 10.4 %collective-permute-start.20 = (bf16[3,24,3968]{2,1,0:T(8,128)(2,1)S(1)}, bf16[3,24,3968]{2,1,0:T(8,128)(2,1)}, u32[]{:S(2)}, u32[]{:S(2)}) collective-permute-start(bf16[3,24,3968]{2,1,0:T(8,128)(2,1)S(1)} %pad_maximum_fusion.refs_5_), channel_id=1, source_target_pairs={{0,1},{1,0},{2,3},{3,2},{4,5},{5,4},{6,7},{7,6},{8,9},{9,8},{10,11... | collective-permute-start | bytes 1714184 | tf_op jit(solution)/shard_map/ppermute | solution.py:425
  60.7 6.3 %collective-permute-start.21 = (bf16[3,24,3968]{2,1,0:T(8,128)(2,1)}, bf16[3,24,3968]{2,1,0:T(8,128)(2,1)}, u32[]{:S(2)}, u32[]{:S(2)}) collective-permute-start(bf16[3,24,3968]{2,1,0:T(8,128)(2,1)} %collective-permute-done.15.refs_7_), channel_id=1, source_target_pairs={{0,1},{1,0},{2,3},{3,2},{4,5},{5,4},{6,7},{7,6},{8,9},{9,8},{10,11... | collective-permute-start | bytes 1714184 | tf_op jit(solution)/shard_map/ppermute | solution.py:425
  66.8 12.8 %collective-permute-start.28 = (bf16[3,24,2304]{2,1,0:T(8,128)(2,1)S(1)}, bf16[3,24,2304]{2,1,0:T(8,128)(2,1)S(1)}, u32[]{:S(2)}, u32[]{:S(2)}) collective-permute-start(bf16[3,24,2304]{2,1,0:T(8,128)(2,1)S(1)} %pad_maximum_fusion.3.refs_4_.refs_11_), channel_id=1, source_target_pairs={{0,1},{1,0},{2,3},{3,2},{4,5},{5,4},{6,7},{7,6},{8,9},{9,8},{10,11... | collective-permute-start | bytes 995336 | tf_op jit(solution)/shard_map/ppermute | solution.py:425
  76.6 25.7 %collective-permute-start.39 = (bf16[4,96,1536]{2,1,0:T(8,128)(2,1)S(1)}, bf16[4,96,1536]{2,1,0:T(8,128)(2,1)S(1)}, u32[]{:S(2)}, u32[]{:S(2)}) collective-permute-start(bf16[4,96,1536]{2,1,0:T(8,128)(2,1)S(1)} %all-to-all-done.refs_6_), channel_id=1, source_target_pairs={{0,1},{1,0},{2,3},{3,2},{4,5},{5,4},{6,7},{7,6},{8,9},{9,8},{10,11... | collective-permute-start | bytes 3538952 | tf_op jit(solution)/shard_map/ppermute | solution.py:425
  77.3 7.5 %collective-permute-start.31 = (bf16[2,24,2304]{2,1,0:T(8,128)(2,1)S(1)}, bf16[2,24,2304]{2,1,0:T(8,128)(2,1)S(1)}, u32[]{:S(2)}, u32[]{:S(2)}) collective-permute-start(bf16[2,24,2304]{2,1,0:T(8,128)(2,1)S(1)} %pad_maximum_fusion.5), channel_id=1, source_target_pairs={{0,4},{1,5},{2,6},{3,7},{4,0},{5,1},{6,2},{7,3},{8,12},{9,13},{10,... | collective-permute-start | bytes 663560 | tf_op jit(solution)/shard_map/ppermute | solution.py:425
  78.1 7.3 %collective-permute-start.33 = (bf16[2,24,2304]{2,1,0:T(8,128)(2,1)S(1)}, bf16[2,24,2304]{2,1,0:T(8,128)(2,1)S(1)}, u32[]{:S(2)}, u32[]{:S(2)}) collective-permute-start(bf16[2,24,2304]{2,1,0:T(8,128)(2,1)S(1)} %slice.35), channel_id=1, source_target_pairs={{0,2},{1,3},{2,0},{3,1},{4,6},{5,7},{6,4},{7,5},{8,10},{9,11},{10,... | collective-permute-start | bytes 663560 | tf_op jit(solution)/shard_map/ppermute | solution.py:425
  91.4 8.1 %collective-permute-start.36 = (bf16[128,512]{1,0:T(8,128)(2,1)S(1)}, bf16[128,512]{1,0:T(8,128)(2,1)S(1)}, u32[]{:S(2)}, u32[]{:S(2)}) collective-permute-start(bf16[128,512]{1,0:T(8,128)(2,1)S(1)} %shard_map.250.refs_0_), channel_id=1, source_target_pairs={{0,4},{1,5},{2,6},{3,7},{4,0},{5,1},{6,2},{7,3},{8,12},{9,13},{10,... | collective-permute-start | bytes 393224 | tf_op jit(solution)/shard_map/ppermute | solution.py:425
  92.8 6.7 %collective-permute-start.37 = (bf16[128,512]{1,0:T(8,128)(2,1)S(1)}, bf16[128,512]{1,0:T(8,128)(2,1)S(1)}, u32[]{:S(2)}, u32[]{:S(2)}) collective-permute-start(bf16[128,512]{1,0:T(8,128)(2,1)S(1)} %shard_map.250.refs_0_), channel_id=1, source_target_pairs={{0,6},{1,7},{2,4},{3,5},{4,2},{5,3},{6,0},{7,1},{8,14},{9,15},{10,... | collective-permute-start | bytes 393224 | tf_op jit(solution)/shard_map/ppermute | solution.py:425
  115.7 32.4 %all-to-all-start.2 = ((bf16[4,192,768]{2,1,0:T(8,128)(2,1)}), bf16[4,192,768]{2,1,0:T(8,128)(2,1)S(1)}, u32[]{:S(2)}, u32[]{:S(2)}) async-start(bf16[4,192,768]{2,1,0:T(8,128)(2,1)} %shard_map.259), calls=%async_computation.2 | async-start | bytes 2359296 | tf_op jit(solution)/shard_map/all_to_all | solution.py:434
  124.7 6.9 %collective-permute-start.44 = (bf16[128,384]{1,0:T(8,128)(2,1)S(1)}, bf16[128,384]{1,0:T(8,128)(2,1)S(1)}, u32[]{:S(2)}, u32[]{:S(2)}) collective-permute-start(bf16[128,384]{1,0:T(8,128)(2,1)S(1)} %get-tuple-element.92), channel_id=1, source_target_pairs={{0,2},{1,3},{2,0},{3,1},{4,6},{5,7},{6,4},{7,5},{8,10},{9,11},{10,... | collective-permute-start | bytes 294920 | tf_op jit(solution)/shard_map/ppermute | solution.py:425
  125.9 6.9 %collective-permute-start.45 = (bf16[128,384]{1,0:T(8,128)(2,1)S(1)}, bf16[128,384]{1,0:T(8,128)(2,1)S(1)}, u32[]{:S(2)}, u32[]{:S(2)}) collective-permute-start(bf16[128,384]{1,0:T(8,128)(2,1)S(1)} %get-tuple-element.92), channel_id=1, source_target_pairs={{0,4},{1,5},{2,6},{3,7},{4,0},{5,1},{6,2},{7,3},{8,12},{9,13},{10,... | collective-permute-start | bytes 294920 | tf_op jit(solution)/shard_map/ppermute | solution.py:425
  129.2 14.6 %collective-permute-start.48 = (bf16[192,768]{1,0:T(8,128)(2,1)S(1)}, bf16[192,768]{1,0:T(8,128)(2,1)S(1)}, u32[]{:S(2)}, u32[]{:S(2)}) collective-permute-start(bf16[192,768]{1,0:T(8,128)(2,1)S(1)} %get-tuple-element.108), channel_id=1, source_target_pairs={{0,2},{1,3},{2,0},{3,1},{4,6},{5,7},{6,4},{7,5},{8,10},{9,11},{10,... | collective-permute-start | bytes 884744 | tf_op jit(solution)/shard_map/ppermute | solution.py:425
  130.4 14.9 %collective-permute-start.49 = (bf16[192,768]{1,0:T(8,128)(2,1)S(1)}, bf16[192,768]{1,0:T(8,128)(2,1)S(1)}, u32[]{:S(2)}, u32[]{:S(2)}) collective-permute-start(bf16[192,768]{1,0:T(8,128)(2,1)S(1)} %get-tuple-element.109), channel_id=1, source_target_pairs={{0,4},{1,5},{2,6},{3,7},{4,0},{5,1},{6,2},{7,3},{8,12},{9,13},{10,... | collective-permute-start | bytes 884744 | tf_op jit(solution)/shard_map/ppermute | solution.py:425
  131.6 13.7 %collective-permute-start.50 = (bf16[192,768]{1,0:T(8,128)(2,1)S(1)}, bf16[192,768]{1,0:T(8,128)(2,1)S(1)}, u32[]{:S(2)}, u32[]{:S(2)}) collective-permute-start(bf16[192,768]{1,0:T(8,128)(2,1)S(1)} %get-tuple-element.110), channel_id=1, source_target_pairs={{0,6},{1,7},{2,4},{3,5},{4,2},{5,3},{6,0},{7,1},{8,14},{9,15},{10,... | collective-permute-start | bytes 884744 | tf_op jit(solution)/shard_map/ppermute | solution.py:425
  148.1 34.7 %all-to-all-start.1 = ((bf16[4,208,768]{2,1,0:T(8,128)(2,1)}), bf16[4,208,768]{2,1,0:T(8,128)(2,1)S(1)}, u32[]{:S(2)}, u32[]{:S(2)}) async-start(bf16[4,208,768]{2,1,0:T(8,128)(2,1)} %shard_map.256), calls=%async_computation.1 | async-start | bytes 2555904 | tf_op jit(solution)/shard_map/all_to_all | solution.py:434
  160.9 8.8 %collective-permute-start.54 = (bf16[128,384]{1,0:T(8,128)(2,1)S(1)}, bf16[128,384]{1,0:T(8,128)(2,1)S(1)}, u32[]{:S(2)}, u32[]{:S(2)}) collective-permute-start(bf16[128,384]{1,0:T(8,128)(2,1)S(1)} %add_convert_fusion.1), channel_id=1, source_target_pairs={{0,1},{1,0},{2,3},{3,2},{4,5},{5,4},{6,7},{7,6},{8,9},{9,8},{10,11... | collective-permute-start | bytes 294920 | tf_op jit(solution)/shard_map/ppermute | solution.py:425
  (90 other events, 673.0 us)

commit v7 on v6

--- a/solution.py
+++ b/solution.py
@@ -1221,7 +1221,7 @@
             x2,
             gains,
             cot,
-            cross_out,
+            (cross_out, (width, width), (0, 0)),
             cq,
             memory,
             visible,
@@ -1252,15 +1252,15 @@
         ],
         [
             here,
-            grad_cq,
-            cq_other,
+            (grad_cq, (rows, half), (0, 0)),
+            (cq_other, (rows, half), (0, 0)),
             (cross_in, (width, width), (0, 0)),
             x1,
             gains,
             dx2,
             (self_out, (width, width), (0, 0)),
             (p1, (rows, 3 * width), (0, 0)),
-            probs,
+            (probs, (heads // 2, 2 * rows, rows), (0, 0, 0)),
             x,
             (proj, (width, 3 * width), (0, 0)),
             gain_grad,

time: 187 us -> 187 us (level)
  no operation moved by 1% of the time
where the time goes in v7:
time: 187 us; the launch traced here: 186 us
  starting transfers between devices  65.8 us (35%)
  waiting for transfers between devices  62.6 us (33%)
  Pallas kernels  34.5 us (18%)
  local copies, waits for them, and re-layouts  17.5 us (9%)
  between operations  2.69 us (1%)
  other arithmetic  1.98 us (1%)
    ppermute x54, waiting for transfers between devices, swap_ctx(): return lax.ppermute(values, 'ctx', [(i, i ^ mask) for i in range(size)])  53.7 us
    ppermute x54, starting transfers between devices, swap_ctx(): return lax.ppermute(values, 'ctx', [(i, i ^ mask) for i in range(size)])  42 us
    pallas_call x15, Pallas kernels, call(): pl.pallas_call(run, grid=grid, out_shape=[pltpu.HBM(*out[:2]) if len(out)...  34.5 us
    all_to_all x3, starting transfers between devices, exchange(): return lax.all_to_all(values, axis, 0, 0, tiled=True)  13.5 us
    unnamed x119, local copies, waits for them, and re-layouts  12.9 us
    ppermute x6, starting transfers between devices, swap_pb(): return lax.ppermute(values, 'pb', [(i, i ^ mask) for i in range(size)])  10.2 us
    all_to_all x3, waiting for transfers between devices, exchange(): return lax.all_to_all(values, axis, 0, 0, tiled=True)  8.89 us
  transfers between devices with their start and end apart: 63, of which 30 were waited for; matrix products, arithmetic and copies ran while one was open for 4% of the time, Pallas kernels for 15%

profile of v7, /device:TPU:0, one launch (start us, length us, event | category | flops | bytes accessed | tf_op | source)
XLA Modules:
  0.0 185.9 jit_solution(2962352277671619288)
XLA Ops:
  4.0 3.0 %collective-permute-start = (bf16[24,3968]{1,0:T(8,128)(2,1)S(1)}, bf16[24,3968]{1,0:T(8,128)(2,1)S(1)}, u32[]{:S(2)}, u32[]{:S(2)}) collective-permute-start(bf16[24,3968]{1,0:T(8,128)(2,1)S(1)} %shard_map.247), channel_id=1, source_target_pairs={{0,8},{8,0},{16,24},{24,16},{1,9},{9,1},{17,25},{25,17},{2,10},{10... | collective-permute-start | bytes 571400 | tf_op jit(solution)/shard_map/ppermute | solution.py:430
  7.0 2.6 %collective-permute-start.1 = (bf16[24,3968]{1,0:T(8,128)(2,1)S(1)}, bf16[24,3968]{1,0:T(8,128)(2,1)S(1)}, u32[]{:S(2)}, u32[]{:S(2)}) collective-permute-start(bf16[24,3968]{1,0:T(8,128)(2,1)S(1)} %shard_map.247), channel_id=1, source_target_pairs={{0,16},{8,24},{16,0},{24,8},{1,17},{9,25},{17,1},{25,9},{2,18},{10... | collective-permute-start | bytes 571400 | tf_op jit(solution)/shard_map/ppermute | solution.py:430
  9.6 1.7 collective-permute-start.11
  13.7 1.6 collective-permute-start.12
  15.7 5.3 %collective-permute-done.12 = bf16[24,3968]{1,0:T(8,128)(2,1)S(1)} collective-permute-done((bf16[24,3968]{1,0:T(8,128)(2,1)S(1)}, bf16[24,3968]{1,0:T(8,128)(2,1)S(1)}, u32[]{:S(2)}, u32[]{:S(2)}) %collective-permute-start.12) | collective-permute-done | bytes 190496 | tf_op jit(solution)/shard_map/ppermute | solution.py:425
  26.9 1.8 collective-permute-start.3
  32.8 3.5 %collective-permute-done.14 = bf16[24,2304]{1,0:T(8,128)(2,1)S(1)} collective-permute-done((bf16[24,2304]{1,0:T(8,128)(2,1)S(1)}, bf16[24,2304]{1,0:T(8,128)(2,1)S(1)}, u32[]{:S(2)}, u32[]{:S(2)}) %collective-permute-start.14) | collective-permute-done | bytes 110624 | tf_op jit(solution)/shard_map/ppermute | solution.py:425
  40.0 4.4 %all-to-all-start = ((bf16[4,96,1536]{2,1,0:T(8,128)(2,1)}), bf16[4,96,1536]{2,1,0:T(8,128)(2,1)S(1)}, u32[]{:S(2)}, u32[]{:S(2)}) async-start(bf16[4,96,1536]{2,1,0:T(8,128)(2,1)} %broadcast_in_dim.8), calls=%async_computation | async-start | bytes 2359296 | tf_op jit(solution)/shard_map/all_to_all | solution.py:434
  44.6 5.6 %collective-permute-done.15.refs_7_ = bf16[3,24,3968]{2,1,0:T(8,128)(2,1)} collective-permute-done((bf16[3,24,3968]{2,1,0:T(8,128)(2,1)S(1)}, bf16[3,24,3968]{2,1,0:T(8,128)(2,1)}, u32[]{:S(2)}, u32[]{:S(2)}) %collective-permute-start.15) | collective-permute-done | bytes 571424 | tf_op jit(solution)/shard_map/ppermute | solution.py:425
  50.2 1.7 collective-permute-start.17
  56.4 4.2 %collective-permute-done.17.refs_6_.refs_13_ = bf16[3,24,2304]{2,1,0:T(8,128)(2,1)S(1)} collective-permute-done((bf16[3,24,2304]{2,1,0:T(8,128)(2,1)S(1)}, bf16[3,24,2304]{2,1,0:T(8,128)(2,1)S(1)}, u32[]{:S(2)}, u32[]{:S(2)}) %collective-permute-start.17) | collective-permute-done | bytes 331808 | tf_op jit(solution)/shard_map/ppermute | solution.py:425
  61.2 3.6 %collective-permute-done.23.refs_11_ = bf16[2,24,3968]{2,1,0:T(8,128)(2,1)} collective-permute-done((bf16[2,24,3968]{2,1,0:T(8,128)(2,1)S(1)}, bf16[2,24,3968]{2,1,0:T(8,128)(2,1)}, u32[]{:S(2)}, u32[]{:S(2)}) %collective-permute-start.23) | collective-permute-done | bytes 380960 | tf_op jit(solution)/shard_map/ppermute | solution.py:425
  67.4 9.2 %shard_map.248 = (bf16[768,2304]{1,0:T(8,128)(2,1)}, bf16[768,768]{1,0:T(8,128)(2,1)}, bf16[768,768]{1,0:T(8,128)(2,1)}, f32[3,768]{1,0:T(4,128)}, bf16[128,2304...) custom-call(s32[1]{0:T(128)S(6)} %copy.30.refs_0_, ...), custom_call_target="tpu_custom_call" | custom-call | tf_op jit(solution)/shard_map/pallas_call | solution.py:104
  80.1 4.7 %collective-permute-done.31.refs_10_.refs_17_ = bf16[2,24,2304]{2,1,0:T(8,128)(2,1)S(1)} collective-permute-done((bf16[2,24,2304]{2,1,0:T(8,128)(2,1)S(1)}, bf16[2,24,2304]{2,1,0:T(8,128)(2,1)S(1)}, u32[]{:S(2)}, u32[]{:S(2)}) %collective-permute-start.31) | collective-permute-done | bytes 221216 | tf_op jit(solution)/shard_map/ppermute | solution.py:425
  86.8 1.9 %shard_map.249 = (bf16[768,1536]{1,0:T(8,128)(2,1)}, bf16[480,768]{1,0:T(8,128)(2,1)S(1)}) custom-call(bf16[240,768]{1,0:T(8,128)(2,1)S(1)} %bitcast.33, bf16[240,768]{1,0:T(8,128)(2,1)S(1)} %copy-done.11, bf16[3,24,2304]{2,1,0:T(8,128)(2,1)S(1)} %pad_maximum_fusion.4.refs_2_.refs_9_, bf16[3,24,2304]{2,1,0:T(8,128)(2,1)S(1)} %collective-permute-done.27.refs_3_.refs_10_, ...), custom_call_target="tpu_custom_call" | custom-call | tf_op jit(solution)/shard_map/pallas_call | solution.py:104
  93.4 2.4 %collective-permute-done.35.refs_1_ = bf16[128,512]{1,0:T(8,128)(2,1)S(1)} collective-permute-done((bf16[128,512]{1,0:T(8,128)(2,1)S(1)}, bf16[128,512]{1,0:T(8,128)(2,1)S(1)}, u32[]{:S(2)}, u32[]{:S(2)}) %collective-permute-start.35) | collective-permute-done | bytes 131104 | tf_op jit(solution)/shard_map/ppermute | solution.py:425
  95.8 3.7 %collective-permute-done.36.refs_2_ = bf16[128,512]{1,0:T(8,128)(2,1)S(1)} collective-permute-done((bf16[128,512]{1,0:T(8,128)(2,1)S(1)}, bf16[128,512]{1,0:T(8,128)(2,1)S(1)}, u32[]{:S(2)}, u32[]{:S(2)}) %collective-permute-start.36) | collective-permute-done | bytes 131104 | tf_op jit(solution)/shard_map/ppermute | solution.py:425
  102.3 2.5 %shard_map.252 = (bf16[768,768]{1,0:T(8,128)(2,1)}, f32[128,768]{1,0:T(8,128)}, bf16[128,768]{1,0:T(8,128)(2,1)S(1)}, bf16[128,768]{1,0:T(8,128)(2,1)S(1)}, bf16...) custom-call(s32[1]{0:T(128)S(6)} %copy.30.refs_0_, ...), custom_call_target="tpu_custom_call" | custom-call | tf_op jit(solution)/shard_map/pallas_call | solution.py:104
  109.0 1.6 collective-permute-done.40
  110.6 1.9 %collective-permute-done.41 = bf16[128,384]{1,0:T(8,128)(2,1)S(1)} collective-permute-done((bf16[128,384]{1,0:T(8,128)(2,1)}, bf16[128,384]{1,0:T(8,128)(2,1)S(1)}, u32[]{:S(2)}, u32[]{:S(2)}) %collective-permute-start.41) | collective-permute-done | bytes 98336 | tf_op jit(solution)/shard_map/ppermute | solution.py:425
  113.5 2.1 %shard_map.259 = bf16[4,192,768]{2,1,0:T(8,128)(2,1)} custom-call(bf16[128,768]{1,0:T(8,128)(2,1)S(1)} %get-tuple-element.122.refs_0_, bf16[128,768]{1,0:T(8,128)(2,1)S(1)} %get-tuple-element.123.refs_1_, bf16[128,768]{1,0:T(8,128)(2,1)S(1)} %get-tuple-element.124.refs_2_, bf16[128,768]{1,0:T(8,128)(2,1)S(1)} %get-tuple-element.125.refs_3_), custom_call_target="tpu_custom_call" | custom-call | tf_op jit(solution)/shard_map/pallas_call | solution.py:104
  115.7 4.0 %all-to-all-start.2 = ((bf16[4,192,768]{2,1,0:T(8,128)(2,1)}), bf16[4,192,768]{2,1,0:T(8,128)(2,1)S(1)}, u32[]{:S(2)}, u32[]{:S(2)}) async-start(bf16[4,192,768]{2,1,0:T(8,128)(2,1)} %shard_map.259), calls=%async_computation.2 | async-start | bytes 2359296 | tf_op jit(solution)/shard_map/all_to_all | solution.py:434
  122.4 2.2 %shard_map.253 = (f32[128,768]{1,0:T(8,128)S(1)}, bf16[128,768]{1,0:T(8,128)(2,1)S(1)}, bf16[128,384]{1,0:T(8,128)(2,1)S(1)}, bf16[240,768]{1,0:T(8,128)(2,1)S(1...) custom-call(s32[1]{0:T(128)S(6)} %copy.30.refs_0_, s32[1]{0:T(128)S(6)} %copy.31.refs_1_, ...), custom_call_target="tpu_custom_call" | custom-call | tf_op jit(solution)/shard_map/pallas_call | solution.py:104
  138.4 5.4 %shard_map.254 = (bf16[128,768]{1,0:T(8,128)(2,1)S(1)}, bf16[128,2304]{1,0:T(8,128)(2,1)S(1)}, bf16[128,768]{1,0:T(8,128)(2,1)}, f32[16,768]{1,0:T(8,128)S(1)}) custom-call(bf16[128,384]{1,0:T(8,128)(2,1)S(1)} %add_convert_fusion.2.refs_0_.refs_4_, bf16[128,384]{1,0:T(8,128)(2,1)S(1)} %collective-permute-done.47.refs_1_.refs_5_, ...), custom_call_target="tpu_custom_call" | custom-call | tf_op jit(solution)/shard_map/pallas_call | solution.py:104
  145.3 2.7 %shard_map.256 = bf16[4,208,768]{2,1,0:T(8,128)(2,1)} custom-call(bf16[128,384]{1,0:T(8,128)(2,1)S(1)} %copy-done.19, bf16[128,384]{1,0:T(8,128)(2,1)S(1)} %copy-done.28, bf16[128,768]{1,0:T(8,128)(2,1)S(1)} %get-tuple-element.90.refs_2_, bf16[128,768]{1,0:T(8,128)(2,1)S(1)} %copy-done.33, bf16[128,384]{1,0:T(8,128)(2,1)S(1)} %add_convert_fusion.2.refs_0_.refs_4_, ...), custom_call_target="tpu_custom_call" | custom-call | tf_op jit(solution)/shard_map/pallas_call | solution.py:104
  148.1 5.2 %all-to-all-start.1 = ((bf16[4,208,768]{2,1,0:T(8,128)(2,1)}), bf16[4,208,768]{2,1,0:T(8,128)(2,1)S(1)}, u32[]{:S(2)}, u32[]{:S(2)}) async-start(bf16[4,208,768]{2,1,0:T(8,128)(2,1)} %shard_map.256), calls=%async_computation.1 | async-start | bytes 2555904 | tf_op jit(solution)/shard_map/all_to_all | solution.py:434
  156.7 1.8 collective-permute-done.51
  158.9 1.9 %collective-permute-done.53 = bf16[128,384]{1,0:T(8,128)(2,1)S(1)} collective-permute-done((bf16[128,384]{1,0:T(8,128)(2,1)S(1)}, bf16[128,384]{1,0:T(8,128)(2,1)S(1)}, u32[]{:S(2)}, u32[]{:S(2)}) %collective-permute-start.53) | collective-permute-done | bytes 98336 | tf_op jit(solution)/shard_map/ppermute | solution.py:425
  161.0 1.7 copy-done.2
  162.6 2.5 %shard_map.257 = bf16[240,768]{1,0:T(8,128)(2,1)} custom-call(bf16[240,768]{1,0:T(8,128)(2,1)S(1)} %copy-done.14, bf16[240,768]{1,0:T(8,128)(2,1)} %collective-permute-done.55.refs_1_, bf16[768,1536]{1,0:T(8,128)(2,1)S(1)} %copy-done.2), custom_call_target="tpu_custom_call" | custom-call | tf_op jit(solution)/shard_map/pallas_call | solution.py:104
  171.1 1.9 %collective-permute-done.59.refs_3_ = bf16[24,768]{1,0:T(8,128)(2,1)S(1)} collective-permute-done((bf16[24,768]{1,0:T(8,128)(2,1)S(1)}, bf16[24,768]{1,0:T(8,128)(2,1)S(1)}, u32[]{:S(2)}, u32[]{:S(2)}) %collective-permute-start.59) | collective-permute-done | bytes 36896 | tf_op jit(solution)/shard_map/ppermute | solution.py:425
  173.9 8.9 %all-to-all-done.1.refs_0_ = bf16[4,208,768]{2,1,0:T(8,128)(2,1)S(1)} async-done(((bf16[4,208,768]{2,1,0:T(8,128)(2,1)}), bf16[4,208,768]{2,1,0:T(8,128)(2,1)S(1)}, u32[]{:S(2)}, u32[]{:S(2)}) %all-to-all-start.1) | async-done | bytes 1277984 | tf_op jit(solution)/shard_map/all_to_all | solution.py:434
  (257 shorter events, 76.0 us)
Async XLA Ops:
  4.0 18.5 %collective-permute-start = (bf16[24,3968]{1,0:T(8,128)(2,1)S(1)}, bf16[24,3968]{1,0:T(8,128)(2,1)S(1)}, u32[]{:S(2)}, u32[]{:S(2)}) collective-permute-start(bf16[24,3968]{1,0:T(8,128)(2,1)S(1)} %shard_map.247), channel_id=1, source_target_pairs={{0,8},{8,0},{16,24},{24,16},{1,9},{9,1},{17,25},{25,17},{2,10},{10... | collective-permute-start | bytes 571400 | tf_op jit(solution)/shard_map/ppermute | solution.py:430
  7.0 16.9 %collective-permute-start.1 = (bf16[24,3968]{1,0:T(8,128)(2,1)S(1)}, bf16[24,3968]{1,0:T(8,128)(2,1)S(1)}, u32[]{:S(2)}, u32[]{:S(2)}) collective-permute-start(bf16[24,3968]{1,0:T(8,128)(2,1)S(1)} %shard_map.247), channel_id=1, source_target_pairs={{0,16},{8,24},{16,0},{24,8},{1,17},{9,25},{17,1},{25,9},{2,18},{10... | collective-permute-start | bytes 571400 | tf_op jit(solution)/shard_map/ppermute | solution.py:430
  9.6 15.7 %collective-permute-start.2 = (bf16[24,3968]{1,0:T(8,128)(2,1)S(1)}, bf16[24,3968]{1,0:T(8,128)(2,1)S(1)}, u32[]{:S(2)}, u32[]{:S(2)}) collective-permute-start(bf16[24,3968]{1,0:T(8,128)(2,1)S(1)} %shard_map.247), channel_id=1, source_target_pairs={{0,24},{8,16},{16,8},{24,0},{1,25},{9,17},{17,9},{25,1},{2,26},{10... | collective-permute-start | bytes 571400 | tf_op jit(solution)/shard_map/ppermute | solution.py:430
  13.7 7.2 %collective-permute-start.12 = (bf16[24,3968]{1,0:T(8,128)(2,1)S(1)}, bf16[24,3968]{1,0:T(8,128)(2,1)S(1)}, u32[]{:S(2)}, u32[]{:S(2)}) collective-permute-start(bf16[24,3968]{1,0:T(8,128)(2,1)S(1)} %shard_map.247), channel_id=1, source_target_pairs={{0,4},{1,5},{2,6},{3,7},{4,0},{5,1},{6,2},{7,3},{8,12},{9,13},{10,... | collective-permute-start | bytes 571400 | tf_op jit(solution)/shard_map/ppermute | solution.py:425
  15.6 20.7 %collective-permute-start.6 = (bf16[240,768]{1,0:T(8,128)(2,1)S(1)}, bf16[240,768]{1,0:T(8,128)(2,1)S(1)}, u32[]{:S(2)}, u32[]{:S(2)}) collective-permute-start(bf16[240,768]{1,0:T(8,128)(2,1)S(1)} %bitcast.32), channel_id=1, source_target_pairs={{0,1},{1,0},{2,3},{3,2},{4,5},{5,4},{6,7},{7,6},{8,9},{9,8},{10,11... | collective-permute-start | bytes 1105928 | tf_op jit(solution)/shard_map/ppermute | solution.py:425
  26.9 11.9 %collective-permute-start.3 = (bf16[24,2304]{1,0:T(8,128)(2,1)S(1)}, bf16[24,2304]{1,0:T(8,128)(2,1)S(1)}, u32[]{:S(2)}, u32[]{:S(2)}) collective-permute-start(bf16[24,2304]{1,0:T(8,128)(2,1)S(1)} %constant_dynamic-update-slice_fusion), channel_id=1, source_target_pairs={{0,8},{8,0},{16,24},{24,16},{1,9},{9,1},{17,25},{25,17},{2,10},{10... | collective-permute-start | bytes 331784 | tf_op jit(solution)/shard_map/ppermute | solution.py:430
  28.7 10.1 %collective-permute-start.4 = (bf16[24,2304]{1,0:T(8,128)(2,1)S(1)}, bf16[24,2304]{1,0:T(8,128)(2,1)S(1)}, u32[]{:S(2)}, u32[]{:S(2)}) collective-permute-start(bf16[24,2304]{1,0:T(8,128)(2,1)S(1)} %constant_dynamic-update-slice_fusion), channel_id=1, source_target_pairs={{0,16},{8,24},{16,0},{24,8},{1,17},{9,25},{17,1},{25,9},{2,18},{10... | collective-permute-start | bytes 331784 | tf_op jit(solution)/shard_map/ppermute | solution.py:430
  30.0 8.8 %collective-permute-start.5 = (bf16[24,2304]{1,0:T(8,128)(2,1)S(1)}, bf16[24,2304]{1,0:T(8,128)(2,1)S(1)}, u32[]{:S(2)}, u32[]{:S(2)}) collective-permute-start(bf16[24,2304]{1,0:T(8,128)(2,1)S(1)} %constant_dynamic-update-slice_fusion), channel_id=1, source_target_pairs={{0,24},{8,16},{16,8},{24,0},{1,25},{9,17},{17,9},{25,1},{2,26},{10... | collective-permute-start | bytes 331784 | tf_op jit(solution)/shard_map/ppermute | solution.py:430
  37.1 13.1 %collective-permute-start.15 = (bf16[3,24,3968]{2,1,0:T(8,128)(2,1)S(1)}, bf16[3,24,3968]{2,1,0:T(8,128)(2,1)}, u32[]{:S(2)}, u32[]{:S(2)}) collective-permute-start(bf16[3,24,3968]{2,1,0:T(8,128)(2,1)S(1)} %pad_maximum_fusion.refs_5_), channel_id=1, source_target_pairs={{0,2},{1,3},{2,0},{3,1},{4,6},{5,7},{6,4},{7,5},{8,10},{9,11},{10,... | collective-permute-start | bytes 1714184 | tf_op jit(solution)/shard_map/ppermute | solution.py:425
  37.6 12.6 %collective-permute-start.16 = (bf16[3,24,3968]{2,1,0:T(8,128)(2,1)S(1)}, bf16[3,24,3968]{2,1,0:T(8,128)(2,1)}, u32[]{:S(2)}, u32[]{:S(2)}) collective-permute-start(bf16[3,24,3968]{2,1,0:T(8,128)(2,1)S(1)} %pad_maximum_fusion.refs_5_), channel_id=1, source_target_pairs={{0,4},{1,5},{2,6},{3,7},{4,0},{5,1},{6,2},{7,3},{8,12},{9,13},{10,... | collective-permute-start | bytes 1714184 | tf_op jit(solution)/shard_map/ppermute | solution.py:425
  40.0 36.6 %all-to-all-start = ((bf16[4,96,1536]{2,1,0:T(8,128)(2,1)}), bf16[4,96,1536]{2,1,0:T(8,128)(2,1)S(1)}, u32[]{:S(2)}, u32[]{:S(2)}) async-start(bf16[4,96,1536]{2,1,0:T(8,128)(2,1)} %broadcast_in_dim.8), calls=%async_computation | async-start | bytes 2359296 | tf_op jit(solution)/shard_map/all_to_all | solution.py:434
  44.5 11.8 %collective-permute-start.19 = (bf16[3,24,3968]{2,1,0:T(8,128)(2,1)S(1)}, bf16[3,24,3968]{2,1,0:T(8,128)(2,1)S(1)}, u32[]{:S(2)}, u32[]{:S(2)}) collective-permute-start(bf16[3,24,3968]{2,1,0:T(8,128)(2,1)S(1)} %pad_maximum_fusion.1.refs_3_), channel_id=1, source_target_pairs={{0,1},{1,0},{2,3},{3,2},{4,5},{5,4},{6,7},{7,6},{8,9},{9,8},{10,11... | collective-permute-start | bytes 1714184 | tf_op jit(solution)/shard_map/ppermute | solution.py:425
  50.2 10.5 %collective-permute-start.17 = (bf16[3,24,2304]{2,1,0:T(8,128)(2,1)S(1)}, bf16[3,24,2304]{2,1,0:T(8,128)(2,1)S(1)}, u32[]{:S(2)}, u32[]{:S(2)}) collective-permute-start(bf16[3,24,2304]{2,1,0:T(8,128)(2,1)S(1)} %pad_maximum_fusion.3.refs_4_.refs_11_), channel_id=1, source_target_pairs={{0,2},{1,3},{2,0},{3,1},{4,6},{5,7},{6,4},{7,5},{8,10},{9,11},{10,... | collective-permute-start | bytes 995336 | tf_op jit(solution)/shard_map/ppermute | solution.py:425
  51.9 8.8 %collective-permute-start.18 = (bf16[3,24,2304]{2,1,0:T(8,128)(2,1)S(1)}, bf16[3,24,2304]{2,1,0:T(8,128)(2,1)S(1)}, u32[]{:S(2)}, u32[]{:S(2)}) collective-permute-start(bf16[3,24,2304]{2,1,0:T(8,128)(2,1)S(1)} %pad_maximum_fusion.3.refs_4_.refs_11_), channel_id=1, source_target_pairs={{0,4},{1,5},{2,6},{3,7},{4,0},{5,1},{6,2},{7,3},{8,12},{9,13},{10,... | collective-permute-start | bytes 995336 | tf_op jit(solution)/shard_map/ppermute | solution.py:425
  53.7 11.1 %collective-permute-start.23 = (bf16[2,24,3968]{2,1,0:T(8,128)(2,1)S(1)}, bf16[2,24,3968]{2,1,0:T(8,128)(2,1)}, u32[]{:S(2)}, u32[]{:S(2)}) collective-permute-start(bf16[2,24,3968]{2,1,0:T(8,128)(2,1)S(1)} %pad_maximum_fusion.2), channel_id=1, source_target_pairs={{0,4},{1,5},{2,6},{3,7},{4,0},{5,1},{6,2},{7,3},{8,12},{9,13},{10,... | collective-permute-start | bytes 1142792 | tf_op jit(solution)/shard_map/ppermute | solution.py:425
  56.0 8.9 %collective-permute-start.25 = (bf16[2,24,3968]{2,1,0:T(8,128)(2,1)S(1)}, bf16[2,24,3968]{2,1,0:T(8,128)(2,1)}, u32[]{:S(2)}, u32[]{:S(2)}) collective-permute-start(bf16[2,24,3968]{2,1,0:T(8,128)(2,1)S(1)} %slice.33), channel_id=1, source_target_pairs={{0,2},{1,3},{2,0},{3,1},{4,6},{5,7},{6,4},{7,5},{8,10},{9,11},{10,... | collective-permute-start | bytes 1142792 | tf_op jit(solution)/shard_map/ppermute | solution.py:425
  56.4 10.4 %collective-permute-start.20 = (bf16[3,24,3968]{2,1,0:T(8,128)(2,1)S(1)}, bf16[3,24,3968]{2,1,0:T(8,128)(2,1)}, u32[]{:S(2)}, u32[]{:S(2)}) collective-permute-start(bf16[3,24,3968]{2,1,0:T(8,128)(2,1)S(1)} %pad_maximum_fusion.refs_5_), channel_id=1, source_target_pairs={{0,1},{1,0},{2,3},{3,2},{4,5},{5,4},{6,7},{7,6},{8,9},{9,8},{10,11... | collective-permute-start | bytes 1714184 | tf_op jit(solution)/shard_map/ppermute | solution.py:425
  60.7 6.3 %collective-permute-start.21 = (bf16[3,24,3968]{2,1,0:T(8,128)(2,1)}, bf16[3,24,3968]{2,1,0:T(8,128)(2,1)}, u32[]{:S(2)}, u32[]{:S(2)}) collective-permute-start(bf16[3,24,3968]{2,1,0:T(8,128)(2,1)} %collective-permute-done.15.refs_7_), channel_id=1, source_target_pairs={{0,1},{1,0},{2,3},{3,2},{4,5},{5,4},{6,7},{7,6},{8,9},{9,8},{10,11... | collective-permute-start | bytes 1714184 | tf_op jit(solution)/shard_map/ppermute | solution.py:425
  66.8 12.8 %collective-permute-start.28 = (bf16[3,24,2304]{2,1,0:T(8,128)(2,1)S(1)}, bf16[3,24,2304]{2,1,0:T(8,128)(2,1)S(1)}, u32[]{:S(2)}, u32[]{:S(2)}) collective-permute-start(bf16[3,24,2304]{2,1,0:T(8,128)(2,1)S(1)} %pad_maximum_fusion.3.refs_4_.refs_11_), channel_id=1, source_target_pairs={{0,1},{1,0},{2,3},{3,2},{4,5},{5,4},{6,7},{7,6},{8,9},{9,8},{10,11... | collective-permute-start | bytes 995336 | tf_op jit(solution)/shard_map/ppermute | solution.py:425
  76.6 25.7 %collective-permute-start.39 = (bf16[4,96,1536]{2,1,0:T(8,128)(2,1)S(1)}, bf16[4,96,1536]{2,1,0:T(8,128)(2,1)S(1)}, u32[]{:S(2)}, u32[]{:S(2)}) collective-permute-start(bf16[4,96,1536]{2,1,0:T(8,128)(2,1)S(1)} %all-to-all-done.refs_6_), channel_id=1, source_target_pairs={{0,1},{1,0},{2,3},{3,2},{4,5},{5,4},{6,7},{7,6},{8,9},{9,8},{10,11... | collective-permute-start | bytes 3538952 | tf_op jit(solution)/shard_map/ppermute | solution.py:425
  77.3 7.5 %collective-permute-start.31 = (bf16[2,24,2304]{2,1,0:T(8,128)(2,1)S(1)}, bf16[2,24,2304]{2,1,0:T(8,128)(2,1)S(1)}, u32[]{:S(2)}, u32[]{:S(2)}) collective-permute-start(bf16[2,24,2304]{2,1,0:T(8,128)(2,1)S(1)} %pad_maximum_fusion.5), channel_id=1, source_target_pairs={{0,4},{1,5},{2,6},{3,7},{4,0},{5,1},{6,2},{7,3},{8,12},{9,13},{10,... | collective-permute-start | bytes 663560 | tf_op jit(solution)/shard_map/ppermute | solution.py:425
  78.1 7.3 %collective-permute-start.33 = (bf16[2,24,2304]{2,1,0:T(8,128)(2,1)S(1)}, bf16[2,24,2304]{2,1,0:T(8,128)(2,1)S(1)}, u32[]{:S(2)}, u32[]{:S(2)}) collective-permute-start(bf16[2,24,2304]{2,1,0:T(8,128)(2,1)S(1)} %slice.35), channel_id=1, source_target_pairs={{0,2},{1,3},{2,0},{3,1},{4,6},{5,7},{6,4},{7,5},{8,10},{9,11},{10,... | collective-permute-start | bytes 663560 | tf_op jit(solution)/shard_map/ppermute | solution.py:425
  91.4 8.1 %collective-permute-start.36 = (bf16[128,512]{1,0:T(8,128)(2,1)S(1)}, bf16[128,512]{1,0:T(8,128)(2,1)S(1)}, u32[]{:S(2)}, u32[]{:S(2)}) collective-permute-start(bf16[128,512]{1,0:T(8,128)(2,1)S(1)} %shard_map.250.refs_0_), channel_id=1, source_target_pairs={{0,4},{1,5},{2,6},{3,7},{4,0},{5,1},{6,2},{7,3},{8,12},{9,13},{10,... | collective-permute-start | bytes 393224 | tf_op jit(solution)/shard_map/ppermute | solution.py:425
  92.8 6.7 %collective-permute-start.37 = (bf16[128,512]{1,0:T(8,128)(2,1)S(1)}, bf16[128,512]{1,0:T(8,128)(2,1)S(1)}, u32[]{:S(2)}, u32[]{:S(2)}) collective-permute-start(bf16[128,512]{1,0:T(8,128)(2,1)S(1)} %shard_map.250.refs_0_), channel_id=1, source_target_pairs={{0,6},{1,7},{2,4},{3,5},{4,2},{5,3},{6,0},{7,1},{8,14},{9,15},{10,... | collective-permute-start | bytes 393224 | tf_op jit(solution)/shard_map/ppermute | solution.py:425
  115.7 32.4 %all-to-all-start.2 = ((bf16[4,192,768]{2,1,0:T(8,128)(2,1)}), bf16[4,192,768]{2,1,0:T(8,128)(2,1)S(1)}, u32[]{:S(2)}, u32[]{:S(2)}) async-start(bf16[4,192,768]{2,1,0:T(8,128)(2,1)} %shard_map.259), calls=%async_computation.2 | async-start | bytes 2359296 | tf_op jit(solution)/shard_map/all_to_all | solution.py:434
  124.7 6.9 %collective-permute-start.44 = (bf16[128,384]{1,0:T(8,128)(2,1)S(1)}, bf16[128,384]{1,0:T(8,128)(2,1)S(1)}, u32[]{:S(2)}, u32[]{:S(2)}) collective-permute-start(bf16[128,384]{1,0:T(8,128)(2,1)S(1)} %get-tuple-element.92), channel_id=1, source_target_pairs={{0,2},{1,3},{2,0},{3,1},{4,6},{5,7},{6,4},{7,5},{8,10},{9,11},{10,... | collective-permute-start | bytes 294920 | tf_op jit(solution)/shard_map/ppermute | solution.py:425
  125.9 6.9 %collective-permute-start.45 = (bf16[128,384]{1,0:T(8,128)(2,1)S(1)}, bf16[128,384]{1,0:T(8,128)(2,1)S(1)}, u32[]{:S(2)}, u32[]{:S(2)}) collective-permute-start(bf16[128,384]{1,0:T(8,128)(2,1)S(1)} %get-tuple-element.92), channel_id=1, source_target_pairs={{0,4},{1,5},{2,6},{3,7},{4,0},{5,1},{6,2},{7,3},{8,12},{9,13},{10,... | collective-permute-start | bytes 294920 | tf_op jit(solution)/shard_map/ppermute | solution.py:425
  129.2 14.6 %collective-permute-start.48 = (bf16[192,768]{1,0:T(8,128)(2,1)S(1)}, bf16[192,768]{1,0:T(8,128)(2,1)S(1)}, u32[]{:S(2)}, u32[]{:S(2)}) collective-permute-start(bf16[192,768]{1,0:T(8,128)(2,1)S(1)} %get-tuple-element.108), channel_id=1, source_target_pairs={{0,2},{1,3},{2,0},{3,1},{4,6},{5,7},{6,4},{7,5},{8,10},{9,11},{10,... | collective-permute-start | bytes 884744 | tf_op jit(solution)/shard_map/ppermute | solution.py:425
  130.4 14.9 %collective-permute-start.49 = (bf16[192,768]{1,0:T(8,128)(2,1)S(1)}, bf16[192,768]{1,0:T(8,128)(2,1)S(1)}, u32[]{:S(2)}, u32[]{:S(2)}) collective-permute-start(bf16[192,768]{1,0:T(8,128)(2,1)S(1)} %get-tuple-element.109), channel_id=1, source_target_pairs={{0,4},{1,5},{2,6},{3,7},{4,0},{5,1},{6,2},{7,3},{8,12},{9,13},{10,... | collective-permute-start | bytes 884744 | tf_op jit(solution)/shard_map/ppermute | solution.py:425
  131.6 13.7 %collective-permute-start.50 = (bf16[192,768]{1,0:T(8,128)(2,1)S(1)}, bf16[192,768]{1,0:T(8,128)(2,1)S(1)}, u32[]{:S(2)}, u32[]{:S(2)}) collective-permute-start(bf16[192,768]{1,0:T(8,128)(2,1)S(1)} %get-tuple-element.110), channel_id=1, source_target_pairs={{0,6},{1,7},{2,4},{3,5},{4,2},{5,3},{6,0},{7,1},{8,14},{9,15},{10,... | collective-permute-start | bytes 884744 | tf_op jit(solution)/shard_map/ppermute | solution.py:425
  148.1 34.7 %all-to-all-start.1 = ((bf16[4,208,768]{2,1,0:T(8,128)(2,1)}), bf16[4,208,768]{2,1,0:T(8,128)(2,1)S(1)}, u32[]{:S(2)}, u32[]{:S(2)}) async-start(bf16[4,208,768]{2,1,0:T(8,128)(2,1)} %shard_map.256), calls=%async_computation.1 | async-start | bytes 2555904 | tf_op jit(solution)/shard_map/all_to_all | solution.py:434
  160.9 8.8 %collective-permute-start.54 = (bf16[128,384]{1,0:T(8,128)(2,1)S(1)}, bf16[128,384]{1,0:T(8,128)(2,1)S(1)}, u32[]{:S(2)}, u32[]{:S(2)}) collective-permute-start(bf16[128,384]{1,0:T(8,128)(2,1)S(1)} %add_convert_fusion.1), channel_id=1, source_target_pairs={{0,1},{1,0},{2,3},{3,2},{4,5},{5,4},{6,7},{7,6},{8,9},{9,8},{10,11... | collective-permute-start | bytes 294920 | tf_op jit(solution)/shard_map/ppermute | solution.py:425
  (90 other events, 673.0 us)
